TPU v7x, 32 devices: a whole 2x2x4 slice. The times are simulated.
32 devices in a mesh: grp: 2 (over y), lon: 4 (over z), lat: 4 (over x, core).
Axes of the slice: x: 2, y: 2, z: 4, core: 2. Of those that a mesh axis runs over, the one named last changes fastest.
Arguments:
- state_old: float32 [8, 256, 512], P('grp', 'lat', 'lon'), parts along dimension 0, may hold values from -6 to 6
- state_now: float32 [8, 256, 512], P('grp', 'lat', 'lon'), parts along dimension 0, may hold values from -6 to 6
- drift: float32 [8, 256, 512], P('grp', 'lat', 'lon'), parts along dimension 0, may hold values from -1 to 1
- ocean: int32 [512, 512], P(('grp', 'lat'), 'lon'), parts along dimension 0, may hold values from 0 to 1, as said below
- w_in: bfloat16 [12, 256], replicated, may hold values from -1.75 to 1.75
- w_mid: bfloat16 [256, 256], replicated, may hold values from -0.375 to 0.375
- w_out: bfloat16 [256, 4], replicated, may hold values from -0.375 to 0.375
- cot_mid: float32 [8, 256, 512], P('grp', 'lat', 'lon'), parts along dimension 0, may hold values from -6 to 6
- cot_new: float32 [8, 256, 512], P('grp', 'lat', 'lon'), parts along dimension 0, may hold values from -6 to 6
Outputs:
- state_mid: float32 [8, 256, 512], P('grp', 'lat', 'lon'), parts along dimension 0
- state_new: float32 [8, 256, 512], P('grp', 'lat', 'lon'), parts along dimension 0
- grad_old: float32 [8, 256, 512], P('grp', 'lat', 'lon'), parts along dimension 0
- grad_now: float32 [8, 256, 512], P('grp', 'lat', 'lon'), parts along dimension 0
- grad_in: float32 [24, 256], P('grp'), parts along dimension 0
- grad_mid: float32 [512, 256], P('grp'), parts along dimension 0
- grad_out: float32 [512, 4], P('grp'), parts along dimension 0
There are 2 independent parts, one for each index of `grp`. A program takes and returns all parts, laid end to end along the dimension named above; an argument that names none is the same for every part. Nothing has to cross between parts.
Inputs may be any that keep to these rules, and one draw needn't show every extreme that they name: 1 marks an ocean column, 0 land; land covers whole latitude rows of some blocks.
All inputs are finite; a program needn't handle non-finite values.
Results may differ from a plain program's by a relative error of at most 0.00055.
The roundings to bfloat16 on the way count: a program that leaves them out, or rounds other values in their place, can miss the bound.
Values may be sent and summed in bfloat16 or wider, within the bound.
No kernel may reach another device: no remote copies, remote signals or barrier semaphores. Data moves between devices by JAX's collectives and lax.ppermute only.
A program may use at most 64 MiB of HBM per device.

v0:
```python
import functools

import jax
import jax.numpy as jnp
from jax import lax
from jax.experimental import pallas as pl
from jax.experimental.pallas import tpu as pltpu
from jax.sharding import PartitionSpec as P

KAPPA = 0.2
DT = 0.1
GAIN_GRAD = 10.0

WIDE = 4
LANES = 128
TILES = 8

F32 = jnp.float32
BF16 = jnp.bfloat16


def dot(left, right):
    return lax.dot_general(left, right, (((1,), (0,)), ((), ())), preferred_element_type=F32)


def dot_nt(left, right):
    return lax.dot_general(left, right, (((1,), (1,)), ((), ())), preferred_element_type=F32)


def planes_of(refs, ocean):
    out = []
    for ref in refs:
        for level in range(ref.shape[0]):
            out.append(ref[level])
    out.append(ocean[...].astype(F32))
    return out


def pack_kernel(now, old, drift, cnew, cmid, ocean, west, east, top, bottom):
    rows = ocean.shape[0]
    lane = lax.broadcasted_iota(jnp.int32, (rows, LANES), 1)
    to_west = jnp.zeros((rows, LANES), F32)
    to_east = jnp.zeros((rows, LANES), F32)
    for p, plane in enumerate(planes_of((now, old, drift, cnew, cmid), ocean)):
        here = (lane >= WIDE * p) & (lane < WIDE * (p + 1))
        to_west = jnp.where(here, pltpu.roll(plane, WIDE * p, 1) if p else plane, to_west)
        to_east = jnp.where(here, pltpu.roll(plane, WIDE * (p + 1), 1), to_east)
        top[pl.ds(WIDE * p, WIDE), :] = plane[:WIDE]
        bottom[pl.ds(WIDE * p, WIDE), :] = plane[rows - WIDE :]
    west[...] = to_west
    east[...] = to_east


def east_of(v):
    return pltpu.roll(v, v.shape[1] - 1, 1)


def west_of(v):
    return pltpu.roll(v, 1, 1)


def north_of(v):
    return pltpu.roll(v, v.shape[0] - 1, 0)


def south_of(v):
    return pltpu.roll(v, 1, 0)


def main_kernel(
    now, old, drift, cnew, cmid, ocean, left, right, low, high,
    w_in, w_in_t, w_mid, w_mid_t, w_out, w_out_t,
    o_mid, o_new, o_old, o_now, o_grad,
    planes, ft, fth, ftx, cl, clh, clx, dc, dch, dcx, df, dfh, dfx,
    keep1, keep2, halo1, halo2, acc_mid, acc_in, acc_out,
):
    rows = ocean.shape[0]
    ext = rows + 2 * WIDE
    levels = now.shape[0]
    count = 5 * levels + 1
    chunks = rows // TILES
    span = TILES * LANES
    packs = rows // 16
    near = [rows, ext - 1]
    corner = rows + 2
    first_pack = rows + 3
    far = [rows + 1, ext - 2, rows + 2, ext - 3]
    slots = {near[0]: rows, near[1]: rows + 1}
    for i, r in enumerate(far):
        slots[r] = first_pack + packs + i
    halo_one = 3 + packs
    halo_two = halo_one + 2
    halo_all = halo_one + 4

    lane = lax.broadcasted_iota(jnp.int32, (ext, LANES), 1)
    strips = planes_base = WIDE * count
    left_all = jnp.concatenate([left[...], high[pl.ds(strips, WIDE), :], low[pl.ds(strips, WIDE), :]], 0)
    right_all = jnp.concatenate([right[...], high[pl.ds(strips + WIDE, WIDE), :], low[pl.ds(strips + WIDE, WIDE), :]], 0)
    for p, plane in enumerate(planes_of((now, old, drift, cnew, cmid), ocean)):
        body = jnp.concatenate([plane, high[pl.ds(WIDE * p, WIDE), :], low[pl.ds(WIDE * p, WIDE), :]], 0)
        from_right = pltpu.roll(right_all, LANES - WIDE * p, 1) if p else right_all
        from_left = pltpu.roll(left_all, LANES - WIDE * (p + 1), 1)
        side = jnp.where(lane < WIDE, from_right, jnp.where(lane >= LANES - WIDE, from_left, 0.0))
        planes[p] = jnp.concatenate([body, side], 1)

    def field(which, level):
        return planes[which * levels + level]

    wet = planes[count - 1]

    ft[...] = jnp.zeros_like(ft)
    fth[...] = jnp.zeros_like(fth)
    ftx[...] = jnp.zeros_like(ftx)
    dc[...] = jnp.zeros_like(dc)
    dch[...] = jnp.zeros_like(dch)
    dcx[...] = jnp.zeros_like(dcx)
    acc_mid[...] = jnp.zeros_like(acc_mid)
    acc_in[...] = jnp.zeros_like(acc_in)
    acc_out[...] = jnp.zeros_like(acc_out)

    def spread(plane, index, deep, main, extra, side):
        main[pl.ds(index, rows, stride=deep), :] = plane[:rows, :LANES]
        extra[pl.ds(index, 2 * WIDE, stride=deep), :] = plane[rows:, :LANES]
        side[pl.ds(index, ext, stride=deep), :] = plane[:, LANES:]

    def gathered(index, deep, main, extra, side):
        body = jnp.concatenate(
            [main[pl.ds(index, rows, stride=deep), :], extra[pl.ds(index, 2 * WIDE, stride=deep), :]], 0
        )
        return jnp.concatenate([body, side[pl.ds(index, ext, stride=deep), :]], 1)

    def pack_halo(deep, main, extra, side):
        where = lax.broadcasted_iota(jnp.int32, (deep, LANES), 1)
        for r, slot in slots.items():
            main[pl.ds(slot * deep, deep), :] = extra[pl.ds((r - rows) * deep, deep), :]
        groups = [(first_pack + q, range(16 * q, 16 * q + 16)) for q in range(packs)]
        groups.append((corner, range(rows, ext)))
        for slot, members in groups:
            total = jnp.zeros((deep, LANES), F32)
            for j, r in enumerate(members):
                moved = pltpu.roll(side[pl.ds(r * deep, deep), :], (2 * WIDE * j + WIDE) % LANES, 1)
                total = jnp.where((where >= 2 * WIDE * j) & (where < 2 * WIDE * (j + 1)), moved, total)
            main[pl.ds(slot * deep, deep), :] = total

    def unpack_halo(deep, main, extra, side, live):
        for r, slot in slots.items():
            if slot < rows + live:
                extra[pl.ds((r - rows) * deep, deep), :] = main[pl.ds(slot * deep, deep), :]
        groups = [(first_pack + q, range(16 * q, 16 * q + 16)) for q in range(packs)]
        groups.append((corner, range(rows, ext)))
        for slot, members in groups:
            tile = main[pl.ds(slot * deep, deep), :]
            for j, r in enumerate(members):
                side[pl.ds(r * deep, deep), :] = pltpu.roll(tile, LANES - (2 * WIDE * j + WIDE) % LANES, 1)

    def lanes_of(ref, deep, base, tiles):
        block = ref[pl.ds(base * deep, tiles * deep), :]
        return jnp.concatenate([block[k * deep : (k + 1) * deep] for k in range(tiles)], 1)

    def put_lanes(ref, deep, base, tiles, value):
        for k in range(tiles):
            ref[pl.ds((base + k) * deep, deep), :] = value[:, k * LANES : (k + 1) * LANES]

    def inputs_at(base, tiles):
        return lanes_of(ft, 16, base, tiles).astype(BF16)

    def cotangents_at(base, tiles):
        part = lanes_of(dc, 8, base, tiles)
        return jnp.concatenate([part, jnp.zeros_like(part)], 0).astype(BF16)

    def forward(x):
        first = jnp.tanh(dot(w_in_t[...], x))
        second = jnp.tanh(dot(w_mid_t[...], first.astype(BF16)))
        return first, second

    def closure(second):
        return dot(w_out_t[...], second.astype(BF16)).astype(BF16).astype(F32)[:8]

    def backward(first, second, cot):
        dz_two = (dot(w_out[...], cot) * (1.0 - second * second)).astype(BF16)
        dz_one = (dot(w_mid[...], dz_two) * (1.0 - first * first)).astype(BF16)
        dfeat = dot(w_in[...], dz_one).astype(BF16).astype(F32)
        return dz_one, dz_two, dfeat

    def add_terms(x, first, second, cot, dz_one, dz_two):
        acc_mid[...] += dot_nt(first.astype(BF16), dz_two)
        acc_in[...] += dot_nt(x, dz_one)
        acc_out[...] += dot_nt(cot, second.astype(BF16))

    def features_from(values):
        for level, v in enumerate(values):
            slope_x = 0.5 * (east_of(v) - west_of(v))
            slope_y = 0.5 * (north_of(v) - south_of(v))
            spread(v, level, 16, ft, ftx, fth)
            spread(slope_x, levels + level, 16, ft, ftx, fth)
            spread(slope_y, 2 * levels + level, 16, ft, ftx, fth)
        pack_halo(16, ft, ftx, fth)

    def force(v, velocity, closed):
        eastward, westward, northward, southward = east_of(v), west_of(v), north_of(v), south_of(v)
        laplace = eastward + westward + northward + southward - 4.0 * v
        return wet_like(v) * (KAPPA * laplace - velocity * (0.5 * (eastward - westward)) + closed)

    def wet_like(v):
        return planes[count - 1]

    features_from([field(0, level) for level in range(levels)])

    def first_step(c, carry):
        base = pl.multiple_of(c * TILES, TILES)
        x = inputs_at(base, TILES)
        first, second = forward(x)
        keep1[c] = first
        keep2[c] = second
        put_lanes(cl, 8, base, TILES, closure(second))
        return carry

    lax.fori_loop(0, chunks, first_step, 0)
    first, second = forward(inputs_at(rows, halo_all))
    halo1[...] = first
    halo2[...] = second
    put_lanes(cl, 8, rows, halo_all, closure(second))
    unpack_halo(8, cl, clx, clh, halo_all)
    mids = []
    for level in range(levels):
        closed = gathered(level, 8, cl, clx, clh)
        mid = field(1, level) + 2.0 * DT * force(field(0, level), field(2, level), closed)
        o_mid[level] = mid[:rows, :LANES]
        mids.append(mid)

    features_from(mids)
    for level in range(levels):
        spread(wet * (2.0 * DT * field(3, level)), level, 8, dc, dcx, dch)
    pack_halo(8, dc, dcx, dch)

    def second_step(c, carry):
        base = pl.multiple_of(c * TILES, TILES)
        x = inputs_at(base, TILES)
        cot = cotangents_at(base, TILES)
        first, second = forward(x)
        put_lanes(cl, 8, base, TILES, closure(second))
        dz_one, dz_two, dfeat = backward(first, second, cot)
        put_lanes(df, 16, base, TILES, dfeat)
        add_terms(x, first, second, cot, dz_one, dz_two)
        return carry

    lax.fori_loop(0, chunks, second_step, 0)
    first, second = forward(inputs_at(rows, halo_two))
    unused_one, unused_two, dfeat = backward(first, second, cotangents_at(rows, halo_two))
    put_lanes(df, 16, rows, halo_two, dfeat)
    unpack_halo(16, df, dfx, dfh, halo_two)
    for level in range(levels):
        mid = mids[level]
        velocity = field(2, level)
        closed = cl[pl.ds(level, rows, stride=8), :]
        eastward, westward, northward, southward = east_of(mid), west_of(mid), north_of(mid), south_of(mid)
        laplace = (eastward + westward + northward + southward - 4.0 * mid)[:rows, :LANES]
        slope = (0.5 * (eastward - westward))[:rows, :LANES]
        total = wet[:rows, :LANES] * (KAPPA * laplace - velocity[:rows, :LANES] * slope + closed)
        o_new[level] = now[level] + 2.0 * DT * total

    def adjoint_planes(weighted, level):
        masked = wet * weighted
        carried = field(2, level) * masked
        a0 = gathered(level, 16, df, dfx, dfh)
        a1 = gathered(levels + level, 16, df, dfx, dfh)
        a2 = gathered(2 * levels + level, 16, df, dfx, dfh)
        result = KAPPA * (east_of(masked) + west_of(masked) + north_of(masked) + south_of(masked) - 4.0 * masked)
        result = result + 0.5 * (east_of(carried) - west_of(carried)) + a0
        return result - 0.5 * (east_of(a1) - west_of(a1)) - 0.5 * (north_of(a2) - south_of(a2))

    olds = []
    for level in range(levels):
        grad = field(4, level) + adjoint_planes(2.0 * DT * field(3, level), level)
        o_old[level] = grad[:rows, :LANES]
        olds.append(grad)
    for level in range(levels):
        spread(wet * (2.0 * DT * olds[level]), level, 8, dc, dcx, dch)
    pack_halo(8, dc, dcx, dch)
    features_again([field(0, level) for level in range(levels)], levels, spread, ft, ftx, fth)

    def third_step(c, carry):
        base = pl.multiple_of(c * TILES, TILES)
        x = inputs_at(base, TILES)
        cot = cotangents_at(base, TILES)
        first = keep1[c]
        second = keep2[c]
        dz_one, dz_two, dfeat = backward(first, second, cot)
        put_lanes(df, 16, base, TILES, dfeat)
        add_terms(x, first, second, cot, dz_one, dz_two)
        return carry

    lax.fori_loop(0, chunks, third_step, 0)
    near_lanes = halo_one * LANES
    unused_one, unused_two, dfeat = backward(
        halo1[:, :near_lanes], halo2[:, :near_lanes], cotangents_at(rows, halo_one)
    )
    put_lanes(df, 16, rows, halo_one, dfeat)
    unpack_halo(16, df, dfx, dfh, halo_one)
    for level in range(levels):
        grad = adjoint_planes(2.0 * DT * olds[level], level)
        o_now[level] = cnew[level] + grad[:rows, :LANES]

    hidden = acc_mid.shape[0]
    o_grad[...] = jnp.zeros_like(o_grad)
    start = 0
    for acc in (acc_mid, acc_in, acc_out):
        deep = acc.shape[0]
        for half in range(hidden // LANES):
            o_grad[pl.ds(start, deep), :] = acc[:, half * LANES : (half + 1) * LANES]
            start += deep


def features_again(values, levels, spread, ft, ftx, fth):
    for level, v in enumerate(values):
        spread(v, level, 16, ft, ftx, fth)
        spread(0.5 * (east_of(v) - west_of(v)), levels + level, 16, ft, ftx, fth)
        spread(0.5 * (north_of(v) - south_of(v)), 2 * levels + level, 16, ft, ftx, fth)


def along(value, axis, step, periodic):
    count = lax.axis_size(axis)
    pairs = [(i, (i + step) % count) for i in range(count) if periodic or 0 <= i + step < count]
    return lax.ppermute(value, axis, pairs)


def body(state_old, state_now, drift, ocean, w_in, w_mid, w_out, cot_mid, cot_new):
    levels, rows, cols = state_now.shape
    width_in, hidden = w_in.shape
    ext = rows + 2 * WIDE
    count = 5 * levels + 1
    fields = (state_now, state_old, drift, cot_new, cot_mid, ocean)
    vmem = pl.BlockSpec(memory_space=pltpu.VMEM)
    strip = jax.ShapeDtypeStruct((rows, LANES), F32)
    edge = jax.ShapeDtypeStruct((WIDE * count, LANES), F32)
    west, east, top, bottom = pl.pallas_call(
        pack_kernel,
        out_shape=(strip, strip, edge, edge),
        in_specs=[vmem] * 6,
        out_specs=(vmem,) * 4,
        compiler_params=pltpu.CompilerParams(vmem_limit_bytes=32 * 2**20),
    )(*fields)
    left = along(east, "lon", 1, True)
    right = along(west, "lon", -1, True)
    up = jnp.concatenate([bottom, left[rows - WIDE :], right[rows - WIDE :]], 0)
    down = jnp.concatenate([top, left[:WIDE], right[:WIDE]], 0)
    low = along(up, "lat", 1, False)
    high = along(down, "lat", -1, False)

    in_pad = jnp.pad(w_in, ((0, 16 - width_in), (0, 0)))
    out_pad = jnp.pad(w_out, ((0, 0), (0, 16 - levels)))
    weights = (in_pad, in_pad.T, w_mid, w_mid.T, out_pad, out_pad.T)

    members = lax.axis_size("lon") * lax.axis_size("lat")
    used = (hidden // LANES) * (hidden + 32)
    piece = -(-used // (8 * members)) * 8
    field = jax.ShapeDtypeStruct((levels, rows, cols), F32)
    packs = rows // 16
    slots = rows + 7 + packs
    chunks = rows // TILES
    span = TILES * LANES
    halo = (7 + packs) * LANES
    state_mid, state_new, grad_old, grad_now, terms = pl.pallas_call(
        main_kernel,
        out_shape=(field, field, field, field, jax.ShapeDtypeStruct((piece * members, LANES), F32)),
        in_specs=[vmem] * 16,
        out_specs=(vmem,) * 5,
        scratch_shapes=[
            pltpu.VMEM((count, ext, 2 * LANES), F32),
            pltpu.VMEM((slots * 16, LANES), F32),
            pltpu.VMEM((ext * 16, LANES), F32),
            pltpu.VMEM((2 * WIDE * 16, LANES), F32),
            pltpu.VMEM((slots * 8, LANES), F32),
            pltpu.VMEM((ext * 8, LANES), F32),
            pltpu.VMEM((2 * WIDE * 8, LANES), F32),
            pltpu.VMEM((slots * 8, LANES), F32),
            pltpu.VMEM((ext * 8, LANES), F32),
            pltpu.VMEM((2 * WIDE * 8, LANES), F32),
            pltpu.VMEM((slots * 16, LANES), F32),
            pltpu.VMEM((ext * 16, LANES), F32),
            pltpu.VMEM((2 * WIDE * 16, LANES), F32),
            pltpu.VMEM((chunks, hidden, span), F32),
            pltpu.VMEM((chunks, hidden, span), F32),
            pltpu.VMEM((hidden, halo), F32),
            pltpu.VMEM((hidden, halo), F32),
            pltpu.VMEM((hidden, hidden), F32),
            pltpu.VMEM((16, hidden), F32),
            pltpu.VMEM((16, hidden), F32),
        ],
        compiler_params=pltpu.CompilerParams(vmem_limit_bytes=56 * 2**20),
    )(*fields, left, right, low, high, *weights)

    pieces = lax.all_to_all(terms.reshape(members, piece, LANES), ("lon", "lat"), 0, 0)
    cells_all = rows * lax.axis_size("lat") * cols * lax.axis_size("lon")
    factor = GAIN_GRAD / jnp.sqrt(jnp.float32(cells_all))
    own = jnp.sum(pieces, 0) * factor
    spread = jnp.broadcast_to(own[None], (members, piece, LANES))
    summed = lax.all_to_all(spread, ("lon", "lat"), 0, 0).reshape(members * piece, LANES)
    halves = hidden // LANES
    parts = []
    start = 0
    for deep in (hidden, 16, 16):
        block = summed[start : start + halves * deep].reshape(halves, deep, LANES)
        parts.append(jnp.swapaxes(block, 0, 1).reshape(deep, hidden))
        start += halves * deep
    return (
        state_mid,
        state_new,
        grad_old,
        grad_now,
        parts[1][:width_in],
        parts[0],
        parts[2][:levels].T,
    )


def solution(mesh):
    field = P("grp", "lat", "lon")
    whole = P("grp", None)
    in_specs = (field, field, field, P(("grp", "lat"), "lon"), P(), P(), P(), field, field)
    out_specs = (field, field, field, field, whole, whole, whole)
    return jax.shard_map(body, mesh=mesh, in_specs=in_specs, out_specs=out_specs, check_vma=False)
```

profile of v0, /device:TPU:0, one launch (start us, length us, event | category | flops | bytes accessed | tf_op | source)
XLA Modules:
  0.0 90.5 jit_solution(6898161736153455224)
XLA Ops:
  0.6 0.0 copy-start
  0.6 0.9 copy-done
  1.5 0.0 copy-start.1
  1.5 0.9 copy-done.1
  2.4 0.0 copy-start.2
  2.4 0.9 copy-done.2
  3.3 0.0 copy-start.3
  3.4 0.9 copy-done.3
  4.3 0.0 copy-start.4
  4.3 0.9 copy-done.4
  5.2 0.0 copy-start.5
  5.2 0.8 copy-done.5
  5.9 0.0 copy-start.11
  5.9 0.4 shard_map.144
  6.3 3.1 %collective-permute-start = (f32[64,128]{1,0:T(8,128)S(1)}, f32[64,128]{1,0:T(8,128)S(1)}, u32[]{:S(2)}, u32[]{:S(2)}) collective-permute-start(f32[64,128]{1,0:T(8,128)S(1)} %get-tuple-element.16), channel_id=1, source_target_pairs={{0,4},{4,8},{8,12},{12,0},{1,5},{5,9},{9,13},{13,1},{2,6},{6,10},{... | collective-permute-start | bytes 98312 | tf_op jit(solution)/shard_map/ppermute | solution.py:324
  9.4 2.1 %collective-permute-start.1 = (f32[64,128]{1,0:T(8,128)S(1)}, f32[64,128]{1,0:T(8,128)S(1)}, u32[]{:S(2)}, u32[]{:S(2)}) collective-permute-start(f32[64,128]{1,0:T(8,128)S(1)} %get-tuple-element.17), channel_id=1, source_target_pairs={{0,12},{4,0},{8,4},{12,8},{1,13},{5,1},{9,5},{13,9},{2,14},{6,2},{... | collective-permute-start | bytes 98312 | tf_op jit(solution)/shard_map/ppermute | solution.py:324
  11.5 0.0 copy-done.11
  11.5 0.1 copy.24
  11.6 0.6 pad_bitcast_fusion.1.w_in_t
  12.3 1.2 %collective-permute-done.left = f32[64,128]{1,0:T(8,128)S(1)} collective-permute-done((f32[64,128]{1,0:T(8,128)S(1)}, f32[64,128]{1,0:T(8,128)S(1)}, u32[]{:S(2)}, u32[]{:S(2)}) %collective-permute-start) | collective-permute-done | bytes 32800 | tf_op jit(solution)/shard_map/ppermute | solution.py:324
  13.4 0.0 copy-start.9
  13.4 0.2 collective-permute-done.1.right
  13.7 0.0 copy-start.10
  13.7 0.3 copy-done.9
  14.0 0.2 copy-done.10
  14.3 1.3 %collective-permute-start.2 = (f32[92,128]{1,0:T(8,128)S(1)}, f32[92,128]{1,0:T(8,128)S(1)}, u32[]{:S(2)}, u32[]{:S(2)}) collective-permute-start(f32[92,128]{1,0:T(8,128)S(1)} %pad_maximum_fusion), channel_id=1, source_target_pairs={{0,1},{1,2},{2,3},{4,5},{5,6},{6,7},{8,9},{9,10},{10,11},{12,13},{... | collective-permute-start | bytes 141320 | tf_op jit(solution)/shard_map/ppermute | solution.py:324
  15.6 0.0 copy-start.12
  15.6 1.3 %collective-permute-start.3 = (f32[92,128]{1,0:T(8,128)S(1)}, f32[92,128]{1,0:T(8,128)S(1)}, u32[]{:S(2)}, u32[]{:S(2)}) collective-permute-start(f32[92,128]{1,0:T(8,128)S(1)} %pad_maximum_fusion.1), channel_id=1, source_target_pairs={{1,0},{2,1},{3,2},{5,4},{6,5},{7,6},{9,8},{10,9},{11,10},{13,12},{... | collective-permute-start | bytes 141320 | tf_op jit(solution)/shard_map/ppermute | solution.py:324
  16.9 0.0 copy-done.12
  16.9 0.6 pad_bitcast_fusion.w_out_t
  17.5 0.0 copy-start.6
  17.5 0.1 copy.32
  17.6 0.2 copy.33
  17.8 0.6 pad.8.clone.w_in
  18.4 0.6 pad.9.clone.w_out
  19.0 0.0 copy-done.6
  19.0 0.8 copy.25
  19.8 0.0 collective-permute-done.2.low
  19.8 0.0 copy-start.7
  19.8 0.7 collective-permute-done.3.high
  20.5 0.0 copy-start.8
  20.5 0.0 copy-done.7
  20.5 0.6 copy-done.8
  21.1 33.6 %shard_map.145 = (f32[4,64,128]{2,1,0:T(8,128)}, f32[4,64,128]{2,1,0:T(8,128)}, f32[4,64,128]{2,1,0:T(8,128)}, f32[4,64,128]{2,1,0:T(8,128)}, f32[640,128]{1,0:T(8,128)}) custom-call(f32[4,64,128]{2,1,0:T(8,128)} %now.3, f32[4,64,128]{2,1,0:T(8,128)} %old.3, f32[4,64,128]{2,1,0:T(8,128)} %drift.3, f32[4,64,128]{2,1,0:T(8,128)} %cnew.3, f32[4,64,128]{2,1,0:T(8,128)} %cmid.3, ...), custom_call_target="tpu_custom_call" | custom-call | tf_op jit(solution)/shard_map/pallas_call | solution.py:363
  54.7 19.4 %all_to_all.10 = f32[16,40,128]{2,1,0:T(8,128)S(1)} all-to-all(f32[16,40,128]{2,1,0:T(8,128)} %bitcast.30), channel_id=1, replica_groups=mesh['grp'=2,'lon'=4,'lat'=4] {'lon','lat'}, dimensions={0} | all-to-all | bytes 655360 | tf_op jit(solution)/shard_map/all_to_all | solution.py:393
  74.2 14.1 %all_to_all.11 = f32[16,40,128]{2,1,0:T(8,128)S(1)} all-to-all(f32[16,40,128]{2,1,0:T(8,128)S(1)} %broadcast_in_dim.2), channel_id=1, replica_groups=mesh['grp'=2,'lon'=4,'lat'=4] {'lon','lat'}, dimensions={0} | all-to-all | bytes 655360 | tf_op jit(solution)/shard_map/all_to_all | solution.py:398
  88.4 0.1 copy.29
  88.5 0.8 copy.30
  89.3 0.6 slice_bitcast_fusion
  89.9 0.6 copy.31
  (11 shorter events, 0.1 us)
Async XLA Ops:
  0.6 0.9 %copy-start = (f32[4,64,128]{2,1,0:T(8,128)S(1)}, f32[4,64,128]{2,1,0:T(8,128)}, u32[]{:S(2)}) copy-start(f32[4,64,128]{2,1,0:T(8,128)} %now.3) | copy-start | bytes 393220
  1.5 0.9 copy-start.1
  2.4 0.9 copy-start.2
  3.3 0.9 copy-start.3
  4.3 0.9 copy-start.4
  5.2 0.8 copy-start.5
  5.9 5.6 %copy-start.11 = (bf16[12,256]{1,0:T(8,128)(2,1)S(1)}, bf16[12,256]{1,0:T(8,128)(2,1)}, u32[]{:S(2)}) copy-start(bf16[12,256]{1,0:T(8,128)(2,1)} %param.13) | copy-start | bytes 18436
  6.3 7.1 %collective-permute-start = (f32[64,128]{1,0:T(8,128)S(1)}, f32[64,128]{1,0:T(8,128)S(1)}, u32[]{:S(2)}, u32[]{:S(2)}) collective-permute-start(f32[64,128]{1,0:T(8,128)S(1)} %get-tuple-element.16), channel_id=1, source_target_pairs={{0,4},{4,8},{8,12},{12,0},{1,5},{5,9},{9,13},{13,1},{2,6},{6,10},{... | collective-permute-start | bytes 98312 | tf_op jit(solution)/shard_map/ppermute | solution.py:324
  9.4 4.3 %collective-permute-start.1 = (f32[64,128]{1,0:T(8,128)S(1)}, f32[64,128]{1,0:T(8,128)S(1)}, u32[]{:S(2)}, u32[]{:S(2)}) collective-permute-start(f32[64,128]{1,0:T(8,128)S(1)} %get-tuple-element.17), channel_id=1, source_target_pairs={{0,12},{4,0},{8,4},{12,8},{1,13},{5,1},{9,5},{13,9},{2,14},{6,2},{... | collective-permute-start | bytes 98312 | tf_op jit(solution)/shard_map/ppermute | solution.py:324
  13.4 0.6 copy-start.9
  13.7 0.6 copy-start.10
  14.3 5.5 %collective-permute-start.2 = (f32[92,128]{1,0:T(8,128)S(1)}, f32[92,128]{1,0:T(8,128)S(1)}, u32[]{:S(2)}, u32[]{:S(2)}) collective-permute-start(f32[92,128]{1,0:T(8,128)S(1)} %pad_maximum_fusion), channel_id=1, source_target_pairs={{0,1},{1,2},{2,3},{4,5},{5,6},{6,7},{8,9},{9,10},{10,11},{12,13},{... | collective-permute-start | bytes 141320 | tf_op jit(solution)/shard_map/ppermute | solution.py:324
  15.6 1.3 %copy-start.12 = (bf16[256,4]{0,1:T(4,128)(2,1)S(1)}, bf16[256,4]{0,1:T(4,128)(2,1)}, u32[]{:S(2)}) copy-start(bf16[256,4]{0,1:T(4,128)(2,1)} %param.15) | copy-start | bytes 6148
  15.6 4.8 %collective-permute-start.3 = (f32[92,128]{1,0:T(8,128)S(1)}, f32[92,128]{1,0:T(8,128)S(1)}, u32[]{:S(2)}, u32[]{:S(2)}) collective-permute-start(f32[92,128]{1,0:T(8,128)S(1)} %pad_maximum_fusion.1), channel_id=1, source_target_pairs={{1,0},{2,1},{3,2},{5,4},{6,5},{7,6},{9,8},{10,9},{11,10},{13,12},{... | collective-permute-start | bytes 141320 | tf_op jit(solution)/shard_map/ppermute | solution.py:324
  17.5 1.5 %copy-start.6 = (bf16[256,256]{1,0:T(8,128)(2,1)S(1)}, bf16[256,256]{1,0:T(8,128)(2,1)}, u32[]{:S(2)}) copy-start(bf16[256,256]{1,0:T(8,128)(2,1)} %w_mid.1) | copy-start | bytes 393220
  19.8 0.7 copy-start.7
  20.5 0.6 copy-start.8
where the time goes:
time: 91 us; the launch traced here: 90.5 us
  Pallas kernels  34.1 us (37%)
  blocking collectives  33.5 us (37%)
  local copies, waits for them, and re-layouts  12.3 us (14%)
  starting transfers between devices  7.74 us (9%)
  waiting for transfers between devices  2.08 us (2%)
    pallas_call x1, Pallas kernels, body(): pl.pallas_call(main_kernel, out_shape=(field, field, field, field, jax.Sh...  33.6 us
    all_to_all x1, blocking collectives, body(): lax.all_to_all(terms.reshape(members, piece, LANES), ('lon', 'lat'), 0, 0)  19.4 us
    all_to_all x1, blocking collectives, body(): lax.all_to_all(spread, ('lon', 'lat'), 0, 0).reshape(members * piece, LANES)  14.1 us
    unnamed x33, local copies, waits for them, and re-layouts  9.07 us
    ppermute x4, starting transfers between devices, along(): return lax.ppermute(value, axis, pairs)  7.74 us
    ppermute x4, waiting for transfers between devices, along(): return lax.ppermute(value, axis, pairs)  2.08 us
  transfers between devices with their start and end apart: 4, of which 3 were waited for; matrix products, arithmetic and copies ran while one was open for 4% of the time, Pallas kernels for 0%

commit v1 on v0

v1 whole, which is shorter than its diff:
```python
import functools

import jax
import jax.numpy as jnp
from jax import lax
from jax.experimental import pallas as pl
from jax.experimental.pallas import tpu as pltpu
from jax.sharding import PartitionSpec as P

KAPPA = 0.2
DT = 0.1
GAIN_GRAD = 10.0

WIDE = 4
LANES = 128
TILES = 8
DEEP = 16
SHALLOW = 8

F32 = jnp.float32
BF16 = jnp.bfloat16


def dot(left, right):
    return lax.dot_general(left, right, (((1,), (0,)), ((), ())), preferred_element_type=F32)


def dot_nt(left, right):
    return lax.dot_general(left, right, (((1,), (1,)), ((), ())), preferred_element_type=F32)


def pack_kernel(now, old, drift, cnew, cmid, ocean, west, east, top, bottom, fields, wet, sems):
    levels, rows, cols = now.shape
    copies = [
        pltpu.make_async_copy(ref, fields.at[pl.ds(levels * f, levels)], sems.at[f])
        for f, ref in enumerate((now, old, drift, cnew, cmid))
    ]
    copies.append(pltpu.make_async_copy(ocean, wet, sems.at[5]))
    for copy in copies:
        copy.start()
    for copy in copies:
        copy.wait()
    count = 5 * levels
    fields[count] = wet[...].astype(F32)
    lane = lax.broadcasted_iota(jnp.int32, (rows, LANES), 1)
    west[...] = jnp.zeros_like(west)
    east[...] = jnp.zeros_like(east)

    def one_plane(p, carry):
        plane = fields[p]
        here = (lane >= WIDE * p) & (lane < WIDE * (p + 1))
        west[...] = jnp.where(here, pltpu.roll(plane, WIDE * p, 1), west[...])
        east[...] = jnp.where(here, pltpu.roll(plane, WIDE * (p + 1), 1), east[...])
        top[p] = plane[:WIDE]
        bottom[p] = plane[rows - WIDE :]
        return carry

    lax.fori_loop(0, count + 1, one_plane, 0)


def east_of(v):
    return pltpu.roll(v, v.shape[1] - 1, 1)


def west_of(v):
    return pltpu.roll(v, 1, 1)


def north_of(v):
    return pltpu.roll(v, v.shape[0] - 1, 0)


def south_of(v):
    return pltpu.roll(v, 1, 0)


def main_kernel(
    fields, left, right, low, high, w_in, w_mid, w_out_t,
    o_mid, o_new, o_old, o_now, o_grad,
    planes, mids, olds, ft1, ft2, fth, ftx, cl, clh, clx, dc, dch, dcx, df, dfh, dfx,
    keep1, keep2, acc_mid, acc_in, acc_out, wi, wi_t, wm_t, wo, wo_t,
):
    levels, rows, cols = o_mid.shape
    width_in, hidden = w_in.shape
    count = 5 * levels + 1
    ext = rows + 2 * WIDE
    chunks = rows // TILES
    packs = -(-ext // 16)
    order = [rows, ext - 1] + [None] * packs + [rows + 1, ext - 2, rows + 2, ext - 3]
    first_pack = rows + 2
    halo_one = 2 + packs
    halo_two = halo_one + 2

    spare = jnp.zeros((DEEP - width_in, hidden), F32)
    wide_in = jnp.concatenate([w_in[...].astype(F32), spare], 0)
    wi[...] = wide_in.astype(BF16)
    wi_t[...] = wide_in.T.astype(BF16)
    wm_t[...] = w_mid[...].astype(F32).T.astype(BF16)
    spare = jnp.zeros((DEEP - levels, hidden), F32)
    wide_out = jnp.concatenate([w_out_t[...].astype(F32), spare], 0)
    wo_t[...] = wide_out.astype(BF16)
    wo[...] = wide_out.T.astype(BF16)

    lane = lax.broadcasted_iota(jnp.int32, (ext, LANES), 1)
    left_all = jnp.concatenate([left[...], high[count], low[count]], 0)
    right_all = jnp.concatenate([right[...], high[count + 1], low[count + 1]], 0)

    def one_plane(p, carry):
        from_right = pltpu.roll(right_all, LANES - WIDE * p, 1)
        from_left = pltpu.roll(left_all, LANES - WIDE * (p + 1), 1)
        side = jnp.where(lane < WIDE, from_right, jnp.where(lane >= LANES - WIDE, from_left, 0.0))
        planes[p, :, pl.ds(0, LANES)] = jnp.concatenate([fields[p], high[p], low[p]], 0)
        planes[p, :, pl.ds(LANES, LANES)] = side
        return carry

    lax.fori_loop(0, count, one_plane, 0)

    for ref in (ft1, ft2, fth, ftx, dc, dch, dcx, acc_mid, acc_in, acc_out):
        ref[...] = jnp.zeros_like(ref)

    def spread(plane, index, deep, main, extra, side):
        main[pl.ds(index, rows, stride=deep), :] = plane[:rows, :LANES]
        extra[pl.ds(index, 2 * WIDE, stride=deep), :] = plane[rows:, :LANES]
        side[pl.ds(index, ext, stride=deep), :] = plane[:, LANES:]

    def gathered(index, deep, main, extra, side):
        body = jnp.concatenate(
            [main[pl.ds(index, rows, stride=deep), :], extra[pl.ds(index, 2 * WIDE, stride=deep), :]], 0
        )
        return jnp.concatenate([body, side[pl.ds(index, ext, stride=deep), :]], 1)

    def pack_halo(deep, main, extra, side):
        where = lax.broadcasted_iota(jnp.int32, (deep, LANES), 1)
        for i, r in enumerate(order):
            if r is not None:
                main[pl.ds((rows + i) * deep, deep), :] = extra[pl.ds((r - rows) * deep, deep), :]

        def one_pack(q, carry):
            total = jnp.zeros((deep, LANES), F32)
            for j in range(16):
                moved = side[pl.ds(pl.multiple_of((16 * q + j) * deep, deep), deep), :]
                moved = pltpu.roll(moved, (2 * WIDE * j + WIDE) % LANES, 1)
                total = jnp.where((where >= 2 * WIDE * j) & (where < 2 * WIDE * (j + 1)), moved, total)
            main[pl.ds(pl.multiple_of((first_pack + q) * deep, deep), deep), :] = total
            return carry

        lax.fori_loop(0, packs, one_pack, 0)

    def unpack_halo(deep, main, extra, side, live):
        for i, r in enumerate(order[:live]):
            if r is not None:
                extra[pl.ds((r - rows) * deep, deep), :] = main[pl.ds((rows + i) * deep, deep), :]

        def one_pack(q, carry):
            tile = main[pl.ds(pl.multiple_of((first_pack + q) * deep, deep), deep), :]
            for j in range(16):
                moved = pltpu.roll(tile, LANES - (2 * WIDE * j + WIDE) % LANES, 1)
                side[pl.ds(pl.multiple_of((16 * q + j) * deep, deep), deep), :] = moved
            return carry

        lax.fori_loop(0, packs, one_pack, 0)

    def lanes_of(ref, deep, base, tiles):
        block = ref[pl.ds(base * deep, tiles * deep), :]
        return jnp.concatenate([block[k * deep : (k + 1) * deep] for k in range(tiles)], 1)

    def put_lanes(ref, deep, base, tiles, value):
        for k in range(tiles):
            ref[pl.ds((base + k) * deep, deep), :] = value[:, k * LANES : (k + 1) * LANES]

    def inputs_at(ref, base, tiles):
        return lanes_of(ref, DEEP, base, tiles).astype(BF16)

    def cotangents_at(base, tiles):
        part = lanes_of(dc, SHALLOW, base, tiles)
        return jnp.concatenate([part, jnp.zeros_like(part)], 0).astype(BF16)

    def forward(x):
        first = jnp.tanh(dot(wi_t[...], x))
        second = jnp.tanh(dot(wm_t[...], first.astype(BF16)))
        return first, second

    def closure(second):
        return dot(wo_t[...], second.astype(BF16)).astype(BF16).astype(F32)[:SHALLOW]

    def backward(first, second, cot):
        dz_two = (dot(wo[...], cot) * (1.0 - second * second)).astype(BF16)
        dz_one = (dot(w_mid[...], dz_two) * (1.0 - first * first)).astype(BF16)
        dfeat = dot(wi[...], dz_one).astype(BF16).astype(F32)
        return dz_one, dz_two, dfeat

    def add_terms(x, first, second, cot, dz_one, dz_two):
        acc_mid[...] += dot_nt(first.astype(BF16), dz_two)
        acc_in[...] += dot_nt(x, dz_one)
        acc_out[...] += dot_nt(cot, second.astype(BF16))

    def features_of(source, ft):
        def one_level(level, carry):
            v = source[level]
            spread(v, level, DEEP, ft, ftx, fth)
            spread(0.5 * (east_of(v) - west_of(v)), levels + level, DEEP, ft, ftx, fth)
            spread(0.5 * (north_of(v) - south_of(v)), 2 * levels + level, DEEP, ft, ftx, fth)
            return carry

        lax.fori_loop(0, levels, one_level, 0)
        pack_halo(DEEP, ft, ftx, fth)

    def cotangents_of(source, offset):
        def one_level(level, carry):
            spread(planes[count - 1] * (2.0 * DT * source[offset + level]), level, SHALLOW, dc, dcx, dch)
            return carry

        lax.fori_loop(0, levels, one_level, 0)
        pack_halo(SHALLOW, dc, dcx, dch)

    def force(v, level, closed):
        eastward, westward, northward, southward = east_of(v), west_of(v), north_of(v), south_of(v)
        laplace = eastward + westward + northward + southward - 4.0 * v
        slope = 0.5 * (eastward - westward)
        return planes[count - 1] * (KAPPA * laplace - planes[2 * levels + level] * slope + closed)

    features_of(planes, ft1)

    def first_step(c, carry):
        base = pl.multiple_of(c * TILES, TILES)
        first, second = forward(inputs_at(ft1, base, TILES))
        keep1[c] = first
        keep2[c] = second
        put_lanes(cl, SHALLOW, base, TILES, closure(second))
        return carry

    lax.fori_loop(0, keep1.shape[0], first_step, 0)
    unpack_halo(SHALLOW, cl, clx, clh, len(order))

    def first_state(level, carry):
        closed = gathered(level, SHALLOW, cl, clx, clh)
        mid = planes[levels + level] + 2.0 * DT * force(planes[level], level, closed)
        o_mid[level] = mid[:rows, :LANES]
        mids[level] = mid
        return carry

    lax.fori_loop(0, levels, first_state, 0)

    features_of(mids, ft2)
    cotangents_of(planes, 3 * levels)

    def second_step(c, carry):
        base = pl.multiple_of(c * TILES, TILES)
        x = inputs_at(ft2, base, TILES)
        cot = cotangents_at(base, TILES)
        first, second = forward(x)
        put_lanes(cl, SHALLOW, base, TILES, closure(second))
        dz_one, dz_two, dfeat = backward(first, second, cot)
        put_lanes(df, DEEP, base, TILES, dfeat)
        add_terms(x, first, second, cot, dz_one, dz_two)
        return carry

    lax.fori_loop(0, chunks, second_step, 0)
    first, second = forward(inputs_at(ft2, rows, halo_two))
    unused_one, unused_two, dfeat = backward(first, second, cotangents_at(rows, halo_two))
    put_lanes(df, DEEP, rows, halo_two, dfeat)
    unpack_halo(DEEP, df, dfx, dfh, halo_two)

    def adjoint_of(weighted, level):
        masked = planes[count - 1] * weighted
        carried = planes[2 * levels + level] * masked
        a0 = gathered(level, DEEP, df, dfx, dfh)
        a1 = gathered(levels + level, DEEP, df, dfx, dfh)
        a2 = gathered(2 * levels + level, DEEP, df, dfx, dfh)
        result = KAPPA * (east_of(masked) + west_of(masked) + north_of(masked) + south_of(masked) - 4.0 * masked)
        result = result + 0.5 * (east_of(carried) - west_of(carried)) + a0
        return result - 0.5 * (east_of(a1) - west_of(a1)) - 0.5 * (north_of(a2) - south_of(a2))

    def second_state(level, carry):
        closed = jnp.concatenate([cl[pl.ds(level, rows, stride=SHALLOW), :], jnp.zeros((2 * WIDE, LANES), F32)], 0)
        closed = jnp.concatenate([closed, jnp.zeros_like(closed)], 1)
        new = planes[level] + 2.0 * DT * force(mids[level], level, closed)
        o_new[level] = new[:rows, :LANES]
        grad = planes[4 * levels + level] + adjoint_of(2.0 * DT * planes[3 * levels + level], level)
        o_old[level] = grad[:rows, :LANES]
        olds[level] = grad
        return carry

    lax.fori_loop(0, levels, second_state, 0)

    cotangents_of(olds, 0)

    def third_step(c, carry):
        base = pl.multiple_of(c * TILES, TILES)
        x = inputs_at(ft1, base, TILES)
        cot = cotangents_at(base, TILES)
        first = keep1[c]
        second = keep2[c]
        dz_one, dz_two, dfeat = backward(first, second, cot)
        put_lanes(df, DEEP, base, TILES, dfeat)
        add_terms(x, first, second, cot, dz_one, dz_two)
        return carry

    lax.fori_loop(0, chunks, third_step, 0)
    near = halo_one * LANES
    unused_one, unused_two, dfeat = backward(
        keep1[chunks, :, pl.ds(0, near)], keep2[chunks, :, pl.ds(0, near)], cotangents_at(rows, halo_one)
    )
    put_lanes(df, DEEP, rows, halo_one, dfeat)
    unpack_halo(DEEP, df, dfx, dfh, halo_one)

    def third_state(level, carry):
        grad = adjoint_of(2.0 * DT * olds[level], level)
        o_now[level] = planes[3 * levels + level, pl.ds(0, rows), pl.ds(0, LANES)] + grad[:rows, :LANES]
        return carry

    lax.fori_loop(0, levels, third_state, 0)

    start = 0
    for acc in (acc_mid, acc_in, acc_out):
        deep = acc.shape[0]
        for half in range(hidden // LANES):
            o_grad[pl.ds(start, deep), :] = acc[:, half * LANES : (half + 1) * LANES]
            start += deep
    if start < o_grad.shape[0]:
        o_grad[pl.ds(start, o_grad.shape[0] - start), :] = jnp.zeros((o_grad.shape[0] - start, LANES), F32)


def scale_kernel(factor, terms, g_in, g_mid, g_out):
    hidden = g_mid.shape[0]
    start = 0
    for ref, deep in ((g_mid, hidden), (g_in, DEEP), (g_out, DEEP)):
        keep = ref.shape[0]
        for half in range(hidden // LANES):
            ref[:, half * LANES : (half + 1) * LANES] = terms[pl.ds(start, keep), :] * factor
            start += deep


def along(value, axis, step, periodic):
    count = lax.axis_size(axis)
    pairs = [(i, (i + step) % count) for i in range(count) if periodic or 0 <= i + step < count]
    return lax.ppermute(value, axis, pairs)


def swapped(value, axis, bit):
    return lax.ppermute(value, axis, [(i, i ^ bit) for i in range(lax.axis_size(axis))])


def summed_over(value, halving, doubling):
    bits = []
    bit = 1
    while bit < lax.axis_size(halving):
        upper = (lax.axis_index(halving) & bit) != 0
        half = value.shape[0] // 2
        lower_part, upper_part = value[:half], value[half:]
        sent = jnp.where(upper, lower_part, upper_part)
        value = jnp.where(upper, upper_part, lower_part) + swapped(sent, halving, bit)
        bits.append((bit, upper))
        bit *= 2
    bit = 1
    while bit < lax.axis_size(doubling):
        value = value + swapped(value, doubling, bit)
        bit *= 2
    for bit, upper in reversed(bits):
        other = swapped(value, halving, bit)
        value = jnp.concatenate([jnp.where(upper, other, value), jnp.where(upper, value, other)], 0)
    return value


def body(state_old, state_now, drift, ocean, w_in, w_mid, w_out, cot_mid, cot_new):
    levels, rows, cols = state_now.shape
    width_in, hidden = w_in.shape
    ext = rows + 2 * WIDE
    count = 5 * levels + 1
    packs = -(-ext // 16)
    steps = -(-(rows + 6 + packs) // TILES)
    slots = steps * TILES
    vmem = pl.BlockSpec(memory_space=pltpu.VMEM)
    hbm = pl.BlockSpec(memory_space=pltpu.HBM)
    strip = jax.ShapeDtypeStruct((rows, LANES), F32)
    edge = jax.ShapeDtypeStruct((count, WIDE, LANES), F32)
    west, east, top, bottom, fields = pl.pallas_call(
        pack_kernel,
        out_shape=(strip, strip, edge, edge, jax.ShapeDtypeStruct((count, rows, cols), F32)),
        in_specs=[hbm] * 6,
        out_specs=(vmem,) * 5,
        scratch_shapes=[pltpu.VMEM((rows, cols), jnp.int32), pltpu.SemaphoreType.DMA((6,))],
        compiler_params=pltpu.CompilerParams(vmem_limit_bytes=8 * 2**20),
    )(state_now, state_old, drift, cot_new, cot_mid, ocean)
    left = along(east, "lon", 1, True)
    right = along(west, "lon", -1, True)
    up = jnp.concatenate([bottom, left[None, rows - WIDE :], right[None, rows - WIDE :]], 0)
    down = jnp.concatenate([top, left[None, :WIDE], right[None, :WIDE]], 0)
    low = along(up, "lat", 1, False)
    high = along(down, "lat", -1, False)

    halves = hidden // LANES
    grain = 8 * lax.axis_size("lat")
    terms_rows = -(-halves * (hidden + 2 * DEEP) // grain) * grain
    field = jax.ShapeDtypeStruct((levels, rows, cols), F32)
    ext_planes = pltpu.VMEM((levels, ext, 2 * LANES), F32)
    side_rows = 16 * packs

    def tiles(deep):
        return [pltpu.VMEM((n * deep, LANES), F32) for n in (slots, side_rows, 2 * WIDE)]

    kept = pltpu.VMEM((steps, hidden, TILES * LANES), F32)
    state_mid, state_new, grad_old, grad_now, terms = pl.pallas_call(
        main_kernel,
        out_shape=(field, field, field, field, jax.ShapeDtypeStruct((terms_rows, LANES), F32)),
        in_specs=[vmem] * 8,
        out_specs=(vmem,) * 5,
        scratch_shapes=[
            pltpu.VMEM((count, ext, 2 * LANES), F32),
            ext_planes,
            ext_planes,
            tiles(DEEP)[0],
            *tiles(DEEP),
            *tiles(SHALLOW),
            *tiles(SHALLOW),
            *tiles(DEEP),
            kept,
            kept,
            pltpu.VMEM((hidden, hidden), F32),
            pltpu.VMEM((DEEP, hidden), F32),
            pltpu.VMEM((DEEP, hidden), F32),
            pltpu.VMEM((DEEP, hidden), BF16),
            pltpu.VMEM((hidden, DEEP), BF16),
            pltpu.VMEM((hidden, hidden), BF16),
            pltpu.VMEM((hidden, DEEP), BF16),
            pltpu.VMEM((DEEP, hidden), BF16),
        ],
        compiler_params=pltpu.CompilerParams(vmem_limit_bytes=44 * 2**20),
    )(fields, left, right, low, high, w_in, w_mid, w_out.T)

    summed = summed_over(terms, "lat", "lon")
    cells_all = rows * lax.axis_size("lat") * cols * lax.axis_size("lon")
    grad_in, grad_mid, grad_out = pl.pallas_call(
        functools.partial(scale_kernel, GAIN_GRAD / cells_all**0.5),
        out_shape=(
            jax.ShapeDtypeStruct((width_in, hidden), F32),
            jax.ShapeDtypeStruct((hidden, hidden), F32),
            jax.ShapeDtypeStruct((levels, hidden), F32),
        ),
        in_specs=[vmem],
        out_specs=(vmem,) * 3,
        compiler_params=pltpu.CompilerParams(vmem_limit_bytes=8 * 2**20),
    )(summed)
    return state_mid, state_new, grad_old, grad_now, grad_in, grad_mid, grad_out.T


def solution(mesh):
    field = P("grp", "lat", "lon")
    whole = P("grp", None)
    in_specs = (field, field, field, P(("grp", "lat"), "lon"), P(), P(), P(), field, field)
    out_specs = (field, field, field, field, whole, whole, whole)
    return jax.shard_map(body, mesh=mesh, in_specs=in_specs, out_specs=out_specs, check_vma=False)
```

time: 91 us -> 85.1 us (0.935)
  blocking collectives: 33.5 us -> 0 us
  waiting for transfers between devices: 2.08 us -> 16.7 us
  starting transfers between devices: 7.74 us -> 19.1 us
  Pallas kernels: 34.1 us -> 42.7 us
  local copies, waits for them, and re-layouts: 12.3 us -> 5.3 us
    all_to_all x2 -> x0, blocking collectives: 33.5 us -> none  [the longest x1 19.4 us: body(): lax.all_to_all(terms.reshape(members, piece, LANES), ('lon', 'lat'), 0, 0)]
    ppermute x0 -> x6, waiting for transfers between devices: none -> 13.7 us  [swapped(): lax.ppermute(value, axis, [(i, i ^ bit) for i in range(lax.axis_size(axis...]
    ppermute x0 -> x6, starting transfers between devices: none -> 9.62 us  [swapped(): lax.ppermute(value, axis, [(i, i ^ bit) for i in range(lax.axis_size(axis...]
    pallas_call x1, Pallas kernels: 33.6 us -> 39.2 us  [body(): pl.pallas_call(main_kernel, out_shape=(field, field, field, field, jax.Sh...]
    unnamed x33 -> x18, local copies, waits for them, and re-layouts: 9.07 us -> 5.29 us
    pallas_call x1 -> x2, Pallas kernels: 0.41 us -> 3.53 us  [the longest x1 2.8 us: body(): pl.pallas_call(pack_kernel, out_shape=(strip, strip, edge, edge, jax.Shap...]
    transpose x4 -> x0, local copies, waits for them, and re-layouts: 1.96 us -> none  [the longest x2 1.24 us: body(): weights = (in_pad, in_pad.T, w_mid, w_mid.T, out_pad, out_pad.T)]
    ppermute x4, starting transfers between devices: 7.74 us -> 9.49 us  [along(): return lax.ppermute(value, axis, pairs)]
  transfers between devices with their start and end apart: 4 -> 10, of which waited for: 3 -> 9; matrix products, arithmetic and copies ran while one was open for 4% -> 0% of each run, Pallas kernels for 0% -> 0%
where the time goes in v1:
time: 85.1 us; the launch traced here: 84.8 us
  Pallas kernels  42.7 us (50%)
  starting transfers between devices  19.1 us (22%)
  waiting for transfers between devices  16.7 us (20%)
  local copies, waits for them, and re-layouts  5.3 us (6%)
    pallas_call x1, Pallas kernels, body(): pl.pallas_call(main_kernel, out_shape=(field, field, field, field, jax.Sh...  39.2 us
    ppermute x6, waiting for transfers between devices, swapped(): lax.ppermute(value, axis, [(i, i ^ bit) for i in range(lax.axis_size(axis...  13.7 us
    ppermute x6, starting transfers between devices, swapped(): lax.ppermute(value, axis, [(i, i ^ bit) for i in range(lax.axis_size(axis...  9.62 us
    ppermute x4, starting transfers between devices, along(): return lax.ppermute(value, axis, pairs)  9.49 us
    unnamed x18, local copies, waits for them, and re-layouts  5.29 us
    ppermute x4, waiting for transfers between devices, along(): return lax.ppermute(value, axis, pairs)  3 us
    pallas_call x1, Pallas kernels, body(): pl.pallas_call(pack_kernel, out_shape=(strip, strip, edge, edge, jax.Shap...  2.8 us
  transfers between devices with their start and end apart: 10, of which 9 were waited for; matrix products, arithmetic and copies ran while one was open for 0% of the time, Pallas kernels for 0%

profile of v1, /device:TPU:0, one launch (start us, length us, event | category | flops | bytes accessed | tf_op | source)
XLA Modules:
  0.0 84.8 jit_solution(17764400076248265877)
XLA Ops:
  0.6 0.0 copy-start.1
  0.6 0.9 %copy-done.1 = f32[4,64,128]{2,1,0:T(8,128)S(1)} copy-done((f32[4,64,128]{2,1,0:T(8,128)S(1)}, f32[4,64,128]{2,1,0:T(8,128)}, u32[]{:S(2)}) %copy-start.1) | copy-done | bytes 131096
  1.5 0.0 copy-start.2
  1.5 0.9 %copy-done.2 = f32[4,64,128]{2,1,0:T(8,128)S(1)} copy-done((f32[4,64,128]{2,1,0:T(8,128)S(1)}, f32[4,64,128]{2,1,0:T(8,128)}, u32[]{:S(2)}) %copy-start.2) | copy-done | bytes 131096
  2.4 0.0 copy-start.3
  2.4 0.9 %copy-done.3 = f32[4,64,128]{2,1,0:T(8,128)S(1)} copy-done((f32[4,64,128]{2,1,0:T(8,128)S(1)}, f32[4,64,128]{2,1,0:T(8,128)}, u32[]{:S(2)}) %copy-start.3) | copy-done | bytes 131096
  3.3 0.0 copy-start.4
  3.4 0.9 %copy-done.4 = f32[4,64,128]{2,1,0:T(8,128)S(1)} copy-done((f32[4,64,128]{2,1,0:T(8,128)S(1)}, f32[4,64,128]{2,1,0:T(8,128)}, u32[]{:S(2)}) %copy-start.4) | copy-done | bytes 131096
  4.3 0.0 copy-start.5
  4.3 0.9 %copy-done.5 = f32[4,64,128]{2,1,0:T(8,128)S(1)} copy-done((f32[4,64,128]{2,1,0:T(8,128)S(1)}, f32[4,64,128]{2,1,0:T(8,128)}, u32[]{:S(2)}) %copy-start.5) | copy-done | bytes 131096
  5.2 0.0 copy-start.6
  5.2 0.8 copy-done.6
  5.9 2.8 %shard_map.144 = (f32[64,128]{1,0:T(8,128)S(1)}, f32[64,128]{1,0:T(8,128)S(1)}, f32[21,4,128]{2,1,0:T(4,128)S(1)}, f32[21,4,128]{2,1,0:T(4,128)S(1)}, f32[21,64,128]{2,1,0:T(8,128)S(1)}) custom-call(f32[4,64,128]{2,1,0:T(8,128)S(1)} %copy-done.1, f32[4,64,128]{2,1,0:T(8,128)S(1)} %copy-done.2, f32[4,64,128]{2,1,0:T(8,128)S(1)} %copy-done.3, ...), custom_call_target="tpu_custom_call" | custom-call | tf_op jit(solution)/shard_map/pallas_call | solution.py:377
  8.7 0.0 copy-start
  8.7 3.1 %collective-permute-start = (f32[64,128]{1,0:T(8,128)S(1)}, f32[64,128]{1,0:T(8,128)S(1)}, u32[]{:S(2)}, u32[]{:S(2)}) collective-permute-start(f32[64,128]{1,0:T(8,128)S(1)} %get-tuple-element.21), channel_id=1, source_target_pairs={{0,4},{4,8},{8,12},{12,0},{1,5},{5,9},{9,13},{13,1},{2,6},{6,10},{... | collective-permute-start | bytes 98312 | tf_op jit(solution)/shard_map/ppermute | solution.py:337
  11.8 2.1 %collective-permute-start.1 = (f32[64,128]{1,0:T(8,128)S(1)}, f32[64,128]{1,0:T(8,128)S(1)}, u32[]{:S(2)}, u32[]{:S(2)}) collective-permute-start(f32[64,128]{1,0:T(8,128)S(1)} %get-tuple-element.22), channel_id=1, source_target_pairs={{0,12},{4,0},{8,4},{12,8},{1,13},{5,1},{9,5},{13,9},{2,14},{6,2},{... | collective-permute-start | bytes 98312 | tf_op jit(solution)/shard_map/ppermute | solution.py:337
  13.9 1.9 %collective-permute-done.left = f32[64,128]{1,0:T(8,128)S(1)} collective-permute-done((f32[64,128]{1,0:T(8,128)S(1)}, f32[64,128]{1,0:T(8,128)S(1)}, u32[]{:S(2)}, u32[]{:S(2)}) %collective-permute-start) | collective-permute-done | bytes 32800 | tf_op jit(solution)/shard_map/ppermute | solution.py:337
  15.8 0.2 collective-permute-done.1.right
  16.1 1.3 %collective-permute-start.3 = (f32[23,4,128]{2,1,0:T(4,128)S(1)}, f32[23,4,128]{2,1,0:T(4,128)S(1)}, u32[]{:S(2)}, u32[]{:S(2)}) collective-permute-start(f32[23,4,128]{2,1,0:T(4,128)S(1)} %pad_maximum_fusion.3), channel_id=1, source_target_pairs={{1,0},{2,1},{3,2},{5,4},{6,5},{7,6},{9,8},{10,9},{11,10},{13,12},{... | collective-permute-start | bytes 141320 | tf_op jit(solution)/shard_map/ppermute | solution.py:337
  17.4 0.0 copy-start.7
  17.4 3.0 %collective-permute-start.2 = (f32[23,4,128]{2,1,0:T(4,128)S(1)}, f32[23,4,128]{2,1,0:T(4,128)S(1)}, u32[]{:S(2)}, u32[]{:S(2)}) collective-permute-start(f32[23,4,128]{2,1,0:T(4,128)S(1)} %pad_maximum_fusion.2), channel_id=1, source_target_pairs={{0,1},{1,2},{2,3},{4,5},{5,6},{6,7},{8,9},{9,10},{10,11},{12,13},{... | collective-permute-start | bytes 141320 | tf_op jit(solution)/shard_map/ppermute | solution.py:337
  20.5 0.0 copy-start.8
  20.5 0.0 collective-permute-done.3.high
  20.5 0.8 collective-permute-done.2.low
  21.3 0.0 copy-done
  21.3 0.0 copy-done.7
  21.3 0.0 copy-done.8
  21.3 39.2 %shard_map.145 = (f32[4,64,128]{2,1,0:T(8,128)}, f32[4,64,128]{2,1,0:T(8,128)}, f32[4,64,128]{2,1,0:T(8,128)}, f32[4,64,128]{2,1,0:T(8,128)}, f32[576,128]{1,0:T(8,128)S(1)}) custom-call(f32[21,64,128]{2,1,0:T(8,128)S(1)} %get-tuple-element.20.fields, f32[64,128]{1,0:T(8,128)S(1)} %collective-permute-done.left, f32[64,128]{1,0:T(8,128)S(1)} %collective-permute-done.1.right, ...), custom_call_target="tpu_custom_call" | custom-call | tf_op jit(solution)/shard_map/pallas_call | solution.py:403
  60.5 1.5 %collective-permute-start.4 = (f32[288,128]{1,0:T(8,128)S(1)}, f32[288,128]{1,0:T(8,128)S(1)}, u32[]{:S(2)}, u32[]{:S(2)}) collective-permute-start(f32[288,128]{1,0:T(8,128)S(1)} %slice_select_fusion), channel_id=1, source_target_pairs={{0,1},{1,0},{2,3},{3,2},{4,5},{5,4},{6,7},{7,6},{8,9},{9,8},{10,11... | collective-permute-start | bytes 442376 | tf_op jit(solution)/shard_map/ppermute | solution.py:341
  62.0 1.0 %collective-permute-done.4 = f32[288,128]{1,0:T(8,128)S(1)} collective-permute-done((f32[288,128]{1,0:T(8,128)S(1)}, f32[288,128]{1,0:T(8,128)S(1)}, u32[]{:S(2)}, u32[]{:S(2)}) %collective-permute-start.4) | collective-permute-done | bytes 147488 | tf_op jit(solution)/shard_map/ppermute | solution.py:341
  63.1 2.7 %collective-permute-start.5 = (f32[144,128]{1,0:T(8,128)S(1)}, f32[144,128]{1,0:T(8,128)S(1)}, u32[]{:S(2)}, u32[]{:S(2)}) collective-permute-start(f32[144,128]{1,0:T(8,128)S(1)} %slice_select_fusion.1), channel_id=1, source_target_pairs={{0,2},{1,3},{2,0},{3,1},{4,6},{5,7},{6,4},{7,5},{8,10},{9,11},{10,... | collective-permute-start | bytes 221192 | tf_op jit(solution)/shard_map/ppermute | solution.py:341
  65.7 2.6 %collective-permute-done.5 = f32[144,128]{1,0:T(8,128)S(1)} collective-permute-done((f32[144,128]{1,0:T(8,128)S(1)}, f32[144,128]{1,0:T(8,128)S(1)}, u32[]{:S(2)}, u32[]{:S(2)}) %collective-permute-start.5) | collective-permute-done | bytes 73760 | tf_op jit(solution)/shard_map/ppermute | solution.py:341
  68.3 1.3 %collective-permute-start.6 = (f32[144,128]{1,0:T(8,128)S(1)}, f32[144,128]{1,0:T(8,128)S(1)}, u32[]{:S(2)}, u32[]{:S(2)}) collective-permute-start(f32[144,128]{1,0:T(8,128)S(1)} %select_add_fusion.1), channel_id=1, source_target_pairs={{0,4},{4,0},{8,12},{12,8},{1,5},{5,1},{9,13},{13,9},{2,6},{6,2},{1... | collective-permute-start | bytes 221192 | tf_op jit(solution)/shard_map/ppermute | solution.py:341
  69.6 3.1 %collective-permute-done.6 = f32[144,128]{1,0:T(8,128)S(1)} collective-permute-done((f32[144,128]{1,0:T(8,128)S(1)}, f32[144,128]{1,0:T(8,128)S(1)}, u32[]{:S(2)}, u32[]{:S(2)}) %collective-permute-start.6) | collective-permute-done | bytes 73760 | tf_op jit(solution)/shard_map/ppermute | solution.py:341
  72.7 2.3 %collective-permute-start.7 = (f32[144,128]{1,0:T(8,128)S(1)}, f32[144,128]{1,0:T(8,128)S(1)}, u32[]{:S(2)}, u32[]{:S(2)}) collective-permute-start(f32[144,128]{1,0:T(8,128)S(1)} %add.14), channel_id=1, source_target_pairs={{0,8},{4,12},{8,0},{12,4},{1,9},{5,13},{9,1},{13,5},{2,10},{6,14},... | collective-permute-start | bytes 221192 | tf_op jit(solution)/shard_map/ppermute | solution.py:341
  75.0 3.0 %collective-permute-done.7 = f32[144,128]{1,0:T(8,128)S(1)} collective-permute-done((f32[144,128]{1,0:T(8,128)S(1)}, f32[144,128]{1,0:T(8,128)S(1)}, u32[]{:S(2)}, u32[]{:S(2)}) %collective-permute-start.7) | collective-permute-done | bytes 73760 | tf_op jit(solution)/shard_map/ppermute | solution.py:341
  78.1 1.8 %collective-permute-start.8 = (f32[144,128]{1,0:T(8,128)S(1)}, f32[144,128]{1,0:T(8,128)S(1)}, u32[]{:S(2)}, u32[]{:S(2)}) collective-permute-start(f32[144,128]{1,0:T(8,128)S(1)} %add.15), channel_id=1, source_target_pairs={{0,2},{1,3},{2,0},{3,1},{4,6},{5,7},{6,4},{7,5},{8,10},{9,11},{10,... | collective-permute-start | bytes 221192 | tf_op jit(solution)/shard_map/ppermute | solution.py:341
  79.9 2.6 %collective-permute-done.8 = f32[144,128]{1,0:T(8,128)S(1)} collective-permute-done((f32[144,128]{1,0:T(8,128)S(1)}, f32[144,128]{1,0:T(8,128)S(1)}, u32[]{:S(2)}, u32[]{:S(2)}) %collective-permute-start.8) | collective-permute-done | bytes 73760 | tf_op jit(solution)/shard_map/ppermute | solution.py:341
  82.5 0.1 collective-permute-start.9
  82.6 1.4 %collective-permute-done.9 = f32[288,128]{1,0:T(8,128)S(1)} collective-permute-done((f32[288,128]{1,0:T(8,128)S(1)}, f32[288,128]{1,0:T(8,128)S(1)}, u32[]{:S(2)}, u32[]{:S(2)}) %collective-permute-start.9) | collective-permute-done | bytes 147488 | tf_op jit(solution)/shard_map/ppermute | solution.py:341
  84.0 0.7 shard_map.146
  (14 shorter events, 0.2 us)
Async XLA Ops:
  0.6 0.9 %copy-start.1 = (f32[4,64,128]{2,1,0:T(8,128)S(1)}, f32[4,64,128]{2,1,0:T(8,128)}, u32[]{:S(2)}) copy-start(f32[4,64,128]{2,1,0:T(8,128)} %now.1) | copy-start | bytes 393220
  1.5 0.9 %copy-start.2 = (f32[4,64,128]{2,1,0:T(8,128)S(1)}, f32[4,64,128]{2,1,0:T(8,128)}, u32[]{:S(2)}) copy-start(f32[4,64,128]{2,1,0:T(8,128)} %old.1) | copy-start | bytes 393220
  2.4 0.9 %copy-start.3 = (f32[4,64,128]{2,1,0:T(8,128)S(1)}, f32[4,64,128]{2,1,0:T(8,128)}, u32[]{:S(2)}) copy-start(f32[4,64,128]{2,1,0:T(8,128)} %drift.1) | copy-start | bytes 393220
  3.3 0.9 %copy-start.4 = (f32[4,64,128]{2,1,0:T(8,128)S(1)}, f32[4,64,128]{2,1,0:T(8,128)}, u32[]{:S(2)}) copy-start(f32[4,64,128]{2,1,0:T(8,128)} %cnew.1) | copy-start | bytes 393220
  4.3 0.9 %copy-start.5 = (f32[4,64,128]{2,1,0:T(8,128)S(1)}, f32[4,64,128]{2,1,0:T(8,128)}, u32[]{:S(2)}) copy-start(f32[4,64,128]{2,1,0:T(8,128)} %cmid.1) | copy-start | bytes 393220
  5.2 0.8 copy-start.6
  8.7 12.6 %copy-start = (bf16[256,256]{1,0:T(8,128)(2,1)S(1)}, bf16[256,256]{1,0:T(8,128)(2,1)}, u32[]{:S(2)}) copy-start(bf16[256,256]{1,0:T(8,128)(2,1)} %w_mid.1) | copy-start | bytes 393220
  8.7 7.1 %collective-permute-start = (f32[64,128]{1,0:T(8,128)S(1)}, f32[64,128]{1,0:T(8,128)S(1)}, u32[]{:S(2)}, u32[]{:S(2)}) collective-permute-start(f32[64,128]{1,0:T(8,128)S(1)} %get-tuple-element.21), channel_id=1, source_target_pairs={{0,4},{4,8},{8,12},{12,0},{1,5},{5,9},{9,13},{13,1},{2,6},{6,10},{... | collective-permute-start | bytes 98312 | tf_op jit(solution)/shard_map/ppermute | solution.py:337
  11.8 4.3 %collective-permute-start.1 = (f32[64,128]{1,0:T(8,128)S(1)}, f32[64,128]{1,0:T(8,128)S(1)}, u32[]{:S(2)}, u32[]{:S(2)}) collective-permute-start(f32[64,128]{1,0:T(8,128)S(1)} %get-tuple-element.22), channel_id=1, source_target_pairs={{0,12},{4,0},{8,4},{12,8},{1,13},{5,1},{9,5},{13,9},{2,14},{6,2},{... | collective-permute-start | bytes 98312 | tf_op jit(solution)/shard_map/ppermute | solution.py:337
  16.1 4.4 %collective-permute-start.3 = (f32[23,4,128]{2,1,0:T(4,128)S(1)}, f32[23,4,128]{2,1,0:T(4,128)S(1)}, u32[]{:S(2)}, u32[]{:S(2)}) collective-permute-start(f32[23,4,128]{2,1,0:T(4,128)S(1)} %pad_maximum_fusion.3), channel_id=1, source_target_pairs={{1,0},{2,1},{3,2},{5,4},{6,5},{7,6},{9,8},{10,9},{11,10},{13,12},{... | collective-permute-start | bytes 141320 | tf_op jit(solution)/shard_map/ppermute | solution.py:337
  17.4 3.9 %copy-start.7 = (bf16[12,256]{1,0:T(8,128)(2,1)S(1)}, bf16[12,256]{1,0:T(8,128)(2,1)}, u32[]{:S(2)}) copy-start(bf16[12,256]{1,0:T(8,128)(2,1)} %w_in.1) | copy-start | bytes 18436
  17.4 3.9 %collective-permute-start.2 = (f32[23,4,128]{2,1,0:T(4,128)S(1)}, f32[23,4,128]{2,1,0:T(4,128)S(1)}, u32[]{:S(2)}, u32[]{:S(2)}) collective-permute-start(f32[23,4,128]{2,1,0:T(4,128)S(1)} %pad_maximum_fusion.2), channel_id=1, source_target_pairs={{0,1},{1,2},{2,3},{4,5},{5,6},{6,7},{8,9},{9,10},{10,11},{12,13},{... | collective-permute-start | bytes 141320 | tf_op jit(solution)/shard_map/ppermute | solution.py:337
  20.5 0.9 %copy-start.8 = (bf16[256,4]{0,1:T(4,128)(2,1)S(1)}, bf16[256,4]{0,1:T(4,128)(2,1)}, u32[]{:S(2)}) copy-start(bf16[256,4]{0,1:T(4,128)(2,1)} %param.15) | copy-start | bytes 6148
  60.5 2.5 %collective-permute-start.4 = (f32[288,128]{1,0:T(8,128)S(1)}, f32[288,128]{1,0:T(8,128)S(1)}, u32[]{:S(2)}, u32[]{:S(2)}) collective-permute-start(f32[288,128]{1,0:T(8,128)S(1)} %slice_select_fusion), channel_id=1, source_target_pairs={{0,1},{1,0},{2,3},{3,2},{4,5},{5,4},{6,7},{7,6},{8,9},{9,8},{10,11... | collective-permute-start | bytes 442376 | tf_op jit(solution)/shard_map/ppermute | solution.py:341
  63.1 5.2 %collective-permute-start.5 = (f32[144,128]{1,0:T(8,128)S(1)}, f32[144,128]{1,0:T(8,128)S(1)}, u32[]{:S(2)}, u32[]{:S(2)}) collective-permute-start(f32[144,128]{1,0:T(8,128)S(1)} %slice_select_fusion.1), channel_id=1, source_target_pairs={{0,2},{1,3},{2,0},{3,1},{4,6},{5,7},{6,4},{7,5},{8,10},{9,11},{10,... | collective-permute-start | bytes 221192 | tf_op jit(solution)/shard_map/ppermute | solution.py:341
  68.3 4.4 %collective-permute-start.6 = (f32[144,128]{1,0:T(8,128)S(1)}, f32[144,128]{1,0:T(8,128)S(1)}, u32[]{:S(2)}, u32[]{:S(2)}) collective-permute-start(f32[144,128]{1,0:T(8,128)S(1)} %select_add_fusion.1), channel_id=1, source_target_pairs={{0,4},{4,0},{8,12},{12,8},{1,5},{5,1},{9,13},{13,9},{2,6},{6,2},{1... | collective-permute-start | bytes 221192 | tf_op jit(solution)/shard_map/ppermute | solution.py:341
  72.7 5.3 %collective-permute-start.7 = (f32[144,128]{1,0:T(8,128)S(1)}, f32[144,128]{1,0:T(8,128)S(1)}, u32[]{:S(2)}, u32[]{:S(2)}) collective-permute-start(f32[144,128]{1,0:T(8,128)S(1)} %add.14), channel_id=1, source_target_pairs={{0,8},{4,12},{8,0},{12,4},{1,9},{5,13},{9,1},{13,5},{2,10},{6,14},... | collective-permute-start | bytes 221192 | tf_op jit(solution)/shard_map/ppermute | solution.py:341
  78.1 4.4 %collective-permute-start.8 = (f32[144,128]{1,0:T(8,128)S(1)}, f32[144,128]{1,0:T(8,128)S(1)}, u32[]{:S(2)}, u32[]{:S(2)}) collective-permute-start(f32[144,128]{1,0:T(8,128)S(1)} %add.15), channel_id=1, source_target_pairs={{0,2},{1,3},{2,0},{3,1},{4,6},{5,7},{6,4},{7,5},{8,10},{9,11},{10,... | collective-permute-start | bytes 221192 | tf_op jit(solution)/shard_map/ppermute | solution.py:341
  82.5 1.4 %collective-permute-start.9 = (f32[288,128]{1,0:T(8,128)S(1)}, f32[288,128]{1,0:T(8,128)S(1)}, u32[]{:S(2)}, u32[]{:S(2)}) collective-permute-start(f32[288,128]{1,0:T(8,128)S(1)} %pad_maximum_fusion.1), channel_id=1, source_target_pairs={{0,1},{1,0},{2,3},{3,2},{4,5},{5,4},{6,7},{7,6},{8,9},{9,8},{10,11... | collective-permute-start | bytes 442376 | tf_op jit(solution)/shard_map/ppermute | solution.py:341

commit v2 on v1

--- a/solution.py
+++ b/solution.py
@@ -29,33 +29,20 @@
     return lax.dot_general(left, right, (((1,), (1,)), ((), ())), preferred_element_type=F32)
 
 
-def pack_kernel(now, old, drift, cnew, cmid, ocean, west, east, top, bottom, fields, wet, sems):
-    levels, rows, cols = now.shape
-    copies = [
-        pltpu.make_async_copy(ref, fields.at[pl.ds(levels * f, levels)], sems.at[f])
-        for f, ref in enumerate((now, old, drift, cnew, cmid))
-    ]
-    copies.append(pltpu.make_async_copy(ocean, wet, sems.at[5]))
-    for copy in copies:
-        copy.start()
-    for copy in copies:
-        copy.wait()
-    count = 5 * levels
-    fields[count] = wet[...].astype(F32)
+def pack_kernel(fields, west, east, top, bottom):
+    count, rows, cols = fields.shape
     lane = lax.broadcasted_iota(jnp.int32, (rows, LANES), 1)
-    west[...] = jnp.zeros_like(west)
-    east[...] = jnp.zeros_like(east)
-
-    def one_plane(p, carry):
+    to_west = jnp.zeros((rows, LANES), F32)
+    to_east = jnp.zeros((rows, LANES), F32)
+    for p in range(count):
         plane = fields[p]
         here = (lane >= WIDE * p) & (lane < WIDE * (p + 1))
-        west[...] = jnp.where(here, pltpu.roll(plane, WIDE * p, 1), west[...])
-        east[...] = jnp.where(here, pltpu.roll(plane, WIDE * (p + 1), 1), east[...])
+        to_west = jnp.where(here, pltpu.roll(plane, WIDE * p, 1) if p else plane, to_west)
+        to_east = jnp.where(here, pltpu.roll(plane, WIDE * (p + 1), 1), to_east)
         top[p] = plane[:WIDE]
         bottom[p] = plane[rows - WIDE :]
-        return carry
-
-    lax.fori_loop(0, count + 1, one_plane, 0)
+    west[...] = to_west
+    east[...] = to_east
 
 
 def east_of(v):
@@ -105,15 +92,12 @@
     left_all = jnp.concatenate([left[...], high[count], low[count]], 0)
     right_all = jnp.concatenate([right[...], high[count + 1], low[count + 1]], 0)
 
-    def one_plane(p, carry):
-        from_right = pltpu.roll(right_all, LANES - WIDE * p, 1)
+    for p in range(count):
+        from_right = pltpu.roll(right_all, LANES - WIDE * p, 1) if p else right_all
         from_left = pltpu.roll(left_all, LANES - WIDE * (p + 1), 1)
         side = jnp.where(lane < WIDE, from_right, jnp.where(lane >= LANES - WIDE, from_left, 0.0))
         planes[p, :, pl.ds(0, LANES)] = jnp.concatenate([fields[p], high[p], low[p]], 0)
         planes[p, :, pl.ds(LANES, LANES)] = side
-        return carry
-
-    lax.fori_loop(0, count, one_plane, 0)
 
     for ref in (ft1, ft2, fth, ftx, dc, dch, dcx, acc_mid, acc_in, acc_out):
         ref[...] = jnp.zeros_like(ref)
@@ -135,30 +119,23 @@
             if r is not None:
                 main[pl.ds((rows + i) * deep, deep), :] = extra[pl.ds((r - rows) * deep, deep), :]
 
-        def one_pack(q, carry):
+        for q in range(packs):
             total = jnp.zeros((deep, LANES), F32)
-            for j in range(16):
-                moved = side[pl.ds(pl.multiple_of((16 * q + j) * deep, deep), deep), :]
-                moved = pltpu.roll(moved, (2 * WIDE * j + WIDE) % LANES, 1)
+            for j in range(min(16, ext - 16 * q)):
+                moved = pltpu.roll(side[pl.ds((16 * q + j) * deep, deep), :], (2 * WIDE * j + WIDE) % LANES, 1)
                 total = jnp.where((where >= 2 * WIDE * j) & (where < 2 * WIDE * (j + 1)), moved, total)
-            main[pl.ds(pl.multiple_of((first_pack + q) * deep, deep), deep), :] = total
-            return carry
-
-        lax.fori_loop(0, packs, one_pack, 0)
+            main[pl.ds((first_pack + q) * deep, deep), :] = total
 
     def unpack_halo(deep, main, extra, side, live):
         for i, r in enumerate(order[:live]):
             if r is not None:
                 extra[pl.ds((r - rows) * deep, deep), :] = main[pl.ds((rows + i) * deep, deep), :]
 
-        def one_pack(q, carry):
-            tile = main[pl.ds(pl.multiple_of((first_pack + q) * deep, deep), deep), :]
-            for j in range(16):
+        for q in range(packs):
+            tile = main[pl.ds((first_pack + q) * deep, deep), :]
+            for j in range(min(16, ext - 16 * q)):
                 moved = pltpu.roll(tile, LANES - (2 * WIDE * j + WIDE) % LANES, 1)
-                side[pl.ds(pl.multiple_of((16 * q + j) * deep, deep), deep), :] = moved
-            return carry
-
-        lax.fori_loop(0, packs, one_pack, 0)
+                side[pl.ds((16 * q + j) * deep, deep), :] = moved
 
     def lanes_of(ref, deep, base, tiles):
         block = ref[pl.ds(base * deep, tiles * deep), :]
@@ -195,22 +172,18 @@
         acc_out[...] += dot_nt(cot, second.astype(BF16))
 
     def features_of(source, ft):
-        def one_level(level, carry):
+        for level in range(levels):
             v = source[level]
             spread(v, level, DEEP, ft, ftx, fth)
             spread(0.5 * (east_of(v) - west_of(v)), levels + level, DEEP, ft, ftx, fth)
             spread(0.5 * (north_of(v) - south_of(v)), 2 * levels + level, DEEP, ft, ftx, fth)
-            return carry
-
-        lax.fori_loop(0, levels, one_level, 0)
+
         pack_halo(DEEP, ft, ftx, fth)
 
     def cotangents_of(source, offset):
-        def one_level(level, carry):
+        for level in range(levels):
             spread(planes[count - 1] * (2.0 * DT * source[offset + level]), level, SHALLOW, dc, dcx, dch)
-            return carry
-
-        lax.fori_loop(0, levels, one_level, 0)
+
         pack_halo(SHALLOW, dc, dcx, dch)
 
     def force(v, level, closed):
@@ -232,14 +205,11 @@
     lax.fori_loop(0, keep1.shape[0], first_step, 0)
     unpack_halo(SHALLOW, cl, clx, clh, len(order))
 
-    def first_state(level, carry):
+    for level in range(levels):
         closed = gathered(level, SHALLOW, cl, clx, clh)
         mid = planes[levels + level] + 2.0 * DT * force(planes[level], level, closed)
         o_mid[level] = mid[:rows, :LANES]
         mids[level] = mid
-        return carry
-
-    lax.fori_loop(0, levels, first_state, 0)
 
     features_of(mids, ft2)
     cotangents_of(planes, 3 * levels)
@@ -271,7 +241,7 @@
         result = result + 0.5 * (east_of(carried) - west_of(carried)) + a0
         return result - 0.5 * (east_of(a1) - west_of(a1)) - 0.5 * (north_of(a2) - south_of(a2))
 
-    def second_state(level, carry):
+    for level in range(levels):
         closed = jnp.concatenate([cl[pl.ds(level, rows, stride=SHALLOW), :], jnp.zeros((2 * WIDE, LANES), F32)], 0)
         closed = jnp.concatenate([closed, jnp.zeros_like(closed)], 1)
         new = planes[level] + 2.0 * DT * force(mids[level], level, closed)
@@ -279,9 +249,6 @@
         grad = planes[4 * levels + level] + adjoint_of(2.0 * DT * planes[3 * levels + level], level)
         o_old[level] = grad[:rows, :LANES]
         olds[level] = grad
-        return carry
-
-    lax.fori_loop(0, levels, second_state, 0)
 
     cotangents_of(olds, 0)
 
@@ -304,12 +271,9 @@
     put_lanes(df, DEEP, rows, halo_one, dfeat)
     unpack_halo(DEEP, df, dfx, dfh, halo_one)
 
-    def third_state(level, carry):
+    for level in range(levels):
         grad = adjoint_of(2.0 * DT * olds[level], level)
         o_now[level] = planes[3 * levels + level, pl.ds(0, rows), pl.ds(0, LANES)] + grad[:rows, :LANES]
-        return carry
-
-    lax.fori_loop(0, levels, third_state, 0)
 
     start = 0
     for acc in (acc_mid, acc_in, acc_out):
@@ -371,17 +335,17 @@
     steps = -(-(rows + 6 + packs) // TILES)
     slots = steps * TILES
     vmem = pl.BlockSpec(memory_space=pltpu.VMEM)
-    hbm = pl.BlockSpec(memory_space=pltpu.HBM)
     strip = jax.ShapeDtypeStruct((rows, LANES), F32)
     edge = jax.ShapeDtypeStruct((count, WIDE, LANES), F32)
-    west, east, top, bottom, fields = pl.pallas_call(
+    wet = ocean.astype(F32)[None]
+    fields = jnp.concatenate([state_now, state_old, drift, cot_new, cot_mid, wet], 0)
+    west, east, top, bottom = pl.pallas_call(
         pack_kernel,
-        out_shape=(strip, strip, edge, edge, jax.ShapeDtypeStruct((count, rows, cols), F32)),
-        in_specs=[hbm] * 6,
-        out_specs=(vmem,) * 5,
-        scratch_shapes=[pltpu.VMEM((rows, cols), jnp.int32), pltpu.SemaphoreType.DMA((6,))],
+        out_shape=(strip, strip, edge, edge),
+        in_specs=[vmem],
+        out_specs=(vmem,) * 4,
         compiler_params=pltpu.CompilerParams(vmem_limit_bytes=8 * 2**20),
-    )(state_now, state_old, drift, cot_new, cot_mid, ocean)
+    )(fields)
     left = along(east, "lon", 1, True)
     right = along(west, "lon", -1, True)
     up = jnp.concatenate([bottom, left[None, rows - WIDE :], right[None, rows - WIDE :]], 0)

time: 85.1 us -> 75.9 us (0.89)
  Pallas kernels: 42.7 us -> 34.4 us
  local copies, waits for them, and re-layouts: 5.3 us -> 4.43 us
    pallas_call x1, Pallas kernels: 39.2 us -> 33.2 us  [body(): pl.pallas_call(main_kernel, out_shape=(field, field, field, field, jax.Sh...]
    pallas_call x1, Pallas kernels: 2.8 us -> 0.41 us  [body(): pl.pallas_call(pack_kernel, out_shape=(strip, strip, edge, edge), in_spec...]
    unnamed x18 -> x21, local copies, waits for them, and re-layouts: 5.29 us -> 4.42 us
where the time goes in v2:
time: 75.9 us; the launch traced here: 75.6 us
  Pallas kernels  34.4 us (45%)
  starting transfers between devices  19.1 us (25%)
  waiting for transfers between devices  16.7 us (22%)
  local copies, waits for them, and re-layouts  4.43 us (6%)
  between operations  0.81 us (1%)
    pallas_call x1, Pallas kernels, body(): pl.pallas_call(main_kernel, out_shape=(field, field, field, field, jax.Sh...  33.2 us
    ppermute x6, waiting for transfers between devices, swapped(): lax.ppermute(value, axis, [(i, i ^ bit) for i in range(lax.axis_size(axis...  13.7 us
    ppermute x6, starting transfers between devices, swapped(): lax.ppermute(value, axis, [(i, i ^ bit) for i in range(lax.axis_size(axis...  9.61 us
    ppermute x4, starting transfers between devices, along(): return lax.ppermute(value, axis, pairs)  9.49 us
    unnamed x21, local copies, waits for them, and re-layouts  4.42 us
    ppermute x4, waiting for transfers between devices, along(): return lax.ppermute(value, axis, pairs)  3 us
  transfers between devices with their start and end apart: 10, of which 9 were waited for; matrix products, arithmetic and copies ran while one was open for 0% of the time, Pallas kernels for 0%

profile of v2, /device:TPU:0, one launch (start us, length us, event | category | flops | bytes accessed | tf_op | source)
XLA Modules:
  0.0 75.6 jit_solution(15788391466281432905)
XLA Ops:
  0.6 0.0 copy-start.3
  0.6 0.9 %constant_dynamic-update-slice_fusion.4 = f32[21,64,128]{2,1,0:T(8,128)S(1)} fusion(f32[4,64,128]{2,1,0:T(8,128)} %param.10), kind=kLoop, calls=%fused_computation.17 | loop fusion | bytes 262144
  1.6 0.0 copy-done.3
  1.6 0.0 copy-start.4
  1.6 0.9 %copy-done.4 = f32[4,64,128]{2,1,0:T(8,128)S(1)} copy-done((f32[4,64,128]{2,1,0:T(8,128)S(1)}, f32[4,64,128]{2,1,0:T(8,128)}, u32[]{:S(2)}) %copy-start.4) | copy-done | bytes 131096
  2.5 0.0 copy-start.5
  2.5 0.9 %copy-done.5 = f32[4,64,128]{2,1,0:T(8,128)S(1)} copy-done((f32[4,64,128]{2,1,0:T(8,128)S(1)}, f32[4,64,128]{2,1,0:T(8,128)}, u32[]{:S(2)}) %copy-start.5) | copy-done | bytes 131096
  3.4 0.0 copy-start.6
  3.4 0.9 %copy-done.6 = f32[4,64,128]{2,1,0:T(8,128)S(1)} copy-done((f32[4,64,128]{2,1,0:T(8,128)S(1)}, f32[4,64,128]{2,1,0:T(8,128)}, u32[]{:S(2)}) %copy-start.6) | copy-done | bytes 131096
  4.3 0.0 copy-start.7
  4.3 0.7 copy-done.7
  5.1 0.4 shard_map.144
  5.5 0.0 copy-start
  5.5 3.1 %collective-permute-start = (f32[64,128]{1,0:T(8,128)S(1)}, f32[64,128]{1,0:T(8,128)S(1)}, u32[]{:S(2)}, u32[]{:S(2)}) collective-permute-start(f32[64,128]{1,0:T(8,128)S(1)} %get-tuple-element.19), channel_id=1, source_target_pairs={{0,4},{4,8},{8,12},{12,0},{1,5},{5,9},{9,13},{13,1},{2,6},{6,10},{... | collective-permute-start | bytes 98312 | tf_op jit(solution)/shard_map/ppermute | solution.py:301
  8.6 2.1 %collective-permute-start.1 = (f32[64,128]{1,0:T(8,128)S(1)}, f32[64,128]{1,0:T(8,128)S(1)}, u32[]{:S(2)}, u32[]{:S(2)}) collective-permute-start(f32[64,128]{1,0:T(8,128)S(1)} %get-tuple-element.20), channel_id=1, source_target_pairs={{0,12},{4,0},{8,4},{12,8},{1,13},{5,1},{9,5},{13,9},{2,14},{6,2},{... | collective-permute-start | bytes 98312 | tf_op jit(solution)/shard_map/ppermute | solution.py:301
  10.7 1.9 %collective-permute-done.left = f32[64,128]{1,0:T(8,128)S(1)} collective-permute-done((f32[64,128]{1,0:T(8,128)S(1)}, f32[64,128]{1,0:T(8,128)S(1)}, u32[]{:S(2)}, u32[]{:S(2)}) %collective-permute-start) | collective-permute-done | bytes 32800 | tf_op jit(solution)/shard_map/ppermute | solution.py:301
  12.6 0.2 collective-permute-done.1.right
  12.9 1.3 %collective-permute-start.3 = (f32[23,4,128]{2,1,0:T(4,128)S(1)}, f32[23,4,128]{2,1,0:T(4,128)S(1)}, u32[]{:S(2)}, u32[]{:S(2)}) collective-permute-start(f32[23,4,128]{2,1,0:T(4,128)S(1)} %pad_maximum_fusion.3), channel_id=1, source_target_pairs={{1,0},{2,1},{3,2},{5,4},{6,5},{7,6},{9,8},{10,9},{11,10},{13,12},{... | collective-permute-start | bytes 141320 | tf_op jit(solution)/shard_map/ppermute | solution.py:301
  14.2 0.0 copy-start.1
  14.2 3.0 %collective-permute-start.2 = (f32[23,4,128]{2,1,0:T(4,128)S(1)}, f32[23,4,128]{2,1,0:T(4,128)S(1)}, u32[]{:S(2)}, u32[]{:S(2)}) collective-permute-start(f32[23,4,128]{2,1,0:T(4,128)S(1)} %pad_maximum_fusion.2), channel_id=1, source_target_pairs={{0,1},{1,2},{2,3},{4,5},{5,6},{6,7},{8,9},{9,10},{10,11},{12,13},{... | collective-permute-start | bytes 141320 | tf_op jit(solution)/shard_map/ppermute | solution.py:301
  17.3 0.0 copy-start.2
  17.3 0.0 collective-permute-done.3.high
  17.3 0.8 %collective-permute-done.2.low = f32[23,4,128]{2,1,0:T(4,128)S(1)} collective-permute-done((f32[23,4,128]{2,1,0:T(4,128)S(1)}, f32[23,4,128]{2,1,0:T(4,128)S(1)}, u32[]{:S(2)}, u32[]{:S(2)}) %collective-permute-start.2) | collective-permute-done | bytes 47136 | tf_op jit(solution)/shard_map/ppermute | solution.py:301
  18.1 0.0 copy-done
  18.1 0.0 copy-done.1
  18.1 0.0 copy-done.2
  18.1 33.2 %shard_map.145 = (f32[4,64,128]{2,1,0:T(8,128)}, f32[4,64,128]{2,1,0:T(8,128)}, f32[4,64,128]{2,1,0:T(8,128)}, f32[4,64,128]{2,1,0:T(8,128)}, f32[576,128]{1,0:T(8,128)S(1)}) custom-call(f32[21,64,128]{2,1,0:T(8,128)S(1)} %bitcast_dynamic-update-slice_fusion.fields, f32[64,128]{1,0:T(8,128)S(1)} %collective-permute-done.left, ...), custom_call_target="tpu_custom_call" | custom-call | tf_op jit(solution)/shard_map/pallas_call | solution.py:367
  51.4 1.5 %collective-permute-start.4 = (f32[288,128]{1,0:T(8,128)S(1)}, f32[288,128]{1,0:T(8,128)S(1)}, u32[]{:S(2)}, u32[]{:S(2)}) collective-permute-start(f32[288,128]{1,0:T(8,128)S(1)} %slice_select_fusion), channel_id=1, source_target_pairs={{0,1},{1,0},{2,3},{3,2},{4,5},{5,4},{6,7},{7,6},{8,9},{9,8},{10,11... | collective-permute-start | bytes 442376 | tf_op jit(solution)/shard_map/ppermute | solution.py:305
  52.8 1.0 %collective-permute-done.4 = f32[288,128]{1,0:T(8,128)S(1)} collective-permute-done((f32[288,128]{1,0:T(8,128)S(1)}, f32[288,128]{1,0:T(8,128)S(1)}, u32[]{:S(2)}, u32[]{:S(2)}) %collective-permute-start.4) | collective-permute-done | bytes 147488 | tf_op jit(solution)/shard_map/ppermute | solution.py:305
  53.9 2.7 %collective-permute-start.5 = (f32[144,128]{1,0:T(8,128)S(1)}, f32[144,128]{1,0:T(8,128)S(1)}, u32[]{:S(2)}, u32[]{:S(2)}) collective-permute-start(f32[144,128]{1,0:T(8,128)S(1)} %slice_select_fusion.1), channel_id=1, source_target_pairs={{0,2},{1,3},{2,0},{3,1},{4,6},{5,7},{6,4},{7,5},{8,10},{9,11},{10,... | collective-permute-start | bytes 221192 | tf_op jit(solution)/shard_map/ppermute | solution.py:305
  56.5 2.6 %collective-permute-done.5 = f32[144,128]{1,0:T(8,128)S(1)} collective-permute-done((f32[144,128]{1,0:T(8,128)S(1)}, f32[144,128]{1,0:T(8,128)S(1)}, u32[]{:S(2)}, u32[]{:S(2)}) %collective-permute-start.5) | collective-permute-done | bytes 73760 | tf_op jit(solution)/shard_map/ppermute | solution.py:305
  59.1 1.3 %collective-permute-start.6 = (f32[144,128]{1,0:T(8,128)S(1)}, f32[144,128]{1,0:T(8,128)S(1)}, u32[]{:S(2)}, u32[]{:S(2)}) collective-permute-start(f32[144,128]{1,0:T(8,128)S(1)} %select_add_fusion.1), channel_id=1, source_target_pairs={{0,4},{4,0},{8,12},{12,8},{1,5},{5,1},{9,13},{13,9},{2,6},{6,2},{1... | collective-permute-start | bytes 221192 | tf_op jit(solution)/shard_map/ppermute | solution.py:305
  60.4 3.1 %collective-permute-done.6 = f32[144,128]{1,0:T(8,128)S(1)} collective-permute-done((f32[144,128]{1,0:T(8,128)S(1)}, f32[144,128]{1,0:T(8,128)S(1)}, u32[]{:S(2)}, u32[]{:S(2)}) %collective-permute-start.6) | collective-permute-done | bytes 73760 | tf_op jit(solution)/shard_map/ppermute | solution.py:305
  63.5 2.3 %collective-permute-start.7 = (f32[144,128]{1,0:T(8,128)S(1)}, f32[144,128]{1,0:T(8,128)S(1)}, u32[]{:S(2)}, u32[]{:S(2)}) collective-permute-start(f32[144,128]{1,0:T(8,128)S(1)} %add.14), channel_id=1, source_target_pairs={{0,8},{4,12},{8,0},{12,4},{1,9},{5,13},{9,1},{13,5},{2,10},{6,14},... | collective-permute-start | bytes 221192 | tf_op jit(solution)/shard_map/ppermute | solution.py:305
  65.9 3.0 %collective-permute-done.7 = f32[144,128]{1,0:T(8,128)S(1)} collective-permute-done((f32[144,128]{1,0:T(8,128)S(1)}, f32[144,128]{1,0:T(8,128)S(1)}, u32[]{:S(2)}, u32[]{:S(2)}) %collective-permute-start.7) | collective-permute-done | bytes 73760 | tf_op jit(solution)/shard_map/ppermute | solution.py:305
  68.9 1.8 %collective-permute-start.8 = (f32[144,128]{1,0:T(8,128)S(1)}, f32[144,128]{1,0:T(8,128)S(1)}, u32[]{:S(2)}, u32[]{:S(2)}) collective-permute-start(f32[144,128]{1,0:T(8,128)S(1)} %add.15), channel_id=1, source_target_pairs={{0,2},{1,3},{2,0},{3,1},{4,6},{5,7},{6,4},{7,5},{8,10},{9,11},{10,... | collective-permute-start | bytes 221192 | tf_op jit(solution)/shard_map/ppermute | solution.py:305
  70.7 2.6 %collective-permute-done.8 = f32[144,128]{1,0:T(8,128)S(1)} collective-permute-done((f32[144,128]{1,0:T(8,128)S(1)}, f32[144,128]{1,0:T(8,128)S(1)}, u32[]{:S(2)}, u32[]{:S(2)}) %collective-permute-start.8) | collective-permute-done | bytes 73760 | tf_op jit(solution)/shard_map/ppermute | solution.py:305
  73.3 0.1 collective-permute-start.9
  73.4 1.4 %collective-permute-done.9 = f32[288,128]{1,0:T(8,128)S(1)} collective-permute-done((f32[288,128]{1,0:T(8,128)S(1)}, f32[288,128]{1,0:T(8,128)S(1)}, u32[]{:S(2)}, u32[]{:S(2)}) %collective-permute-start.9) | collective-permute-done | bytes 147488 | tf_op jit(solution)/shard_map/ppermute | solution.py:305
  74.8 0.7 shard_map.146
  (19 shorter events, 0.2 us)
Async XLA Ops:
  0.6 1.0 %copy-start.3 = (f32[4,64,128]{2,1,0:T(8,128)S(1)}, f32[4,64,128]{2,1,0:T(8,128)}, u32[]{:S(2)}) copy-start(f32[4,64,128]{2,1,0:T(8,128)} %param.9) | copy-start | bytes 393220
  1.6 0.9 %copy-start.4 = (f32[4,64,128]{2,1,0:T(8,128)S(1)}, f32[4,64,128]{2,1,0:T(8,128)}, u32[]{:S(2)}) copy-start(f32[4,64,128]{2,1,0:T(8,128)} %param.11) | copy-start | bytes 393220
  2.5 0.9 %copy-start.5 = (f32[4,64,128]{2,1,0:T(8,128)S(1)}, f32[4,64,128]{2,1,0:T(8,128)}, u32[]{:S(2)}) copy-start(f32[4,64,128]{2,1,0:T(8,128)} %param.17) | copy-start | bytes 393220
  3.4 0.9 %copy-start.6 = (f32[4,64,128]{2,1,0:T(8,128)S(1)}, f32[4,64,128]{2,1,0:T(8,128)}, u32[]{:S(2)}) copy-start(f32[4,64,128]{2,1,0:T(8,128)} %param.16) | copy-start | bytes 393220
  4.3 0.8 %copy-start.7 = (s32[64,128]{1,0:T(8,128)S(1)}, s32[64,128]{1,0:T(8,128)}, u32[]{:S(2)}) copy-start(s32[64,128]{1,0:T(8,128)} %param.12) | copy-start | bytes 98308
  5.5 12.6 %copy-start = (bf16[256,256]{1,0:T(8,128)(2,1)S(1)}, bf16[256,256]{1,0:T(8,128)(2,1)}, u32[]{:S(2)}) copy-start(bf16[256,256]{1,0:T(8,128)(2,1)} %w_mid.1) | copy-start | bytes 393220
  5.5 7.1 %collective-permute-start = (f32[64,128]{1,0:T(8,128)S(1)}, f32[64,128]{1,0:T(8,128)S(1)}, u32[]{:S(2)}, u32[]{:S(2)}) collective-permute-start(f32[64,128]{1,0:T(8,128)S(1)} %get-tuple-element.19), channel_id=1, source_target_pairs={{0,4},{4,8},{8,12},{12,0},{1,5},{5,9},{9,13},{13,1},{2,6},{6,10},{... | collective-permute-start | bytes 98312 | tf_op jit(solution)/shard_map/ppermute | solution.py:301
  8.6 4.3 %collective-permute-start.1 = (f32[64,128]{1,0:T(8,128)S(1)}, f32[64,128]{1,0:T(8,128)S(1)}, u32[]{:S(2)}, u32[]{:S(2)}) collective-permute-start(f32[64,128]{1,0:T(8,128)S(1)} %get-tuple-element.20), channel_id=1, source_target_pairs={{0,12},{4,0},{8,4},{12,8},{1,13},{5,1},{9,5},{13,9},{2,14},{6,2},{... | collective-permute-start | bytes 98312 | tf_op jit(solution)/shard_map/ppermute | solution.py:301
  12.9 4.4 %collective-permute-start.3 = (f32[23,4,128]{2,1,0:T(4,128)S(1)}, f32[23,4,128]{2,1,0:T(4,128)S(1)}, u32[]{:S(2)}, u32[]{:S(2)}) collective-permute-start(f32[23,4,128]{2,1,0:T(4,128)S(1)} %pad_maximum_fusion.3), channel_id=1, source_target_pairs={{1,0},{2,1},{3,2},{5,4},{6,5},{7,6},{9,8},{10,9},{11,10},{13,12},{... | collective-permute-start | bytes 141320 | tf_op jit(solution)/shard_map/ppermute | solution.py:301
  14.2 3.9 %copy-start.1 = (bf16[12,256]{1,0:T(8,128)(2,1)S(1)}, bf16[12,256]{1,0:T(8,128)(2,1)}, u32[]{:S(2)}) copy-start(bf16[12,256]{1,0:T(8,128)(2,1)} %w_in.1) | copy-start | bytes 18436
  14.2 3.9 %collective-permute-start.2 = (f32[23,4,128]{2,1,0:T(4,128)S(1)}, f32[23,4,128]{2,1,0:T(4,128)S(1)}, u32[]{:S(2)}, u32[]{:S(2)}) collective-permute-start(f32[23,4,128]{2,1,0:T(4,128)S(1)} %pad_maximum_fusion.2), channel_id=1, source_target_pairs={{0,1},{1,2},{2,3},{4,5},{5,6},{6,7},{8,9},{9,10},{10,11},{12,13},{... | collective-permute-start | bytes 141320 | tf_op jit(solution)/shard_map/ppermute | solution.py:301
  17.3 0.9 %copy-start.2 = (bf16[256,4]{0,1:T(4,128)(2,1)S(1)}, bf16[256,4]{0,1:T(4,128)(2,1)}, u32[]{:S(2)}) copy-start(bf16[256,4]{0,1:T(4,128)(2,1)} %param.15) | copy-start | bytes 6148
  51.4 2.5 %collective-permute-start.4 = (f32[288,128]{1,0:T(8,128)S(1)}, f32[288,128]{1,0:T(8,128)S(1)}, u32[]{:S(2)}, u32[]{:S(2)}) collective-permute-start(f32[288,128]{1,0:T(8,128)S(1)} %slice_select_fusion), channel_id=1, source_target_pairs={{0,1},{1,0},{2,3},{3,2},{4,5},{5,4},{6,7},{7,6},{8,9},{9,8},{10,11... | collective-permute-start | bytes 442376 | tf_op jit(solution)/shard_map/ppermute | solution.py:305
  53.9 5.2 %collective-permute-start.5 = (f32[144,128]{1,0:T(8,128)S(1)}, f32[144,128]{1,0:T(8,128)S(1)}, u32[]{:S(2)}, u32[]{:S(2)}) collective-permute-start(f32[144,128]{1,0:T(8,128)S(1)} %slice_select_fusion.1), channel_id=1, source_target_pairs={{0,2},{1,3},{2,0},{3,1},{4,6},{5,7},{6,4},{7,5},{8,10},{9,11},{10,... | collective-permute-start | bytes 221192 | tf_op jit(solution)/shard_map/ppermute | solution.py:305
  59.1 4.4 %collective-permute-start.6 = (f32[144,128]{1,0:T(8,128)S(1)}, f32[144,128]{1,0:T(8,128)S(1)}, u32[]{:S(2)}, u32[]{:S(2)}) collective-permute-start(f32[144,128]{1,0:T(8,128)S(1)} %select_add_fusion.1), channel_id=1, source_target_pairs={{0,4},{4,0},{8,12},{12,8},{1,5},{5,1},{9,13},{13,9},{2,6},{6,2},{1... | collective-permute-start | bytes 221192 | tf_op jit(solution)/shard_map/ppermute | solution.py:305
  63.5 5.3 %collective-permute-start.7 = (f32[144,128]{1,0:T(8,128)S(1)}, f32[144,128]{1,0:T(8,128)S(1)}, u32[]{:S(2)}, u32[]{:S(2)}) collective-permute-start(f32[144,128]{1,0:T(8,128)S(1)} %add.14), channel_id=1, source_target_pairs={{0,8},{4,12},{8,0},{12,4},{1,9},{5,13},{9,1},{13,5},{2,10},{6,14},... | collective-permute-start | bytes 221192 | tf_op jit(solution)/shard_map/ppermute | solution.py:305
  68.9 4.4 %collective-permute-start.8 = (f32[144,128]{1,0:T(8,128)S(1)}, f32[144,128]{1,0:T(8,128)S(1)}, u32[]{:S(2)}, u32[]{:S(2)}) collective-permute-start(f32[144,128]{1,0:T(8,128)S(1)} %add.15), channel_id=1, source_target_pairs={{0,2},{1,3},{2,0},{3,1},{4,6},{5,7},{6,4},{7,5},{8,10},{9,11},{10,... | collective-permute-start | bytes 221192 | tf_op jit(solution)/shard_map/ppermute | solution.py:305
  73.3 1.4 %collective-permute-start.9 = (f32[288,128]{1,0:T(8,128)S(1)}, f32[288,128]{1,0:T(8,128)S(1)}, u32[]{:S(2)}, u32[]{:S(2)}) collective-permute-start(f32[288,128]{1,0:T(8,128)S(1)} %pad_maximum_fusion.1), channel_id=1, source_target_pairs={{0,1},{1,0},{2,3},{3,2},{4,5},{5,4},{6,7},{7,6},{8,9},{9,8},{10,11... | collective-permute-start | bytes 442376 | tf_op jit(solution)/shard_map/ppermute | solution.py:305

commit v3 on v2

--- a/solution.py
+++ b/solution.py
@@ -14,6 +14,7 @@
 WIDE = 4
 LANES = 128
 TILES = 8
+PART = 2
 DEEP = 16
 SHALLOW = 8
 
@@ -29,12 +30,24 @@
     return lax.dot_general(left, right, (((1,), (1,)), ((), ())), preferred_element_type=F32)
 
 
-def pack_kernel(fields, west, east, top, bottom):
-    count, rows, cols = fields.shape
+def pack_kernel(now, old, drift, cnew, cmid, ocean, west, east, top, bottom, fields, wet, sems):
+    levels, rows, cols = now.shape
+    copies = [
+        pltpu.make_async_copy(ref, fields.at[pl.ds(levels * f, levels)], sems.at[f])
+        for f, ref in enumerate((now, old, drift, cnew, cmid))
+    ]
+    copies.append(pltpu.make_async_copy(ocean, wet, sems.at[5]))
+    for copy in copies:
+        copy.start()
     lane = lax.broadcasted_iota(jnp.int32, (rows, LANES), 1)
     to_west = jnp.zeros((rows, LANES), F32)
     to_east = jnp.zeros((rows, LANES), F32)
+    count = fields.shape[0]
     for p in range(count):
+        if p % levels == 0:
+            copies[p // levels].wait()
+        if p == count - 1:
+            fields[p] = wet[...].astype(F32)
         plane = fields[p]
         here = (lane >= WIDE * p) & (lane < WIDE * (p + 1))
         to_west = jnp.where(here, pltpu.roll(plane, WIDE * p, 1) if p else plane, to_west)
@@ -167,9 +180,9 @@
         return dz_one, dz_two, dfeat
 
     def add_terms(x, first, second, cot, dz_one, dz_two):
-        acc_mid[...] += dot_nt(first.astype(BF16), dz_two)
+        acc_mid[...] += dot_nt(first, dz_two)
         acc_in[...] += dot_nt(x, dz_one)
-        acc_out[...] += dot_nt(cot, second.astype(BF16))
+        acc_out[...] += dot_nt(cot, second)
 
     def features_of(source, ft):
         for level in range(levels):
@@ -195,11 +208,12 @@
     features_of(planes, ft1)
 
     def first_step(c, carry):
-        base = pl.multiple_of(c * TILES, TILES)
-        first, second = forward(inputs_at(ft1, base, TILES))
-        keep1[c] = first
-        keep2[c] = second
-        put_lanes(cl, SHALLOW, base, TILES, closure(second))
+        for k in range(0, TILES, PART):
+            base = pl.multiple_of(c * TILES + k, PART)
+            first, second = forward(inputs_at(ft1, base, PART))
+            keep1[c, :, pl.ds(k * LANES, PART * LANES)] = first
+            keep2[c, :, pl.ds(k * LANES, PART * LANES)] = second
+            put_lanes(cl, SHALLOW, base, PART, closure(second))
         return carry
 
     lax.fori_loop(0, keep1.shape[0], first_step, 0)
@@ -215,14 +229,17 @@
     cotangents_of(planes, 3 * levels)
 
     def second_step(c, carry):
-        base = pl.multiple_of(c * TILES, TILES)
-        x = inputs_at(ft2, base, TILES)
-        cot = cotangents_at(base, TILES)
-        first, second = forward(x)
-        put_lanes(cl, SHALLOW, base, TILES, closure(second))
-        dz_one, dz_two, dfeat = backward(first, second, cot)
-        put_lanes(df, DEEP, base, TILES, dfeat)
-        add_terms(x, first, second, cot, dz_one, dz_two)
+        parts = []
+        for k in range(0, TILES, PART):
+            base = pl.multiple_of(c * TILES + k, PART)
+            x = inputs_at(ft2, base, PART)
+            cot = cotangents_at(base, PART)
+            first, second = forward(x)
+            put_lanes(cl, SHALLOW, base, PART, closure(second))
+            dz_one, dz_two, dfeat = backward(first, second, cot)
+            put_lanes(df, DEEP, base, PART, dfeat)
+            parts.append((x, first.astype(BF16), second.astype(BF16), cot, dz_one, dz_two))
+        add_terms(*(jnp.concatenate(part, 1) for part in zip(*parts)))
         return carry
 
     lax.fori_loop(0, chunks, second_step, 0)
@@ -253,14 +270,17 @@
     cotangents_of(olds, 0)
 
     def third_step(c, carry):
-        base = pl.multiple_of(c * TILES, TILES)
-        x = inputs_at(ft1, base, TILES)
-        cot = cotangents_at(base, TILES)
-        first = keep1[c]
-        second = keep2[c]
-        dz_one, dz_two, dfeat = backward(first, second, cot)
-        put_lanes(df, DEEP, base, TILES, dfeat)
-        add_terms(x, first, second, cot, dz_one, dz_two)
+        parts = []
+        for k in range(0, TILES, PART):
+            base = pl.multiple_of(c * TILES + k, PART)
+            x = inputs_at(ft1, base, PART)
+            cot = cotangents_at(base, PART)
+            first = keep1[c, :, pl.ds(k * LANES, PART * LANES)]
+            second = keep2[c, :, pl.ds(k * LANES, PART * LANES)]
+            dz_one, dz_two, dfeat = backward(first, second, cot)
+            put_lanes(df, DEEP, base, PART, dfeat)
+            parts.append((x, first.astype(BF16), second.astype(BF16), cot, dz_one, dz_two))
+        add_terms(*(jnp.concatenate(part, 1) for part in zip(*parts)))
         return carry
 
     lax.fori_loop(0, chunks, third_step, 0)
@@ -306,24 +326,16 @@
 
 
 def summed_over(value, halving, doubling):
-    bits = []
-    bit = 1
-    while bit < lax.axis_size(halving):
-        upper = (lax.axis_index(halving) & bit) != 0
-        half = value.shape[0] // 2
-        lower_part, upper_part = value[:half], value[half:]
-        sent = jnp.where(upper, lower_part, upper_part)
-        value = jnp.where(upper, upper_part, lower_part) + swapped(sent, halving, bit)
-        bits.append((bit, upper))
-        bit *= 2
+    members = lax.axis_size(halving)
+    piece = value.shape[0] // members
+    value = lax.all_to_all(value.reshape(members, piece, LANES), halving, 0, 0)
+    value = jnp.sum(value, 0)
     bit = 1
     while bit < lax.axis_size(doubling):
         value = value + swapped(value, doubling, bit)
         bit *= 2
-    for bit, upper in reversed(bits):
-        other = swapped(value, halving, bit)
-        value = jnp.concatenate([jnp.where(upper, other, value), jnp.where(upper, value, other)], 0)
-    return value
+    value = jnp.broadcast_to(value[None], (members, piece, LANES))
+    return lax.all_to_all(value, halving, 0, 0).reshape(members * piece, LANES)
 
 
 def body(state_old, state_now, drift, ocean, w_in, w_mid, w_out, cot_mid, cot_new):
@@ -337,15 +349,17 @@
     vmem = pl.BlockSpec(memory_space=pltpu.VMEM)
     strip = jax.ShapeDtypeStruct((rows, LANES), F32)
     edge = jax.ShapeDtypeStruct((count, WIDE, LANES), F32)
-    wet = ocean.astype(F32)[None]
-    fields = jnp.concatenate([state_now, state_old, drift, cot_new, cot_mid, wet], 0)
-    west, east, top, bottom = pl.pallas_call(
+    place = pl.BlockSpec(memory_space=pltpu.HBM)
+    arrays = (state_now, state_old, drift, cot_new, cot_mid, ocean)
+    arrays = tuple(pltpu.with_memory_space_constraint(a, pltpu.HBM) for a in arrays)
+    west, east, top, bottom, fields = pl.pallas_call(
         pack_kernel,
-        out_shape=(strip, strip, edge, edge),
-        in_specs=[vmem],
-        out_specs=(vmem,) * 4,
+        out_shape=(strip, strip, edge, edge, jax.ShapeDtypeStruct((count, rows, cols), F32)),
+        in_specs=[place] * 6,
+        out_specs=(vmem,) * 5,
+        scratch_shapes=[pltpu.VMEM((rows, cols), jnp.int32), pltpu.SemaphoreType.DMA((6,))],
         compiler_params=pltpu.CompilerParams(vmem_limit_bytes=8 * 2**20),
-    )(fields)
+    )(*arrays)
     left = along(east, "lon", 1, True)
     right = along(west, "lon", -1, True)
     up = jnp.concatenate([bottom, left[None, rows - WIDE :], right[None, rows - WIDE :]], 0)

time: 75.9 us -> 112 us (1.48)
  Pallas kernels: 34.4 us -> 68.4 us
  blocking collectives: 0 us -> 19 us
  starting transfers between devices: 19.1 us -> 11.4 us
  waiting for transfers between devices: 16.7 us -> 11.8 us
  local copies, waits for them, and re-layouts: 4.43 us -> 0.05 us
    pallas_call x1, Pallas kernels: 33.2 us -> 65.9 us  [body(): pl.pallas_call(main_kernel, out_shape=(field, field, field, field, jax.Sh...]
    all_to_all x0 -> x2, blocking collectives: none -> 19 us  [the longest x1 10.2 us: summed_over(): value = lax.all_to_all(value.reshape(members, piece, LANES), halving, 0, 0)]
    ppermute x6 -> x2, waiting for transfers between devices: 13.7 us -> 6.11 us  [swapped(): lax.ppermute(value, axis, [(i, i ^ bit) for i in range(lax.axis_size(axis...]
    ppermute x6 -> x2, starting transfers between devices: 9.61 us -> 3.64 us  [swapped(): lax.ppermute(value, axis, [(i, i ^ bit) for i in range(lax.axis_size(axis...]
    unnamed x21 -> x6, local copies, waits for them, and re-layouts: 4.42 us -> 0.02 us
    ppermute x4, waiting for transfers between devices: 3 us -> 5.71 us  [along(): return lax.ppermute(value, axis, pairs)]
    ppermute x4, starting transfers between devices: 9.49 us -> 7.75 us  [along(): return lax.ppermute(value, axis, pairs)]
    pallas_call x1, Pallas kernels: 0.41 us -> 1.71 us  [body(): pl.pallas_call(pack_kernel, out_shape=(strip, strip, edge, edge, jax.Shap...]
  transfers between devices with their start and end apart: 10 -> 6, of which waited for: 9 -> 5; matrix products, arithmetic and copies ran while one was open for 0% -> 0% of each run, Pallas kernels for 0% -> 0%
where the time goes in v3:
time: 112 us; the launch traced here: 111 us
  Pallas kernels  68.4 us (61%)
  blocking collectives  19 us (17%)
  waiting for transfers between devices  11.8 us (11%)
  starting transfers between devices  11.4 us (10%)
    pallas_call x1, Pallas kernels, body(): pl.pallas_call(main_kernel, out_shape=(field, field, field, field, jax.Sh...  65.9 us
    all_to_all x1, blocking collectives, summed_over(): value = lax.all_to_all(value.reshape(members, piece, LANES), halving, 0, 0)  10.2 us
    all_to_all x1, blocking collectives, summed_over(): return lax.all_to_all(value, halving, 0, 0).reshape(members * piece, LANES)  8.75 us
    ppermute x4, starting transfers between devices, along(): return lax.ppermute(value, axis, pairs)  7.75 us
    ppermute x2, waiting for transfers between devices, swapped(): lax.ppermute(value, axis, [(i, i ^ bit) for i in range(lax.axis_size(axis...  6.11 us
    ppermute x4, waiting for transfers between devices, along(): return lax.ppermute(value, axis, pairs)  5.71 us
    ppermute x2, starting transfers between devices, swapped(): lax.ppermute(value, axis, [(i, i ^ bit) for i in range(lax.axis_size(axis...  3.64 us
  transfers between devices with their start and end apart: 6, of which 5 were waited for; matrix products, arithmetic and copies ran while one was open for 0% of the time, Pallas kernels for 0%

profile of v3, /device:TPU:0, one launch (start us, length us, event | category | flops | bytes accessed | tf_op | source)
XLA Modules:
  0.0 111.4 jit_solution(16210393033871177602)
XLA Ops:
  0.6 1.7 %shard_map.144 = (f32[64,128]{1,0:T(8,128)S(1)}, f32[64,128]{1,0:T(8,128)S(1)}, f32[21,4,128]{2,1,0:T(4,128)S(1)}, f32[21,4,128]{2,1,0:T(4,128)S(1)}, f32[21,64,128]{2,1,0:T(8,128)S(1)}) custom-call(f32[4,64,128]{2,1,0:T(8,128)} %now.1, f32[4,64,128]{2,1,0:T(8,128)} %old.1, f32[4,64,128]{2,1,0:T(8,128)} %drift.1, f32[4,64,128]{2,1,0:T(8,128)} %cnew.1, ...), custom_call_target="tpu_custom_call" | custom-call | tf_op jit(solution)/shard_map/pallas_call | solution.py:355
  2.3 0.0 copy-start
  2.4 3.1 %collective-permute-start = (f32[64,128]{1,0:T(8,128)S(1)}, f32[64,128]{1,0:T(8,128)S(1)}, u32[]{:S(2)}, u32[]{:S(2)}) collective-permute-start(f32[64,128]{1,0:T(8,128)S(1)} %get-tuple-element.21), channel_id=1, source_target_pairs={{0,4},{4,8},{8,12},{12,0},{1,5},{5,9},{9,13},{13,1},{2,6},{6,10},{... | collective-permute-start | bytes 98312 | tf_op jit(solution)/shard_map/ppermute | solution.py:321
  5.4 2.1 %collective-permute-start.1 = (f32[64,128]{1,0:T(8,128)S(1)}, f32[64,128]{1,0:T(8,128)S(1)}, u32[]{:S(2)}, u32[]{:S(2)}) collective-permute-start(f32[64,128]{1,0:T(8,128)S(1)} %get-tuple-element.22), channel_id=1, source_target_pairs={{0,12},{4,0},{8,4},{12,8},{1,13},{5,1},{9,5},{13,9},{2,14},{6,2},{... | collective-permute-start | bytes 98312 | tf_op jit(solution)/shard_map/ppermute | solution.py:321
  7.5 1.9 %collective-permute-done.left = f32[64,128]{1,0:T(8,128)S(1)} collective-permute-done((f32[64,128]{1,0:T(8,128)S(1)}, f32[64,128]{1,0:T(8,128)S(1)}, u32[]{:S(2)}, u32[]{:S(2)}) %collective-permute-start) | collective-permute-done | bytes 32800 | tf_op jit(solution)/shard_map/ppermute | solution.py:321
  9.5 0.2 collective-permute-done.1.right
  9.7 1.3 %collective-permute-start.2 = (f32[23,4,128]{2,1,0:T(4,128)S(1)}, f32[23,4,128]{2,1,0:T(4,128)S(1)}, u32[]{:S(2)}, u32[]{:S(2)}) collective-permute-start(f32[23,4,128]{2,1,0:T(4,128)S(1)} %pad_maximum_fusion), channel_id=1, source_target_pairs={{0,1},{1,2},{2,3},{4,5},{5,6},{6,7},{8,9},{9,10},{10,11},{12,13},{... | collective-permute-start | bytes 141320 | tf_op jit(solution)/shard_map/ppermute | solution.py:321
  11.0 0.0 copy-start.1
  11.1 0.0 copy-start.2
  11.1 1.3 %collective-permute-start.3 = (f32[23,4,128]{2,1,0:T(4,128)S(1)}, f32[23,4,128]{2,1,0:T(4,128)S(1)}, u32[]{:S(2)}, u32[]{:S(2)}) collective-permute-start(f32[23,4,128]{2,1,0:T(4,128)S(1)} %pad_maximum_fusion.1), channel_id=1, source_target_pairs={{1,0},{2,1},{3,2},{5,4},{6,5},{7,6},{9,8},{10,9},{11,10},{13,12},{... | collective-permute-start | bytes 141320 | tf_op jit(solution)/shard_map/ppermute | solution.py:321
  12.4 0.0 collective-permute-done.2.low
  12.4 3.5 %collective-permute-done.3.high = f32[23,4,128]{2,1,0:T(4,128)S(1)} collective-permute-done((f32[23,4,128]{2,1,0:T(4,128)S(1)}, f32[23,4,128]{2,1,0:T(4,128)S(1)}, u32[]{:S(2)}, u32[]{:S(2)}) %collective-permute-start.3) | collective-permute-done | bytes 47136 | tf_op jit(solution)/shard_map/ppermute | solution.py:321
  15.9 0.0 copy-done
  15.9 0.0 copy-done.1
  15.9 0.0 copy-done.2
  15.9 65.9 %shard_map.145 = (f32[4,64,128]{2,1,0:T(8,128)}, f32[4,64,128]{2,1,0:T(8,128)}, f32[4,64,128]{2,1,0:T(8,128)}, f32[4,64,128]{2,1,0:T(8,128)}, f32[576,128]{1,0:T(8,128)S(1)}) custom-call(f32[21,64,128]{2,1,0:T(8,128)S(1)} %get-tuple-element.20.fields, f32[64,128]{1,0:T(8,128)S(1)} %collective-permute-done.left, f32[64,128]{1,0:T(8,128)S(1)} %collective-permute-done.1.right, ...), custom_call_target="tpu_custom_call" | custom-call | tf_op jit(solution)/shard_map/pallas_call | solution.py:381
  81.8 10.2 %all_to_all.10 = f32[4,144,128]{2,1,0:T(8,128)S(1)} all-to-all(f32[4,144,128]{2,1,0:T(8,128)S(1)} %bitcast.13), channel_id=1, replica_groups=mesh['grp'=2,'lon'=4,'lat'=4] {'lat'}, dimensions={0} | all-to-all | bytes 589824 | tf_op jit(solution)/shard_map/all_to_all | solution.py:331
  92.1 1.3 %collective-permute-start.4 = (f32[144,128]{1,0:T(8,128)S(1)}, f32[144,128]{1,0:T(8,128)S(1)}, u32[]{:S(2)}, u32[]{:S(2)}) collective-permute-start(f32[144,128]{1,0:T(8,128)S(1)} %reduce_sum.9), channel_id=1, source_target_pairs={{0,4},{4,0},{8,12},{12,8},{1,5},{5,1},{9,13},{13,9},{2,6},{6,2},{1... | collective-permute-start | bytes 221192 | tf_op jit(solution)/shard_map/ppermute | solution.py:325
  93.4 3.1 %collective-permute-done.4 = f32[144,128]{1,0:T(8,128)S(1)} collective-permute-done((f32[144,128]{1,0:T(8,128)S(1)}, f32[144,128]{1,0:T(8,128)S(1)}, u32[]{:S(2)}, u32[]{:S(2)}) %collective-permute-start.4) | collective-permute-done | bytes 73760 | tf_op jit(solution)/shard_map/ppermute | solution.py:325
  96.5 2.3 %collective-permute-start.5 = (f32[144,128]{1,0:T(8,128)S(1)}, f32[144,128]{1,0:T(8,128)S(1)}, u32[]{:S(2)}, u32[]{:S(2)}) collective-permute-start(f32[144,128]{1,0:T(8,128)S(1)} %add.6), channel_id=1, source_target_pairs={{0,8},{4,12},{8,0},{12,4},{1,9},{5,13},{9,1},{13,5},{2,10},{6,14},... | collective-permute-start | bytes 221192 | tf_op jit(solution)/shard_map/ppermute | solution.py:325
  98.9 3.0 %collective-permute-done.5 = f32[144,128]{1,0:T(8,128)S(1)} collective-permute-done((f32[144,128]{1,0:T(8,128)S(1)}, f32[144,128]{1,0:T(8,128)S(1)}, u32[]{:S(2)}, u32[]{:S(2)}) %collective-permute-start.5) | collective-permute-done | bytes 73760 | tf_op jit(solution)/shard_map/ppermute | solution.py:325
  101.9 8.8 %all_to_all.11 = f32[4,144,128]{2,1,0:T(8,128)S(1)} all-to-all(f32[4,144,128]{2,1,0:T(8,128)S(1)} %broadcast_in_dim.22), channel_id=1, replica_groups=mesh['grp'=2,'lon'=4,'lat'=4] {'lat'}, dimensions={0} | all-to-all | bytes 589824 | tf_op jit(solution)/shard_map/all_to_all | solution.py:338
  110.6 0.7 shard_map.146
  (8 shorter events, 0.1 us)
Async XLA Ops:
  2.3 13.6 %copy-start = (bf16[256,256]{1,0:T(8,128)(2,1)S(1)}, bf16[256,256]{1,0:T(8,128)(2,1)}, u32[]{:S(2)}) copy-start(bf16[256,256]{1,0:T(8,128)(2,1)} %w_mid.1) | copy-start | bytes 393220
  2.4 7.1 %collective-permute-start = (f32[64,128]{1,0:T(8,128)S(1)}, f32[64,128]{1,0:T(8,128)S(1)}, u32[]{:S(2)}, u32[]{:S(2)}) collective-permute-start(f32[64,128]{1,0:T(8,128)S(1)} %get-tuple-element.21), channel_id=1, source_target_pairs={{0,4},{4,8},{8,12},{12,0},{1,5},{5,9},{9,13},{13,1},{2,6},{6,10},{... | collective-permute-start | bytes 98312 | tf_op jit(solution)/shard_map/ppermute | solution.py:321
  5.4 4.3 %collective-permute-start.1 = (f32[64,128]{1,0:T(8,128)S(1)}, f32[64,128]{1,0:T(8,128)S(1)}, u32[]{:S(2)}, u32[]{:S(2)}) collective-permute-start(f32[64,128]{1,0:T(8,128)S(1)} %get-tuple-element.22), channel_id=1, source_target_pairs={{0,12},{4,0},{8,4},{12,8},{1,13},{5,1},{9,5},{13,9},{2,14},{6,2},{... | collective-permute-start | bytes 98312 | tf_op jit(solution)/shard_map/ppermute | solution.py:321
  9.7 2.6 %collective-permute-start.2 = (f32[23,4,128]{2,1,0:T(4,128)S(1)}, f32[23,4,128]{2,1,0:T(4,128)S(1)}, u32[]{:S(2)}, u32[]{:S(2)}) collective-permute-start(f32[23,4,128]{2,1,0:T(4,128)S(1)} %pad_maximum_fusion), channel_id=1, source_target_pairs={{0,1},{1,2},{2,3},{4,5},{5,6},{6,7},{8,9},{9,10},{10,11},{12,13},{... | collective-permute-start | bytes 141320 | tf_op jit(solution)/shard_map/ppermute | solution.py:321
  11.0 4.9 %copy-start.1 = (bf16[12,256]{1,0:T(8,128)(2,1)S(1)}, bf16[12,256]{1,0:T(8,128)(2,1)}, u32[]{:S(2)}) copy-start(bf16[12,256]{1,0:T(8,128)(2,1)} %w_in.1) | copy-start | bytes 18436
  11.1 4.9 %copy-start.2 = (bf16[256,4]{0,1:T(4,128)(2,1)S(1)}, bf16[256,4]{0,1:T(4,128)(2,1)}, u32[]{:S(2)}) copy-start(bf16[256,4]{0,1:T(4,128)(2,1)} %param.15) | copy-start | bytes 6148
  11.1 4.8 %collective-permute-start.3 = (f32[23,4,128]{2,1,0:T(4,128)S(1)}, f32[23,4,128]{2,1,0:T(4,128)S(1)}, u32[]{:S(2)}, u32[]{:S(2)}) collective-permute-start(f32[23,4,128]{2,1,0:T(4,128)S(1)} %pad_maximum_fusion.1), channel_id=1, source_target_pairs={{1,0},{2,1},{3,2},{5,4},{6,5},{7,6},{9,8},{10,9},{11,10},{13,12},{... | collective-permute-start | bytes 141320 | tf_op jit(solution)/shard_map/ppermute | solution.py:321
  92.1 4.4 %collective-permute-start.4 = (f32[144,128]{1,0:T(8,128)S(1)}, f32[144,128]{1,0:T(8,128)S(1)}, u32[]{:S(2)}, u32[]{:S(2)}) collective-permute-start(f32[144,128]{1,0:T(8,128)S(1)} %reduce_sum.9), channel_id=1, source_target_pairs={{0,4},{4,0},{8,12},{12,8},{1,5},{5,1},{9,13},{13,9},{2,6},{6,2},{1... | collective-permute-start | bytes 221192 | tf_op jit(solution)/shard_map/ppermute | solution.py:325
  96.5 5.3 %collective-permute-start.5 = (f32[144,128]{1,0:T(8,128)S(1)}, f32[144,128]{1,0:T(8,128)S(1)}, u32[]{:S(2)}, u32[]{:S(2)}) collective-permute-start(f32[144,128]{1,0:T(8,128)S(1)} %add.6), channel_id=1, source_target_pairs={{0,8},{4,12},{8,0},{12,4},{1,9},{5,13},{9,1},{13,5},{2,10},{6,14},... | collective-permute-start | bytes 221192 | tf_op jit(solution)/shard_map/ppermute | solution.py:325

commit v4 on v3

--- a/solution.py
+++ b/solution.py
@@ -13,8 +13,8 @@
 
 WIDE = 4
 LANES = 128
-TILES = 8
-PART = 2
+TILES = 16
+PART = 16
 DEEP = 16
 SHALLOW = 8
 
@@ -326,16 +326,24 @@
 
 
 def summed_over(value, halving, doubling):
-    members = lax.axis_size(halving)
-    piece = value.shape[0] // members
-    value = lax.all_to_all(value.reshape(members, piece, LANES), halving, 0, 0)
-    value = jnp.sum(value, 0)
+    bits = []
+    bit = 1
+    while bit < lax.axis_size(halving):
+        upper = (lax.axis_index(halving) & bit) != 0
+        half = value.shape[0] // 2
+        lower_part, upper_part = value[:half], value[half:]
+        sent = jnp.where(upper, lower_part, upper_part)
+        value = jnp.where(upper, upper_part, lower_part) + swapped(sent, halving, bit)
+        bits.append((bit, upper))
+        bit *= 2
     bit = 1
     while bit < lax.axis_size(doubling):
         value = value + swapped(value, doubling, bit)
         bit *= 2
-    value = jnp.broadcast_to(value[None], (members, piece, LANES))
-    return lax.all_to_all(value, halving, 0, 0).reshape(members * piece, LANES)
+    for bit, upper in reversed(bits):
+        other = swapped(value, halving, bit)
+        value = jnp.concatenate([jnp.where(upper, other, value), jnp.where(upper, value, other)], 0)
+    return value
 
 
 def body(state_old, state_now, drift, ocean, w_in, w_mid, w_out, cot_mid, cot_new):

time: 112 us -> 67.7 us (0.60)
  Pallas kernels: 68.4 us -> 30.8 us
  blocking collectives: 19 us -> 0 us
  starting transfers between devices: 11.4 us -> 19.1 us
  waiting for transfers between devices: 11.8 us -> 16.7 us
    pallas_call x1, Pallas kernels: 65.9 us -> 28.3 us  [body(): pl.pallas_call(main_kernel, out_shape=(field, field, field, field, jax.Sh...]
    all_to_all x2 -> x0, blocking collectives: 19 us -> none  [the longest x1 10.2 us: summed_over(): value = lax.all_to_all(value.reshape(members, piece, LANES), halving, 0, 0)]
    ppermute x2 -> x6, waiting for transfers between devices: 6.11 us -> 13.7 us  [swapped(): lax.ppermute(value, axis, [(i, i ^ bit) for i in range(lax.axis_size(axis...]
    ppermute x2 -> x6, starting transfers between devices: 3.64 us -> 9.63 us  [swapped(): lax.ppermute(value, axis, [(i, i ^ bit) for i in range(lax.axis_size(axis...]
    ppermute x4, waiting for transfers between devices: 5.71 us -> 3 us  [along(): return lax.ppermute(value, axis, pairs)]
    ppermute x4, starting transfers between devices: 7.75 us -> 9.49 us  [along(): return lax.ppermute(value, axis, pairs)]
  transfers between devices with their start and end apart: 6 -> 10, of which waited for: 5 -> 9; matrix products, arithmetic and copies ran while one was open for 0% -> 0% of each run, Pallas kernels for 0% -> 0%
where the time goes in v4:
time: 67.7 us; the launch traced here: 67.5 us
  Pallas kernels  30.8 us (45%)
  starting transfers between devices  19.1 us (28%)
  waiting for transfers between devices  16.7 us (25%)
  between operations  0.77 us (1%)
    pallas_call x1, Pallas kernels, body(): pl.pallas_call(main_kernel, out_shape=(field, field, field, field, jax.Sh...  28.3 us
    ppermute x6, waiting for transfers between devices, swapped(): lax.ppermute(value, axis, [(i, i ^ bit) for i in range(lax.axis_size(axis...  13.7 us
    ppermute x6, starting transfers between devices, swapped(): lax.ppermute(value, axis, [(i, i ^ bit) for i in range(lax.axis_size(axis...  9.63 us
    ppermute x4, starting transfers between devices, along(): return lax.ppermute(value, axis, pairs)  9.49 us
    ppermute x4, waiting for transfers between devices, along(): return lax.ppermute(value, axis, pairs)  3 us
    pallas_call x1, Pallas kernels, body(): pl.pallas_call(pack_kernel, out_shape=(strip, strip, edge, edge, jax.Shap...  1.71 us
  transfers between devices with their start and end apart: 10, of which 9 were waited for; matrix products, arithmetic and copies ran while one was open for 0% of the time, Pallas kernels for 0%

profile of v4, /device:TPU:0, one launch (start us, length us, event | category | flops | bytes accessed | tf_op | source)
XLA Modules:
  0.0 67.5 jit_solution(11995994823066507350)
XLA Ops:
  0.6 1.7 %shard_map.144 = (f32[64,128]{1,0:T(8,128)S(1)}, f32[64,128]{1,0:T(8,128)S(1)}, f32[21,4,128]{2,1,0:T(4,128)S(1)}, f32[21,4,128]{2,1,0:T(4,128)S(1)}, f32[21,64,128]{2,1,0:T(8,128)S(1)}) custom-call(f32[4,64,128]{2,1,0:T(8,128)} %now.1, f32[4,64,128]{2,1,0:T(8,128)} %old.1, f32[4,64,128]{2,1,0:T(8,128)} %drift.1, f32[4,64,128]{2,1,0:T(8,128)} %cnew.1, ...), custom_call_target="tpu_custom_call" | custom-call | tf_op jit(solution)/shard_map/pallas_call | solution.py:363
  2.3 0.0 copy-start
  2.4 3.1 %collective-permute-start = (f32[64,128]{1,0:T(8,128)S(1)}, f32[64,128]{1,0:T(8,128)S(1)}, u32[]{:S(2)}, u32[]{:S(2)}) collective-permute-start(f32[64,128]{1,0:T(8,128)S(1)} %get-tuple-element.21), channel_id=1, source_target_pairs={{0,4},{4,8},{8,12},{12,0},{1,5},{5,9},{9,13},{13,1},{2,6},{6,10},{... | collective-permute-start | bytes 98312 | tf_op jit(solution)/shard_map/ppermute | solution.py:321
  5.4 2.1 %collective-permute-start.1 = (f32[64,128]{1,0:T(8,128)S(1)}, f32[64,128]{1,0:T(8,128)S(1)}, u32[]{:S(2)}, u32[]{:S(2)}) collective-permute-start(f32[64,128]{1,0:T(8,128)S(1)} %get-tuple-element.22), channel_id=1, source_target_pairs={{0,12},{4,0},{8,4},{12,8},{1,13},{5,1},{9,5},{13,9},{2,14},{6,2},{... | collective-permute-start | bytes 98312 | tf_op jit(solution)/shard_map/ppermute | solution.py:321
  7.5 1.9 %collective-permute-done.left = f32[64,128]{1,0:T(8,128)S(1)} collective-permute-done((f32[64,128]{1,0:T(8,128)S(1)}, f32[64,128]{1,0:T(8,128)S(1)}, u32[]{:S(2)}, u32[]{:S(2)}) %collective-permute-start) | collective-permute-done | bytes 32800 | tf_op jit(solution)/shard_map/ppermute | solution.py:321
  9.5 0.2 collective-permute-done.1.right
  9.7 1.3 %collective-permute-start.3 = (f32[23,4,128]{2,1,0:T(4,128)S(1)}, f32[23,4,128]{2,1,0:T(4,128)S(1)}, u32[]{:S(2)}, u32[]{:S(2)}) collective-permute-start(f32[23,4,128]{2,1,0:T(4,128)S(1)} %pad_maximum_fusion.3), channel_id=1, source_target_pairs={{1,0},{2,1},{3,2},{5,4},{6,5},{7,6},{9,8},{10,9},{11,10},{13,12},{... | collective-permute-start | bytes 141320 | tf_op jit(solution)/shard_map/ppermute | solution.py:321
  11.0 0.0 copy-start.1
  11.1 3.0 %collective-permute-start.2 = (f32[23,4,128]{2,1,0:T(4,128)S(1)}, f32[23,4,128]{2,1,0:T(4,128)S(1)}, u32[]{:S(2)}, u32[]{:S(2)}) collective-permute-start(f32[23,4,128]{2,1,0:T(4,128)S(1)} %pad_maximum_fusion.2), channel_id=1, source_target_pairs={{0,1},{1,2},{2,3},{4,5},{5,6},{6,7},{8,9},{9,10},{10,11},{12,13},{... | collective-permute-start | bytes 141320 | tf_op jit(solution)/shard_map/ppermute | solution.py:321
  14.1 0.0 copy-start.2
  14.1 0.0 collective-permute-done.3.high
  14.1 0.8 %collective-permute-done.2.low = f32[23,4,128]{2,1,0:T(4,128)S(1)} collective-permute-done((f32[23,4,128]{2,1,0:T(4,128)S(1)}, f32[23,4,128]{2,1,0:T(4,128)S(1)}, u32[]{:S(2)}, u32[]{:S(2)}) %collective-permute-start.2) | collective-permute-done | bytes 47136 | tf_op jit(solution)/shard_map/ppermute | solution.py:321
  15.0 0.0 copy-done
  15.0 0.0 copy-done.1
  15.0 0.0 copy-done.2
  15.0 28.3 %shard_map.145 = (f32[4,64,128]{2,1,0:T(8,128)}, f32[4,64,128]{2,1,0:T(8,128)}, f32[4,64,128]{2,1,0:T(8,128)}, f32[4,64,128]{2,1,0:T(8,128)}, f32[576,128]{1,0:T(8,128)S(1)}) custom-call(f32[21,64,128]{2,1,0:T(8,128)S(1)} %get-tuple-element.20.fields, f32[64,128]{1,0:T(8,128)S(1)} %collective-permute-done.left, f32[64,128]{1,0:T(8,128)S(1)} %collective-permute-done.1.right, ...), custom_call_target="tpu_custom_call" | custom-call | tf_op jit(solution)/shard_map/pallas_call | solution.py:389
  43.3 1.5 %collective-permute-start.4 = (f32[288,128]{1,0:T(8,128)S(1)}, f32[288,128]{1,0:T(8,128)S(1)}, u32[]{:S(2)}, u32[]{:S(2)}) collective-permute-start(f32[288,128]{1,0:T(8,128)S(1)} %slice_select_fusion), channel_id=1, source_target_pairs={{0,1},{1,0},{2,3},{3,2},{4,5},{5,4},{6,7},{7,6},{8,9},{9,8},{10,11... | collective-permute-start | bytes 442376 | tf_op jit(solution)/shard_map/ppermute | solution.py:325
  44.8 1.0 %collective-permute-done.4 = f32[288,128]{1,0:T(8,128)S(1)} collective-permute-done((f32[288,128]{1,0:T(8,128)S(1)}, f32[288,128]{1,0:T(8,128)S(1)}, u32[]{:S(2)}, u32[]{:S(2)}) %collective-permute-start.4) | collective-permute-done | bytes 147488 | tf_op jit(solution)/shard_map/ppermute | solution.py:325
  45.8 2.7 %collective-permute-start.5 = (f32[144,128]{1,0:T(8,128)S(1)}, f32[144,128]{1,0:T(8,128)S(1)}, u32[]{:S(2)}, u32[]{:S(2)}) collective-permute-start(f32[144,128]{1,0:T(8,128)S(1)} %slice_select_fusion.1), channel_id=1, source_target_pairs={{0,2},{1,3},{2,0},{3,1},{4,6},{5,7},{6,4},{7,5},{8,10},{9,11},{10,... | collective-permute-start | bytes 221192 | tf_op jit(solution)/shard_map/ppermute | solution.py:325
  48.5 2.6 %collective-permute-done.5 = f32[144,128]{1,0:T(8,128)S(1)} collective-permute-done((f32[144,128]{1,0:T(8,128)S(1)}, f32[144,128]{1,0:T(8,128)S(1)}, u32[]{:S(2)}, u32[]{:S(2)}) %collective-permute-start.5) | collective-permute-done | bytes 73760 | tf_op jit(solution)/shard_map/ppermute | solution.py:325
  51.1 1.3 %collective-permute-start.6 = (f32[144,128]{1,0:T(8,128)S(1)}, f32[144,128]{1,0:T(8,128)S(1)}, u32[]{:S(2)}, u32[]{:S(2)}) collective-permute-start(f32[144,128]{1,0:T(8,128)S(1)} %select_add_fusion.1), channel_id=1, source_target_pairs={{0,4},{4,0},{8,12},{12,8},{1,5},{5,1},{9,13},{13,9},{2,6},{6,2},{1... | collective-permute-start | bytes 221192 | tf_op jit(solution)/shard_map/ppermute | solution.py:325
  52.4 3.1 %collective-permute-done.6 = f32[144,128]{1,0:T(8,128)S(1)} collective-permute-done((f32[144,128]{1,0:T(8,128)S(1)}, f32[144,128]{1,0:T(8,128)S(1)}, u32[]{:S(2)}, u32[]{:S(2)}) %collective-permute-start.6) | collective-permute-done | bytes 73760 | tf_op jit(solution)/shard_map/ppermute | solution.py:325
  55.5 2.3 %collective-permute-start.7 = (f32[144,128]{1,0:T(8,128)S(1)}, f32[144,128]{1,0:T(8,128)S(1)}, u32[]{:S(2)}, u32[]{:S(2)}) collective-permute-start(f32[144,128]{1,0:T(8,128)S(1)} %add.14), channel_id=1, source_target_pairs={{0,8},{4,12},{8,0},{12,4},{1,9},{5,13},{9,1},{13,5},{2,10},{6,14},... | collective-permute-start | bytes 221192 | tf_op jit(solution)/shard_map/ppermute | solution.py:325
  57.8 3.0 %collective-permute-done.7 = f32[144,128]{1,0:T(8,128)S(1)} collective-permute-done((f32[144,128]{1,0:T(8,128)S(1)}, f32[144,128]{1,0:T(8,128)S(1)}, u32[]{:S(2)}, u32[]{:S(2)}) %collective-permute-start.7) | collective-permute-done | bytes 73760 | tf_op jit(solution)/shard_map/ppermute | solution.py:325
  60.9 1.8 %collective-permute-start.8 = (f32[144,128]{1,0:T(8,128)S(1)}, f32[144,128]{1,0:T(8,128)S(1)}, u32[]{:S(2)}, u32[]{:S(2)}) collective-permute-start(f32[144,128]{1,0:T(8,128)S(1)} %add.15), channel_id=1, source_target_pairs={{0,2},{1,3},{2,0},{3,1},{4,6},{5,7},{6,4},{7,5},{8,10},{9,11},{10,... | collective-permute-start | bytes 221192 | tf_op jit(solution)/shard_map/ppermute | solution.py:325
  62.7 2.6 %collective-permute-done.8 = f32[144,128]{1,0:T(8,128)S(1)} collective-permute-done((f32[144,128]{1,0:T(8,128)S(1)}, f32[144,128]{1,0:T(8,128)S(1)}, u32[]{:S(2)}, u32[]{:S(2)}) %collective-permute-start.8) | collective-permute-done | bytes 73760 | tf_op jit(solution)/shard_map/ppermute | solution.py:325
  65.3 0.1 collective-permute-start.9
  65.4 1.4 %collective-permute-done.9 = f32[288,128]{1,0:T(8,128)S(1)} collective-permute-done((f32[288,128]{1,0:T(8,128)S(1)}, f32[288,128]{1,0:T(8,128)S(1)}, u32[]{:S(2)}, u32[]{:S(2)}) %collective-permute-start.9) | collective-permute-done | bytes 147488 | tf_op jit(solution)/shard_map/ppermute | solution.py:325
  66.8 0.7 %shard_map.146 = (f32[12,256]{1,0:T(8,128)}, f32[256,256]{1,0:T(8,128)}, f32[4,256]{1,0:T(4,128)}) custom-call(f32[576,128]{1,0:T(8,128)S(1)} %pad_maximum_fusion.terms), custom_call_target="tpu_custom_call" | custom-call | tf_op jit(solution)/shard_map/pallas_call | solution.py:419
  (14 shorter events, 0.2 us)
Async XLA Ops:
  2.3 12.6 %copy-start = (bf16[256,256]{1,0:T(8,128)(2,1)S(1)}, bf16[256,256]{1,0:T(8,128)(2,1)}, u32[]{:S(2)}) copy-start(bf16[256,256]{1,0:T(8,128)(2,1)} %w_mid.1) | copy-start | bytes 393220
  2.4 7.1 %collective-permute-start = (f32[64,128]{1,0:T(8,128)S(1)}, f32[64,128]{1,0:T(8,128)S(1)}, u32[]{:S(2)}, u32[]{:S(2)}) collective-permute-start(f32[64,128]{1,0:T(8,128)S(1)} %get-tuple-element.21), channel_id=1, source_target_pairs={{0,4},{4,8},{8,12},{12,0},{1,5},{5,9},{9,13},{13,1},{2,6},{6,10},{... | collective-permute-start | bytes 98312 | tf_op jit(solution)/shard_map/ppermute | solution.py:321
  5.4 4.3 %collective-permute-start.1 = (f32[64,128]{1,0:T(8,128)S(1)}, f32[64,128]{1,0:T(8,128)S(1)}, u32[]{:S(2)}, u32[]{:S(2)}) collective-permute-start(f32[64,128]{1,0:T(8,128)S(1)} %get-tuple-element.22), channel_id=1, source_target_pairs={{0,12},{4,0},{8,4},{12,8},{1,13},{5,1},{9,5},{13,9},{2,14},{6,2},{... | collective-permute-start | bytes 98312 | tf_op jit(solution)/shard_map/ppermute | solution.py:321
  9.7 4.4 %collective-permute-start.3 = (f32[23,4,128]{2,1,0:T(4,128)S(1)}, f32[23,4,128]{2,1,0:T(4,128)S(1)}, u32[]{:S(2)}, u32[]{:S(2)}) collective-permute-start(f32[23,4,128]{2,1,0:T(4,128)S(1)} %pad_maximum_fusion.3), channel_id=1, source_target_pairs={{1,0},{2,1},{3,2},{5,4},{6,5},{7,6},{9,8},{10,9},{11,10},{13,12},{... | collective-permute-start | bytes 141320 | tf_op jit(solution)/shard_map/ppermute | solution.py:321
  11.0 3.9 %copy-start.1 = (bf16[12,256]{1,0:T(8,128)(2,1)S(1)}, bf16[12,256]{1,0:T(8,128)(2,1)}, u32[]{:S(2)}) copy-start(bf16[12,256]{1,0:T(8,128)(2,1)} %w_in.1) | copy-start | bytes 18436
  11.1 3.9 %collective-permute-start.2 = (f32[23,4,128]{2,1,0:T(4,128)S(1)}, f32[23,4,128]{2,1,0:T(4,128)S(1)}, u32[]{:S(2)}, u32[]{:S(2)}) collective-permute-start(f32[23,4,128]{2,1,0:T(4,128)S(1)} %pad_maximum_fusion.2), channel_id=1, source_target_pairs={{0,1},{1,2},{2,3},{4,5},{5,6},{6,7},{8,9},{9,10},{10,11},{12,13},{... | collective-permute-start | bytes 141320 | tf_op jit(solution)/shard_map/ppermute | solution.py:321
  14.1 0.9 %copy-start.2 = (bf16[256,4]{0,1:T(4,128)(2,1)S(1)}, bf16[256,4]{0,1:T(4,128)(2,1)}, u32[]{:S(2)}) copy-start(bf16[256,4]{0,1:T(4,128)(2,1)} %param.15) | copy-start | bytes 6148
  43.3 2.5 %collective-permute-start.4 = (f32[288,128]{1,0:T(8,128)S(1)}, f32[288,128]{1,0:T(8,128)S(1)}, u32[]{:S(2)}, u32[]{:S(2)}) collective-permute-start(f32[288,128]{1,0:T(8,128)S(1)} %slice_select_fusion), channel_id=1, source_target_pairs={{0,1},{1,0},{2,3},{3,2},{4,5},{5,4},{6,7},{7,6},{8,9},{9,8},{10,11... | collective-permute-start | bytes 442376 | tf_op jit(solution)/shard_map/ppermute | solution.py:325
  45.8 5.2 %collective-permute-start.5 = (f32[144,128]{1,0:T(8,128)S(1)}, f32[144,128]{1,0:T(8,128)S(1)}, u32[]{:S(2)}, u32[]{:S(2)}) collective-permute-start(f32[144,128]{1,0:T(8,128)S(1)} %slice_select_fusion.1), channel_id=1, source_target_pairs={{0,2},{1,3},{2,0},{3,1},{4,6},{5,7},{6,4},{7,5},{8,10},{9,11},{10,... | collective-permute-start | bytes 221192 | tf_op jit(solution)/shard_map/ppermute | solution.py:325
  51.1 4.4 %collective-permute-start.6 = (f32[144,128]{1,0:T(8,128)S(1)}, f32[144,128]{1,0:T(8,128)S(1)}, u32[]{:S(2)}, u32[]{:S(2)}) collective-permute-start(f32[144,128]{1,0:T(8,128)S(1)} %select_add_fusion.1), channel_id=1, source_target_pairs={{0,4},{4,0},{8,12},{12,8},{1,5},{5,1},{9,13},{13,9},{2,6},{6,2},{1... | collective-permute-start | bytes 221192 | tf_op jit(solution)/shard_map/ppermute | solution.py:325
  55.5 5.3 %collective-permute-start.7 = (f32[144,128]{1,0:T(8,128)S(1)}, f32[144,128]{1,0:T(8,128)S(1)}, u32[]{:S(2)}, u32[]{:S(2)}) collective-permute-start(f32[144,128]{1,0:T(8,128)S(1)} %add.14), channel_id=1, source_target_pairs={{0,8},{4,12},{8,0},{12,4},{1,9},{5,13},{9,1},{13,5},{2,10},{6,14},... | collective-permute-start | bytes 221192 | tf_op jit(solution)/shard_map/ppermute | solution.py:325
  60.9 4.4 %collective-permute-start.8 = (f32[144,128]{1,0:T(8,128)S(1)}, f32[144,128]{1,0:T(8,128)S(1)}, u32[]{:S(2)}, u32[]{:S(2)}) collective-permute-start(f32[144,128]{1,0:T(8,128)S(1)} %add.15), channel_id=1, source_target_pairs={{0,2},{1,3},{2,0},{3,1},{4,6},{5,7},{6,4},{7,5},{8,10},{9,11},{10,... | collective-permute-start | bytes 221192 | tf_op jit(solution)/shard_map/ppermute | solution.py:325
  65.3 1.4 %collective-permute-start.9 = (f32[288,128]{1,0:T(8,128)S(1)}, f32[288,128]{1,0:T(8,128)S(1)}, u32[]{:S(2)}, u32[]{:S(2)}) collective-permute-start(f32[288,128]{1,0:T(8,128)S(1)} %pad_maximum_fusion.1), channel_id=1, source_target_pairs={{0,1},{1,0},{2,3},{3,2},{4,5},{5,4},{6,7},{7,6},{8,9},{9,8},{10,11... | collective-permute-start | bytes 442376 | tf_op jit(solution)/shard_map/ppermute | solution.py:325

commit v5 on v4

--- a/solution.py
+++ b/solution.py
@@ -13,8 +13,8 @@
 
 WIDE = 4
 LANES = 128
-TILES = 16
-PART = 16
+TILES = 32
+PART = 8
 DEEP = 16
 SHALLOW = 8
 
@@ -78,13 +78,13 @@
     fields, left, right, low, high, w_in, w_mid, w_out_t,
     o_mid, o_new, o_old, o_now, o_grad,
     planes, mids, olds, ft1, ft2, fth, ftx, cl, clh, clx, dc, dch, dcx, df, dfh, dfx,
-    keep1, keep2, acc_mid, acc_in, acc_out, wi, wi_t, wm_t, wo, wo_t,
+    keep1, keep2, halo1, halo2, acc_mid, acc_in, acc_out, wi, wi_t, wm_t, wo, wo_t,
 ):
     levels, rows, cols = o_mid.shape
     width_in, hidden = w_in.shape
     count = 5 * levels + 1
     ext = rows + 2 * WIDE
-    chunks = rows // TILES
+    parts = min(TILES, rows) // PART
     packs = -(-ext // 16)
     order = [rows, ext - 1] + [None] * packs + [rows + 1, ext - 2, rows + 2, ext - 3]
     first_pack = rows + 2
@@ -165,24 +165,77 @@
         part = lanes_of(dc, SHALLOW, base, tiles)
         return jnp.concatenate([part, jnp.zeros_like(part)], 0).astype(BF16)
 
-    def forward(x):
-        first = jnp.tanh(dot(wi_t[...], x))
-        second = jnp.tanh(dot(wm_t[...], first.astype(BF16)))
-        return first, second
-
-    def closure(second):
-        return dot(wo_t[...], second.astype(BF16)).astype(BF16).astype(F32)[:SHALLOW]
-
-    def backward(first, second, cot):
-        dz_two = (dot(wo[...], cot) * (1.0 - second * second)).astype(BF16)
-        dz_one = (dot(w_mid[...], dz_two) * (1.0 - first * first)).astype(BF16)
-        dfeat = dot(wi[...], dz_one).astype(BF16).astype(F32)
-        return dz_one, dz_two, dfeat
-
-    def add_terms(x, first, second, cot, dz_one, dz_two):
-        acc_mid[...] += dot_nt(first, dz_two)
-        acc_in[...] += dot_nt(x, dz_one)
-        acc_out[...] += dot_nt(cot, second)
+    def forward_stages(x):
+        z_one = dot(wi_t[...], x)
+        yield
+        first = jnp.tanh(z_one)
+        low_first = first.astype(BF16)
+        yield
+        z_two = dot(wm_t[...], low_first)
+        yield
+        second = jnp.tanh(z_two)
+        return first, second, low_first, second.astype(BF16)
+
+    def closure(low_second):
+        return dot(wo_t[...], low_second).astype(BF16).astype(F32)[:SHALLOW]
+
+    def backward_stages(first, second, cot):
+        g_two = dot(wo[...], cot)
+        yield
+        dz_two = (g_two * (1.0 - second * second)).astype(BF16)
+        yield
+        g_one = dot(w_mid[...], dz_two)
+        yield
+        dz_one = (g_one * (1.0 - first * first)).astype(BF16)
+        yield
+        return dz_one, dz_two, dot(wi[...], dz_one).astype(BF16).astype(F32)
+
+    def first_part(base, tiles, kept1, kept2):
+        first, second, unused, low_second = yield from forward_stages(inputs_at(ft1, base, tiles))
+        kept1[...] = first
+        kept2[...] = second
+        yield
+        put_lanes(cl, SHALLOW, base, tiles, closure(low_second))
+
+    def second_part(base, tiles, sums):
+        x = inputs_at(ft2, base, tiles)
+        cot = cotangents_at(base, tiles)
+        first, second, low_first, low_second = yield from forward_stages(x)
+        yield
+        if sums is not None:
+            put_lanes(cl, SHALLOW, base, tiles, closure(low_second))
+        dz_one, dz_two, dfeat = yield from backward_stages(first, second, cot)
+        if sums is not None:
+            sums.append((dot_nt(low_first, dz_two), dot_nt(x, dz_one), dot_nt(cot, low_second)))
+        yield
+        put_lanes(df, DEEP, base, tiles, dfeat)
+
+    def third_part(base, tiles, kept1, kept2, sums):
+        cot = cotangents_at(base, tiles)
+        first = kept1[...]
+        second = kept2[...]
+        dz_one, dz_two, dfeat = yield from backward_stages(first, second, cot)
+        if sums is not None:
+            x = inputs_at(ft1, base, tiles)
+            sums.append((dot_nt(first.astype(BF16), dz_two), dot_nt(x, dz_one), dot_nt(cot, second.astype(BF16))))
+        yield
+        put_lanes(df, DEEP, base, tiles, dfeat)
+
+    def staggered(generators):
+        live = []
+        waiting = list(generators)
+        while live or waiting:
+            if waiting:
+                live.append(waiting.pop(0))
+            for part in list(live):
+                try:
+                    next(part)
+                except StopIteration:
+                    live.remove(part)
+
+    def add_terms(sums):
+        for acc, terms in zip((acc_mid, acc_in, acc_out), zip(*sums)):
+            acc[...] += functools.reduce(jnp.add, terms)
 
     def features_of(source, ft):
         for level in range(levels):
@@ -208,15 +261,14 @@
     features_of(planes, ft1)
 
     def first_step(c, carry):
-        for k in range(0, TILES, PART):
-            base = pl.multiple_of(c * TILES + k, PART)
-            first, second = forward(inputs_at(ft1, base, PART))
-            keep1[c, :, pl.ds(k * LANES, PART * LANES)] = first
-            keep2[c, :, pl.ds(k * LANES, PART * LANES)] = second
-            put_lanes(cl, SHALLOW, base, PART, closure(second))
+        staggered(
+            first_part(pl.multiple_of((c * parts + k) * PART, PART), PART, keep1.at[c * parts + k], keep2.at[c * parts + k])
+            for k in range(parts)
+        )
         return carry
 
-    lax.fori_loop(0, keep1.shape[0], first_step, 0)
+    lax.fori_loop(0, rows // (parts * PART), first_step, 0)
+    staggered([first_part(rows, len(order), halo1, halo2)])
     unpack_halo(SHALLOW, cl, clx, clh, len(order))
 
     for level in range(levels):
@@ -229,23 +281,13 @@
     cotangents_of(planes, 3 * levels)
 
     def second_step(c, carry):
-        parts = []
-        for k in range(0, TILES, PART):
-            base = pl.multiple_of(c * TILES + k, PART)
-            x = inputs_at(ft2, base, PART)
-            cot = cotangents_at(base, PART)
-            first, second = forward(x)
-            put_lanes(cl, SHALLOW, base, PART, closure(second))
-            dz_one, dz_two, dfeat = backward(first, second, cot)
-            put_lanes(df, DEEP, base, PART, dfeat)
-            parts.append((x, first.astype(BF16), second.astype(BF16), cot, dz_one, dz_two))
-        add_terms(*(jnp.concatenate(part, 1) for part in zip(*parts)))
+        sums = []
+        staggered(second_part(pl.multiple_of((c * parts + k) * PART, PART), PART, sums) for k in range(parts))
+        add_terms(sums)
         return carry
 
-    lax.fori_loop(0, chunks, second_step, 0)
-    first, second = forward(inputs_at(ft2, rows, halo_two))
-    unused_one, unused_two, dfeat = backward(first, second, cotangents_at(rows, halo_two))
-    put_lanes(df, DEEP, rows, halo_two, dfeat)
+    lax.fori_loop(0, rows // (parts * PART), second_step, 0)
+    staggered([second_part(rows, halo_two, None)])
     unpack_halo(DEEP, df, dfx, dfh, halo_two)
 
     def adjoint_of(weighted, level):
@@ -270,25 +312,19 @@
     cotangents_of(olds, 0)
 
     def third_step(c, carry):
-        parts = []
-        for k in range(0, TILES, PART):
-            base = pl.multiple_of(c * TILES + k, PART)
-            x = inputs_at(ft1, base, PART)
-            cot = cotangents_at(base, PART)
-            first = keep1[c, :, pl.ds(k * LANES, PART * LANES)]
-            second = keep2[c, :, pl.ds(k * LANES, PART * LANES)]
-            dz_one, dz_two, dfeat = backward(first, second, cot)
-            put_lanes(df, DEEP, base, PART, dfeat)
-            parts.append((x, first.astype(BF16), second.astype(BF16), cot, dz_one, dz_two))
-        add_terms(*(jnp.concatenate(part, 1) for part in zip(*parts)))
+        sums = []
+        staggered(
+            third_part(
+                pl.multiple_of((c * parts + k) * PART, PART), PART, keep1.at[c * parts + k], keep2.at[c * parts + k], sums
+            )
+            for k in range(parts)
+        )
+        add_terms(sums)
         return carry
 
-    lax.fori_loop(0, chunks, third_step, 0)
-    near = halo_one * LANES
-    unused_one, unused_two, dfeat = backward(
-        keep1[chunks, :, pl.ds(0, near)], keep2[chunks, :, pl.ds(0, near)], cotangents_at(rows, halo_one)
-    )
-    put_lanes(df, DEEP, rows, halo_one, dfeat)
+    lax.fori_loop(0, rows // (parts * PART), third_step, 0)
+    near = pl.ds(0, halo_one * LANES)
+    staggered([third_part(rows, halo_one, halo1.at[:, near], halo2.at[:, near], None)])
     unpack_halo(DEEP, df, dfx, dfh, halo_one)
 
     for level in range(levels):
@@ -352,8 +388,7 @@
     ext = rows + 2 * WIDE
     count = 5 * levels + 1
     packs = -(-ext // 16)
-    steps = -(-(rows + 6 + packs) // TILES)
-    slots = steps * TILES
+    slots = rows + 6 + packs
     vmem = pl.BlockSpec(memory_space=pltpu.VMEM)
     strip = jax.ShapeDtypeStruct((rows, LANES), F32)
     edge = jax.ShapeDtypeStruct((count, WIDE, LANES), F32)
@@ -385,7 +420,8 @@
     def tiles(deep):
         return [pltpu.VMEM((n * deep, LANES), F32) for n in (slots, side_rows, 2 * WIDE)]
 
-    kept = pltpu.VMEM((steps, hidden, TILES * LANES), F32)
+    kept = pltpu.VMEM((rows // PART, hidden, PART * LANES), F32)
+    kept_halo = pltpu.VMEM((hidden, (6 + packs) * LANES), F32)
     state_mid, state_new, grad_old, grad_now, terms = pl.pallas_call(
         main_kernel,
         out_shape=(field, field, field, field, jax.ShapeDtypeStruct((terms_rows, LANES), F32)),
@@ -402,6 +438,8 @@
             *tiles(DEEP),
             kept,
             kept,
+            kept_halo,
+            kept_halo,
             pltpu.VMEM((hidden, hidden), F32),
             pltpu.VMEM((DEEP, hidden), F32),
             pltpu.VMEM((DEEP, hidden), F32),
@@ -411,7 +449,7 @@
             pltpu.VMEM((hidden, DEEP), BF16),
             pltpu.VMEM((DEEP, hidden), BF16),
         ],
-        compiler_params=pltpu.CompilerParams(vmem_limit_bytes=44 * 2**20),
+        compiler_params=pltpu.CompilerParams(vmem_limit_bytes=48 * 2**20),
     )(fields, left, right, low, high, w_in, w_mid, w_out.T)
 
     summed = summed_over(terms, "lat", "lon")

time: 67.7 us -> 64.8 us (0.957)
  Pallas kernels: 30.8 us -> 27.8 us
    pallas_call x1, Pallas kernels: 28.3 us -> 25.4 us  [body(): pl.pallas_call(main_kernel, out_shape=(field, field, field, field, jax.Sh...]
where the time goes in v5:
time: 64.8 us; the launch traced here: 64.6 us
  Pallas kernels  27.8 us (43%)
  starting transfers between devices  19.1 us (29%)
  waiting for transfers between devices  16.7 us (26%)
  between operations  0.77 us (1%)
    pallas_call x1, Pallas kernels, body(): pl.pallas_call(main_kernel, out_shape=(field, field, field, field, jax.Sh...  25.4 us
    ppermute x6, waiting for transfers between devices, swapped(): lax.ppermute(value, axis, [(i, i ^ bit) for i in range(lax.axis_size(axis...  13.7 us
    ppermute x6, starting transfers between devices, swapped(): lax.ppermute(value, axis, [(i, i ^ bit) for i in range(lax.axis_size(axis...  9.62 us
    ppermute x4, starting transfers between devices, along(): return lax.ppermute(value, axis, pairs)  9.49 us
    ppermute x4, waiting for transfers between devices, along(): return lax.ppermute(value, axis, pairs)  3 us
    pallas_call x1, Pallas kernels, body(): pl.pallas_call(pack_kernel, out_shape=(strip, strip, edge, edge, jax.Shap...  1.71 us
  transfers between devices with their start and end apart: 10, of which 9 were waited for; matrix products, arithmetic and copies ran while one was open for 0% of the time, Pallas kernels for 0%

profile of v5, /device:TPU:0, one launch (start us, length us, event | category | flops | bytes accessed | tf_op | source)
XLA Modules:
  0.0 64.6 jit_solution(8432443731332972258)
XLA Ops:
  0.6 1.7 %shard_map.144 = (f32[64,128]{1,0:T(8,128)S(1)}, f32[64,128]{1,0:T(8,128)S(1)}, f32[21,4,128]{2,1,0:T(4,128)S(1)}, f32[21,4,128]{2,1,0:T(4,128)S(1)}, f32[21,64,128]{2,1,0:T(8,128)S(1)}) custom-call(f32[4,64,128]{2,1,0:T(8,128)} %now.1, f32[4,64,128]{2,1,0:T(8,128)} %old.1, f32[4,64,128]{2,1,0:T(8,128)} %drift.1, f32[4,64,128]{2,1,0:T(8,128)} %cnew.1, ...), custom_call_target="tpu_custom_call" | custom-call | tf_op jit(solution)/shard_map/pallas_call | solution.py:398
  2.3 0.0 copy-start
  2.4 3.1 %collective-permute-start = (f32[64,128]{1,0:T(8,128)S(1)}, f32[64,128]{1,0:T(8,128)S(1)}, u32[]{:S(2)}, u32[]{:S(2)}) collective-permute-start(f32[64,128]{1,0:T(8,128)S(1)} %get-tuple-element.21), channel_id=1, source_target_pairs={{0,4},{4,8},{8,12},{12,0},{1,5},{5,9},{9,13},{13,1},{2,6},{6,10},{... | collective-permute-start | bytes 98312 | tf_op jit(solution)/shard_map/ppermute | solution.py:357
  5.4 2.1 %collective-permute-start.1 = (f32[64,128]{1,0:T(8,128)S(1)}, f32[64,128]{1,0:T(8,128)S(1)}, u32[]{:S(2)}, u32[]{:S(2)}) collective-permute-start(f32[64,128]{1,0:T(8,128)S(1)} %get-tuple-element.22), channel_id=1, source_target_pairs={{0,12},{4,0},{8,4},{12,8},{1,13},{5,1},{9,5},{13,9},{2,14},{6,2},{... | collective-permute-start | bytes 98312 | tf_op jit(solution)/shard_map/ppermute | solution.py:357
  7.5 1.9 %collective-permute-done.left = f32[64,128]{1,0:T(8,128)S(1)} collective-permute-done((f32[64,128]{1,0:T(8,128)S(1)}, f32[64,128]{1,0:T(8,128)S(1)}, u32[]{:S(2)}, u32[]{:S(2)}) %collective-permute-start) | collective-permute-done | bytes 32800 | tf_op jit(solution)/shard_map/ppermute | solution.py:357
  9.5 0.2 collective-permute-done.1.right
  9.7 1.3 %collective-permute-start.3 = (f32[23,4,128]{2,1,0:T(4,128)S(1)}, f32[23,4,128]{2,1,0:T(4,128)S(1)}, u32[]{:S(2)}, u32[]{:S(2)}) collective-permute-start(f32[23,4,128]{2,1,0:T(4,128)S(1)} %pad_maximum_fusion.3), channel_id=1, source_target_pairs={{1,0},{2,1},{3,2},{5,4},{6,5},{7,6},{9,8},{10,9},{11,10},{13,12},{... | collective-permute-start | bytes 141320 | tf_op jit(solution)/shard_map/ppermute | solution.py:357
  11.0 0.0 copy-start.1
  11.1 3.0 %collective-permute-start.2 = (f32[23,4,128]{2,1,0:T(4,128)S(1)}, f32[23,4,128]{2,1,0:T(4,128)S(1)}, u32[]{:S(2)}, u32[]{:S(2)}) collective-permute-start(f32[23,4,128]{2,1,0:T(4,128)S(1)} %pad_maximum_fusion.2), channel_id=1, source_target_pairs={{0,1},{1,2},{2,3},{4,5},{5,6},{6,7},{8,9},{9,10},{10,11},{12,13},{... | collective-permute-start | bytes 141320 | tf_op jit(solution)/shard_map/ppermute | solution.py:357
  14.1 0.0 copy-start.2
  14.1 0.0 collective-permute-done.3.high
  14.1 0.8 %collective-permute-done.2.low = f32[23,4,128]{2,1,0:T(4,128)S(1)} collective-permute-done((f32[23,4,128]{2,1,0:T(4,128)S(1)}, f32[23,4,128]{2,1,0:T(4,128)S(1)}, u32[]{:S(2)}, u32[]{:S(2)}) %collective-permute-start.2) | collective-permute-done | bytes 47136 | tf_op jit(solution)/shard_map/ppermute | solution.py:357
  15.0 0.0 copy-done
  15.0 0.0 copy-done.1
  15.0 0.0 copy-done.2
  15.0 25.4 %shard_map.145 = (f32[4,64,128]{2,1,0:T(8,128)}, f32[4,64,128]{2,1,0:T(8,128)}, f32[4,64,128]{2,1,0:T(8,128)}, f32[4,64,128]{2,1,0:T(8,128)}, f32[576,128]{1,0:T(8,128)S(1)}) custom-call(f32[21,64,128]{2,1,0:T(8,128)S(1)} %get-tuple-element.20.fields, f32[64,128]{1,0:T(8,128)S(1)} %collective-permute-done.left, f32[64,128]{1,0:T(8,128)S(1)} %collective-permute-done.1.right, ...), custom_call_target="tpu_custom_call" | custom-call | tf_op jit(solution)/shard_map/pallas_call | solution.py:425
  40.4 1.5 %collective-permute-start.4 = (f32[288,128]{1,0:T(8,128)S(1)}, f32[288,128]{1,0:T(8,128)S(1)}, u32[]{:S(2)}, u32[]{:S(2)}) collective-permute-start(f32[288,128]{1,0:T(8,128)S(1)} %slice_select_fusion), channel_id=1, source_target_pairs={{0,1},{1,0},{2,3},{3,2},{4,5},{5,4},{6,7},{7,6},{8,9},{9,8},{10,11... | collective-permute-start | bytes 442376 | tf_op jit(solution)/shard_map/ppermute | solution.py:361
  41.8 1.0 %collective-permute-done.4 = f32[288,128]{1,0:T(8,128)S(1)} collective-permute-done((f32[288,128]{1,0:T(8,128)S(1)}, f32[288,128]{1,0:T(8,128)S(1)}, u32[]{:S(2)}, u32[]{:S(2)}) %collective-permute-start.4) | collective-permute-done | bytes 147488 | tf_op jit(solution)/shard_map/ppermute | solution.py:361
  42.9 2.7 %collective-permute-start.5 = (f32[144,128]{1,0:T(8,128)S(1)}, f32[144,128]{1,0:T(8,128)S(1)}, u32[]{:S(2)}, u32[]{:S(2)}) collective-permute-start(f32[144,128]{1,0:T(8,128)S(1)} %slice_select_fusion.1), channel_id=1, source_target_pairs={{0,2},{1,3},{2,0},{3,1},{4,6},{5,7},{6,4},{7,5},{8,10},{9,11},{10,... | collective-permute-start | bytes 221192 | tf_op jit(solution)/shard_map/ppermute | solution.py:361
  45.5 2.6 %collective-permute-done.5 = f32[144,128]{1,0:T(8,128)S(1)} collective-permute-done((f32[144,128]{1,0:T(8,128)S(1)}, f32[144,128]{1,0:T(8,128)S(1)}, u32[]{:S(2)}, u32[]{:S(2)}) %collective-permute-start.5) | collective-permute-done | bytes 73760 | tf_op jit(solution)/shard_map/ppermute | solution.py:361
  48.1 1.3 %collective-permute-start.6 = (f32[144,128]{1,0:T(8,128)S(1)}, f32[144,128]{1,0:T(8,128)S(1)}, u32[]{:S(2)}, u32[]{:S(2)}) collective-permute-start(f32[144,128]{1,0:T(8,128)S(1)} %select_add_fusion.1), channel_id=1, source_target_pairs={{0,4},{4,0},{8,12},{12,8},{1,5},{5,1},{9,13},{13,9},{2,6},{6,2},{1... | collective-permute-start | bytes 221192 | tf_op jit(solution)/shard_map/ppermute | solution.py:361
  49.4 3.1 %collective-permute-done.6 = f32[144,128]{1,0:T(8,128)S(1)} collective-permute-done((f32[144,128]{1,0:T(8,128)S(1)}, f32[144,128]{1,0:T(8,128)S(1)}, u32[]{:S(2)}, u32[]{:S(2)}) %collective-permute-start.6) | collective-permute-done | bytes 73760 | tf_op jit(solution)/shard_map/ppermute | solution.py:361
  52.6 2.3 %collective-permute-start.7 = (f32[144,128]{1,0:T(8,128)S(1)}, f32[144,128]{1,0:T(8,128)S(1)}, u32[]{:S(2)}, u32[]{:S(2)}) collective-permute-start(f32[144,128]{1,0:T(8,128)S(1)} %add.14), channel_id=1, source_target_pairs={{0,8},{4,12},{8,0},{12,4},{1,9},{5,13},{9,1},{13,5},{2,10},{6,14},... | collective-permute-start | bytes 221192 | tf_op jit(solution)/shard_map/ppermute | solution.py:361
  54.9 3.0 %collective-permute-done.7 = f32[144,128]{1,0:T(8,128)S(1)} collective-permute-done((f32[144,128]{1,0:T(8,128)S(1)}, f32[144,128]{1,0:T(8,128)S(1)}, u32[]{:S(2)}, u32[]{:S(2)}) %collective-permute-start.7) | collective-permute-done | bytes 73760 | tf_op jit(solution)/shard_map/ppermute | solution.py:361
  57.9 1.8 %collective-permute-start.8 = (f32[144,128]{1,0:T(8,128)S(1)}, f32[144,128]{1,0:T(8,128)S(1)}, u32[]{:S(2)}, u32[]{:S(2)}) collective-permute-start(f32[144,128]{1,0:T(8,128)S(1)} %add.15), channel_id=1, source_target_pairs={{0,2},{1,3},{2,0},{3,1},{4,6},{5,7},{6,4},{7,5},{8,10},{9,11},{10,... | collective-permute-start | bytes 221192 | tf_op jit(solution)/shard_map/ppermute | solution.py:361
  59.8 2.6 %collective-permute-done.8 = f32[144,128]{1,0:T(8,128)S(1)} collective-permute-done((f32[144,128]{1,0:T(8,128)S(1)}, f32[144,128]{1,0:T(8,128)S(1)}, u32[]{:S(2)}, u32[]{:S(2)}) %collective-permute-start.8) | collective-permute-done | bytes 73760 | tf_op jit(solution)/shard_map/ppermute | solution.py:361
  62.4 0.1 collective-permute-start.9
  62.4 1.4 %collective-permute-done.9 = f32[288,128]{1,0:T(8,128)S(1)} collective-permute-done((f32[288,128]{1,0:T(8,128)S(1)}, f32[288,128]{1,0:T(8,128)S(1)}, u32[]{:S(2)}, u32[]{:S(2)}) %collective-permute-start.9) | collective-permute-done | bytes 147488 | tf_op jit(solution)/shard_map/ppermute | solution.py:361
  63.9 0.7 %shard_map.146 = (f32[12,256]{1,0:T(8,128)}, f32[256,256]{1,0:T(8,128)}, f32[4,256]{1,0:T(4,128)}) custom-call(f32[576,128]{1,0:T(8,128)S(1)} %pad_maximum_fusion.terms), custom_call_target="tpu_custom_call" | custom-call | tf_op jit(solution)/shard_map/pallas_call | solution.py:457
  (14 shorter events, 0.2 us)
Async XLA Ops:
  2.3 12.6 %copy-start = (bf16[256,256]{1,0:T(8,128)(2,1)S(1)}, bf16[256,256]{1,0:T(8,128)(2,1)}, u32[]{:S(2)}) copy-start(bf16[256,256]{1,0:T(8,128)(2,1)} %w_mid.1) | copy-start | bytes 393220
  2.4 7.1 %collective-permute-start = (f32[64,128]{1,0:T(8,128)S(1)}, f32[64,128]{1,0:T(8,128)S(1)}, u32[]{:S(2)}, u32[]{:S(2)}) collective-permute-start(f32[64,128]{1,0:T(8,128)S(1)} %get-tuple-element.21), channel_id=1, source_target_pairs={{0,4},{4,8},{8,12},{12,0},{1,5},{5,9},{9,13},{13,1},{2,6},{6,10},{... | collective-permute-start | bytes 98312 | tf_op jit(solution)/shard_map/ppermute | solution.py:357
  5.4 4.3 %collective-permute-start.1 = (f32[64,128]{1,0:T(8,128)S(1)}, f32[64,128]{1,0:T(8,128)S(1)}, u32[]{:S(2)}, u32[]{:S(2)}) collective-permute-start(f32[64,128]{1,0:T(8,128)S(1)} %get-tuple-element.22), channel_id=1, source_target_pairs={{0,12},{4,0},{8,4},{12,8},{1,13},{5,1},{9,5},{13,9},{2,14},{6,2},{... | collective-permute-start | bytes 98312 | tf_op jit(solution)/shard_map/ppermute | solution.py:357
  9.7 4.4 %collective-permute-start.3 = (f32[23,4,128]{2,1,0:T(4,128)S(1)}, f32[23,4,128]{2,1,0:T(4,128)S(1)}, u32[]{:S(2)}, u32[]{:S(2)}) collective-permute-start(f32[23,4,128]{2,1,0:T(4,128)S(1)} %pad_maximum_fusion.3), channel_id=1, source_target_pairs={{1,0},{2,1},{3,2},{5,4},{6,5},{7,6},{9,8},{10,9},{11,10},{13,12},{... | collective-permute-start | bytes 141320 | tf_op jit(solution)/shard_map/ppermute | solution.py:357
  11.0 3.9 %copy-start.1 = (bf16[12,256]{1,0:T(8,128)(2,1)S(1)}, bf16[12,256]{1,0:T(8,128)(2,1)}, u32[]{:S(2)}) copy-start(bf16[12,256]{1,0:T(8,128)(2,1)} %w_in.1) | copy-start | bytes 18436
  11.1 3.9 %collective-permute-start.2 = (f32[23,4,128]{2,1,0:T(4,128)S(1)}, f32[23,4,128]{2,1,0:T(4,128)S(1)}, u32[]{:S(2)}, u32[]{:S(2)}) collective-permute-start(f32[23,4,128]{2,1,0:T(4,128)S(1)} %pad_maximum_fusion.2), channel_id=1, source_target_pairs={{0,1},{1,2},{2,3},{4,5},{5,6},{6,7},{8,9},{9,10},{10,11},{12,13},{... | collective-permute-start | bytes 141320 | tf_op jit(solution)/shard_map/ppermute | solution.py:357
  14.1 0.9 %copy-start.2 = (bf16[256,4]{0,1:T(4,128)(2,1)S(1)}, bf16[256,4]{0,1:T(4,128)(2,1)}, u32[]{:S(2)}) copy-start(bf16[256,4]{0,1:T(4,128)(2,1)} %param.15) | copy-start | bytes 6148
  40.4 2.5 %collective-permute-start.4 = (f32[288,128]{1,0:T(8,128)S(1)}, f32[288,128]{1,0:T(8,128)S(1)}, u32[]{:S(2)}, u32[]{:S(2)}) collective-permute-start(f32[288,128]{1,0:T(8,128)S(1)} %slice_select_fusion), channel_id=1, source_target_pairs={{0,1},{1,0},{2,3},{3,2},{4,5},{5,4},{6,7},{7,6},{8,9},{9,8},{10,11... | collective-permute-start | bytes 442376 | tf_op jit(solution)/shard_map/ppermute | solution.py:361
  42.9 5.2 %collective-permute-start.5 = (f32[144,128]{1,0:T(8,128)S(1)}, f32[144,128]{1,0:T(8,128)S(1)}, u32[]{:S(2)}, u32[]{:S(2)}) collective-permute-start(f32[144,128]{1,0:T(8,128)S(1)} %slice_select_fusion.1), channel_id=1, source_target_pairs={{0,2},{1,3},{2,0},{3,1},{4,6},{5,7},{6,4},{7,5},{8,10},{9,11},{10,... | collective-permute-start | bytes 221192 | tf_op jit(solution)/shard_map/ppermute | solution.py:361
  48.1 4.4 %collective-permute-start.6 = (f32[144,128]{1,0:T(8,128)S(1)}, f32[144,128]{1,0:T(8,128)S(1)}, u32[]{:S(2)}, u32[]{:S(2)}) collective-permute-start(f32[144,128]{1,0:T(8,128)S(1)} %select_add_fusion.1), channel_id=1, source_target_pairs={{0,4},{4,0},{8,12},{12,8},{1,5},{5,1},{9,13},{13,9},{2,6},{6,2},{1... | collective-permute-start | bytes 221192 | tf_op jit(solution)/shard_map/ppermute | solution.py:361
  52.6 5.3 %collective-permute-start.7 = (f32[144,128]{1,0:T(8,128)S(1)}, f32[144,128]{1,0:T(8,128)S(1)}, u32[]{:S(2)}, u32[]{:S(2)}) collective-permute-start(f32[144,128]{1,0:T(8,128)S(1)} %add.14), channel_id=1, source_target_pairs={{0,8},{4,12},{8,0},{12,4},{1,9},{5,13},{9,1},{13,5},{2,10},{6,14},... | collective-permute-start | bytes 221192 | tf_op jit(solution)/shard_map/ppermute | solution.py:361
  57.9 4.4 %collective-permute-start.8 = (f32[144,128]{1,0:T(8,128)S(1)}, f32[144,128]{1,0:T(8,128)S(1)}, u32[]{:S(2)}, u32[]{:S(2)}) collective-permute-start(f32[144,128]{1,0:T(8,128)S(1)} %add.15), channel_id=1, source_target_pairs={{0,2},{1,3},{2,0},{3,1},{4,6},{5,7},{6,4},{7,5},{8,10},{9,11},{10,... | collective-permute-start | bytes 221192 | tf_op jit(solution)/shard_map/ppermute | solution.py:361
  62.4 1.4 %collective-permute-start.9 = (f32[288,128]{1,0:T(8,128)S(1)}, f32[288,128]{1,0:T(8,128)S(1)}, u32[]{:S(2)}, u32[]{:S(2)}) collective-permute-start(f32[288,128]{1,0:T(8,128)S(1)} %pad_maximum_fusion.1), channel_id=1, source_target_pairs={{0,1},{1,0},{2,3},{3,2},{4,5},{5,4},{6,7},{7,6},{8,9},{9,8},{10,11... | collective-permute-start | bytes 442376 | tf_op jit(solution)/shard_map/ppermute | solution.py:361

commit v6 on v5

v6 whole, which is shorter than its diff:
```python
import functools

import jax
import jax.numpy as jnp
from jax import lax
from jax.experimental import pallas as pl
from jax.experimental.pallas import tpu as pltpu
from jax.sharding import PartitionSpec as P

KAPPA = 0.2
DT = 0.1
GAIN_GRAD = 10.0

WIDE = 4
LANES = 128
PART = 8
EARLY = 2
DEEP = 16
SHALLOW = 8

F32 = jnp.float32
BF16 = jnp.bfloat16


def dot(left, right):
    return lax.dot_general(left, right, (((1,), (0,)), ((), ())), preferred_element_type=F32)


def dot_nt(left, right):
    return lax.dot_general(left, right, (((1,), (1,)), ((), ())), preferred_element_type=F32)


def pack_kernel(now, old, drift, cnew, cmid, ocean, west, east, top, bottom, fields, wet, sems):
    levels, rows, cols = now.shape
    copies = [
        pltpu.make_async_copy(ref, fields.at[pl.ds(levels * f, levels)], sems.at[f])
        for f, ref in enumerate((now, old, drift, cnew, cmid))
    ]
    copies.append(pltpu.make_async_copy(ocean, wet, sems.at[5]))
    for copy in copies:
        copy.start()
    lane = lax.broadcasted_iota(jnp.int32, (rows, LANES), 1)
    to_west = jnp.zeros((rows, LANES), F32)
    to_east = jnp.zeros((rows, LANES), F32)
    count = fields.shape[0]
    for p in range(count):
        if p % levels == 0:
            copies[p // levels].wait()
        if p == count - 1:
            fields[p] = wet[...].astype(F32)
        plane = fields[p]
        here = (lane >= WIDE * p) & (lane < WIDE * (p + 1))
        to_west = jnp.where(here, pltpu.roll(plane, WIDE * p, 1) if p else plane, to_west)
        to_east = jnp.where(here, pltpu.roll(plane, WIDE * (p + 1), 1), to_east)
        top[p] = plane[:WIDE]
        bottom[p] = plane[rows - WIDE :]
    west[...] = to_west
    east[...] = to_east


def east_of(v):
    return pltpu.roll(v, v.shape[1] - 1, 1)


def west_of(v):
    return pltpu.roll(v, 1, 1)


def north_of(v):
    return pltpu.roll(v, v.shape[0] - 1, 0)


def south_of(v):
    return pltpu.roll(v, 1, 0)


def forward_stages(x, w_first_t, w_second_t):
    z_one = dot(w_first_t[...], x)
    yield
    first = jnp.tanh(z_one)
    low_first = first.astype(BF16)
    yield
    z_two = dot(w_second_t[...], low_first)
    yield
    second = jnp.tanh(z_two)
    return first, second, low_first, second.astype(BF16)


def closure(low_second, w_last_t):
    return dot(w_last_t[...], low_second).astype(BF16).astype(F32)[:SHALLOW]


def staggered(generators):
    live = []
    waiting = list(generators)
    while live or waiting:
        if waiting:
            live.append(waiting.pop(0))
        for part in list(live):
            try:
                next(part)
            except StopIteration:
                live.remove(part)


def lanes_of(ref, deep, base, tiles):
    block = ref[pl.ds(base * deep, tiles * deep), :]
    return jnp.concatenate([block[k * deep : (k + 1) * deep] for k in range(tiles)], 1)


def put_lanes(ref, deep, base, tiles, value):
    for k in range(tiles):
        ref[pl.ds((base + k) * deep, deep), :] = value[:, k * LANES : (k + 1) * LANES]


def early_kernel(start, fields, *refs):
    if start == 0:
        w_in, w_mid, w_out_t, keep1, keep2, cl, wi, wi_t, wm_t, wo, wo_t, ft = refs
        width_in, hidden = w_in.shape
        levels = w_out_t.shape[0]
        spare = jnp.zeros((DEEP - width_in, hidden), F32)
        wide_in = jnp.concatenate([w_in[...].astype(F32), spare], 0)
        wi[...] = wide_in.astype(BF16)
        wi_t[...] = wide_in.T.astype(BF16)
        wm_t[...] = w_mid[...].astype(F32).T.astype(BF16)
        spare = jnp.zeros((DEEP - levels, hidden), F32)
        wide_out = jnp.concatenate([w_out_t[...].astype(F32), spare], 0)
        wo_t[...] = wide_out.astype(BF16)
        wo[...] = wide_out.T.astype(BF16)
    else:
        unused, wi_t, wm_t, wo_t, keep1, keep2, cl, ft = refs
        levels = (fields.shape[0] - 1) // 5
    tall = cl.shape[0] // SHALLOW
    ft[...] = jnp.zeros_like(ft)
    for level in range(levels):
        v = fields[level]
        slope_x = 0.5 * (east_of(v) - west_of(v))
        slope_y = 0.5 * (north_of(v) - south_of(v))
        for f, plane in enumerate((v, slope_x, slope_y)):
            ft[pl.ds(f * levels + level, tall, stride=DEEP), :] = plane[start : start + tall]

    def part(base, kept1, kept2):
        x = lanes_of(ft, DEEP, base, PART).astype(BF16)
        first, second, unused_low, low_second = yield from forward_stages(x, wi_t, wm_t)
        kept1[...] = first
        kept2[...] = second
        yield
        put_lanes(cl, SHALLOW, base, PART, closure(low_second, wo_t))

    staggered(part(k * PART, keep1.at[k], keep2.at[k]) for k in range(tall // PART))


def main_kernel(*refs):
    fields, left, right, low, high, wi, wi_t, wm_t, w_mid, wo, wo_t, *refs = refs
    early, refs = refs[: 3 * EARLY], refs[3 * EARLY :]
    o_mid, o_new, o_old, o_now, o_grad, planes, mids, olds, *refs = refs
    ft1, ft2, fth, ftx, cl, clh, clx, dc, dch, dcx, df, dfh, dfx, halo1, halo2, acc_mid, acc_in, acc_out = refs
    levels, rows, cols = o_mid.shape
    hidden = w_mid.shape[0]
    count = 5 * levels + 1
    ext = rows + 2 * WIDE
    packs = -(-ext // 16)
    kept1 = [ref.at[k] for ref in early[0::3] for k in range(ref.shape[0])]
    kept2 = [ref.at[k] for ref in early[1::3] for k in range(ref.shape[0])]
    packed = [None] * packs
    rim = [0, rows - 1, rows, ext - 1] + packed + [rows + 1, ext - 2, rows + 2, ext - 3]
    rim_near = 4 + packs
    outer = [rows, ext - 1] + packed + [rows + 1, ext - 2]

    lane = lax.broadcasted_iota(jnp.int32, (ext, LANES), 1)
    left_all = jnp.concatenate([left[...], high[count], low[count]], 0)
    right_all = jnp.concatenate([right[...], high[count + 1], low[count + 1]], 0)
    for p in range(count):
        from_right = pltpu.roll(right_all, LANES - WIDE * p, 1) if p else right_all
        from_left = pltpu.roll(left_all, LANES - WIDE * (p + 1), 1)
        side = jnp.where(lane < WIDE, from_right, jnp.where(lane >= LANES - WIDE, from_left, 0.0))
        planes[p, :, pl.ds(0, LANES)] = jnp.concatenate([fields[p], high[p], low[p]], 0)
        planes[p, :, pl.ds(LANES, LANES)] = side

    for ref in (ft1, ft2, fth, ftx, dc, dch, dcx):
        ref[...] = jnp.zeros_like(ref)

    def with_rim(plane):
        body, side = plane[:, :LANES], plane[:, LANES:]
        own = jnp.where(lane == LANES - WIDE, pltpu.roll(body, LANES - WIDE, 1), pltpu.roll(body, WIDE, 1))
        return jnp.where((lane == LANES - WIDE) | (lane == WIDE - 1), own, side)

    def from_rim(body, side):
        own = jnp.where(lane == 0, pltpu.roll(side, WIDE, 1), pltpu.roll(side, LANES - WIDE, 1))
        return jnp.where((lane == 0) | (lane == LANES - 1), own, body)

    def spread(plane, index, deep, main, extra, side, rimmed):
        main[pl.ds(index, rows, stride=deep), :] = plane[:rows, :LANES]
        extra[pl.ds(index, 2 * WIDE, stride=deep), :] = plane[rows:, :LANES]
        side[pl.ds(index, ext, stride=deep), :] = with_rim(plane) if rimmed else plane[:, LANES:]

    def gathered(index, deep, main, extra, side, rimmed):
        body = jnp.concatenate(
            [main[pl.ds(index, rows, stride=deep), :], extra[pl.ds(index, 2 * WIDE, stride=deep), :]], 0
        )
        beside = side[pl.ds(index, ext, stride=deep), :]
        return jnp.concatenate([from_rim(body, beside) if rimmed else body, beside], 1)

    def home(r, deep, main, extra):
        return main.at[pl.ds(r * deep, deep)] if r < rows else extra.at[pl.ds((r - rows) * deep, deep)]

    def pack_halo(order, deep, main, extra, side, rim_too=True):
        where = lax.broadcasted_iota(jnp.int32, (deep, LANES), 1)
        for i, r in enumerate(order):
            if r is not None and (rim_too or r >= rows):
                main[pl.ds((rows + i) * deep, deep), :] = home(r, deep, main, extra)[...]
        first_pack = rows + order.index(None)
        for q in range(packs):
            total = jnp.zeros((deep, LANES), F32)
            for j in range(min(16, ext - 16 * q)):
                moved = pltpu.roll(side[pl.ds((16 * q + j) * deep, deep), :], (2 * WIDE * j + WIDE) % LANES, 1)
                total = jnp.where((where >= 2 * WIDE * j) & (where < 2 * WIDE * (j + 1)), moved, total)
            main[pl.ds((first_pack + q) * deep, deep), :] = total

    def unpack_halo(order, deep, main, extra, side):
        for i, r in enumerate(order):
            if r is not None:
                home(r, deep, main, extra)[...] = main[pl.ds((rows + i) * deep, deep), :]
        first_pack = rows + order.index(None)
        for q in range(packs):
            tile = main[pl.ds((first_pack + q) * deep, deep), :]
            for j in range(min(16, ext - 16 * q)):
                moved = pltpu.roll(tile, LANES - (2 * WIDE * j + WIDE) % LANES, 1)
                side[pl.ds((16 * q + j) * deep, deep), :] = moved

    def inputs_at(ref, base, tiles):
        return lanes_of(ref, DEEP, base, tiles).astype(BF16)

    def cotangents_at(base, tiles):
        part = lanes_of(dc, SHALLOW, base, tiles)
        return jnp.concatenate([part, jnp.zeros_like(part)], 0).astype(BF16)

    def backward_stages(first, second, cot):
        g_two = dot(wo[...], cot)
        yield
        dz_two = (g_two * (1.0 - second * second)).astype(BF16)
        yield
        g_one = dot(w_mid[...], dz_two)
        yield
        dz_one = (g_one * (1.0 - first * first)).astype(BF16)
        yield
        return dz_one, dz_two, dot(wi[...], dz_one).astype(BF16).astype(F32)

    def second_part(base, tiles, sums):
        x = inputs_at(ft2, base, tiles)
        cot = cotangents_at(base, tiles)
        first, second, low_first, low_second = yield from forward_stages(x, wi_t, wm_t)
        yield
        if sums is not None:
            put_lanes(cl, SHALLOW, base, tiles, closure(low_second, wo_t))
        dz_one, dz_two, dfeat = yield from backward_stages(first, second, cot)
        if sums is not None:
            add_terms(sums, (low_first, dz_two), (x, dz_one), (cot, low_second))
        yield
        put_lanes(df, DEEP, base, tiles, dfeat)

    def third_part(base, tiles, held1, held2, counted, sums):
        cot = cotangents_at(base, tiles)
        first = held1[...]
        second = held2[...]
        dz_one, dz_two, dfeat = yield from backward_stages(first, second, cot)
        x = inputs_at(ft1, base, tiles)
        if counted is not None:
            dz_one, dz_two, cot = (jnp.where(counted, v.astype(F32), 0.0).astype(BF16) for v in (dz_one, dz_two, cot))
        add_terms(sums, (first.astype(BF16), dz_two), (x, dz_one), (cot, second.astype(BF16)))
        yield
        put_lanes(df, DEEP, base, tiles, dfeat)

    def add_terms(sums, *pairs):
        for k, pair in enumerate(pairs):
            sums[k] = dot_nt(*pair) if sums[k] is None else sums[k] + dot_nt(*pair)

    def keep_terms(sums, again):
        for acc, total in zip((acc_mid, acc_in, acc_out), sums):
            acc[...] = acc[...] + total if again else total

    def features_of(source, ft, order, rimmed):
        for level in range(levels):
            v = source[level]
            spread(v, level, DEEP, ft, ftx, fth, rimmed)
            spread(0.5 * (east_of(v) - west_of(v)), levels + level, DEEP, ft, ftx, fth, rimmed)
            spread(0.5 * (north_of(v) - south_of(v)), 2 * levels + level, DEEP, ft, ftx, fth, rimmed)
        pack_halo(order, DEEP, ft, ftx, fth)

    def force(v, level, closed):
        eastward, westward, northward, southward = east_of(v), west_of(v), north_of(v), south_of(v)
        laplace = eastward + westward + northward + southward - 4.0 * v
        slope = 0.5 * (eastward - westward)
        return planes[count - 1] * (KAPPA * laplace - planes[2 * levels + level] * slope + closed)

    features_of(planes, ft1, rim, True)
    for k, ref in enumerate(early[2::3]):
        cl[pl.ds(k * ref.shape[0], ref.shape[0]), :] = ref[...]

    def first_part(base, tiles):
        first, second, unused, low_second = yield from forward_stages(inputs_at(ft1, base, tiles), wi_t, wm_t)
        halo1[...] = first
        halo2[...] = second
        yield
        put_lanes(cl, SHALLOW, base, tiles, closure(low_second, wo_t))

    staggered([first_part(rows, len(rim))])
    unpack_halo(rim, SHALLOW, cl, clx, clh)
    for level in range(levels):
        closed = gathered(level, SHALLOW, cl, clx, clh, True)
        mid = planes[levels + level] + 2.0 * DT * force(planes[level], level, closed)
        o_mid[level] = mid[:rows, :LANES]
        mids[level] = mid

    features_of(mids, ft2, outer, False)
    for level in range(levels):
        masked = planes[count - 1] * (2.0 * DT * planes[3 * levels + level])
        spread(masked, level, SHALLOW, dc, dcx, dch, False)
    pack_halo(outer, SHALLOW, dc, dcx, dch)
    sums = [None] * 3
    staggered(
        [second_part(rows, len(outer), None)] + [second_part(k * PART, PART, sums) for k in range(rows // PART)]
    )
    keep_terms(sums, False)
    unpack_halo(outer, DEEP, df, dfx, dfh)

    def adjoint_of(weighted, level, rimmed):
        masked = planes[count - 1] * weighted
        carried = planes[2 * levels + level] * masked
        a0 = gathered(level, DEEP, df, dfx, dfh, rimmed)
        a1 = gathered(levels + level, DEEP, df, dfx, dfh, rimmed)
        a2 = gathered(2 * levels + level, DEEP, df, dfx, dfh, rimmed)
        result = KAPPA * (east_of(masked) + west_of(masked) + north_of(masked) + south_of(masked) - 4.0 * masked)
        result = result + 0.5 * (east_of(carried) - west_of(carried)) + a0
        return result - 0.5 * (east_of(a1) - west_of(a1)) - 0.5 * (north_of(a2) - south_of(a2))

    for level in range(levels):
        closed = jnp.concatenate([cl[pl.ds(level, rows, stride=SHALLOW), :], jnp.zeros((2 * WIDE, LANES), F32)], 0)
        closed = jnp.concatenate([closed, jnp.zeros_like(closed)], 1)
        new = planes[level] + 2.0 * DT * force(mids[level], level, closed)
        o_new[level] = new[:rows, :LANES]
        grad = planes[4 * levels + level] + adjoint_of(2.0 * DT * planes[3 * levels + level], level, False)
        o_old[level] = grad[:rows, :LANES]
        olds[level] = grad

    row = lax.broadcasted_iota(jnp.int32, (ext, LANES), 0)
    inside = (lane > 0) & (lane < LANES - 1) & (row > 0) & (row < rows - 1)
    for level in range(levels):
        masked = planes[count - 1] * (2.0 * DT * olds[level])
        body = masked[:, :LANES]
        dc[pl.ds(level, rows, stride=SHALLOW), :] = jnp.where(inside, body, 0.0)[:rows]
        dcx[pl.ds(level, 2 * WIDE, stride=SHALLOW), :] = body[rows:]
        dch[pl.ds(level, ext, stride=SHALLOW), :] = with_rim(masked)
        for k, r in enumerate(rim[:2]):
            dc[pl.ds((rows + k) * SHALLOW + level, 1), :] = body[r : r + 1]
    pack_halo(rim[:rim_near], SHALLOW, dc, dcx, dch, False)
    at = lax.broadcasted_iota(jnp.int32, (1, rim_near * LANES), 1)
    tile, place = at >> 7, at & (LANES - 1)
    side_row = (tile - 4) * 16 + (place >> 3)
    edge = ((place & 7) == 0) | ((place & 7) == 7)
    counted = (tile < 2) | ((tile >= 4) & edge & (side_row > 0) & (side_row < rows - 1))
    near = pl.ds(0, rim_near * LANES)
    sums = [None] * 3
    staggered(
        [third_part(rows, rim_near, halo1.at[:, near], halo2.at[:, near], counted, sums)]
        + [third_part(k * PART, PART, kept1[k], kept2[k], None, sums) for k in range(rows // PART)]
    )
    keep_terms(sums, True)
    unpack_halo(rim[:rim_near], DEEP, df, dfx, dfh)
    for level in range(levels):
        grad = adjoint_of(2.0 * DT * olds[level], level, True)
        o_now[level] = planes[3 * levels + level, pl.ds(0, rows), pl.ds(0, LANES)] + grad[:rows, :LANES]

    start = 0
    for acc in (acc_mid, acc_in, acc_out):
        deep = acc.shape[0]
        for half in range(hidden // LANES):
            o_grad[pl.ds(start, deep), :] = acc[:, half * LANES : (half + 1) * LANES]
            start += deep
    if start < o_grad.shape[0]:
        o_grad[pl.ds(start, o_grad.shape[0] - start), :] = jnp.zeros((o_grad.shape[0] - start, LANES), F32)


def scale_kernel(factor, terms, g_in, g_mid, g_out):
    hidden = g_mid.shape[0]
    start = 0
    for ref, deep in ((g_mid, hidden), (g_in, DEEP), (g_out, DEEP)):
        keep = ref.shape[0]
        for half in range(hidden // LANES):
            ref[:, half * LANES : (half + 1) * LANES] = terms[pl.ds(start, keep), :] * factor
            start += deep


def along(value, axis, step, periodic):
    count = lax.axis_size(axis)
    pairs = [(i, (i + step) % count) for i in range(count) if periodic or 0 <= i + step < count]
    return lax.ppermute(value, axis, pairs)


def swapped(value, axis, bit):
    return lax.ppermute(value, axis, [(i, i ^ bit) for i in range(lax.axis_size(axis))])


def summed_over(value, halving, doubling):
    bits = []
    bit = 1
    while bit < lax.axis_size(halving):
        upper = (lax.axis_index(halving) & bit) != 0
        half = value.shape[0] // 2
        lower_part, upper_part = value[:half], value[half:]
        sent = jnp.where(upper, lower_part, upper_part)
        value = jnp.where(upper, upper_part, lower_part) + swapped(sent, halving, bit)
        bits.append((bit, upper))
        bit *= 2
    bit = 1
    while bit < lax.axis_size(doubling):
        value = value + swapped(value, doubling, bit)
        bit *= 2
    for bit, upper in reversed(bits):
        other = swapped(value, halving, bit)
        value = jnp.concatenate([jnp.where(upper, other, value), jnp.where(upper, value, other)], 0)
    return value


def body(state_old, state_now, drift, ocean, w_in, w_mid, w_out, cot_mid, cot_new):
    levels, rows, cols = state_now.shape
    width_in, hidden = w_in.shape
    ext = rows + 2 * WIDE
    count = 5 * levels + 1
    packs = -(-ext // 16)
    slots = rows + 8 + packs
    tall = rows // EARLY
    vmem = pl.BlockSpec(memory_space=pltpu.VMEM)
    strip = jax.ShapeDtypeStruct((rows, LANES), F32)
    edge = jax.ShapeDtypeStruct((count, WIDE, LANES), F32)
    arrays = (state_now, state_old, drift, cot_new, cot_mid, ocean)
    west, east, top, bottom, fields = pl.pallas_call(
        pack_kernel,
        out_shape=(strip, strip, edge, edge, jax.ShapeDtypeStruct((count, rows, cols), F32)),
        in_specs=[pl.BlockSpec(memory_space=pltpu.HBM)] * 6,
        out_specs=(vmem,) * 5,
        scratch_shapes=[pltpu.VMEM((rows, cols), jnp.int32), pltpu.SemaphoreType.DMA((6,))],
        compiler_params=pltpu.CompilerParams(vmem_limit_bytes=8 * 2**20),
    )(*(pltpu.with_memory_space_constraint(a, pltpu.HBM) for a in arrays))

    kept = jax.ShapeDtypeStruct((tall // PART, hidden, PART * LANES), F32)
    closed = jax.ShapeDtypeStruct((tall * SHALLOW, LANES), F32)
    tall_weight = jax.ShapeDtypeStruct((hidden, DEEP), BF16)
    flat_weight = jax.ShapeDtypeStruct((DEEP, hidden), BF16)
    prepared = (flat_weight, tall_weight, jax.ShapeDtypeStruct((hidden, hidden), BF16), tall_weight, flat_weight)

    def early(k, extra, extra_out):
        return pl.pallas_call(
            functools.partial(early_kernel, k * tall),
            out_shape=(kept, kept, closed) + extra_out,
            in_specs=[vmem] * (1 + len(extra)),
            out_specs=(vmem,) * (3 + len(extra_out)),
            scratch_shapes=[pltpu.VMEM((tall * DEEP, LANES), F32)],
            compiler_params=pltpu.CompilerParams(vmem_limit_bytes=36 * 2**20),
            cost_estimate=pl.CostEstimate(
                flops=6 * hidden * hidden * tall * cols, bytes_accessed=0, transcendentals=2 * hidden * tall * cols
            ),
        )(fields, *extra)

    left = along(east, "lon", 1, True)
    right = along(west, "lon", -1, True)
    *first_kept, wi, wi_t, wm_t, wo, wo_t = early(0, (w_in, w_mid, w_out.T), prepared)
    up = jnp.concatenate([bottom, left[None, rows - WIDE :], right[None, rows - WIDE :]], 0)
    down = jnp.concatenate([top, left[None, :WIDE], right[None, :WIDE]], 0)
    low = along(up, "lat", 1, False)
    high = along(down, "lat", -1, False)
    done = list(first_kept)
    for k in range(1, EARLY):
        done += early(k, (left, wi_t, wm_t, wo_t), ())

    halves = hidden // LANES
    grain = 8 * lax.axis_size("lat")
    terms_rows = -(-halves * (hidden + 2 * DEEP) // grain) * grain
    field = jax.ShapeDtypeStruct((levels, rows, cols), F32)
    ext_planes = pltpu.VMEM((levels, ext, 2 * LANES), F32)

    def tiles(deep):
        return [pltpu.VMEM((n * deep, LANES), F32) for n in (slots, 16 * packs, 2 * WIDE)]

    kept_halo = pltpu.VMEM((hidden, (8 + packs) * LANES), F32)
    state_mid, state_new, grad_old, grad_now, terms = pl.pallas_call(
        main_kernel,
        out_shape=(field, field, field, field, jax.ShapeDtypeStruct((terms_rows, LANES), F32)),
        in_specs=[vmem] * (11 + 3 * EARLY),
        out_specs=(vmem,) * 5,
        scratch_shapes=[
            pltpu.VMEM((count, ext, 2 * LANES), F32),
            ext_planes,
            ext_planes,
            tiles(DEEP)[0],
            *tiles(DEEP),
            *tiles(SHALLOW),
            *tiles(SHALLOW),
            *tiles(DEEP),
            kept_halo,
            kept_halo,
            pltpu.VMEM((hidden, hidden), F32),
            pltpu.VMEM((DEEP, hidden), F32),
            pltpu.VMEM((DEEP, hidden), F32),
        ],
        compiler_params=pltpu.CompilerParams(vmem_limit_bytes=36 * 2**20),
    )(fields, left, right, low, high, wi, wi_t, wm_t, w_mid, wo, wo_t, *done)

    summed = summed_over(terms, "lat", "lon")
    cells_all = rows * lax.axis_size("lat") * cols * lax.axis_size("lon")
    grad_in, grad_mid, grad_out = pl.pallas_call(
        functools.partial(scale_kernel, GAIN_GRAD / cells_all**0.5),
        out_shape=(
            jax.ShapeDtypeStruct((width_in, hidden), F32),
            jax.ShapeDtypeStruct((hidden, hidden), F32),
            jax.ShapeDtypeStruct((levels, hidden), F32),
        ),
        in_specs=[vmem],
        out_specs=(vmem,) * 3,
        compiler_params=pltpu.CompilerParams(vmem_limit_bytes=8 * 2**20),
    )(summed)
    return state_mid, state_new, grad_old, grad_now, grad_in, grad_mid, grad_out.T


def solution(mesh):
    field = P("grp", "lat", "lon")
    whole = P("grp", None)
    in_specs = (field, field, field, P(("grp", "lat"), "lon"), P(), P(), P(), field, field)
    out_specs = (field, field, field, field, whole, whole, whole)
    return jax.shard_map(body, mesh=mesh, in_specs=in_specs, out_specs=out_specs, check_vma=False)
```

time: 64.8 us -> 68.8 us (1.062)
  local copies, waits for them, and re-layouts: 0.03 us -> 8.45 us
  starting transfers between devices: 19.1 us -> 16 us
  Pallas kernels: 27.8 us -> 26.3 us
    unnamed x6 -> x16, local copies, waits for them, and re-layouts: 0.02 us -> 8.44 us
    pallas_call x1, Pallas kernels: 25.4 us -> 20.6 us  [body(): pl.pallas_call(main_kernel, out_shape=(field, field, field, field, jax.Sh...]
    ppermute x6, starting transfers between devices: 9.62 us -> 6.02 us  [swapped(): lax.ppermute(value, axis, [(i, i ^ bit) for i in range(lax.axis_size(axis...]
    pallas_call x0 -> x2, Pallas kernels: none -> 3.35 us  [early(): pl.pallas_call(functools.partial(early_kernel, k * tall), out_shape=(kept...]
    ppermute x6, waiting for transfers between devices: 13.7 us -> 16.7 us  [swapped(): lax.ppermute(value, axis, [(i, i ^ bit) for i in range(lax.axis_size(axis...]
    ppermute x4, waiting for transfers between devices: 3 us -> 0.02 us  [along(): return lax.ppermute(value, axis, pairs)]
  transfers between devices with their start and end apart: 10 -> 10, of which waited for: 9 -> 6; matrix products, arithmetic and copies ran while one was open for 0% -> 0% of each run, Pallas kernels for 0% -> 5%
where the time goes in v6:
time: 68.8 us; the launch traced here: 68.5 us
  Pallas kernels  26.3 us (38%)
  waiting for transfers between devices  16.8 us (24%)
  starting transfers between devices  16 us (23%)
  local copies, waits for them, and re-layouts  8.45 us (12%)
  between operations  0.8 us (1%)
    pallas_call x1, Pallas kernels, body(): pl.pallas_call(main_kernel, out_shape=(field, field, field, field, jax.Sh...  20.6 us
    ppermute x6, waiting for transfers between devices, swapped(): lax.ppermute(value, axis, [(i, i ^ bit) for i in range(lax.axis_size(axis...  16.7 us
    ppermute x4, starting transfers between devices, along(): return lax.ppermute(value, axis, pairs)  9.94 us
    unnamed x16, local copies, waits for them, and re-layouts  8.44 us
    ppermute x6, starting transfers between devices, swapped(): lax.ppermute(value, axis, [(i, i ^ bit) for i in range(lax.axis_size(axis...  6.02 us
    pallas_call x2, Pallas kernels, early(): pl.pallas_call(functools.partial(early_kernel, k * tall), out_shape=(kept...  3.35 us
    pallas_call x1, Pallas kernels, body(): pl.pallas_call(pack_kernel, out_shape=(strip, strip, edge, edge, jax.Shap...  1.71 us
  transfers between devices with their start and end apart: 10, of which 6 were waited for; matrix products, arithmetic and copies ran while one was open for 0% of the time, Pallas kernels for 5%

profile of v6, /device:TPU:0, one launch (start us, length us, event | category | flops | bytes accessed | tf_op | source)
XLA Modules:
  0.0 68.5 jit_solution(4518255722644497750)
XLA Ops:
  0.6 1.7 %shard_map.144 = (f32[64,128]{1,0:T(8,128)S(1)}, f32[64,128]{1,0:T(8,128)S(1)}, f32[21,4,128]{2,1,0:T(4,128)S(1)}, f32[21,4,128]{2,1,0:T(4,128)S(1)}, f32[21,64,128]{2,1,0:T(8,128)S(1)}) custom-call(f32[4,64,128]{2,1,0:T(8,128)} %now.1, f32[4,64,128]{2,1,0:T(8,128)} %old.1, f32[4,64,128]{2,1,0:T(8,128)} %drift.1, f32[4,64,128]{2,1,0:T(8,128)} %cnew.1, ...), custom_call_target="tpu_custom_call" | custom-call | tf_op jit(solution)/shard_map/pallas_call | solution.py:437
  2.3 3.1 %collective-permute-start = (f32[64,128]{1,0:T(8,128)S(1)}, f32[64,128]{1,0:T(8,128)S(1)}, u32[]{:S(2)}, u32[]{:S(2)}) collective-permute-start(f32[64,128]{1,0:T(8,128)S(1)} %get-tuple-element.32), channel_id=1, source_target_pairs={{0,4},{4,8},{8,12},{12,0},{1,5},{5,9},{9,13},{13,1},{2,6},{6,10},{... | collective-permute-start | bytes 98312 | tf_op jit(solution)/shard_map/ppermute | solution.py:397
  5.4 2.1 %collective-permute-start.1 = (f32[64,128]{1,0:T(8,128)S(1)}, f32[64,128]{1,0:T(8,128)S(1)}, u32[]{:S(2)}, u32[]{:S(2)}) collective-permute-start(f32[64,128]{1,0:T(8,128)S(1)} %get-tuple-element.33), channel_id=1, source_target_pairs={{0,12},{4,0},{8,4},{12,8},{1,13},{5,1},{9,5},{13,9},{2,14},{6,2},{... | collective-permute-start | bytes 98312 | tf_op jit(solution)/shard_map/ppermute | solution.py:397
  7.5 0.0 copy-start.4
  7.5 0.9 %copy-done.4 = bf16[256,256]{1,0:T(8,128)(2,1)S(1)} copy-done((bf16[256,256]{1,0:T(8,128)(2,1)S(1)}, bf16[256,256]{1,0:T(8,128)(2,1)}, u32[]{:S(2)}) %copy-start.4) | copy-done | bytes 131096
  8.4 0.0 copy-start.6
  8.4 0.7 %copy-done.6 = bf16[12,256]{1,0:T(8,128)(2,1)S(1)} copy-done((bf16[12,256]{1,0:T(8,128)(2,1)S(1)}, bf16[12,256]{1,0:T(8,128)(2,1)}, u32[]{:S(2)}) %copy-start.6) | copy-done | bytes 6168
  9.1 0.0 copy-start.7
  9.1 0.7 copy-done.7
  9.8 1.7 %shard_map.145 = (f32[4,256,1024]{2,1,0:T(8,128)S(1)}, f32[4,256,1024]{2,1,0:T(8,128)S(1)}, f32[256,128]{1,0:T(8,128)S(1)}, bf16[16,256]{1,0:T(8,128)(2,1)S(1)},...) custom-call(f32[21,64,128]{2,1,0:T(8,128)S(1)} %get-tuple-element.31, ...), custom_call_target="tpu_custom_call" | custom-call | flops 1610612736 | tf_op jit(solution)/shard_map/pallas_call | solution.py:453
  11.5 0.0 copy-start
  11.5 1.9 %copy-done = f32[4,256,1024]{2,1,0:T(8,128)} copy-done((f32[4,256,1024]{2,1,0:T(8,128)}, f32[4,256,1024]{2,1,0:T(8,128)S(1)}, u32[]{:S(2)}) %copy-start) | copy-done | bytes 4194328
  13.5 0.0 copy-start.2
  13.5 2.0 %copy-done.2 = f32[4,256,1024]{2,1,0:T(8,128)} copy-done((f32[4,256,1024]{2,1,0:T(8,128)}, f32[4,256,1024]{2,1,0:T(8,128)S(1)}, u32[]{:S(2)}) %copy-start.2) | copy-done | bytes 4194328
  15.5 0.0 copy-start.5
  15.5 0.0 copy-start.1
  15.5 0.0 collective-permute-done.refs_0_.refs_1_
  15.5 0.0 collective-permute-done.1.refs_2_
  15.5 1.6 %collective-permute-start.3 = (f32[23,4,128]{2,1,0:T(4,128)S(1)}, f32[23,4,128]{2,1,0:T(4,128)S(1)}, u32[]{:S(2)}, u32[]{:S(2)}) collective-permute-start(f32[23,4,128]{2,1,0:T(4,128)S(1)} %pad_maximum_fusion.3), channel_id=1, source_target_pairs={{1,0},{2,1},{3,2},{5,4},{6,5},{7,6},{9,8},{10,9},{11,10},{13,12},{... | collective-permute-start | bytes 141320 | tf_op jit(solution)/shard_map/ppermute | solution.py:397
  17.1 3.2 %collective-permute-start.2 = (f32[23,4,128]{2,1,0:T(4,128)S(1)}, f32[23,4,128]{2,1,0:T(4,128)S(1)}, u32[]{:S(2)}, u32[]{:S(2)}) collective-permute-start(f32[23,4,128]{2,1,0:T(4,128)S(1)} %pad_maximum_fusion.2), channel_id=1, source_target_pairs={{0,1},{1,2},{2,3},{4,5},{5,6},{6,7},{8,9},{9,10},{10,11},{12,13},{... | collective-permute-start | bytes 141320 | tf_op jit(solution)/shard_map/ppermute | solution.py:397
  20.3 1.6 %shard_map.146 = (f32[4,256,1024]{2,1,0:T(8,128)S(1)}, f32[4,256,1024]{2,1,0:T(8,128)S(1)}, f32[256,128]{1,0:T(8,128)S(1)}) custom-call(f32[21,64,128]{2,1,0:T(8,128)S(1)} %get-tuple-element.31.fields.refs_0_, f32[64,128]{1,0:T(8,128)S(1)} %collective-permute-done.refs_0_.refs_1_, bf16[256,16]{1,0:T(8,128)(2,1)S(1)} %get-tuple-element.37.refs_1_.refs_6_, ...), custom_call_target="tpu_custom_call" | custom-call | flops 1610612736 | tf_op jit(solution)/shard_map/pallas_call | solution.py:453
  22.0 0.0 collective-permute-done.3.refs_4_
  22.0 0.0 collective-permute-done.2.refs_3_
  22.0 0.0 copy-done.5
  22.0 0.0 copy-done.1
  22.0 0.0 copy-start.3
  22.0 2.2 %copy-done.3 = f32[4,256,1024]{2,1,0:T(8,128)S(1)} copy-done((f32[4,256,1024]{2,1,0:T(8,128)S(1)}, f32[4,256,1024]{2,1,0:T(8,128)}, u32[]{:S(2)}) %copy-start.3) | copy-done | bytes 4194328
  24.2 20.6 %shard_map.147 = (f32[4,64,128]{2,1,0:T(8,128)}, f32[4,64,128]{2,1,0:T(8,128)}, f32[4,64,128]{2,1,0:T(8,128)}, f32[4,64,128]{2,1,0:T(8,128)}, f32[576,128]{1,0:T(8,128)S(1)}) custom-call(f32[21,64,128]{2,1,0:T(8,128)S(1)} %get-tuple-element.31.fields.refs_0_, f32[64,128]{1,0:T(8,128)S(1)} %collective-permute-done.refs_0_.refs_1_, ...), custom_call_target="tpu_custom_call" | custom-call | tf_op jit(solution)/shard_map/pallas_call | solution.py:486
  44.8 1.3 %collective-permute-start.4 = (f32[288,128]{1,0:T(8,128)S(1)}, f32[288,128]{1,0:T(8,128)S(1)}, u32[]{:S(2)}, u32[]{:S(2)}) collective-permute-start(f32[288,128]{1,0:T(8,128)S(1)} %slice_select_fusion), channel_id=1, source_target_pairs={{0,1},{1,0},{2,3},{3,2},{4,5},{5,4},{6,7},{7,6},{8,9},{9,8},{10,11... | collective-permute-start | bytes 442376 | tf_op jit(solution)/shard_map/ppermute | solution.py:401
  46.1 1.0 %collective-permute-done.4 = f32[288,128]{1,0:T(8,128)S(1)} collective-permute-done((f32[288,128]{1,0:T(8,128)S(1)}, f32[288,128]{1,0:T(8,128)S(1)}, u32[]{:S(2)}, u32[]{:S(2)}) %collective-permute-start.4) | collective-permute-done | bytes 147488 | tf_op jit(solution)/shard_map/ppermute | solution.py:401
  47.2 1.9 %collective-permute-start.5 = (f32[144,128]{1,0:T(8,128)S(1)}, f32[144,128]{1,0:T(8,128)S(1)}, u32[]{:S(2)}, u32[]{:S(2)}) collective-permute-start(f32[144,128]{1,0:T(8,128)S(1)} %slice_select_fusion.1), channel_id=1, source_target_pairs={{0,2},{1,3},{2,0},{3,1},{4,6},{5,7},{6,4},{7,5},{8,10},{9,11},{10,... | collective-permute-start | bytes 221192 | tf_op jit(solution)/shard_map/ppermute | solution.py:401
  49.1 2.7 %collective-permute-done.5 = f32[144,128]{1,0:T(8,128)S(1)} collective-permute-done((f32[144,128]{1,0:T(8,128)S(1)}, f32[144,128]{1,0:T(8,128)S(1)}, u32[]{:S(2)}, u32[]{:S(2)}) %collective-permute-start.5) | collective-permute-done | bytes 73760 | tf_op jit(solution)/shard_map/ppermute | solution.py:401
  51.8 0.1 collective-permute-start.6
  51.9 4.3 %collective-permute-done.6 = f32[144,128]{1,0:T(8,128)S(1)} collective-permute-done((f32[144,128]{1,0:T(8,128)S(1)}, f32[144,128]{1,0:T(8,128)S(1)}, u32[]{:S(2)}, u32[]{:S(2)}) %collective-permute-start.6) | collective-permute-done | bytes 73760 | tf_op jit(solution)/shard_map/ppermute | solution.py:401
  56.2 0.8 %collective-permute-start.7 = (f32[144,128]{1,0:T(8,128)S(1)}, f32[144,128]{1,0:T(8,128)S(1)}, u32[]{:S(2)}, u32[]{:S(2)}) collective-permute-start(f32[144,128]{1,0:T(8,128)S(1)} %add.14), channel_id=1, source_target_pairs={{0,8},{4,12},{8,0},{12,4},{1,9},{5,13},{9,1},{13,5},{2,10},{6,14},... | collective-permute-start | bytes 221192 | tf_op jit(solution)/shard_map/ppermute | solution.py:401
  57.1 4.7 %collective-permute-done.7 = f32[144,128]{1,0:T(8,128)S(1)} collective-permute-done((f32[144,128]{1,0:T(8,128)S(1)}, f32[144,128]{1,0:T(8,128)S(1)}, u32[]{:S(2)}, u32[]{:S(2)}) %collective-permute-start.7) | collective-permute-done | bytes 73760 | tf_op jit(solution)/shard_map/ppermute | solution.py:401
  61.8 1.8 %collective-permute-start.8 = (f32[144,128]{1,0:T(8,128)S(1)}, f32[144,128]{1,0:T(8,128)S(1)}, u32[]{:S(2)}, u32[]{:S(2)}) collective-permute-start(f32[144,128]{1,0:T(8,128)S(1)} %add.15), channel_id=1, source_target_pairs={{0,2},{1,3},{2,0},{3,1},{4,6},{5,7},{6,4},{7,5},{8,10},{9,11},{10,... | collective-permute-start | bytes 221192 | tf_op jit(solution)/shard_map/ppermute | solution.py:401
  63.6 2.7 %collective-permute-done.8 = f32[144,128]{1,0:T(8,128)S(1)} collective-permute-done((f32[144,128]{1,0:T(8,128)S(1)}, f32[144,128]{1,0:T(8,128)S(1)}, u32[]{:S(2)}, u32[]{:S(2)}) %collective-permute-start.8) | collective-permute-done | bytes 73760 | tf_op jit(solution)/shard_map/ppermute | solution.py:401
  66.3 0.1 collective-permute-start.9
  66.3 1.4 %collective-permute-done.9 = f32[288,128]{1,0:T(8,128)S(1)} collective-permute-done((f32[288,128]{1,0:T(8,128)S(1)}, f32[288,128]{1,0:T(8,128)S(1)}, u32[]{:S(2)}, u32[]{:S(2)}) %collective-permute-start.9) | collective-permute-done | bytes 147488 | tf_op jit(solution)/shard_map/ppermute | solution.py:401
  67.8 0.7 %shard_map.148 = (f32[12,256]{1,0:T(8,128)}, f32[256,256]{1,0:T(8,128)}, f32[4,256]{1,0:T(4,128)}) custom-call(f32[576,128]{1,0:T(8,128)S(1)} %pad_maximum_fusion.terms), custom_call_target="tpu_custom_call" | custom-call | tf_op jit(solution)/shard_map/pallas_call | solution.py:511
  (14 shorter events, 0.2 us)
Async XLA Ops:
  2.3 13.1 %collective-permute-start = (f32[64,128]{1,0:T(8,128)S(1)}, f32[64,128]{1,0:T(8,128)S(1)}, u32[]{:S(2)}, u32[]{:S(2)}) collective-permute-start(f32[64,128]{1,0:T(8,128)S(1)} %get-tuple-element.32), channel_id=1, source_target_pairs={{0,4},{4,8},{8,12},{12,0},{1,5},{5,9},{9,13},{13,1},{2,6},{6,10},{... | collective-permute-start | bytes 98312 | tf_op jit(solution)/shard_map/ppermute | solution.py:397
  5.4 10.1 %collective-permute-start.1 = (f32[64,128]{1,0:T(8,128)S(1)}, f32[64,128]{1,0:T(8,128)S(1)}, u32[]{:S(2)}, u32[]{:S(2)}) collective-permute-start(f32[64,128]{1,0:T(8,128)S(1)} %get-tuple-element.33), channel_id=1, source_target_pairs={{0,12},{4,0},{8,4},{12,8},{1,13},{5,1},{9,5},{13,9},{2,14},{6,2},{... | collective-permute-start | bytes 98312 | tf_op jit(solution)/shard_map/ppermute | solution.py:397
  7.5 0.9 %copy-start.4 = (bf16[256,256]{1,0:T(8,128)(2,1)S(1)}, bf16[256,256]{1,0:T(8,128)(2,1)}, u32[]{:S(2)}) copy-start(bf16[256,256]{1,0:T(8,128)(2,1)} %refs_8_.1) | copy-start | bytes 393220
  8.4 0.7 %copy-start.6 = (bf16[12,256]{1,0:T(8,128)(2,1)S(1)}, bf16[12,256]{1,0:T(8,128)(2,1)}, u32[]{:S(2)}) copy-start(bf16[12,256]{1,0:T(8,128)(2,1)} %refs_0_.1) | copy-start | bytes 18436
  9.1 0.7 copy-start.7
  11.5 1.9 %copy-start = (f32[4,256,1024]{2,1,0:T(8,128)}, f32[4,256,1024]{2,1,0:T(8,128)S(1)}, u32[]{:S(2)}) copy-start(f32[4,256,1024]{2,1,0:T(8,128)S(1)} %get-tuple-element.41.refs_11_) | copy-start | bytes 12582916
  13.5 2.0 %copy-start.2 = (f32[4,256,1024]{2,1,0:T(8,128)}, f32[4,256,1024]{2,1,0:T(8,128)S(1)}, u32[]{:S(2)}) copy-start(f32[4,256,1024]{2,1,0:T(8,128)S(1)} %get-tuple-element.42.refs_12_) | copy-start | bytes 12582916
  15.5 6.5 %copy-start.5 = (bf16[256,256]{1,0:T(8,128)(2,1)S(1)}, bf16[256,256]{1,0:T(8,128)(2,1)}, u32[]{:S(2)}) copy-start(bf16[256,256]{1,0:T(8,128)(2,1)} %refs_8_.1) | copy-start | bytes 393220
  15.5 6.5 %copy-start.1 = (f32[4,256,1024]{2,1,0:T(8,128)S(1)}, f32[4,256,1024]{2,1,0:T(8,128)}, u32[]{:S(2)}) copy-start(f32[4,256,1024]{2,1,0:T(8,128)} %copy-done) | copy-start | bytes 12582916
  15.5 6.4 %collective-permute-start.3 = (f32[23,4,128]{2,1,0:T(4,128)S(1)}, f32[23,4,128]{2,1,0:T(4,128)S(1)}, u32[]{:S(2)}, u32[]{:S(2)}) collective-permute-start(f32[23,4,128]{2,1,0:T(4,128)S(1)} %pad_maximum_fusion.3), channel_id=1, source_target_pairs={{1,0},{2,1},{3,2},{5,4},{6,5},{7,6},{9,8},{10,9},{11,10},{13,12},{... | collective-permute-start | bytes 141320 | tf_op jit(solution)/shard_map/ppermute | solution.py:397
  17.1 4.9 %collective-permute-start.2 = (f32[23,4,128]{2,1,0:T(4,128)S(1)}, f32[23,4,128]{2,1,0:T(4,128)S(1)}, u32[]{:S(2)}, u32[]{:S(2)}) collective-permute-start(f32[23,4,128]{2,1,0:T(4,128)S(1)} %pad_maximum_fusion.2), channel_id=1, source_target_pairs={{0,1},{1,2},{2,3},{4,5},{5,6},{6,7},{8,9},{9,10},{10,11},{12,13},{... | collective-permute-start | bytes 141320 | tf_op jit(solution)/shard_map/ppermute | solution.py:397
  22.0 2.2 %copy-start.3 = (f32[4,256,1024]{2,1,0:T(8,128)S(1)}, f32[4,256,1024]{2,1,0:T(8,128)}, u32[]{:S(2)}) copy-start(f32[4,256,1024]{2,1,0:T(8,128)} %copy-done.2) | copy-start | bytes 12582916
  44.8 2.3 %collective-permute-start.4 = (f32[288,128]{1,0:T(8,128)S(1)}, f32[288,128]{1,0:T(8,128)S(1)}, u32[]{:S(2)}, u32[]{:S(2)}) collective-permute-start(f32[288,128]{1,0:T(8,128)S(1)} %slice_select_fusion), channel_id=1, source_target_pairs={{0,1},{1,0},{2,3},{3,2},{4,5},{5,4},{6,7},{7,6},{8,9},{9,8},{10,11... | collective-permute-start | bytes 442376 | tf_op jit(solution)/shard_map/ppermute | solution.py:401
  47.2 4.6 %collective-permute-start.5 = (f32[144,128]{1,0:T(8,128)S(1)}, f32[144,128]{1,0:T(8,128)S(1)}, u32[]{:S(2)}, u32[]{:S(2)}) collective-permute-start(f32[144,128]{1,0:T(8,128)S(1)} %slice_select_fusion.1), channel_id=1, source_target_pairs={{0,2},{1,3},{2,0},{3,1},{4,6},{5,7},{6,4},{7,5},{8,10},{9,11},{10,... | collective-permute-start | bytes 221192 | tf_op jit(solution)/shard_map/ppermute | solution.py:401
  51.8 4.4 %collective-permute-start.6 = (f32[144,128]{1,0:T(8,128)S(1)}, f32[144,128]{1,0:T(8,128)S(1)}, u32[]{:S(2)}, u32[]{:S(2)}) collective-permute-start(f32[144,128]{1,0:T(8,128)S(1)} %select_add_fusion.1), channel_id=1, source_target_pairs={{0,4},{4,0},{8,12},{12,8},{1,5},{5,1},{9,13},{13,9},{2,6},{6,2},{1... | collective-permute-start | bytes 221192 | tf_op jit(solution)/shard_map/ppermute | solution.py:401
  56.2 5.5 %collective-permute-start.7 = (f32[144,128]{1,0:T(8,128)S(1)}, f32[144,128]{1,0:T(8,128)S(1)}, u32[]{:S(2)}, u32[]{:S(2)}) collective-permute-start(f32[144,128]{1,0:T(8,128)S(1)} %add.14), channel_id=1, source_target_pairs={{0,8},{4,12},{8,0},{12,4},{1,9},{5,13},{9,1},{13,5},{2,10},{6,14},... | collective-permute-start | bytes 221192 | tf_op jit(solution)/shard_map/ppermute | solution.py:401
  61.8 4.4 %collective-permute-start.8 = (f32[144,128]{1,0:T(8,128)S(1)}, f32[144,128]{1,0:T(8,128)S(1)}, u32[]{:S(2)}, u32[]{:S(2)}) collective-permute-start(f32[144,128]{1,0:T(8,128)S(1)} %add.15), channel_id=1, source_target_pairs={{0,2},{1,3},{2,0},{3,1},{4,6},{5,7},{6,4},{7,5},{8,10},{9,11},{10,... | collective-permute-start | bytes 221192 | tf_op jit(solution)/shard_map/ppermute | solution.py:401
  66.3 1.4 %collective-permute-start.9 = (f32[288,128]{1,0:T(8,128)S(1)}, f32[288,128]{1,0:T(8,128)S(1)}, u32[]{:S(2)}, u32[]{:S(2)}) collective-permute-start(f32[288,128]{1,0:T(8,128)S(1)} %pad_maximum_fusion.1), channel_id=1, source_target_pairs={{0,1},{1,0},{2,3},{3,2},{4,5},{5,4},{6,7},{7,6},{8,9},{9,8},{10,11... | collective-permute-start | bytes 442376 | tf_op jit(solution)/shard_map/ppermute | solution.py:401

commit v7 on v6

--- a/solution.py
+++ b/solution.py
@@ -15,6 +15,7 @@
 LANES = 128
 PART = 8
 EARLY = 2
+SHARES = 2
 DEEP = 16
 SHALLOW = 8
 
@@ -58,6 +59,16 @@
     east[...] = to_east
 
 
+def join_kernel(top, bottom, left, right, up, down):
+    count = top.shape[0]
+    rows = left.shape[0]
+    up[pl.ds(0, count)] = bottom[...]
+    down[pl.ds(0, count)] = top[...]
+    for k, strip in enumerate((left, right)):
+        up[count + k] = strip[pl.ds(rows - WIDE, WIDE), :]
+        down[count + k] = strip[pl.ds(0, WIDE), :]
+
+
 def east_of(v):
     return pltpu.roll(v, v.shape[1] - 1, 1)
 
@@ -150,10 +161,10 @@
     staggered(part(k * PART, keep1.at[k], keep2.at[k]) for k in range(tall // PART))
 
 
-def main_kernel(*refs):
+def main_kernel(bands, *refs):
     fields, left, right, low, high, wi, wi_t, wm_t, w_mid, wo, wo_t, *refs = refs
     early, refs = refs[: 3 * EARLY], refs[3 * EARLY :]
-    o_mid, o_new, o_old, o_now, o_grad, planes, mids, olds, *refs = refs
+    o_mid, o_new, o_old, o_now, o_grad, o_place, planes, mids, olds, *refs = refs
     ft1, ft2, fth, ftx, cl, clh, clx, dc, dch, dcx, df, dfh, dfx, halo1, halo2, acc_mid, acc_in, acc_out = refs
     levels, rows, cols = o_mid.shape
     hidden = w_mid.shape[0]
@@ -168,13 +179,21 @@
     outer = [rows, ext - 1] + packed + [rows + 1, ext - 2]
 
     lane = lax.broadcasted_iota(jnp.int32, (ext, LANES), 1)
-    left_all = jnp.concatenate([left[...], high[count], low[count]], 0)
-    right_all = jnp.concatenate([right[...], high[count + 1], low[count + 1]], 0)
+    band = lax.axis_index("lat")
+    o_place[...] = jnp.zeros_like(o_place) + band
+    has_low = jnp.where(band > 0, 1.0, 0.0)
+    has_high = jnp.where(band < bands - 1, 1.0, 0.0)
+
+    def beyond(p):
+        return [high[p] * has_high, low[p] * has_low]
+
+    left_all = jnp.concatenate([left[...]] + beyond(count), 0)
+    right_all = jnp.concatenate([right[...]] + beyond(count + 1), 0)
     for p in range(count):
         from_right = pltpu.roll(right_all, LANES - WIDE * p, 1) if p else right_all
         from_left = pltpu.roll(left_all, LANES - WIDE * (p + 1), 1)
         side = jnp.where(lane < WIDE, from_right, jnp.where(lane >= LANES - WIDE, from_left, 0.0))
-        planes[p, :, pl.ds(0, LANES)] = jnp.concatenate([fields[p], high[p], low[p]], 0)
+        planes[p, :, pl.ds(0, LANES)] = jnp.concatenate([fields[p]] + beyond(p), 0)
         planes[p, :, pl.ds(LANES, LANES)] = side
 
     for ref in (ft1, ft2, fth, ftx, dc, dch, dcx):
@@ -381,45 +400,53 @@
         o_grad[pl.ds(start, o_grad.shape[0] - start), :] = jnp.zeros((o_grad.shape[0] - start, LANES), F32)
 
 
-def scale_kernel(factor, terms, g_in, g_mid, g_out):
+def scale_kernel(factor, *refs):
+    terms, (g_in, g_mid, g_out) = refs[:SHARES], refs[SHARES:]
+    share = terms[0].shape[0]
     hidden = g_mid.shape[0]
     start = 0
     for ref, deep in ((g_mid, hidden), (g_in, DEEP), (g_out, DEEP)):
-        keep = ref.shape[0]
         for half in range(hidden // LANES):
-            ref[:, half * LANES : (half + 1) * LANES] = terms[pl.ds(start, keep), :] * factor
+            at, end = start, start + ref.shape[0]
+            while at < end:
+                k, first = divmod(at, share)
+                some = min(end - at, share - first)
+                piece = terms[k][pl.ds(first, some), :]
+                ref[pl.ds(at - start, some), half * LANES : (half + 1) * LANES] = piece * factor
+                at += some
             start += deep
 
 
-def along(value, axis, step, periodic):
+def along(value, axis, step):
     count = lax.axis_size(axis)
-    pairs = [(i, (i + step) % count) for i in range(count) if periodic or 0 <= i + step < count]
-    return lax.ppermute(value, axis, pairs)
+    return lax.ppermute(value, axis, [(i, (i + step) % count) for i in range(count)])
 
 
 def swapped(value, axis, bit):
     return lax.ppermute(value, axis, [(i, i ^ bit) for i in range(lax.axis_size(axis))])
 
 
-def summed_over(value, halving, doubling):
+def summed_over(values, place, halving, doubling):
     bits = []
     bit = 1
     while bit < lax.axis_size(halving):
-        upper = (lax.axis_index(halving) & bit) != 0
-        half = value.shape[0] // 2
-        lower_part, upper_part = value[:half], value[half:]
-        sent = jnp.where(upper, lower_part, upper_part)
-        value = jnp.where(upper, upper_part, lower_part) + swapped(sent, halving, bit)
+        upper = (place & bit) != 0
+        half = values[0].shape[0] // 2
+        got = [swapped(jnp.where(upper, v[:half], v[half:]), halving, bit) for v in values]
+        values = [jnp.where(upper, v[half:], v[:half]) + g for v, g in zip(values, got)]
         bits.append((bit, upper))
         bit *= 2
     bit = 1
     while bit < lax.axis_size(doubling):
-        value = value + swapped(value, doubling, bit)
+        got = [swapped(v, doubling, bit) for v in values]
+        values = [v + g for v, g in zip(values, got)]
         bit *= 2
     for bit, upper in reversed(bits):
-        other = swapped(value, halving, bit)
-        value = jnp.concatenate([jnp.where(upper, other, value), jnp.where(upper, value, other)], 0)
-    return value
+        got = [swapped(v, halving, bit) for v in values]
+        values = [
+            jnp.concatenate([jnp.where(upper, g, v), jnp.where(upper, v, g)], 0) for v, g in zip(values, got)
+        ]
+    return values
 
 
 def body(state_old, state_now, drift, ocean, w_in, w_mid, w_out, cot_mid, cot_new):
@@ -456,25 +483,31 @@
             in_specs=[vmem] * (1 + len(extra)),
             out_specs=(vmem,) * (3 + len(extra_out)),
             scratch_shapes=[pltpu.VMEM((tall * DEEP, LANES), F32)],
-            compiler_params=pltpu.CompilerParams(vmem_limit_bytes=36 * 2**20),
+            compiler_params=pltpu.CompilerParams(vmem_limit_bytes=12 * 2**20),
             cost_estimate=pl.CostEstimate(
                 flops=6 * hidden * hidden * tall * cols, bytes_accessed=0, transcendentals=2 * hidden * tall * cols
             ),
         )(fields, *extra)
 
-    left = along(east, "lon", 1, True)
-    right = along(west, "lon", -1, True)
+    left = along(east, "lon", 1)
+    right = along(west, "lon", -1)
     *first_kept, wi, wi_t, wm_t, wo, wo_t = early(0, (w_in, w_mid, w_out.T), prepared)
-    up = jnp.concatenate([bottom, left[None, rows - WIDE :], right[None, rows - WIDE :]], 0)
-    down = jnp.concatenate([top, left[None, :WIDE], right[None, :WIDE]], 0)
-    low = along(up, "lat", 1, False)
-    high = along(down, "lat", -1, False)
+    message = jax.ShapeDtypeStruct((count + 2, WIDE, LANES), F32)
+    up, down = pl.pallas_call(
+        join_kernel,
+        out_shape=(message, message),
+        in_specs=[vmem] * 4,
+        out_specs=(vmem,) * 2,
+        compiler_params=pltpu.CompilerParams(vmem_limit_bytes=4 * 2**20),
+    )(top, bottom, left, right)
+    low = along(up, "lat", 1)
+    high = along(down, "lat", -1)
     done = list(first_kept)
     for k in range(1, EARLY):
         done += early(k, (left, wi_t, wm_t, wo_t), ())
 
     halves = hidden // LANES
-    grain = 8 * lax.axis_size("lat")
+    grain = 8 * SHARES * lax.axis_size("lat")
     terms_rows = -(-halves * (hidden + 2 * DEEP) // grain) * grain
     field = jax.ShapeDtypeStruct((levels, rows, cols), F32)
     ext_planes = pltpu.VMEM((levels, ext, 2 * LANES), F32)
@@ -483,11 +516,11 @@
         return [pltpu.VMEM((n * deep, LANES), F32) for n in (slots, 16 * packs, 2 * WIDE)]
 
     kept_halo = pltpu.VMEM((hidden, (8 + packs) * LANES), F32)
-    state_mid, state_new, grad_old, grad_now, terms = pl.pallas_call(
-        main_kernel,
-        out_shape=(field, field, field, field, jax.ShapeDtypeStruct((terms_rows, LANES), F32)),
+    state_mid, state_new, grad_old, grad_now, terms, place = pl.pallas_call(
+        functools.partial(main_kernel, lax.axis_size("lat")),
+        out_shape=(field, field, field, field, jax.ShapeDtypeStruct((terms_rows, LANES), F32), jax.ShapeDtypeStruct((8, LANES), jnp.int32)),
         in_specs=[vmem] * (11 + 3 * EARLY),
-        out_specs=(vmem,) * 5,
+        out_specs=(vmem,) * 6,
         scratch_shapes=[
             pltpu.VMEM((count, ext, 2 * LANES), F32),
             ext_planes,
@@ -503,10 +536,10 @@
             pltpu.VMEM((DEEP, hidden), F32),
             pltpu.VMEM((DEEP, hidden), F32),
         ],
-        compiler_params=pltpu.CompilerParams(vmem_limit_bytes=36 * 2**20),
+        compiler_params=pltpu.CompilerParams(vmem_limit_bytes=34 * 2**20),
     )(fields, left, right, low, high, wi, wi_t, wm_t, w_mid, wo, wo_t, *done)
 
-    summed = summed_over(terms, "lat", "lon")
+    summed = summed_over(jnp.split(terms, SHARES), place[:1], "lat", "lon")
     cells_all = rows * lax.axis_size("lat") * cols * lax.axis_size("lon")
     grad_in, grad_mid, grad_out = pl.pallas_call(
         functools.partial(scale_kernel, GAIN_GRAD / cells_all**0.5),
@@ -515,10 +548,10 @@
             jax.ShapeDtypeStruct((hidden, hidden), F32),
             jax.ShapeDtypeStruct((levels, hidden), F32),
         ),
-        in_specs=[vmem],
+        in_specs=[vmem] * SHARES,
         out_specs=(vmem,) * 3,
         compiler_params=pltpu.CompilerParams(vmem_limit_bytes=8 * 2**20),
-    )(summed)
+    )(*summed)
     return state_mid, state_new, grad_old, grad_now, grad_in, grad_mid, grad_out.T
 
 

time: 68.8 us -> 75.2 us (1.093)
  waiting for transfers between devices: 16.8 us -> 32.9 us
  local copies, waits for them, and re-layouts: 8.45 us -> 2.28 us
  starting transfers between devices: 16 us -> 12.3 us
    ppermute x6 -> x12, waiting for transfers between devices: 16.7 us -> 32.8 us  [swapped(): lax.ppermute(value, axis, [(i, i ^ bit) for i in range(lax.axis_size(axis...]
    unnamed x16 -> x8, local copies, waits for them, and re-layouts: 8.44 us -> 2.28 us
    ppermute x4, starting transfers between devices: 9.94 us -> 6.96 us  [along(): lax.ppermute(value, axis, [(i, (i + step) % count) for i in range(count)])]
    ppermute x6 -> x12, starting transfers between devices: 6.02 us -> 5.34 us  [swapped(): lax.ppermute(value, axis, [(i, i ^ bit) for i in range(lax.axis_size(axis...]
    pallas_call x1 -> x2, Pallas kernels: 20.6 us -> 20.7 us  [the longest x1 20.7 us: body(): pl.pallas_call(functools.partial(main_kernel, lax.axis_size('lat')), out_...]
  transfers between devices with their start and end apart: 10 -> 16, of which waited for: 6 -> 12; matrix products, arithmetic and copies ran while one was open for 0% -> 0% of each run, Pallas kernels for 5% -> 4%
where the time goes in v7:
time: 75.2 us; the launch traced here: 74.9 us
  waiting for transfers between devices  32.9 us (44%)
  Pallas kernels  26.5 us (35%)
  starting transfers between devices  12.3 us (16%)
  local copies, waits for them, and re-layouts  2.28 us (3%)
  between operations  0.77 us (1%)
    ppermute x12, waiting for transfers between devices, swapped(): lax.ppermute(value, axis, [(i, i ^ bit) for i in range(lax.axis_size(axis...  32.8 us
    pallas_call x1, Pallas kernels, body(): pl.pallas_call(functools.partial(main_kernel, lax.axis_size('lat')), out_...  20.7 us
    ppermute x4, starting transfers between devices, along(): lax.ppermute(value, axis, [(i, (i + step) % count) for i in range(count)])  6.96 us
    ppermute x12, starting transfers between devices, swapped(): lax.ppermute(value, axis, [(i, i ^ bit) for i in range(lax.axis_size(axis...  5.34 us
    pallas_call x2, Pallas kernels, early(): pl.pallas_call(functools.partial(early_kernel, k * tall), out_shape=(kept...  3.36 us
    unnamed x8, local copies, waits for them, and re-layouts  2.28 us
    pallas_call x1, Pallas kernels, body(): pl.pallas_call(pack_kernel, out_shape=(strip, strip, edge, edge, jax.Shap...  1.71 us
  transfers between devices with their start and end apart: 16, of which 12 were waited for; matrix products, arithmetic and copies ran while one was open for 0% of the time, Pallas kernels for 4%

profile of v7, /device:TPU:0, one launch (start us, length us, event | category | flops | bytes accessed | tf_op | source)
XLA Modules:
  0.0 74.9 jit_solution(5177033482810398827)
XLA Ops:
  0.6 1.7 %shard_map.144 = (f32[64,128]{1,0:T(8,128)S(1)}, f32[64,128]{1,0:T(8,128)S(1)}, f32[21,4,128]{2,1,0:T(4,128)S(1)}, f32[21,4,128]{2,1,0:T(4,128)S(1)}, f32[21,64,128]{2,1,0:T(8,128)S(1)}) custom-call(f32[4,64,128]{2,1,0:T(8,128)} %now.1, f32[4,64,128]{2,1,0:T(8,128)} %old.1, f32[4,64,128]{2,1,0:T(8,128)} %drift.1, f32[4,64,128]{2,1,0:T(8,128)} %cnew.1, ...), custom_call_target="tpu_custom_call" | custom-call | tf_op jit(solution)/shard_map/pallas_call | solution.py:464
  2.3 3.1 %collective-permute-start = (f32[64,128]{1,0:T(8,128)S(1)}, f32[64,128]{1,0:T(8,128)S(1)}, u32[]{:S(2)}, u32[]{:S(2)}) collective-permute-start(f32[64,128]{1,0:T(8,128)S(1)} %get-tuple-element.35), channel_id=1, source_target_pairs={{0,4},{4,8},{8,12},{12,0},{1,5},{5,9},{9,13},{13,1},{2,6},{6,10},{... | collective-permute-start | bytes 98312 | tf_op jit(solution)/shard_map/ppermute | solution.py:422
  5.4 2.1 %collective-permute-start.1 = (f32[64,128]{1,0:T(8,128)S(1)}, f32[64,128]{1,0:T(8,128)S(1)}, u32[]{:S(2)}, u32[]{:S(2)}) collective-permute-start(f32[64,128]{1,0:T(8,128)S(1)} %get-tuple-element.36), channel_id=1, source_target_pairs={{0,12},{4,0},{8,4},{12,8},{1,13},{5,1},{9,5},{13,9},{2,14},{6,2},{... | collective-permute-start | bytes 98312 | tf_op jit(solution)/shard_map/ppermute | solution.py:422
  7.5 0.0 copy-start
  7.5 0.9 %copy-done = bf16[256,256]{1,0:T(8,128)(2,1)S(1)} copy-done((bf16[256,256]{1,0:T(8,128)(2,1)S(1)}, bf16[256,256]{1,0:T(8,128)(2,1)}, u32[]{:S(2)}) %copy-start) | copy-done | bytes 131096
  8.4 0.0 copy-start.2
  8.4 0.7 copy-done.2
  9.1 0.0 copy-start.3
  9.1 0.7 copy-done.3
  9.8 1.7 %shard_map.146 = (f32[4,256,1024]{2,1,0:T(8,128)S(1)}, f32[4,256,1024]{2,1,0:T(8,128)S(1)}, f32[256,128]{1,0:T(8,128)S(1)}, bf16[16,256]{1,0:T(8,128)(2,1)S(1)},...) custom-call(f32[21,64,128]{2,1,0:T(8,128)S(1)} %get-tuple-element.34, ...), custom_call_target="tpu_custom_call" | custom-call | flops 1610612736 | tf_op jit(solution)/shard_map/pallas_call | solution.py:480
  11.5 0.0 copy-start.1
  11.5 0.0 collective-permute-done.left.refs_0_.refs_1_
  11.5 0.0 collective-permute-done.1.right.refs_2_
  11.6 0.1 collective-permute-start.2
  11.6 1.7 %collective-permute-start.3 = (f32[23,4,128]{2,1,0:T(4,128)S(1)}, f32[23,4,128]{2,1,0:T(4,128)S(1)}, u32[]{:S(2)}, u32[]{:S(2)}) collective-permute-start(f32[23,4,128]{2,1,0:T(4,128)S(1)} %get-tuple-element.40), channel_id=1, source_target_pairs={{0,3},{1,0},{2,1},{3,2},{4,7},{5,4},{6,5},{7,6},{8,11},{9,8},{10,9... | collective-permute-start | bytes 141320 | tf_op jit(solution)/shard_map/ppermute | solution.py:422
  13.4 1.6 %shard_map.147 = (f32[4,256,1024]{2,1,0:T(8,128)S(1)}, f32[4,256,1024]{2,1,0:T(8,128)S(1)}, f32[256,128]{1,0:T(8,128)S(1)}) custom-call(f32[21,64,128]{2,1,0:T(8,128)S(1)} %get-tuple-element.34.fields.refs_0_, f32[64,128]{1,0:T(8,128)S(1)} %collective-permute-done.left.refs_0_.refs_1_, bf16[256,16]{1,0:T(8,128)(2,1)S(1)} %get-tuple-element.42.refs_1_.refs_6_, ...), custom_call_target="tpu_custom_call" | custom-call | flops 1610612736 | tf_op jit(solution)/shard_map/pallas_call | solution.py:480
  15.0 0.1 collective-permute-done.2.refs_3_
  15.1 0.0 collective-permute-done.3.refs_4_
  15.1 0.0 copy-done.1
  15.1 20.7 %shard_map.148 = (f32[4,64,128]{2,1,0:T(8,128)}, f32[4,64,128]{2,1,0:T(8,128)}, f32[4,64,128]{2,1,0:T(8,128)}, f32[4,64,128]{2,1,0:T(8,128)}, f32[576,128]{1,0:T(8,128)S(1)}, /*index=5*/s32[8,128]{1,0:T(8,128)S(1)}) custom-call(f32[21,64,128]{2,1,0:T(8,128)S(1)} %get-tuple-element.34.fields.refs_0_, f32[64,128]{1,0:T(8,128)S(1)} %collective-permute-done.left.refs_0_.refs_1_, ...), custom_call_target="tpu_custom_call" | custom-call | tf_op jit(solution)/shard_map/pallas_call | solution.py:519
  35.8 1.8 %collective-permute-start.10 = (f32[144,128]{1,0:T(8,128)S(1)}, f32[144,128]{1,0:T(8,128)S(1)}, u32[]{:S(2)}, u32[]{:S(2)}) collective-permute-start(f32[144,128]{1,0:T(8,128)S(1)} %get-tuple-element.63), channel_id=1, source_target_pairs={{0,1},{1,0},{2,3},{3,2},{4,5},{5,4},{6,7},{7,6},{8,9},{9,8},{10,11... | collective-permute-start | bytes 221192 | tf_op jit(solution)/shard_map/ppermute | solution.py:426
  37.7 0.1 collective-permute-start.4
  37.8 0.8 %collective-permute-done.10 = f32[144,128]{1,0:T(8,128)S(1)} collective-permute-done((f32[144,128]{1,0:T(8,128)S(1)}, f32[144,128]{1,0:T(8,128)S(1)}, u32[]{:S(2)}, u32[]{:S(2)}) %collective-permute-start.10) | collective-permute-done | bytes 73760 | tf_op jit(solution)/shard_map/ppermute | solution.py:426
  38.6 0.4 collective-permute-done.4
  39.0 0.4 collective-permute-start.11
  39.4 3.6 %collective-permute-done.11 = f32[72,128]{1,0:T(8,128)S(1)} collective-permute-done((f32[72,128]{1,0:T(8,128)S(1)}, f32[72,128]{1,0:T(8,128)S(1)}, u32[]{:S(2)}, u32[]{:S(2)}) %collective-permute-start.11) | collective-permute-done | bytes 36896 | tf_op jit(solution)/shard_map/ppermute | solution.py:426
  43.0 0.1 collective-permute-start.12
  43.1 3.9 %collective-permute-done.12 = f32[72,128]{1,0:T(8,128)S(1)} collective-permute-done((f32[72,128]{1,0:T(8,128)S(1)}, f32[72,128]{1,0:T(8,128)S(1)}, u32[]{:S(2)}, u32[]{:S(2)}) %collective-permute-start.12) | collective-permute-done | bytes 36896 | tf_op jit(solution)/shard_map/ppermute | solution.py:426
  47.1 0.8 %collective-permute-start.13 = (f32[72,128]{1,0:T(8,128)S(1)}, f32[72,128]{1,0:T(8,128)S(1)}, u32[]{:S(2)}, u32[]{:S(2)}) collective-permute-start(f32[72,128]{1,0:T(8,128)S(1)} %add.30), channel_id=1, source_target_pairs={{0,8},{4,12},{8,0},{12,4},{1,9},{5,13},{9,1},{13,5},{2,10},{6,14},... | collective-permute-start | bytes 110600 | tf_op jit(solution)/shard_map/ppermute | solution.py:426
  47.9 4.1 %collective-permute-done.13 = f32[72,128]{1,0:T(8,128)S(1)} collective-permute-done((f32[72,128]{1,0:T(8,128)S(1)}, f32[72,128]{1,0:T(8,128)S(1)}, u32[]{:S(2)}, u32[]{:S(2)}) %collective-permute-start.13) | collective-permute-done | bytes 36896 | tf_op jit(solution)/shard_map/ppermute | solution.py:426
  51.9 0.4 collective-permute-start.14
  52.3 3.6 %collective-permute-done.14 = f32[72,128]{1,0:T(8,128)S(1)} collective-permute-done((f32[72,128]{1,0:T(8,128)S(1)}, f32[72,128]{1,0:T(8,128)S(1)}, u32[]{:S(2)}, u32[]{:S(2)}) %collective-permute-start.14) | collective-permute-done | bytes 36896 | tf_op jit(solution)/shard_map/ppermute | solution.py:426
  55.9 0.4 collective-permute-start.5
  56.3 3.6 %collective-permute-done.5 = f32[72,128]{1,0:T(8,128)S(1)} collective-permute-done((f32[72,128]{1,0:T(8,128)S(1)}, f32[72,128]{1,0:T(8,128)S(1)}, u32[]{:S(2)}, u32[]{:S(2)}) %collective-permute-start.5) | collective-permute-done | bytes 36896 | tf_op jit(solution)/shard_map/ppermute | solution.py:426
  59.9 0.1 collective-permute-start.6
  60.0 3.9 %collective-permute-done.6 = f32[72,128]{1,0:T(8,128)S(1)} collective-permute-done((f32[72,128]{1,0:T(8,128)S(1)}, f32[72,128]{1,0:T(8,128)S(1)}, u32[]{:S(2)}, u32[]{:S(2)}) %collective-permute-start.6) | collective-permute-done | bytes 36896 | tf_op jit(solution)/shard_map/ppermute | solution.py:426
  64.0 0.8 %collective-permute-start.7 = (f32[72,128]{1,0:T(8,128)S(1)}, f32[72,128]{1,0:T(8,128)S(1)}, u32[]{:S(2)}, u32[]{:S(2)}) collective-permute-start(f32[72,128]{1,0:T(8,128)S(1)} %add.26), channel_id=1, source_target_pairs={{0,8},{4,12},{8,0},{12,4},{1,9},{5,13},{9,1},{13,5},{2,10},{6,14},... | collective-permute-start | bytes 110600 | tf_op jit(solution)/shard_map/ppermute | solution.py:426
  64.8 4.0 %collective-permute-done.7 = f32[72,128]{1,0:T(8,128)S(1)} collective-permute-done((f32[72,128]{1,0:T(8,128)S(1)}, f32[72,128]{1,0:T(8,128)S(1)}, u32[]{:S(2)}, u32[]{:S(2)}) %collective-permute-start.7) | collective-permute-done | bytes 36896 | tf_op jit(solution)/shard_map/ppermute | solution.py:426
  68.8 0.4 collective-permute-start.8
  69.2 0.0 collective-permute-start.15
  69.2 3.6 %collective-permute-done.8 = f32[72,128]{1,0:T(8,128)S(1)} collective-permute-done((f32[72,128]{1,0:T(8,128)S(1)}, f32[72,128]{1,0:T(8,128)S(1)}, u32[]{:S(2)}, u32[]{:S(2)}) %collective-permute-start.8) | collective-permute-done | bytes 36896 | tf_op jit(solution)/shard_map/ppermute | solution.py:426
  72.8 0.1 collective-permute-start.9
  72.9 0.0 collective-permute-done.15
  72.9 1.2 %collective-permute-done.9 = f32[144,128]{1,0:T(8,128)S(1)} collective-permute-done((f32[144,128]{1,0:T(8,128)S(1)}, f32[144,128]{1,0:T(8,128)S(1)}, u32[]{:S(2)}, u32[]{:S(2)}) %collective-permute-start.9) | collective-permute-done | bytes 73760 | tf_op jit(solution)/shard_map/ppermute | solution.py:426
  74.2 0.7 shard_map.149
  (17 shorter events, 0.2 us)
Async XLA Ops:
  2.3 9.2 %collective-permute-start = (f32[64,128]{1,0:T(8,128)S(1)}, f32[64,128]{1,0:T(8,128)S(1)}, u32[]{:S(2)}, u32[]{:S(2)}) collective-permute-start(f32[64,128]{1,0:T(8,128)S(1)} %get-tuple-element.35), channel_id=1, source_target_pairs={{0,4},{4,8},{8,12},{12,0},{1,5},{5,9},{9,13},{13,1},{2,6},{6,10},{... | collective-permute-start | bytes 98312 | tf_op jit(solution)/shard_map/ppermute | solution.py:422
  5.4 6.1 %collective-permute-start.1 = (f32[64,128]{1,0:T(8,128)S(1)}, f32[64,128]{1,0:T(8,128)S(1)}, u32[]{:S(2)}, u32[]{:S(2)}) collective-permute-start(f32[64,128]{1,0:T(8,128)S(1)} %get-tuple-element.36), channel_id=1, source_target_pairs={{0,12},{4,0},{8,4},{12,8},{1,13},{5,1},{9,5},{13,9},{2,14},{6,2},{... | collective-permute-start | bytes 98312 | tf_op jit(solution)/shard_map/ppermute | solution.py:422
  7.5 0.9 %copy-start = (bf16[256,256]{1,0:T(8,128)(2,1)S(1)}, bf16[256,256]{1,0:T(8,128)(2,1)}, u32[]{:S(2)}) copy-start(bf16[256,256]{1,0:T(8,128)(2,1)} %refs_8_.1) | copy-start | bytes 393220
  8.4 0.7 copy-start.2
  9.1 0.7 copy-start.3
  11.5 3.6 %copy-start.1 = (bf16[256,256]{1,0:T(8,128)(2,1)S(1)}, bf16[256,256]{1,0:T(8,128)(2,1)}, u32[]{:S(2)}) copy-start(bf16[256,256]{1,0:T(8,128)(2,1)} %refs_8_.1) | copy-start | bytes 393220
  11.6 3.5 %collective-permute-start.2 = (f32[23,4,128]{2,1,0:T(4,128)S(1)}, f32[23,4,128]{2,1,0:T(4,128)S(1)}, u32[]{:S(2)}, u32[]{:S(2)}) collective-permute-start(f32[23,4,128]{2,1,0:T(4,128)S(1)} %get-tuple-element.39), channel_id=1, source_target_pairs={{0,1},{1,2},{2,3},{3,0},{4,5},{5,6},{6,7},{7,4},{8,9},{9,10},{10,1... | collective-permute-start | bytes 141320 | tf_op jit(solution)/shard_map/ppermute | solution.py:422
  11.6 3.5 %collective-permute-start.3 = (f32[23,4,128]{2,1,0:T(4,128)S(1)}, f32[23,4,128]{2,1,0:T(4,128)S(1)}, u32[]{:S(2)}, u32[]{:S(2)}) collective-permute-start(f32[23,4,128]{2,1,0:T(4,128)S(1)} %get-tuple-element.40), channel_id=1, source_target_pairs={{0,3},{1,0},{2,1},{3,2},{4,7},{5,4},{6,5},{7,6},{8,11},{9,8},{10,9... | collective-permute-start | bytes 141320 | tf_op jit(solution)/shard_map/ppermute | solution.py:422
  35.8 2.8 %collective-permute-start.10 = (f32[144,128]{1,0:T(8,128)S(1)}, f32[144,128]{1,0:T(8,128)S(1)}, u32[]{:S(2)}, u32[]{:S(2)}) collective-permute-start(f32[144,128]{1,0:T(8,128)S(1)} %get-tuple-element.63), channel_id=1, source_target_pairs={{0,1},{1,0},{2,3},{3,2},{4,5},{5,4},{6,7},{7,6},{8,9},{9,8},{10,11... | collective-permute-start | bytes 221192 | tf_op jit(solution)/shard_map/ppermute | solution.py:426
  37.7 1.3 %collective-permute-start.4 = (f32[144,128]{1,0:T(8,128)S(1)}, f32[144,128]{1,0:T(8,128)S(1)}, u32[]{:S(2)}, u32[]{:S(2)}) collective-permute-start(f32[144,128]{1,0:T(8,128)S(1)} %get-tuple-element.64), channel_id=1, source_target_pairs={{0,1},{1,0},{2,3},{3,2},{4,5},{5,4},{6,7},{7,6},{8,9},{9,8},{10,11... | collective-permute-start | bytes 221192 | tf_op jit(solution)/shard_map/ppermute | solution.py:426
  39.0 4.0 %collective-permute-start.11 = (f32[72,128]{1,0:T(8,128)S(1)}, f32[72,128]{1,0:T(8,128)S(1)}, u32[]{:S(2)}, u32[]{:S(2)}) collective-permute-start(f32[72,128]{1,0:T(8,128)S(1)} %slice_select_fusion.2), channel_id=1, source_target_pairs={{0,2},{1,3},{2,0},{3,1},{4,6},{5,7},{6,4},{7,5},{8,10},{9,11},{10,... | collective-permute-start | bytes 110600 | tf_op jit(solution)/shard_map/ppermute | solution.py:426
  43.0 4.0 %collective-permute-start.12 = (f32[72,128]{1,0:T(8,128)S(1)}, f32[72,128]{1,0:T(8,128)S(1)}, u32[]{:S(2)}, u32[]{:S(2)}) collective-permute-start(f32[72,128]{1,0:T(8,128)S(1)} %select_add_fusion.2), channel_id=1, source_target_pairs={{0,4},{4,0},{8,12},{12,8},{1,5},{5,1},{9,13},{13,9},{2,6},{6,2},{1... | collective-permute-start | bytes 110600 | tf_op jit(solution)/shard_map/ppermute | solution.py:426
  47.1 4.9 %collective-permute-start.13 = (f32[72,128]{1,0:T(8,128)S(1)}, f32[72,128]{1,0:T(8,128)S(1)}, u32[]{:S(2)}, u32[]{:S(2)}) collective-permute-start(f32[72,128]{1,0:T(8,128)S(1)} %add.30), channel_id=1, source_target_pairs={{0,8},{4,12},{8,0},{12,4},{1,9},{5,13},{9,1},{13,5},{2,10},{6,14},... | collective-permute-start | bytes 110600 | tf_op jit(solution)/shard_map/ppermute | solution.py:426
  51.9 4.0 %collective-permute-start.14 = (f32[72,128]{1,0:T(8,128)S(1)}, f32[72,128]{1,0:T(8,128)S(1)}, u32[]{:S(2)}, u32[]{:S(2)}) collective-permute-start(f32[72,128]{1,0:T(8,128)S(1)} %add.31), channel_id=1, source_target_pairs={{0,2},{1,3},{2,0},{3,1},{4,6},{5,7},{6,4},{7,5},{8,10},{9,11},{10,... | collective-permute-start | bytes 110600 | tf_op jit(solution)/shard_map/ppermute | solution.py:426
  55.9 4.0 %collective-permute-start.5 = (f32[72,128]{1,0:T(8,128)S(1)}, f32[72,128]{1,0:T(8,128)S(1)}, u32[]{:S(2)}, u32[]{:S(2)}) collective-permute-start(f32[72,128]{1,0:T(8,128)S(1)} %get-tuple-element.77), channel_id=1, source_target_pairs={{0,2},{1,3},{2,0},{3,1},{4,6},{5,7},{6,4},{7,5},{8,10},{9,11},{10,... | collective-permute-start | bytes 110600 | tf_op jit(solution)/shard_map/ppermute | solution.py:426
  59.9 4.0 %collective-permute-start.6 = (f32[72,128]{1,0:T(8,128)S(1)}, f32[72,128]{1,0:T(8,128)S(1)}, u32[]{:S(2)}, u32[]{:S(2)}) collective-permute-start(f32[72,128]{1,0:T(8,128)S(1)} %select_add_fusion.3), channel_id=1, source_target_pairs={{0,4},{4,0},{8,12},{12,8},{1,5},{5,1},{9,13},{13,9},{2,6},{6,2},{1... | collective-permute-start | bytes 110600 | tf_op jit(solution)/shard_map/ppermute | solution.py:426
  64.0 4.9 %collective-permute-start.7 = (f32[72,128]{1,0:T(8,128)S(1)}, f32[72,128]{1,0:T(8,128)S(1)}, u32[]{:S(2)}, u32[]{:S(2)}) collective-permute-start(f32[72,128]{1,0:T(8,128)S(1)} %add.26), channel_id=1, source_target_pairs={{0,8},{4,12},{8,0},{12,4},{1,9},{5,13},{9,1},{13,5},{2,10},{6,14},... | collective-permute-start | bytes 110600 | tf_op jit(solution)/shard_map/ppermute | solution.py:426
  68.8 4.0 %collective-permute-start.8 = (f32[72,128]{1,0:T(8,128)S(1)}, f32[72,128]{1,0:T(8,128)S(1)}, u32[]{:S(2)}, u32[]{:S(2)}) collective-permute-start(f32[72,128]{1,0:T(8,128)S(1)} %add.27), channel_id=1, source_target_pairs={{0,2},{1,3},{2,0},{3,1},{4,6},{5,7},{6,4},{7,5},{8,10},{9,11},{10,... | collective-permute-start | bytes 110600 | tf_op jit(solution)/shard_map/ppermute | solution.py:426
  69.2 3.7 %collective-permute-start.15 = (f32[144,128]{1,0:T(8,128)S(1)}, f32[144,128]{1,0:T(8,128)S(1)}, u32[]{:S(2)}, u32[]{:S(2)}) collective-permute-start(f32[144,128]{1,0:T(8,128)S(1)} %pad_maximum_fusion.3), channel_id=1, source_target_pairs={{0,1},{1,0},{2,3},{3,2},{4,5},{5,4},{6,7},{7,6},{8,9},{9,8},{10,11... | collective-permute-start | bytes 221192 | tf_op jit(solution)/shard_map/ppermute | solution.py:426
  72.8 1.3 %collective-permute-start.9 = (f32[144,128]{1,0:T(8,128)S(1)}, f32[144,128]{1,0:T(8,128)S(1)}, u32[]{:S(2)}, u32[]{:S(2)}) collective-permute-start(f32[144,128]{1,0:T(8,128)S(1)} %pad_maximum_fusion.2), channel_id=1, source_target_pairs={{0,1},{1,0},{2,3},{3,2},{4,5},{5,4},{6,7},{7,6},{8,9},{9,8},{10,11... | collective-permute-start | bytes 221192 | tf_op jit(solution)/shard_map/ppermute | solution.py:426

commit v8 on v7

--- a/solution.py
+++ b/solution.py
@@ -15,7 +15,7 @@
 LANES = 128
 PART = 8
 EARLY = 2
-SHARES = 2
+SHARES = 1
 DEEP = 16
 SHALLOW = 8
 
@@ -274,7 +274,7 @@
             put_lanes(cl, SHALLOW, base, tiles, closure(low_second, wo_t))
         dz_one, dz_two, dfeat = yield from backward_stages(first, second, cot)
         if sums is not None:
-            add_terms(sums, (low_first, dz_two), (x, dz_one), (cot, low_second))
+            add_terms(sums, (low_first, dz_two), (x, dz_one), (low_second, cot))
         yield
         put_lanes(df, DEEP, base, tiles, dfeat)
 
@@ -286,7 +286,7 @@
         x = inputs_at(ft1, base, tiles)
         if counted is not None:
             dz_one, dz_two, cot = (jnp.where(counted, v.astype(F32), 0.0).astype(BF16) for v in (dz_one, dz_two, cot))
-        add_terms(sums, (first.astype(BF16), dz_two), (x, dz_one), (cot, second.astype(BF16)))
+        add_terms(sums, (first.astype(BF16), dz_two), (x, dz_one), (second.astype(BF16), cot))
         yield
         put_lanes(df, DEEP, base, tiles, dfeat)
 
@@ -391,10 +391,10 @@
         o_now[level] = planes[3 * levels + level, pl.ds(0, rows), pl.ds(0, LANES)] + grad[:rows, :LANES]
 
     start = 0
-    for acc in (acc_mid, acc_in, acc_out):
-        deep = acc.shape[0]
+    for total in (acc_mid[...], acc_in[...], acc_out[...].T):
+        deep = total.shape[0]
         for half in range(hidden // LANES):
-            o_grad[pl.ds(start, deep), :] = acc[:, half * LANES : (half + 1) * LANES]
+            o_grad[pl.ds(start, deep), :] = total[:, half * LANES : (half + 1) * LANES]
             start += deep
     if start < o_grad.shape[0]:
         o_grad[pl.ds(start, o_grad.shape[0] - start), :] = jnp.zeros((o_grad.shape[0] - start, LANES), F32)
@@ -534,7 +534,7 @@
             kept_halo,
             pltpu.VMEM((hidden, hidden), F32),
             pltpu.VMEM((DEEP, hidden), F32),
-            pltpu.VMEM((DEEP, hidden), F32),
+            pltpu.VMEM((hidden, DEEP), F32),
         ],
         compiler_params=pltpu.CompilerParams(vmem_limit_bytes=34 * 2**20),
     )(fields, left, right, low, high, wi, wi_t, wm_t, w_mid, wo, wo_t, *done)

time: 75.2 us -> 60.2 us (0.80)
  waiting for transfers between devices: 32.9 us -> 19.7 us
  starting transfers between devices: 12.3 us -> 10.7 us
    ppermute x12 -> x6, waiting for transfers between devices: 32.8 us -> 19.5 us  [swapped(): lax.ppermute(value, axis, [(i, i ^ bit) for i in range(lax.axis_size(axis...]
    ppermute x12 -> x6, starting transfers between devices: 5.34 us -> 3.71 us  [swapped(): lax.ppermute(value, axis, [(i, i ^ bit) for i in range(lax.axis_size(axis...]
  transfers between devices with their start and end apart: 16 -> 10, of which waited for: 12 -> 7; matrix products, arithmetic and copies ran while one was open for 0% -> 0% of each run, Pallas kernels for 4% -> 6%
where the time goes in v8:
time: 60.2 us; the launch traced here: 59.9 us
  Pallas kernels  26.4 us (44%)
  waiting for transfers between devices  19.7 us (33%)
  starting transfers between devices  10.7 us (18%)
  local copies, waits for them, and re-layouts  2.28 us (4%)
  between operations  0.74 us (1%)
    pallas_call x1, Pallas kernels, body(): pl.pallas_call(functools.partial(main_kernel, lax.axis_size('lat')), out_...  20.6 us
    ppermute x6, waiting for transfers between devices, swapped(): lax.ppermute(value, axis, [(i, i ^ bit) for i in range(lax.axis_size(axis...  19.5 us
    ppermute x4, starting transfers between devices, along(): lax.ppermute(value, axis, [(i, (i + step) % count) for i in range(count)])  6.96 us
    ppermute x6, starting transfers between devices, swapped(): lax.ppermute(value, axis, [(i, i ^ bit) for i in range(lax.axis_size(axis...  3.71 us
    pallas_call x2, Pallas kernels, early(): pl.pallas_call(functools.partial(early_kernel, k * tall), out_shape=(kept...  3.35 us
    unnamed x8, local copies, waits for them, and re-layouts  2.28 us
    pallas_call x1, Pallas kernels, body(): pl.pallas_call(pack_kernel, out_shape=(strip, strip, edge, edge, jax.Shap...  1.71 us
  transfers between devices with their start and end apart: 10, of which 7 were waited for; matrix products, arithmetic and copies ran while one was open for 0% of the time, Pallas kernels for 6%

profile of v8, /device:TPU:0, one launch (start us, length us, event | category | flops | bytes accessed | tf_op | source)
XLA Modules:
  0.0 59.9 jit_solution(10274275580239663989)
XLA Ops:
  0.6 1.7 %shard_map.144 = (f32[64,128]{1,0:T(8,128)S(1)}, f32[64,128]{1,0:T(8,128)S(1)}, f32[21,4,128]{2,1,0:T(4,128)S(1)}, f32[21,4,128]{2,1,0:T(4,128)S(1)}, f32[21,64,128]{2,1,0:T(8,128)S(1)}) custom-call(f32[4,64,128]{2,1,0:T(8,128)} %now.1, f32[4,64,128]{2,1,0:T(8,128)} %old.1, f32[4,64,128]{2,1,0:T(8,128)} %drift.1, f32[4,64,128]{2,1,0:T(8,128)} %cnew.1, ...), custom_call_target="tpu_custom_call" | custom-call | tf_op jit(solution)/shard_map/pallas_call | solution.py:464
  2.3 3.1 %collective-permute-start = (f32[64,128]{1,0:T(8,128)S(1)}, f32[64,128]{1,0:T(8,128)S(1)}, u32[]{:S(2)}, u32[]{:S(2)}) collective-permute-start(f32[64,128]{1,0:T(8,128)S(1)} %get-tuple-element.35), channel_id=1, source_target_pairs={{0,4},{4,8},{8,12},{12,0},{1,5},{5,9},{9,13},{13,1},{2,6},{6,10},{... | collective-permute-start | bytes 98312 | tf_op jit(solution)/shard_map/ppermute | solution.py:422
  5.4 2.1 %collective-permute-start.1 = (f32[64,128]{1,0:T(8,128)S(1)}, f32[64,128]{1,0:T(8,128)S(1)}, u32[]{:S(2)}, u32[]{:S(2)}) collective-permute-start(f32[64,128]{1,0:T(8,128)S(1)} %get-tuple-element.36), channel_id=1, source_target_pairs={{0,12},{4,0},{8,4},{12,8},{1,13},{5,1},{9,5},{13,9},{2,14},{6,2},{... | collective-permute-start | bytes 98312 | tf_op jit(solution)/shard_map/ppermute | solution.py:422
  7.5 0.0 copy-start
  7.5 0.9 %copy-done = bf16[256,256]{1,0:T(8,128)(2,1)S(1)} copy-done((bf16[256,256]{1,0:T(8,128)(2,1)S(1)}, bf16[256,256]{1,0:T(8,128)(2,1)}, u32[]{:S(2)}) %copy-start) | copy-done | bytes 131096
  8.4 0.0 copy-start.2
  8.4 0.7 %copy-done.2 = bf16[12,256]{1,0:T(8,128)(2,1)S(1)} copy-done((bf16[12,256]{1,0:T(8,128)(2,1)S(1)}, bf16[12,256]{1,0:T(8,128)(2,1)}, u32[]{:S(2)}) %copy-start.2) | copy-done | bytes 6168
  9.1 0.0 copy-start.3
  9.1 0.7 %copy-done.3 = bf16[256,4]{0,1:T(4,128)(2,1)S(1)} copy-done((bf16[256,4]{0,1:T(4,128)(2,1)S(1)}, bf16[256,4]{0,1:T(4,128)(2,1)}, u32[]{:S(2)}) %copy-start.3) | copy-done | bytes 2072
  9.8 1.7 %shard_map.146 = (f32[4,256,1024]{2,1,0:T(8,128)S(1)}, f32[4,256,1024]{2,1,0:T(8,128)S(1)}, f32[256,128]{1,0:T(8,128)S(1)}, bf16[16,256]{1,0:T(8,128)(2,1)S(1)},...) custom-call(f32[21,64,128]{2,1,0:T(8,128)S(1)} %get-tuple-element.34, ...), custom_call_target="tpu_custom_call" | custom-call | flops 1610612736 | tf_op jit(solution)/shard_map/pallas_call | solution.py:480
  11.5 0.0 copy-start.1
  11.5 0.0 collective-permute-done.left.refs_0_.refs_1_
  11.5 0.0 collective-permute-done.1.right.refs_2_
  11.6 0.1 collective-permute-start.2
  11.6 1.7 %collective-permute-start.3 = (f32[23,4,128]{2,1,0:T(4,128)S(1)}, f32[23,4,128]{2,1,0:T(4,128)S(1)}, u32[]{:S(2)}, u32[]{:S(2)}) collective-permute-start(f32[23,4,128]{2,1,0:T(4,128)S(1)} %get-tuple-element.40), channel_id=1, source_target_pairs={{0,3},{1,0},{2,1},{3,2},{4,7},{5,4},{6,5},{7,6},{8,11},{9,8},{10,9... | collective-permute-start | bytes 141320 | tf_op jit(solution)/shard_map/ppermute | solution.py:422
  13.4 1.6 %shard_map.147 = (f32[4,256,1024]{2,1,0:T(8,128)S(1)}, f32[4,256,1024]{2,1,0:T(8,128)S(1)}, f32[256,128]{1,0:T(8,128)S(1)}) custom-call(f32[21,64,128]{2,1,0:T(8,128)S(1)} %get-tuple-element.34.fields.refs_0_, f32[64,128]{1,0:T(8,128)S(1)} %collective-permute-done.left.refs_0_.refs_1_, bf16[256,16]{1,0:T(8,128)(2,1)S(1)} %get-tuple-element.42.refs_1_.refs_6_, ...), custom_call_target="tpu_custom_call" | custom-call | flops 1610612736 | tf_op jit(solution)/shard_map/pallas_call | solution.py:480
  15.0 0.1 collective-permute-done.2.refs_3_
  15.1 0.0 collective-permute-done.3.refs_4_
  15.1 0.0 copy-done.1
  15.1 20.6 %shard_map.148 = (f32[4,64,128]{2,1,0:T(8,128)}, f32[4,64,128]{2,1,0:T(8,128)}, f32[4,64,128]{2,1,0:T(8,128)}, f32[4,64,128]{2,1,0:T(8,128)}, f32[576,128]{1,0:T(8,128)S(1)}, /*index=5*/s32[8,128]{1,0:T(8,128)S(1)}) custom-call(f32[21,64,128]{2,1,0:T(8,128)S(1)} %get-tuple-element.34.fields.refs_0_, f32[64,128]{1,0:T(8,128)S(1)} %collective-permute-done.left.refs_0_.refs_1_, ...), custom_call_target="tpu_custom_call" | custom-call | tf_op jit(solution)/shard_map/pallas_call | solution.py:519
  35.7 1.8 %collective-permute-start.4 = (f32[288,128]{1,0:T(8,128)S(1)}, f32[288,128]{1,0:T(8,128)S(1)}, u32[]{:S(2)}, u32[]{:S(2)}) collective-permute-start(f32[288,128]{1,0:T(8,128)S(1)} %slice_select_fusion), channel_id=1, source_target_pairs={{0,1},{1,0},{2,3},{3,2},{4,5},{5,4},{6,7},{7,6},{8,9},{9,8},{10,11... | collective-permute-start | bytes 442376 | tf_op jit(solution)/shard_map/ppermute | solution.py:426
  37.6 1.0 %collective-permute-done.4 = f32[288,128]{1,0:T(8,128)S(1)} collective-permute-done((f32[288,128]{1,0:T(8,128)S(1)}, f32[288,128]{1,0:T(8,128)S(1)}, u32[]{:S(2)}, u32[]{:S(2)}) %collective-permute-start.4) | collective-permute-done | bytes 147488 | tf_op jit(solution)/shard_map/ppermute | solution.py:426
  38.6 0.4 collective-permute-start.5
  39.1 4.2 %collective-permute-done.5 = f32[144,128]{1,0:T(8,128)S(1)} collective-permute-done((f32[144,128]{1,0:T(8,128)S(1)}, f32[144,128]{1,0:T(8,128)S(1)}, u32[]{:S(2)}, u32[]{:S(2)}) %collective-permute-start.5) | collective-permute-done | bytes 73760 | tf_op jit(solution)/shard_map/ppermute | solution.py:426
  43.3 0.1 collective-permute-start.6
  43.3 4.3 %collective-permute-done.6 = f32[144,128]{1,0:T(8,128)S(1)} collective-permute-done((f32[144,128]{1,0:T(8,128)S(1)}, f32[144,128]{1,0:T(8,128)S(1)}, u32[]{:S(2)}, u32[]{:S(2)}) %collective-permute-start.6) | collective-permute-done | bytes 73760 | tf_op jit(solution)/shard_map/ppermute | solution.py:426
  47.7 0.8 %collective-permute-start.7 = (f32[144,128]{1,0:T(8,128)S(1)}, f32[144,128]{1,0:T(8,128)S(1)}, u32[]{:S(2)}, u32[]{:S(2)}) collective-permute-start(f32[144,128]{1,0:T(8,128)S(1)} %add.14), channel_id=1, source_target_pairs={{0,8},{4,12},{8,0},{12,4},{1,9},{5,13},{9,1},{13,5},{2,10},{6,14},... | collective-permute-start | bytes 221192 | tf_op jit(solution)/shard_map/ppermute | solution.py:426
  48.5 4.7 %collective-permute-done.7 = f32[144,128]{1,0:T(8,128)S(1)} collective-permute-done((f32[144,128]{1,0:T(8,128)S(1)}, f32[144,128]{1,0:T(8,128)S(1)}, u32[]{:S(2)}, u32[]{:S(2)}) %collective-permute-start.7) | collective-permute-done | bytes 73760 | tf_op jit(solution)/shard_map/ppermute | solution.py:426
  53.3 0.4 collective-permute-start.8
  53.7 4.0 %collective-permute-done.8 = f32[144,128]{1,0:T(8,128)S(1)} collective-permute-done((f32[144,128]{1,0:T(8,128)S(1)}, f32[144,128]{1,0:T(8,128)S(1)}, u32[]{:S(2)}, u32[]{:S(2)}) %collective-permute-start.8) | collective-permute-done | bytes 73760 | tf_op jit(solution)/shard_map/ppermute | solution.py:426
  57.7 0.1 collective-permute-start.9
  57.8 1.4 %collective-permute-done.9 = f32[288,128]{1,0:T(8,128)S(1)} collective-permute-done((f32[288,128]{1,0:T(8,128)S(1)}, f32[288,128]{1,0:T(8,128)S(1)}, u32[]{:S(2)}, u32[]{:S(2)}) %collective-permute-start.9) | collective-permute-done | bytes 147488 | tf_op jit(solution)/shard_map/ppermute | solution.py:426
  59.2 0.7 %shard_map.149 = (f32[12,256]{1,0:T(8,128)}, f32[256,256]{1,0:T(8,128)}, f32[4,256]{1,0:T(4,128)}) custom-call(f32[576,128]{1,0:T(8,128)S(1)} %pad_maximum_fusion.refs_0_), custom_call_target="tpu_custom_call" | custom-call | tf_op jit(solution)/shard_map/pallas_call | solution.py:544
  (12 shorter events, 0.2 us)
Async XLA Ops:
  2.3 9.2 %collective-permute-start = (f32[64,128]{1,0:T(8,128)S(1)}, f32[64,128]{1,0:T(8,128)S(1)}, u32[]{:S(2)}, u32[]{:S(2)}) collective-permute-start(f32[64,128]{1,0:T(8,128)S(1)} %get-tuple-element.35), channel_id=1, source_target_pairs={{0,4},{4,8},{8,12},{12,0},{1,5},{5,9},{9,13},{13,1},{2,6},{6,10},{... | collective-permute-start | bytes 98312 | tf_op jit(solution)/shard_map/ppermute | solution.py:422
  5.4 6.1 %collective-permute-start.1 = (f32[64,128]{1,0:T(8,128)S(1)}, f32[64,128]{1,0:T(8,128)S(1)}, u32[]{:S(2)}, u32[]{:S(2)}) collective-permute-start(f32[64,128]{1,0:T(8,128)S(1)} %get-tuple-element.36), channel_id=1, source_target_pairs={{0,12},{4,0},{8,4},{12,8},{1,13},{5,1},{9,5},{13,9},{2,14},{6,2},{... | collective-permute-start | bytes 98312 | tf_op jit(solution)/shard_map/ppermute | solution.py:422
  7.5 0.9 %copy-start = (bf16[256,256]{1,0:T(8,128)(2,1)S(1)}, bf16[256,256]{1,0:T(8,128)(2,1)}, u32[]{:S(2)}) copy-start(bf16[256,256]{1,0:T(8,128)(2,1)} %refs_8_.1) | copy-start | bytes 393220
  8.4 0.7 %copy-start.2 = (bf16[12,256]{1,0:T(8,128)(2,1)S(1)}, bf16[12,256]{1,0:T(8,128)(2,1)}, u32[]{:S(2)}) copy-start(bf16[12,256]{1,0:T(8,128)(2,1)} %refs_0_.1) | copy-start | bytes 18436
  9.1 0.7 %copy-start.3 = (bf16[256,4]{0,1:T(4,128)(2,1)S(1)}, bf16[256,4]{0,1:T(4,128)(2,1)}, u32[]{:S(2)}) copy-start(bf16[256,4]{0,1:T(4,128)(2,1)} %param.15) | copy-start | bytes 6148
  11.5 3.6 %copy-start.1 = (bf16[256,256]{1,0:T(8,128)(2,1)S(1)}, bf16[256,256]{1,0:T(8,128)(2,1)}, u32[]{:S(2)}) copy-start(bf16[256,256]{1,0:T(8,128)(2,1)} %refs_8_.1) | copy-start | bytes 393220
  11.6 3.5 %collective-permute-start.2 = (f32[23,4,128]{2,1,0:T(4,128)S(1)}, f32[23,4,128]{2,1,0:T(4,128)S(1)}, u32[]{:S(2)}, u32[]{:S(2)}) collective-permute-start(f32[23,4,128]{2,1,0:T(4,128)S(1)} %get-tuple-element.39), channel_id=1, source_target_pairs={{0,1},{1,2},{2,3},{3,0},{4,5},{5,6},{6,7},{7,4},{8,9},{9,10},{10,1... | collective-permute-start | bytes 141320 | tf_op jit(solution)/shard_map/ppermute | solution.py:422
  11.6 3.5 %collective-permute-start.3 = (f32[23,4,128]{2,1,0:T(4,128)S(1)}, f32[23,4,128]{2,1,0:T(4,128)S(1)}, u32[]{:S(2)}, u32[]{:S(2)}) collective-permute-start(f32[23,4,128]{2,1,0:T(4,128)S(1)} %get-tuple-element.40), channel_id=1, source_target_pairs={{0,3},{1,0},{2,1},{3,2},{4,7},{5,4},{6,5},{7,6},{8,11},{9,8},{10,9... | collective-permute-start | bytes 141320 | tf_op jit(solution)/shard_map/ppermute | solution.py:422
  35.7 2.8 %collective-permute-start.4 = (f32[288,128]{1,0:T(8,128)S(1)}, f32[288,128]{1,0:T(8,128)S(1)}, u32[]{:S(2)}, u32[]{:S(2)}) collective-permute-start(f32[288,128]{1,0:T(8,128)S(1)} %slice_select_fusion), channel_id=1, source_target_pairs={{0,1},{1,0},{2,3},{3,2},{4,5},{5,4},{6,7},{7,6},{8,9},{9,8},{10,11... | collective-permute-start | bytes 442376 | tf_op jit(solution)/shard_map/ppermute | solution.py:426
  38.6 4.6 %collective-permute-start.5 = (f32[144,128]{1,0:T(8,128)S(1)}, f32[144,128]{1,0:T(8,128)S(1)}, u32[]{:S(2)}, u32[]{:S(2)}) collective-permute-start(f32[144,128]{1,0:T(8,128)S(1)} %slice_select_fusion.1), channel_id=1, source_target_pairs={{0,2},{1,3},{2,0},{3,1},{4,6},{5,7},{6,4},{7,5},{8,10},{9,11},{10,... | collective-permute-start | bytes 221192 | tf_op jit(solution)/shard_map/ppermute | solution.py:426
  43.3 4.4 %collective-permute-start.6 = (f32[144,128]{1,0:T(8,128)S(1)}, f32[144,128]{1,0:T(8,128)S(1)}, u32[]{:S(2)}, u32[]{:S(2)}) collective-permute-start(f32[144,128]{1,0:T(8,128)S(1)} %select_add_fusion.1), channel_id=1, source_target_pairs={{0,4},{4,0},{8,12},{12,8},{1,5},{5,1},{9,13},{13,9},{2,6},{6,2},{1... | collective-permute-start | bytes 221192 | tf_op jit(solution)/shard_map/ppermute | solution.py:426
  47.7 5.5 %collective-permute-start.7 = (f32[144,128]{1,0:T(8,128)S(1)}, f32[144,128]{1,0:T(8,128)S(1)}, u32[]{:S(2)}, u32[]{:S(2)}) collective-permute-start(f32[144,128]{1,0:T(8,128)S(1)} %add.14), channel_id=1, source_target_pairs={{0,8},{4,12},{8,0},{12,4},{1,9},{5,13},{9,1},{13,5},{2,10},{6,14},... | collective-permute-start | bytes 221192 | tf_op jit(solution)/shard_map/ppermute | solution.py:426
  53.3 4.4 %collective-permute-start.8 = (f32[144,128]{1,0:T(8,128)S(1)}, f32[144,128]{1,0:T(8,128)S(1)}, u32[]{:S(2)}, u32[]{:S(2)}) collective-permute-start(f32[144,128]{1,0:T(8,128)S(1)} %add.15), channel_id=1, source_target_pairs={{0,2},{1,3},{2,0},{3,1},{4,6},{5,7},{6,4},{7,5},{8,10},{9,11},{10,... | collective-permute-start | bytes 221192 | tf_op jit(solution)/shard_map/ppermute | solution.py:426
  57.7 1.4 %collective-permute-start.9 = (f32[288,128]{1,0:T(8,128)S(1)}, f32[288,128]{1,0:T(8,128)S(1)}, u32[]{:S(2)}, u32[]{:S(2)}) collective-permute-start(f32[288,128]{1,0:T(8,128)S(1)} %pad_maximum_fusion.1), channel_id=1, source_target_pairs={{0,1},{1,0},{2,3},{3,2},{4,5},{5,4},{6,7},{7,6},{8,9},{9,8},{10,11... | collective-permute-start | bytes 442376 | tf_op jit(solution)/shard_map/ppermute | solution.py:426

commit v9 on v8

--- a/solution.py
+++ b/solution.py
@@ -31,13 +31,18 @@
     return lax.dot_general(left, right, (((1,), (1,)), ((), ())), preferred_element_type=F32)
 
 
-def pack_kernel(now, old, drift, cnew, cmid, ocean, west, east, top, bottom, fields, wet, sems):
+def pack_kernel(
+    now, old, drift, cnew, cmid, ocean, w_in, w_mid, w_out,
+    west, east, top, bottom, fields, v_in, v_mid, v_out, wet, sems,
+):
     levels, rows, cols = now.shape
     copies = [
         pltpu.make_async_copy(ref, fields.at[pl.ds(levels * f, levels)], sems.at[f])
         for f, ref in enumerate((now, old, drift, cnew, cmid))
     ]
     copies.append(pltpu.make_async_copy(ocean, wet, sems.at[5]))
+    for k, pair in enumerate(((w_in, v_in), (w_mid, v_mid), (w_out, v_out))):
+        copies.append(pltpu.make_async_copy(*pair, sems.at[6 + k]))
     for copy in copies:
         copy.start()
     lane = lax.broadcasted_iota(jnp.int32, (rows, LANES), 1)
@@ -57,6 +62,8 @@
         bottom[p] = plane[rows - WIDE :]
     west[...] = to_west
     east[...] = to_east
+    for copy in copies[6:]:
+        copy.wait()
 
 
 def join_kernel(top, bottom, left, right, up, down):
@@ -161,10 +168,17 @@
     staggered(part(k * PART, keep1.at[k], keep2.at[k]) for k in range(tall // PART))
 
 
+def copied_out(pairs, sems):
+    copies = [pltpu.make_async_copy(*pair, sems.at[k]) for k, pair in enumerate(pairs)]
+    for copy in copies:
+        copy.start()
+    return copies
+
+
 def main_kernel(bands, *refs):
     fields, left, right, low, high, wi, wi_t, wm_t, w_mid, wo, wo_t, *refs = refs
     early, refs = refs[: 3 * EARLY], refs[3 * EARLY :]
-    o_mid, o_new, o_old, o_now, o_grad, o_place, planes, mids, olds, *refs = refs
+    h_mid, h_new, h_old, h_now, o_grad, o_place, o_mid, o_new, o_old, o_now, sems, planes, mids, olds, *refs = refs
     ft1, ft2, fth, ftx, cl, clh, clx, dc, dch, dcx, df, dfh, dfx, halo1, halo2, acc_mid, acc_in, acc_out = refs
     levels, rows, cols = o_mid.shape
     hidden = w_mid.shape[0]
@@ -330,6 +344,7 @@
         mid = planes[levels + level] + 2.0 * DT * force(planes[level], level, closed)
         o_mid[level] = mid[:rows, :LANES]
         mids[level] = mid
+    copies = copied_out([(o_mid, h_mid)], sems.at[pl.ds(0, 1)])
 
     features_of(mids, ft2, outer, False)
     for level in range(levels):
@@ -361,6 +376,7 @@
         grad = planes[4 * levels + level] + adjoint_of(2.0 * DT * planes[3 * levels + level], level, False)
         o_old[level] = grad[:rows, :LANES]
         olds[level] = grad
+    copies += copied_out([(o_new, h_new), (o_old, h_old)], sems.at[pl.ds(1, 2)])
 
     row = lax.broadcasted_iota(jnp.int32, (ext, LANES), 0)
     inside = (lane > 0) & (lane < LANES - 1) & (row > 0) & (row < rows - 1)
@@ -389,6 +405,7 @@
     for level in range(levels):
         grad = adjoint_of(2.0 * DT * olds[level], level, True)
         o_now[level] = planes[3 * levels + level, pl.ds(0, rows), pl.ds(0, LANES)] + grad[:rows, :LANES]
+    copies += copied_out([(o_now, h_now)], sems.at[pl.ds(3, 1)])
 
     start = 0
     for total in (acc_mid[...], acc_in[...], acc_out[...].T):
@@ -398,6 +415,8 @@
             start += deep
     if start < o_grad.shape[0]:
         o_grad[pl.ds(start, o_grad.shape[0] - start), :] = jnp.zeros((o_grad.shape[0] - start, LANES), F32)
+    for copy in copies:
+        copy.wait()
 
 
 def scale_kernel(factor, *refs):
@@ -439,8 +458,13 @@
     bit = 1
     while bit < lax.axis_size(doubling):
         got = [swapped(v, doubling, bit) for v in values]
-        values = [v + g for v, g in zip(values, got)]
-        bit *= 2
+        if 2 * bit < lax.axis_size(doubling):
+            far = [(swapped(v, doubling, 2 * bit), swapped(v, doubling, 3 * bit)) for v in values]
+            values = [(v + g) + (a + b) for v, g, (a, b) in zip(values, got, far)]
+            bit *= 4
+        else:
+            values = [v + g for v, g in zip(values, got)]
+            bit *= 2
     for bit, upper in reversed(bits):
         got = [swapped(v, halving, bit) for v in values]
         values = [
@@ -458,15 +482,17 @@
     slots = rows + 8 + packs
     tall = rows // EARLY
     vmem = pl.BlockSpec(memory_space=pltpu.VMEM)
+    hbm = pl.BlockSpec(memory_space=pltpu.HBM)
     strip = jax.ShapeDtypeStruct((rows, LANES), F32)
     edge = jax.ShapeDtypeStruct((count, WIDE, LANES), F32)
-    arrays = (state_now, state_old, drift, cot_new, cot_mid, ocean)
-    west, east, top, bottom, fields = pl.pallas_call(
+    arrays = (state_now, state_old, drift, cot_new, cot_mid, ocean, w_in, w_mid, w_out.T)
+    weights = tuple(jax.ShapeDtypeStruct(a.shape, a.dtype) for a in arrays[6:])
+    west, east, top, bottom, fields, *weights = pl.pallas_call(
         pack_kernel,
-        out_shape=(strip, strip, edge, edge, jax.ShapeDtypeStruct((count, rows, cols), F32)),
-        in_specs=[pl.BlockSpec(memory_space=pltpu.HBM)] * 6,
-        out_specs=(vmem,) * 5,
-        scratch_shapes=[pltpu.VMEM((rows, cols), jnp.int32), pltpu.SemaphoreType.DMA((6,))],
+        out_shape=(strip, strip, edge, edge, jax.ShapeDtypeStruct((count, rows, cols), F32)) + weights,
+        in_specs=[hbm] * 9,
+        out_specs=(vmem,) * 8,
+        scratch_shapes=[pltpu.VMEM((rows, cols), jnp.int32), pltpu.SemaphoreType.DMA((9,))],
         compiler_params=pltpu.CompilerParams(vmem_limit_bytes=8 * 2**20),
     )(*(pltpu.with_memory_space_constraint(a, pltpu.HBM) for a in arrays))
 
@@ -491,7 +517,7 @@
 
     left = along(east, "lon", 1)
     right = along(west, "lon", -1)
-    *first_kept, wi, wi_t, wm_t, wo, wo_t = early(0, (w_in, w_mid, w_out.T), prepared)
+    *first_kept, wi, wi_t, wm_t, wo, wo_t = early(0, tuple(weights), prepared)
     message = jax.ShapeDtypeStruct((count + 2, WIDE, LANES), F32)
     up, down = pl.pallas_call(
         join_kernel,
@@ -520,8 +546,10 @@
         functools.partial(main_kernel, lax.axis_size("lat")),
         out_shape=(field, field, field, field, jax.ShapeDtypeStruct((terms_rows, LANES), F32), jax.ShapeDtypeStruct((8, LANES), jnp.int32)),
         in_specs=[vmem] * (11 + 3 * EARLY),
-        out_specs=(vmem,) * 6,
+        out_specs=(hbm,) * 4 + (vmem,) * 2,
         scratch_shapes=[
+            *[pltpu.VMEM((levels, rows, cols), F32)] * 4,
+            pltpu.SemaphoreType.DMA((4,)),
             pltpu.VMEM((count, ext, 2 * LANES), F32),
             ext_planes,
             ext_planes,
@@ -537,7 +565,7 @@
             pltpu.VMEM((hidden, DEEP), F32),
         ],
         compiler_params=pltpu.CompilerParams(vmem_limit_bytes=34 * 2**20),
-    )(fields, left, right, low, high, wi, wi_t, wm_t, w_mid, wo, wo_t, *done)
+    )(fields, left, right, low, high, wi, wi_t, wm_t, weights[1], wo, wo_t, *done)
 
     summed = summed_over(jnp.split(terms, SHARES), place[:1], "lat", "lon")
     cells_all = rows * lax.axis_size("lat") * cols * lax.axis_size("lon")

time: 60.2 us -> 57.6 us (0.957)
  waiting for transfers between devices: 19.7 us -> 16.1 us
  starting transfers between devices: 10.7 us -> 14.2 us
  local copies, waits for them, and re-layouts: 2.28 us -> 0 us
    ppermute x6 -> x7, waiting for transfers between devices: 19.5 us -> 15.6 us  [swapped(): lax.ppermute(value, axis, [(i, i ^ bit) for i in range(lax.axis_size(axis...]
    ppermute x6 -> x7, starting transfers between devices: 3.71 us -> 7.25 us  [swapped(): lax.ppermute(value, axis, [(i, i ^ bit) for i in range(lax.axis_size(axis...]
    unnamed x8 -> x0, local copies, waits for them, and re-layouts: 2.28 us -> none
  transfers between devices with their start and end apart: 10 -> 11, of which waited for: 7 -> 9; matrix products, arithmetic and copies ran while one was open for 0% -> 0% of each run, Pallas kernels for 6% -> 6%
where the time goes in v9:
time: 57.6 us; the launch traced here: 57.5 us
  Pallas kernels  26.2 us (45%)
  waiting for transfers between devices  16.1 us (28%)
  starting transfers between devices  14.2 us (25%)
  between operations  0.73 us (1%)
    pallas_call x1, Pallas kernels, body(): pl.pallas_call(functools.partial(main_kernel, lax.axis_size('lat')), out_...  20.4 us
    ppermute x7, waiting for transfers between devices, swapped(): lax.ppermute(value, axis, [(i, i ^ bit) for i in range(lax.axis_size(axis...  15.6 us
    ppermute x7, starting transfers between devices, swapped(): lax.ppermute(value, axis, [(i, i ^ bit) for i in range(lax.axis_size(axis...  7.25 us
    ppermute x4, starting transfers between devices, along(): lax.ppermute(value, axis, [(i, (i + step) % count) for i in range(count)])  6.96 us
    pallas_call x2, Pallas kernels, early(): pl.pallas_call(functools.partial(early_kernel, k * tall), out_shape=(kept...  3.36 us
    pallas_call x1, Pallas kernels, body(): pl.pallas_call(pack_kernel, out_shape=(strip, strip, edge, edge, jax.Shap...  1.74 us
  transfers between devices with their start and end apart: 11, of which 9 were waited for; matrix products, arithmetic and copies ran while one was open for 0% of the time, Pallas kernels for 6%

profile of v9, /device:TPU:0, one launch (start us, length us, event | category | flops | bytes accessed | tf_op | source)
XLA Modules:
  0.0 57.5 jit_solution(10305471481400146363)
XLA Ops:
  0.6 1.7 %shard_map.144 = (f32[64,128]{1,0:T(8,128)S(1)}, f32[64,128]{1,0:T(8,128)S(1)}, f32[21,4,128]{2,1,0:T(4,128)S(1)}, f32[21,4,128]{2,1,0:T(4,128)S(1)}, f32[21,64,...) custom-call(f32[4,64,128]{2,1,0:T(8,128)} %now.1, ...), custom_call_target="tpu_custom_call" | custom-call | tf_op jit(solution)/shard_map/pallas_call | solution.py:490
  2.4 3.1 %collective-permute-start = (f32[64,128]{1,0:T(8,128)S(1)}, f32[64,128]{1,0:T(8,128)S(1)}, u32[]{:S(2)}, u32[]{:S(2)}) collective-permute-start(f32[64,128]{1,0:T(8,128)S(1)} %get-tuple-element.38), channel_id=1, source_target_pairs={{0,4},{4,8},{8,12},{12,0},{1,5},{5,9},{9,13},{13,1},{2,6},{6,10},{... | collective-permute-start | bytes 98312 | tf_op jit(solution)/shard_map/ppermute | solution.py:441
  5.5 2.1 %collective-permute-start.1 = (f32[64,128]{1,0:T(8,128)S(1)}, f32[64,128]{1,0:T(8,128)S(1)}, u32[]{:S(2)}, u32[]{:S(2)}) collective-permute-start(f32[64,128]{1,0:T(8,128)S(1)} %get-tuple-element.39), channel_id=1, source_target_pairs={{0,12},{4,0},{8,4},{12,8},{1,13},{5,1},{9,5},{13,9},{2,14},{6,2},{... | collective-permute-start | bytes 98312 | tf_op jit(solution)/shard_map/ppermute | solution.py:441
  7.6 1.7 %shard_map.146 = (f32[4,256,1024]{2,1,0:T(8,128)S(1)}, f32[4,256,1024]{2,1,0:T(8,128)S(1)}, f32[256,128]{1,0:T(8,128)S(1)}, bf16[16,256]{1,0:T(8,128)(2,1)S(1)},...) custom-call(f32[21,64,128]{2,1,0:T(8,128)S(1)} %get-tuple-element.37, ...), custom_call_target="tpu_custom_call" | custom-call | flops 1610612736 | tf_op jit(solution)/shard_map/pallas_call | solution.py:506
  9.3 0.2 collective-permute-done.left.refs_0_.refs_1_
  9.5 0.2 collective-permute-done.1.right.refs_2_
  9.7 0.1 collective-permute-start.2
  9.8 1.7 %collective-permute-start.3 = (f32[23,4,128]{2,1,0:T(4,128)S(1)}, f32[23,4,128]{2,1,0:T(4,128)S(1)}, u32[]{:S(2)}, u32[]{:S(2)}) collective-permute-start(f32[23,4,128]{2,1,0:T(4,128)S(1)} %get-tuple-element.43), channel_id=1, source_target_pairs={{0,3},{1,0},{2,1},{3,2},{4,7},{5,4},{6,5},{7,6},{8,11},{9,8},{10,9... | collective-permute-start | bytes 141320 | tf_op jit(solution)/shard_map/ppermute | solution.py:441
  11.5 1.6 %shard_map.147 = (f32[4,256,1024]{2,1,0:T(8,128)S(1)}, f32[4,256,1024]{2,1,0:T(8,128)S(1)}, f32[256,128]{1,0:T(8,128)S(1)}) custom-call(f32[21,64,128]{2,1,0:T(8,128)S(1)} %get-tuple-element.37.fields.refs_0_, f32[64,128]{1,0:T(8,128)S(1)} %collective-permute-done.left.refs_0_.refs_1_, bf16[256,16]{1,0:T(8,128)(2,1)S(1)} %get-tuple-element.48.refs_1_.refs_6_, ...), custom_call_target="tpu_custom_call" | custom-call | flops 1610612736 | tf_op jit(solution)/shard_map/pallas_call | solution.py:506
  13.2 0.1 collective-permute-done.2.refs_3_
  13.3 0.0 collective-permute-done.3.refs_4_
  13.3 20.4 %shard_map.148 = (f32[4,64,128]{2,1,0:T(8,128)}, f32[4,64,128]{2,1,0:T(8,128)}, f32[4,64,128]{2,1,0:T(8,128)}, f32[4,64,128]{2,1,0:T(8,128)}, f32[576,128]{1,0:T(8,128)S(1)}, /*index=5*/s32[8,128]{1,0:T(8,128)S(1)}) custom-call(f32[21,64,128]{2,1,0:T(8,128)S(1)} %get-tuple-element.37.fields.refs_0_, f32[64,128]{1,0:T(8,128)S(1)} %collective-permute-done.left.refs_0_.refs_1_, ...), custom_call_target="tpu_custom_call" | custom-call | tf_op jit(solution)/shard_map/pallas_call | solution.py:545
  33.7 1.7 %collective-permute-start.4 = (f32[288,128]{1,0:T(8,128)S(1)}, f32[288,128]{1,0:T(8,128)S(1)}, u32[]{:S(2)}, u32[]{:S(2)}) collective-permute-start(f32[288,128]{1,0:T(8,128)S(1)} %slice_select_fusion), channel_id=1, source_target_pairs={{0,1},{1,0},{2,3},{3,2},{4,5},{5,4},{6,7},{7,6},{8,9},{9,8},{10,11... | collective-permute-start | bytes 442376 | tf_op jit(solution)/shard_map/ppermute | solution.py:445
  35.4 1.0 %collective-permute-done.4 = f32[288,128]{1,0:T(8,128)S(1)} collective-permute-done((f32[288,128]{1,0:T(8,128)S(1)}, f32[288,128]{1,0:T(8,128)S(1)}, u32[]{:S(2)}, u32[]{:S(2)}) %collective-permute-start.4) | collective-permute-done | bytes 147488 | tf_op jit(solution)/shard_map/ppermute | solution.py:445
  36.4 0.6 %collective-permute-start.5 = (f32[144,128]{1,0:T(8,128)S(1)}, f32[144,128]{1,0:T(8,128)S(1)}, u32[]{:S(2)}, u32[]{:S(2)}) collective-permute-start(f32[144,128]{1,0:T(8,128)S(1)} %slice_select_fusion.1), channel_id=1, source_target_pairs={{0,2},{1,3},{2,0},{3,1},{4,6},{5,7},{6,4},{7,5},{8,10},{9,11},{10,... | collective-permute-start | bytes 221192 | tf_op jit(solution)/shard_map/ppermute | solution.py:445
  37.0 4.0 %collective-permute-done.5 = f32[144,128]{1,0:T(8,128)S(1)} collective-permute-done((f32[144,128]{1,0:T(8,128)S(1)}, f32[144,128]{1,0:T(8,128)S(1)}, u32[]{:S(2)}, u32[]{:S(2)}) %collective-permute-start.5) | collective-permute-done | bytes 73760 | tf_op jit(solution)/shard_map/ppermute | solution.py:445
  41.1 3.8 %collective-permute-start.8 = (f32[144,128]{1,0:T(8,128)S(1)}, f32[144,128]{1,0:T(8,128)S(1)}, u32[]{:S(2)}, u32[]{:S(2)}) collective-permute-start(f32[144,128]{1,0:T(8,128)S(1)} %select_add_fusion.1), channel_id=1, source_target_pairs={{0,12},{4,8},{8,4},{12,0},{1,13},{5,9},{9,5},{13,1},{2,14},{6,10},... | collective-permute-start | bytes 221192 | tf_op jit(solution)/shard_map/ppermute | solution.py:445
  44.8 0.0 collective-permute-start.7
  44.8 0.7 %collective-permute-start.6 = (f32[144,128]{1,0:T(8,128)S(1)}, f32[144,128]{1,0:T(8,128)S(1)}, u32[]{:S(2)}, u32[]{:S(2)}) collective-permute-start(f32[144,128]{1,0:T(8,128)S(1)} %select_add_fusion.1), channel_id=1, source_target_pairs={{0,4},{4,0},{8,12},{12,8},{1,5},{5,1},{9,13},{13,9},{2,6},{6,2},{1... | collective-permute-start | bytes 221192 | tf_op jit(solution)/shard_map/ppermute | solution.py:445
  45.5 2.3 %collective-permute-done.8 = f32[144,128]{1,0:T(8,128)S(1)} collective-permute-done((f32[144,128]{1,0:T(8,128)S(1)}, f32[144,128]{1,0:T(8,128)S(1)}, u32[]{:S(2)}, u32[]{:S(2)}) %collective-permute-start.8) | collective-permute-done | bytes 73760 | tf_op jit(solution)/shard_map/ppermute | solution.py:445
  47.8 2.9 %collective-permute-done.7 = f32[144,128]{1,0:T(8,128)S(1)} collective-permute-done((f32[144,128]{1,0:T(8,128)S(1)}, f32[144,128]{1,0:T(8,128)S(1)}, u32[]{:S(2)}, u32[]{:S(2)}) %collective-permute-start.7) | collective-permute-done | bytes 73760 | tf_op jit(solution)/shard_map/ppermute | solution.py:445
  50.7 0.0 collective-permute-done.6
  50.8 0.4 collective-permute-start.9
  51.2 4.0 %collective-permute-done.9 = f32[144,128]{1,0:T(8,128)S(1)} collective-permute-done((f32[144,128]{1,0:T(8,128)S(1)}, f32[144,128]{1,0:T(8,128)S(1)}, u32[]{:S(2)}, u32[]{:S(2)}) %collective-permute-start.9) | collective-permute-done | bytes 73760 | tf_op jit(solution)/shard_map/ppermute | solution.py:445
  55.2 0.1 collective-permute-start.10
  55.3 1.4 %collective-permute-done.10 = f32[288,128]{1,0:T(8,128)S(1)} collective-permute-done((f32[288,128]{1,0:T(8,128)S(1)}, f32[288,128]{1,0:T(8,128)S(1)}, u32[]{:S(2)}, u32[]{:S(2)}) %collective-permute-start.10) | collective-permute-done | bytes 147488 | tf_op jit(solution)/shard_map/ppermute | solution.py:445
  56.7 0.7 %shard_map.149 = (f32[12,256]{1,0:T(8,128)}, f32[256,256]{1,0:T(8,128)}, f32[4,256]{1,0:T(4,128)}) custom-call(f32[576,128]{1,0:T(8,128)S(1)} %pad_maximum_fusion.refs_0_), custom_call_target="tpu_custom_call" | custom-call | tf_op jit(solution)/shard_map/pallas_call | solution.py:572
  (11 shorter events, 0.2 us)
Async XLA Ops:
  2.4 7.1 %collective-permute-start = (f32[64,128]{1,0:T(8,128)S(1)}, f32[64,128]{1,0:T(8,128)S(1)}, u32[]{:S(2)}, u32[]{:S(2)}) collective-permute-start(f32[64,128]{1,0:T(8,128)S(1)} %get-tuple-element.38), channel_id=1, source_target_pairs={{0,4},{4,8},{8,12},{12,0},{1,5},{5,9},{9,13},{13,1},{2,6},{6,10},{... | collective-permute-start | bytes 98312 | tf_op jit(solution)/shard_map/ppermute | solution.py:441
  5.5 4.3 %collective-permute-start.1 = (f32[64,128]{1,0:T(8,128)S(1)}, f32[64,128]{1,0:T(8,128)S(1)}, u32[]{:S(2)}, u32[]{:S(2)}) collective-permute-start(f32[64,128]{1,0:T(8,128)S(1)} %get-tuple-element.39), channel_id=1, source_target_pairs={{0,12},{4,0},{8,4},{12,8},{1,13},{5,1},{9,5},{13,9},{2,14},{6,2},{... | collective-permute-start | bytes 98312 | tf_op jit(solution)/shard_map/ppermute | solution.py:441
  9.7 3.5 %collective-permute-start.2 = (f32[23,4,128]{2,1,0:T(4,128)S(1)}, f32[23,4,128]{2,1,0:T(4,128)S(1)}, u32[]{:S(2)}, u32[]{:S(2)}) collective-permute-start(f32[23,4,128]{2,1,0:T(4,128)S(1)} %get-tuple-element.42), channel_id=1, source_target_pairs={{0,1},{1,2},{2,3},{3,0},{4,5},{5,6},{6,7},{7,4},{8,9},{9,10},{10,1... | collective-permute-start | bytes 141320 | tf_op jit(solution)/shard_map/ppermute | solution.py:441
  9.8 3.5 %collective-permute-start.3 = (f32[23,4,128]{2,1,0:T(4,128)S(1)}, f32[23,4,128]{2,1,0:T(4,128)S(1)}, u32[]{:S(2)}, u32[]{:S(2)}) collective-permute-start(f32[23,4,128]{2,1,0:T(4,128)S(1)} %get-tuple-element.43), channel_id=1, source_target_pairs={{0,3},{1,0},{2,1},{3,2},{4,7},{5,4},{6,5},{7,6},{8,11},{9,8},{10,9... | collective-permute-start | bytes 141320 | tf_op jit(solution)/shard_map/ppermute | solution.py:441
  33.7 2.7 %collective-permute-start.4 = (f32[288,128]{1,0:T(8,128)S(1)}, f32[288,128]{1,0:T(8,128)S(1)}, u32[]{:S(2)}, u32[]{:S(2)}) collective-permute-start(f32[288,128]{1,0:T(8,128)S(1)} %slice_select_fusion), channel_id=1, source_target_pairs={{0,1},{1,0},{2,3},{3,2},{4,5},{5,4},{6,7},{7,6},{8,9},{9,8},{10,11... | collective-permute-start | bytes 442376 | tf_op jit(solution)/shard_map/ppermute | solution.py:445
  36.4 4.6 %collective-permute-start.5 = (f32[144,128]{1,0:T(8,128)S(1)}, f32[144,128]{1,0:T(8,128)S(1)}, u32[]{:S(2)}, u32[]{:S(2)}) collective-permute-start(f32[144,128]{1,0:T(8,128)S(1)} %slice_select_fusion.1), channel_id=1, source_target_pairs={{0,2},{1,3},{2,0},{3,1},{4,6},{5,7},{6,4},{7,5},{8,10},{9,11},{10,... | collective-permute-start | bytes 221192 | tf_op jit(solution)/shard_map/ppermute | solution.py:445
  41.1 6.8 %collective-permute-start.8 = (f32[144,128]{1,0:T(8,128)S(1)}, f32[144,128]{1,0:T(8,128)S(1)}, u32[]{:S(2)}, u32[]{:S(2)}) collective-permute-start(f32[144,128]{1,0:T(8,128)S(1)} %select_add_fusion.1), channel_id=1, source_target_pairs={{0,12},{4,8},{8,4},{12,0},{1,13},{5,9},{9,5},{13,1},{2,14},{6,10},... | collective-permute-start | bytes 221192 | tf_op jit(solution)/shard_map/ppermute | solution.py:445
  44.8 5.9 %collective-permute-start.7 = (f32[144,128]{1,0:T(8,128)S(1)}, f32[144,128]{1,0:T(8,128)S(1)}, u32[]{:S(2)}, u32[]{:S(2)}) collective-permute-start(f32[144,128]{1,0:T(8,128)S(1)} %select_add_fusion.1), channel_id=1, source_target_pairs={{0,8},{4,12},{8,0},{12,4},{1,9},{5,13},{9,1},{13,5},{2,10},{6,14},... | collective-permute-start | bytes 221192 | tf_op jit(solution)/shard_map/ppermute | solution.py:445
  44.8 5.9 %collective-permute-start.6 = (f32[144,128]{1,0:T(8,128)S(1)}, f32[144,128]{1,0:T(8,128)S(1)}, u32[]{:S(2)}, u32[]{:S(2)}) collective-permute-start(f32[144,128]{1,0:T(8,128)S(1)} %select_add_fusion.1), channel_id=1, source_target_pairs={{0,4},{4,0},{8,12},{12,8},{1,5},{5,1},{9,13},{13,9},{2,6},{6,2},{1... | collective-permute-start | bytes 221192 | tf_op jit(solution)/shard_map/ppermute | solution.py:445
  50.8 4.4 %collective-permute-start.9 = (f32[144,128]{1,0:T(8,128)S(1)}, f32[144,128]{1,0:T(8,128)S(1)}, u32[]{:S(2)}, u32[]{:S(2)}) collective-permute-start(f32[144,128]{1,0:T(8,128)S(1)} %add_add_fusion), channel_id=1, source_target_pairs={{0,2},{1,3},{2,0},{3,1},{4,6},{5,7},{6,4},{7,5},{8,10},{9,11},{10,... | collective-permute-start | bytes 221192 | tf_op jit(solution)/shard_map/ppermute | solution.py:445
  55.2 1.4 %collective-permute-start.10 = (f32[288,128]{1,0:T(8,128)S(1)}, f32[288,128]{1,0:T(8,128)S(1)}, u32[]{:S(2)}, u32[]{:S(2)}) collective-permute-start(f32[288,128]{1,0:T(8,128)S(1)} %pad_maximum_fusion.1), channel_id=1, source_target_pairs={{0,1},{1,0},{2,3},{3,2},{4,5},{5,4},{6,7},{7,6},{8,9},{9,8},{10,11... | collective-permute-start | bytes 442376 | tf_op jit(solution)/shard_map/ppermute | solution.py:445

commit v10 on v9

v10 whole, which is shorter than its diff:
```python
import functools

import jax
import jax.numpy as jnp
from jax import lax
from jax.experimental import pallas as pl
from jax.experimental.pallas import tpu as pltpu
from jax.sharding import PartitionSpec as P

KAPPA = 0.2
DT = 0.1
GAIN_GRAD = 10.0

WIDE = 4
LANES = 128
PART = 8
EARLY = 2
DEEP = 16
SHALLOW = 8

F32 = jnp.float32
BF16 = jnp.bfloat16


def dot(left, right):
    return lax.dot_general(left, right, (((1,), (0,)), ((), ())), preferred_element_type=F32)


def dot_nt(left, right):
    return lax.dot_general(left, right, (((1,), (1,)), ((), ())), preferred_element_type=F32)


def pack_kernel(
    now, old, drift, cnew, cmid, ocean, w_in, w_mid, w_out,
    west, east, top, bottom, fields, v_in, v_mid, v_out, wet, sems,
):
    levels, rows, cols = now.shape
    copies = [
        pltpu.make_async_copy(ref, fields.at[pl.ds(levels * f, levels)], sems.at[f])
        for f, ref in enumerate((now, old, drift, cnew, cmid))
    ]
    copies.append(pltpu.make_async_copy(ocean, wet, sems.at[5]))
    for k, pair in enumerate(((w_in, v_in), (w_mid, v_mid), (w_out, v_out))):
        copies.append(pltpu.make_async_copy(*pair, sems.at[6 + k]))
    for copy in copies:
        copy.start()
    lane = lax.broadcasted_iota(jnp.int32, (rows, LANES), 1)
    to_west = jnp.zeros((rows, LANES), F32)
    to_east = jnp.zeros((rows, LANES), F32)
    count = fields.shape[0]
    for p in range(count):
        if p % levels == 0:
            copies[p // levels].wait()
        if p == count - 1:
            fields[p] = wet[...].astype(F32)
        plane = fields[p]
        here = (lane >= WIDE * p) & (lane < WIDE * (p + 1))
        to_west = jnp.where(here, pltpu.roll(plane, WIDE * p, 1) if p else plane, to_west)
        to_east = jnp.where(here, pltpu.roll(plane, WIDE * (p + 1), 1), to_east)
        top[p] = plane[:WIDE]
        bottom[p] = plane[rows - WIDE :]
    west[...] = to_west
    east[...] = to_east
    for copy in copies[6:]:
        copy.wait()


def join_kernel(top, bottom, left, right, up, down):
    count = top.shape[0]
    rows = left.shape[0]
    up[pl.ds(0, count)] = bottom[...]
    down[pl.ds(0, count)] = top[...]
    for k, strip in enumerate((left, right)):
        up[count + k] = strip[pl.ds(rows - WIDE, WIDE), :]
        down[count + k] = strip[pl.ds(0, WIDE), :]


def east_of(v):
    return pltpu.roll(v, v.shape[1] - 1, 1)


def west_of(v):
    return pltpu.roll(v, 1, 1)


def north_of(v):
    return pltpu.roll(v, v.shape[0] - 1, 0)


def south_of(v):
    return pltpu.roll(v, 1, 0)


def forward_stages(x, w_first_t, w_second_t):
    z_one = dot(w_first_t[...], x)
    yield
    first = jnp.tanh(z_one)
    low_first = first.astype(BF16)
    yield
    z_two = dot(w_second_t[...], low_first)
    yield
    second = jnp.tanh(z_two)
    return first, second, low_first, second.astype(BF16)


def closure(low_second, w_last_t):
    return dot(w_last_t[...], low_second).astype(BF16).astype(F32)[:SHALLOW]


def staggered(generators):
    live = []
    waiting = list(generators)
    while live or waiting:
        if waiting:
            live.append(waiting.pop(0))
        for part in list(live):
            try:
                next(part)
            except StopIteration:
                live.remove(part)


def lanes_of(ref, deep, base, tiles):
    block = ref[pl.ds(base * deep, tiles * deep), :]
    return jnp.concatenate([block[k * deep : (k + 1) * deep] for k in range(tiles)], 1)


def put_lanes(ref, deep, base, tiles, value):
    for k in range(tiles):
        ref[pl.ds((base + k) * deep, deep), :] = value[:, k * LANES : (k + 1) * LANES]


def early_kernel(start, fields, *refs):
    if start == 0:
        w_in, w_mid, w_out_t, keep1, keep2, cl, wi, wi_t, wm_t, wo, wo_t, ft = refs
        width_in, hidden = w_in.shape
        levels = w_out_t.shape[0]
        spare = jnp.zeros((DEEP - width_in, hidden), F32)
        wide_in = jnp.concatenate([w_in[...].astype(F32), spare], 0)
        wi[...] = wide_in.astype(BF16)
        wi_t[...] = wide_in.T.astype(BF16)
        wm_t[...] = w_mid[...].astype(F32).T.astype(BF16)
        spare = jnp.zeros((DEEP - levels, hidden), F32)
        wide_out = jnp.concatenate([w_out_t[...].astype(F32), spare], 0)
        wo_t[...] = wide_out.astype(BF16)
        wo[...] = wide_out.T.astype(BF16)
    else:
        unused, wi_t, wm_t, wo_t, keep1, keep2, cl, ft = refs
        levels = (fields.shape[0] - 1) // 5
    tall = cl.shape[0] // SHALLOW
    ft[...] = jnp.zeros_like(ft)
    for level in range(levels):
        v = fields[level]
        slope_x = 0.5 * (east_of(v) - west_of(v))
        slope_y = 0.5 * (north_of(v) - south_of(v))
        for f, plane in enumerate((v, slope_x, slope_y)):
            ft[pl.ds(f * levels + level, tall, stride=DEEP), :] = plane[start : start + tall]

    def part(base, kept1, kept2):
        x = lanes_of(ft, DEEP, base, PART).astype(BF16)
        first, second, unused_low, low_second = yield from forward_stages(x, wi_t, wm_t)
        kept1[...] = first
        kept2[...] = second
        yield
        put_lanes(cl, SHALLOW, base, PART, closure(low_second, wo_t))

    staggered(part(k * PART, keep1.at[k], keep2.at[k]) for k in range(tall // PART))


def copied_out(pairs, sems):
    copies = [pltpu.make_async_copy(*pair, sems.at[k]) for k, pair in enumerate(pairs)]
    for copy in copies:
        copy.start()
    return copies


class Block:
    def __init__(self, levels, rows):
        self.levels, self.rows = levels, rows
        self.ext = rows + 2 * WIDE
        self.packs = -(-self.ext // 16)
        self.wet = 5 * levels
        packed = [None] * self.packs
        ext = self.ext
        self.rim = [0, rows - 1, rows, ext - 1] + packed + [rows + 1, ext - 2, rows + 2, ext - 3]
        self.rim_near = self.rim[: 4 + self.packs]
        self.outer = [rows, ext - 1] + packed + [rows + 1, ext - 2]
        self.lane = lax.broadcasted_iota(jnp.int32, (ext, LANES), 1)

    def with_rim(self, plane):
        lane = self.lane
        body, side = plane[:, :LANES], plane[:, LANES:]
        own = jnp.where(lane == LANES - WIDE, pltpu.roll(body, LANES - WIDE, 1), pltpu.roll(body, WIDE, 1))
        return jnp.where((lane == LANES - WIDE) | (lane == WIDE - 1), own, side)

    def from_rim(self, body, side):
        lane = self.lane
        own = jnp.where(lane == 0, pltpu.roll(side, WIDE, 1), pltpu.roll(side, LANES - WIDE, 1))
        return jnp.where((lane == 0) | (lane == LANES - 1), own, body)

    def spread(self, plane, index, deep, main, extra, side, rimmed):
        main[pl.ds(index, self.rows, stride=deep), :] = plane[: self.rows, :LANES]
        extra[pl.ds(index, 2 * WIDE, stride=deep), :] = plane[self.rows :, :LANES]
        side[pl.ds(index, self.ext, stride=deep), :] = self.with_rim(plane) if rimmed else plane[:, LANES:]

    def gathered(self, index, deep, main, extra, side, rimmed):
        body = jnp.concatenate(
            [main[pl.ds(index, self.rows, stride=deep), :], extra[pl.ds(index, 2 * WIDE, stride=deep), :]], 0
        )
        beside = side[pl.ds(index, self.ext, stride=deep), :]
        return jnp.concatenate([self.from_rim(body, beside) if rimmed else body, beside], 1)

    def home(self, r, deep, main, extra):
        return main.at[pl.ds(r * deep, deep)] if r < self.rows else extra.at[pl.ds((r - self.rows) * deep, deep)]

    def pack_halo(self, order, deep, main, extra, side, rim_too=True):
        where = lax.broadcasted_iota(jnp.int32, (deep, LANES), 1)
        for i, r in enumerate(order):
            if r is not None and (rim_too or r >= self.rows):
                main[pl.ds((self.rows + i) * deep, deep), :] = self.home(r, deep, main, extra)[...]
        first_pack = self.rows + order.index(None)
        for q in range(self.packs):
            total = jnp.zeros((deep, LANES), F32)
            for j in range(min(16, self.ext - 16 * q)):
                moved = pltpu.roll(side[pl.ds((16 * q + j) * deep, deep), :], (2 * WIDE * j + WIDE) % LANES, 1)
                total = jnp.where((where >= 2 * WIDE * j) & (where < 2 * WIDE * (j + 1)), moved, total)
            main[pl.ds((first_pack + q) * deep, deep), :] = total

    def unpack_halo(self, order, deep, main, extra, side):
        for i, r in enumerate(order):
            if r is not None:
                self.home(r, deep, main, extra)[...] = main[pl.ds((self.rows + i) * deep, deep), :]
        first_pack = self.rows + order.index(None)
        for q in range(self.packs):
            tile = main[pl.ds((first_pack + q) * deep, deep), :]
            for j in range(min(16, self.ext - 16 * q)):
                moved = pltpu.roll(tile, LANES - (2 * WIDE * j + WIDE) % LANES, 1)
                side[pl.ds((16 * q + j) * deep, deep), :] = moved

    def force(self, planes, v, level, closed):
        eastward, westward, northward, southward = east_of(v), west_of(v), north_of(v), south_of(v)
        laplace = eastward + westward + northward + southward - 4.0 * v
        slope = 0.5 * (eastward - westward)
        return planes[self.wet] * (KAPPA * laplace - planes[2 * self.levels + level] * slope + closed)

    def adjoint(self, planes, weighted, level, tiles, rimmed):
        levels = self.levels
        masked = planes[self.wet] * weighted
        carried = planes[2 * levels + level] * masked
        a0, a1, a2 = (self.gathered(f * levels + level, DEEP, *tiles, rimmed) for f in range(3))
        result = KAPPA * (east_of(masked) + west_of(masked) + north_of(masked) + south_of(masked) - 4.0 * masked)
        result = result + 0.5 * (east_of(carried) - west_of(carried)) + a0
        return result - 0.5 * (east_of(a1) - west_of(a1)) - 0.5 * (north_of(a2) - south_of(a2))


def feature_gradients(dz_one, w_in):
    return dot(w_in[...], dz_one).astype(BF16).astype(F32)


def main_kernel(bands, *refs):
    fields, left, right, low, high, wi, wi_t, wm_t, w_mid, wo, wo_t, *refs = refs
    early, refs = refs[: 3 * EARLY], refs[3 * EARLY :]
    h_mid, h_old, o_sent, o_kept, planes, mids, olds, cl, df, *refs = refs
    o_mid, o_old, sems, ft1, ft2, fth, ftx, clh, clx, dc, dch, dcx, dfh, dfx, halo1, halo2, *refs = refs
    acc_mid, acc_in, acc_out, o_grad = refs
    levels, rows, cols = o_mid.shape
    hidden = w_mid.shape[0]
    block = Block(levels, rows)
    count, ext, lane = block.wet + 1, block.ext, block.lane
    kept1 = [ref.at[k] for ref in early[0::3] for k in range(ref.shape[0])]
    kept2 = [ref.at[k] for ref in early[1::3] for k in range(ref.shape[0])]

    band = lax.axis_index("lat")
    has_low = jnp.where(band > 0, 1.0, 0.0)
    has_high = jnp.where(band < bands - 1, 1.0, 0.0)

    def beyond(p):
        return [high[p] * has_high, low[p] * has_low]

    left_all = jnp.concatenate([left[...]] + beyond(count), 0)
    right_all = jnp.concatenate([right[...]] + beyond(count + 1), 0)
    for p in range(count):
        from_right = pltpu.roll(right_all, LANES - WIDE * p, 1) if p else right_all
        from_left = pltpu.roll(left_all, LANES - WIDE * (p + 1), 1)
        side = jnp.where(lane < WIDE, from_right, jnp.where(lane >= LANES - WIDE, from_left, 0.0))
        planes[p, :, pl.ds(0, LANES)] = jnp.concatenate([fields[p]] + beyond(p), 0)
        planes[p, :, pl.ds(LANES, LANES)] = side

    for ref in (ft1, ft2, fth, ftx, dc, dch, dcx):
        ref[...] = jnp.zeros_like(ref)

    def inputs_at(ref, base, tiles):
        return lanes_of(ref, DEEP, base, tiles).astype(BF16)

    def cotangents_at(base, tiles):
        part = lanes_of(dc, SHALLOW, base, tiles)
        return jnp.concatenate([part, jnp.zeros_like(part)], 0).astype(BF16)

    def backward_stages(first, second, cot):
        g_two = dot(wo[...], cot)
        yield
        dz_two = (g_two * (1.0 - second * second)).astype(BF16)
        yield
        g_one = dot(w_mid[...], dz_two)
        yield
        dz_one = (g_one * (1.0 - first * first)).astype(BF16)
        yield
        return dz_one, dz_two

    def second_part(base, tiles, sums):
        x = inputs_at(ft2, base, tiles)
        cot = cotangents_at(base, tiles)
        first, second, low_first, low_second = yield from forward_stages(x, wi_t, wm_t)
        yield
        if sums is not None:
            put_lanes(cl, SHALLOW, base, tiles, closure(low_second, wo_t))
        dz_one, dz_two = yield from backward_stages(first, second, cot)
        dfeat = feature_gradients(dz_one, wi)
        if sums is not None:
            add_terms(sums, (low_first, dz_two), (x, dz_one), (low_second, cot))
        yield
        put_lanes(df, DEEP, base, tiles, dfeat)

    def third_part(base, tiles, held1, held2, counted, sums):
        cot = cotangents_at(base, tiles)
        first = held1[...]
        second = held2[...]
        dz_one, dz_two = yield from backward_stages(first, second, cot)
        dfeat = feature_gradients(dz_one, wi)
        x = inputs_at(ft1, base, tiles)
        if counted is not None:
            dz_one, dz_two, cot = (jnp.where(counted, v.astype(F32), 0.0).astype(BF16) for v in (dz_one, dz_two, cot))
        add_terms(sums, (first.astype(BF16), dz_two), (x, dz_one), (second.astype(BF16), cot))
        yield
        put_lanes(df, DEEP, base, tiles, dfeat)

    def add_terms(sums, *pairs):
        for k, pair in enumerate(pairs):
            sums[k] = dot_nt(*pair) if sums[k] is None else sums[k] + dot_nt(*pair)

    def features_of(source, ft, order, rimmed):
        for level in range(levels):
            v = source[level]
            for f, plane in enumerate((v, 0.5 * (east_of(v) - west_of(v)), 0.5 * (north_of(v) - south_of(v)))):
                block.spread(plane, f * levels + level, DEEP, ft, ftx, fth, rimmed)
        block.pack_halo(order, DEEP, ft, ftx, fth)

    features_of(planes, ft1, block.rim, True)
    for k, ref in enumerate(early[2::3]):
        cl[pl.ds(k * ref.shape[0], ref.shape[0]), :] = ref[...]

    def first_part(base, tiles):
        first, second, unused, low_second = yield from forward_stages(inputs_at(ft1, base, tiles), wi_t, wm_t)
        halo1[...] = first
        halo2[...] = second
        yield
        put_lanes(cl, SHALLOW, base, tiles, closure(low_second, wo_t))

    staggered([first_part(rows, len(block.rim))])
    block.unpack_halo(block.rim, SHALLOW, cl, clx, clh)
    for level in range(levels):
        closed = block.gathered(level, SHALLOW, cl, clx, clh, True)
        mid = planes[levels + level] + 2.0 * DT * block.force(planes, planes[level], level, closed)
        o_mid[level] = mid[:rows, :LANES]
        mids[level] = mid
    copies = copied_out([(o_mid, h_mid)], sems.at[pl.ds(0, 1)])

    features_of(mids, ft2, block.outer, False)
    for level in range(levels):
        masked = planes[block.wet] * (2.0 * DT * planes[3 * levels + level])
        block.spread(masked, level, SHALLOW, dc, dcx, dch, False)
    block.pack_halo(block.outer, SHALLOW, dc, dcx, dch)
    sums = [None] * 3
    staggered(
        [second_part(rows, len(block.outer), None)]
        + [second_part(k * PART, PART, sums) for k in range(rows // PART)]
    )
    for acc, total in zip((acc_mid, acc_in, acc_out), sums):
        acc[...] = total
    block.unpack_halo(block.outer, DEEP, df, dfx, dfh)
    for level in range(levels):
        weighted = 2.0 * DT * planes[3 * levels + level]
        grad = planes[4 * levels + level] + block.adjoint(planes, weighted, level, (df, dfx, dfh), False)
        o_old[level] = grad[:rows, :LANES]
        olds[level] = grad
    copies += copied_out([(o_old, h_old)], sems.at[pl.ds(1, 1)])

    near = block.rim_near
    row = lax.broadcasted_iota(jnp.int32, (ext, LANES), 0)
    inside = (lane > 0) & (lane < LANES - 1) & (row > 0) & (row < rows - 1)
    for level in range(levels):
        masked = planes[block.wet] * (2.0 * DT * olds[level])
        body = masked[:, :LANES]
        dc[pl.ds(level, rows, stride=SHALLOW), :] = jnp.where(inside, body, 0.0)[:rows]
        dcx[pl.ds(level, 2 * WIDE, stride=SHALLOW), :] = body[rows:]
        dch[pl.ds(level, ext, stride=SHALLOW), :] = block.with_rim(masked)
        for k, r in enumerate(near[:2]):
            dc[pl.ds((rows + k) * SHALLOW + level, 1), :] = body[r : r + 1]
    block.pack_halo(near, SHALLOW, dc, dcx, dch, False)
    at = lax.broadcasted_iota(jnp.int32, (1, len(near) * LANES), 1)
    tile, place = at >> 7, at & (LANES - 1)
    side_row = (tile - 4) * 16 + (place >> 3)
    edge = ((place & 7) == 0) | ((place & 7) == 7)
    counted = (tile < 2) | ((tile >= 4) & edge & (side_row > 0) & (side_row < rows - 1))
    wide = pl.ds(0, len(near) * LANES)
    sums = [None] * 3
    staggered(
        [third_part(rows, len(near), halo1.at[:, wide], halo2.at[:, wide], counted, sums)]
        + [third_part(k * PART, PART, kept1[k], kept2[k], None, sums) for k in range(rows // PART)]
    )

    start = 0
    for total in (acc_mid[...] + sums[0], acc_in[...] + sums[1], (acc_out[...] + sums[2]).T):
        deep = total.shape[0]
        for half in range(hidden // LANES):
            o_grad[pl.ds(start, deep), :] = total[:, half * LANES : (half + 1) * LANES]
            start += deep
    if start < o_grad.shape[0]:
        o_grad[pl.ds(start, o_grad.shape[0] - start), :] = jnp.zeros((o_grad.shape[0] - start, LANES), F32)
    halve(o_grad[...], 1, o_sent, o_kept)
    for copy in copies:
        copy.wait()


def halve(value, bit, sent, kept):
    half = value.shape[0] // 2
    upper = (lax.axis_index("lat") & bit) != 0
    sent[...] = jnp.where(upper, value[:half], value[half:])
    kept[...] = jnp.where(upper, value[half:], value[:half])


def halve_kernel(bit, held, got, sent, kept):
    halve(held[...] + got[...], bit, sent, kept)


def late_kernel(
    fields, planes, mids, olds, cl, gradients, held, h_new, h_now, o_held, o_place, o_new, o_now, sems, df, dfh, dfx
):
    levels, rows, cols = o_new.shape
    block = Block(levels, rows)
    o_held[...] = held[...]
    o_place[...] = jnp.zeros_like(o_place) + lax.axis_index("lat")
    df[...] = gradients[...]
    beside = jnp.zeros((rows, LANES), F32)
    beyond = jnp.zeros((2 * WIDE, 2 * LANES), F32)
    for level in range(levels):
        closed = jnp.concatenate([cl[pl.ds(level, rows, stride=SHALLOW), :], beside], 1)
        closed = jnp.concatenate([closed, beyond], 0)
        new = planes[level] + 2.0 * DT * block.force(planes, mids[level], level, closed)
        o_new[level] = new[:rows, :LANES]
    copies = copied_out([(o_new, h_new)], sems.at[pl.ds(0, 1)])
    block.unpack_halo(block.rim_near, DEEP, df, dfx, dfh)
    for level in range(levels):
        grad = block.adjoint(planes, 2.0 * DT * olds[level], level, (df, dfx, dfh), True)
        o_now[level] = fields[3 * levels + level] + grad[:rows, :LANES]
    copies += copied_out([(o_now, h_now)], sems.at[pl.ds(1, 1)])
    for copy in copies:
        copy.wait()


def scale_kernel(factor, terms, g_in, g_mid, g_out):
    hidden = g_mid.shape[0]
    start = 0
    for ref, deep in ((g_mid, hidden), (g_in, DEEP), (g_out, DEEP)):
        for half in range(hidden // LANES):
            ref[:, half * LANES : (half + 1) * LANES] = terms[pl.ds(start, ref.shape[0]), :] * factor
            start += deep


def along(value, axis, step):
    count = lax.axis_size(axis)
    return lax.ppermute(value, axis, [(i, (i + step) % count) for i in range(count)])


def swapped(value, axis, bit):
    return lax.ppermute(value, axis, [(i, i ^ bit) for i in range(lax.axis_size(axis))])


def added_up(value, axis):
    bit = 1
    while bit < lax.axis_size(axis):
        near = swapped(value, axis, bit)
        if 2 * bit < lax.axis_size(axis):
            value = (value + near) + (swapped(value, axis, 2 * bit) + swapped(value, axis, 3 * bit))
            bit *= 4
        else:
            value = value + near
            bit *= 2
    return value


def put_together(value, place, axis):
    bit = lax.axis_size(axis) // 2
    while bit:
        upper = (place & bit) != 0
        other = swapped(value, axis, bit)
        value = jnp.concatenate([jnp.where(upper, other, value), jnp.where(upper, value, other)], 0)
        bit //= 2
    return value


def body(state_old, state_now, drift, ocean, w_in, w_mid, w_out, cot_mid, cot_new):
    levels, rows, cols = state_now.shape
    width_in, hidden = w_in.shape
    ext = rows + 2 * WIDE
    count = 5 * levels + 1
    packs = -(-ext // 16)
    slots = rows + 8 + packs
    tall = rows // EARLY
    vmem = pl.BlockSpec(memory_space=pltpu.VMEM)
    hbm = pl.BlockSpec(memory_space=pltpu.HBM)
    strip = jax.ShapeDtypeStruct((rows, LANES), F32)
    edge = jax.ShapeDtypeStruct((count, WIDE, LANES), F32)
    arrays = (state_now, state_old, drift, cot_new, cot_mid, ocean, w_in, w_mid, w_out.T)
    weights = tuple(jax.ShapeDtypeStruct(a.shape, a.dtype) for a in arrays[6:])
    west, east, top, bottom, fields, *weights = pl.pallas_call(
        pack_kernel,
        out_shape=(strip, strip, edge, edge, jax.ShapeDtypeStruct((count, rows, cols), F32)) + weights,
        in_specs=[hbm] * 9,
        out_specs=(vmem,) * 8,
        scratch_shapes=[pltpu.VMEM((rows, cols), jnp.int32), pltpu.SemaphoreType.DMA((9,))],
        compiler_params=pltpu.CompilerParams(vmem_limit_bytes=8 * 2**20),
    )(*(pltpu.with_memory_space_constraint(a, pltpu.HBM) for a in arrays))

    kept = jax.ShapeDtypeStruct((tall // PART, hidden, PART * LANES), F32)
    closed = jax.ShapeDtypeStruct((tall * SHALLOW, LANES), F32)
    tall_weight = jax.ShapeDtypeStruct((hidden, DEEP), BF16)
    flat_weight = jax.ShapeDtypeStruct((DEEP, hidden), BF16)
    prepared = (flat_weight, tall_weight, jax.ShapeDtypeStruct((hidden, hidden), BF16), tall_weight, flat_weight)

    def early(k, extra, extra_out):
        return pl.pallas_call(
            functools.partial(early_kernel, k * tall),
            out_shape=(kept, kept, closed) + extra_out,
            in_specs=[vmem] * (1 + len(extra)),
            out_specs=(vmem,) * (3 + len(extra_out)),
            scratch_shapes=[pltpu.VMEM((tall * DEEP, LANES), F32)],
            compiler_params=pltpu.CompilerParams(vmem_limit_bytes=12 * 2**20),
            cost_estimate=pl.CostEstimate(
                flops=6 * hidden * hidden * tall * cols, bytes_accessed=0, transcendentals=2 * hidden * tall * cols
            ),
        )(fields, *extra)

    left = along(east, "lon", 1)
    right = along(west, "lon", -1)
    *first_kept, wi, wi_t, wm_t, wo, wo_t = early(0, tuple(weights), prepared)
    message = jax.ShapeDtypeStruct((count + 2, WIDE, LANES), F32)
    up, down = pl.pallas_call(
        join_kernel,
        out_shape=(message, message),
        in_specs=[vmem] * 4,
        out_specs=(vmem,) * 2,
        compiler_params=pltpu.CompilerParams(vmem_limit_bytes=4 * 2**20),
    )(top, bottom, left, right)
    low = along(up, "lat", 1)
    high = along(down, "lat", -1)
    done = list(first_kept)
    for k in range(1, EARLY):
        done += early(k, (left, wi_t, wm_t, wo_t), ())

    bands = lax.axis_size("lat")
    halves = hidden // LANES
    terms_rows = -(-halves * (hidden + 2 * DEEP) // (8 * bands)) * 8 * bands
    field = jax.ShapeDtypeStruct((levels, rows, cols), F32)
    ext_planes = jax.ShapeDtypeStruct((levels, ext, 2 * LANES), F32)
    staged = pltpu.VMEM((levels, rows, cols), F32)

    def tiles(deep):
        return [pltpu.VMEM((n * deep, LANES), F32) for n in (slots, 16 * packs, 2 * WIDE)]

    def half_terms(parts):
        return (jax.ShapeDtypeStruct((terms_rows // parts, LANES), F32),) * 2

    kept_halo = pltpu.VMEM((hidden, (8 + packs) * LANES), F32)
    state_mid, grad_old, sent, held, planes, mids, olds, closures, gradients = pl.pallas_call(
        functools.partial(main_kernel, bands),
        out_shape=(field, field, *half_terms(2))
        + (jax.ShapeDtypeStruct((count, ext, 2 * LANES), F32), ext_planes, ext_planes)
        + tuple(jax.ShapeDtypeStruct((slots * deep, LANES), F32) for deep in (SHALLOW, DEEP)),
        in_specs=[vmem] * (11 + 3 * EARLY),
        out_specs=(hbm,) * 2 + (vmem,) * 7,
        scratch_shapes=[
            staged,
            staged,
            pltpu.SemaphoreType.DMA((2,)),
            tiles(DEEP)[0],
            *tiles(DEEP),
            *tiles(SHALLOW)[1:],
            *tiles(SHALLOW),
            *tiles(DEEP)[1:],
            kept_halo,
            kept_halo,
            pltpu.VMEM((hidden, hidden), F32),
            pltpu.VMEM((DEEP, hidden), F32),
            pltpu.VMEM((hidden, DEEP), F32),
            pltpu.VMEM((terms_rows, LANES), F32),
        ],
        compiler_params=pltpu.CompilerParams(vmem_limit_bytes=32 * 2**20),
    )(fields, left, right, low, high, wi, wi_t, wm_t, weights[1], wo, wo_t, *done)

    bit = 1
    while 2 * bit < bands:
        got = swapped(sent, "lat", bit)
        bit *= 2
        sent, held = pl.pallas_call(
            functools.partial(halve_kernel, bit),
            out_shape=half_terms(2 * bit),
            in_specs=[vmem] * 2,
            out_specs=(vmem,) * 2,
            compiler_params=pltpu.CompilerParams(vmem_limit_bytes=4 * 2**20),
        )(held, got)
    got = swapped(sent, "lat", bit)
    state_new, grad_now, held, place = pl.pallas_call(
        late_kernel,
        out_shape=(field, field, half_terms(bands)[0], jax.ShapeDtypeStruct((8, LANES), jnp.int32)),
        in_specs=[vmem] * 7,
        out_specs=(hbm,) * 2 + (vmem,) * 2,
        scratch_shapes=[staged, staged, pltpu.SemaphoreType.DMA((2,)), *tiles(DEEP)],
        compiler_params=pltpu.CompilerParams(vmem_limit_bytes=16 * 2**20),
        cost_estimate=pl.CostEstimate(
            flops=2 * hidden * hidden * rows * cols, bytes_accessed=0, transcendentals=0
        ),
    )(fields, planes, mids, olds, closures, gradients, held)
    summed = put_together(added_up(held + got, "lon"), place[:1], "lat")
    cells_all = rows * lax.axis_size("lat") * cols * lax.axis_size("lon")
    grad_in, grad_mid, grad_out = pl.pallas_call(
        functools.partial(scale_kernel, GAIN_GRAD / cells_all**0.5),
        out_shape=(
            jax.ShapeDtypeStruct((width_in, hidden), F32),
            jax.ShapeDtypeStruct((hidden, hidden), F32),
            jax.ShapeDtypeStruct((levels, hidden), F32),
        ),
        in_specs=[vmem],
        out_specs=(vmem,) * 3,
        compiler_params=pltpu.CompilerParams(vmem_limit_bytes=8 * 2**20),
    )(summed)
    return state_mid, state_new, grad_old, grad_now, grad_in, grad_mid, grad_out.T


def solution(mesh):
    field = P("grp", "lat", "lon")
    whole = P("grp", None)
    in_specs = (field, field, field, P(("grp", "lat"), "lon"), P(), P(), P(), field, field)
    out_specs = (field, field, field, field, whole, whole, whole)
    return jax.shard_map(body, mesh=mesh, in_specs=in_specs, out_specs=out_specs, check_vma=False)
```

time: 57.6 us -> 57.5 us (level)
  Pallas kernels: 26.2 us -> 28 us
  waiting for transfers between devices: 16.1 us -> 14.3 us
    ppermute x7, waiting for transfers between devices: 15.6 us -> 13.7 us  [swapped(): lax.ppermute(value, axis, [(i, i ^ bit) for i in range(lax.axis_size(axis...]
    pallas_call x1 -> x3, Pallas kernels: 20.4 us -> 22.2 us  [the longest x1 20.4 us: body(): pl.pallas_call(functools.partial(main_kernel, bands), out_shape=(field, f...]
  transfers between devices with their start and end apart: 11 -> 11, of which waited for: 9 -> 9; matrix products, arithmetic and copies ran while one was open for 0% -> 0% of each run, Pallas kernels for 6% -> 9%
where the time goes in v10:
time: 57.5 us; the launch traced here: 57.4 us
  Pallas kernels  28 us (49%)
  waiting for transfers between devices  14.3 us (25%)
  starting transfers between devices  14.2 us (25%)
  between operations  0.72 us (1%)
    pallas_call x1, Pallas kernels, body(): pl.pallas_call(functools.partial(main_kernel, bands), out_shape=(field, f...  20.4 us
    ppermute x7, waiting for transfers between devices, swapped(): lax.ppermute(value, axis, [(i, i ^ bit) for i in range(lax.axis_size(axis...  13.7 us
    ppermute x7, starting transfers between devices, swapped(): lax.ppermute(value, axis, [(i, i ^ bit) for i in range(lax.axis_size(axis...  7.27 us
    ppermute x4, starting transfers between devices, along(): lax.ppermute(value, axis, [(i, (i + step) % count) for i in range(count)])  6.96 us
    pallas_call x2, Pallas kernels, early(): pl.pallas_call(functools.partial(early_kernel, k * tall), out_shape=(kept...  3.36 us
    pallas_call x1, Pallas kernels, body(): pl.pallas_call(late_kernel, out_shape=(field, field, half_terms(bands)[0]...  1.82 us
    pallas_call x1, Pallas kernels, body(): pl.pallas_call(pack_kernel, out_shape=(strip, strip, edge, edge, jax.Shap...  1.74 us
  transfers between devices with their start and end apart: 11, of which 9 were waited for; matrix products, arithmetic and copies ran while one was open for 0% of the time, Pallas kernels for 9%

profile of v10, /device:TPU:0, one launch (start us, length us, event | category | flops | bytes accessed | tf_op | source)
XLA Modules:
  0.0 57.4 jit_solution(9197547187439633117)
XLA Ops:
  0.6 1.7 %shard_map.144 = (f32[64,128]{1,0:T(8,128)S(1)}, f32[64,128]{1,0:T(8,128)S(1)}, f32[21,4,128]{2,1,0:T(4,128)S(1)}, f32[21,4,128]{2,1,0:T(4,128)S(1)}, f32[21,64,...) custom-call(f32[4,64,128]{2,1,0:T(8,128)} %now.1, ...), custom_call_target="tpu_custom_call" | custom-call | tf_op jit(solution)/shard_map/pallas_call | solution.py:516
  2.4 3.1 %collective-permute-start = (f32[64,128]{1,0:T(8,128)S(1)}, f32[64,128]{1,0:T(8,128)S(1)}, u32[]{:S(2)}, u32[]{:S(2)}) collective-permute-start(f32[64,128]{1,0:T(8,128)S(1)} %get-tuple-element.47), channel_id=1, source_target_pairs={{0,4},{4,8},{8,12},{12,0},{1,5},{5,9},{9,13},{13,1},{2,6},{6,10},{... | collective-permute-start | bytes 98312 | tf_op jit(solution)/shard_map/ppermute | solution.py:472
  5.5 2.1 %collective-permute-start.1 = (f32[64,128]{1,0:T(8,128)S(1)}, f32[64,128]{1,0:T(8,128)S(1)}, u32[]{:S(2)}, u32[]{:S(2)}) collective-permute-start(f32[64,128]{1,0:T(8,128)S(1)} %get-tuple-element.48), channel_id=1, source_target_pairs={{0,12},{4,0},{8,4},{12,8},{1,13},{5,1},{9,5},{13,9},{2,14},{6,2},{... | collective-permute-start | bytes 98312 | tf_op jit(solution)/shard_map/ppermute | solution.py:472
  7.6 1.7 %shard_map.146 = (f32[4,256,1024]{2,1,0:T(8,128)S(1)}, f32[4,256,1024]{2,1,0:T(8,128)S(1)}, f32[256,128]{1,0:T(8,128)S(1)}, bf16[16,256]{1,0:T(8,128)(2,1)S(1)},...) custom-call(f32[21,64,128]{2,1,0:T(8,128)S(1)} %get-tuple-element.46, ...), custom_call_target="tpu_custom_call" | custom-call | flops 1610612736 | tf_op jit(solution)/shard_map/pallas_call | solution.py:532
  9.3 0.2 collective-permute-done.left.refs_0_.refs_1_
  9.5 0.2 collective-permute-done.1.right.refs_2_
  9.7 0.1 collective-permute-start.2
  9.8 1.7 %collective-permute-start.3 = (f32[23,4,128]{2,1,0:T(4,128)S(1)}, f32[23,4,128]{2,1,0:T(4,128)S(1)}, u32[]{:S(2)}, u32[]{:S(2)}) collective-permute-start(f32[23,4,128]{2,1,0:T(4,128)S(1)} %get-tuple-element.52), channel_id=1, source_target_pairs={{0,3},{1,0},{2,1},{3,2},{4,7},{5,4},{6,5},{7,6},{8,11},{9,8},{10,9... | collective-permute-start | bytes 141320 | tf_op jit(solution)/shard_map/ppermute | solution.py:472
  11.5 1.6 %shard_map.147 = (f32[4,256,1024]{2,1,0:T(8,128)S(1)}, f32[4,256,1024]{2,1,0:T(8,128)S(1)}, f32[256,128]{1,0:T(8,128)S(1)}) custom-call(f32[21,64,128]{2,1,0:T(8,128)S(1)} %get-tuple-element.46.fields.refs_0_, f32[64,128]{1,0:T(8,128)S(1)} %collective-permute-done.left.refs_0_.refs_1_, bf16[256,16]{1,0:T(8,128)(2,1)S(1)} %get-tuple-element.57.refs_1_.refs_6_, ...), custom_call_target="tpu_custom_call" | custom-call | flops 1610612736 | tf_op jit(solution)/shard_map/pallas_call | solution.py:532
  13.2 0.1 collective-permute-done.2.refs_3_
  13.3 0.0 collective-permute-done.3.refs_4_
  13.3 20.4 %shard_map.148 = (f32[4,64,128]{2,1,0:T(8,128)}, f32[4,64,128]{2,1,0:T(8,128)}, f32[288,128]{1,0:T(8,128)S(1)}, f32[288,128]{1,0:T(8,128)S(1)}, f32[21,72,256]{2...) custom-call(f32[21,64,128]{2,1,0:T(8,128)S(1)} %get-tuple-element.46, ...), custom_call_target="tpu_custom_call" | custom-call | tf_op jit(solution)/shard_map/pallas_call | solution.py:575
  33.7 1.7 %collective-permute-start.4 = (f32[288,128]{1,0:T(8,128)S(1)}, f32[288,128]{1,0:T(8,128)S(1)}, u32[]{:S(2)}, u32[]{:S(2)}) collective-permute-start(f32[288,128]{1,0:T(8,128)S(1)} %get-tuple-element.74), channel_id=1, source_target_pairs={{0,1},{1,0},{2,3},{3,2},{4,5},{5,4},{6,7},{7,6},{8,9},{9,8},{10,11... | collective-permute-start | bytes 442376 | tf_op jit(solution)/shard_map/ppermute | solution.py:476
  35.3 1.0 %collective-permute-done.4.got = f32[288,128]{1,0:T(8,128)S(1)} collective-permute-done((f32[288,128]{1,0:T(8,128)S(1)}, f32[288,128]{1,0:T(8,128)S(1)}, u32[]{:S(2)}, u32[]{:S(2)}) %collective-permute-start.4) | collective-permute-done | bytes 147488 | tf_op jit(solution)/shard_map/ppermute | solution.py:476
  36.4 0.6 %collective-permute-start.5 = (f32[144,128]{1,0:T(8,128)S(1)}, f32[144,128]{1,0:T(8,128)S(1)}, u32[]{:S(2)}, u32[]{:S(2)}) collective-permute-start(f32[144,128]{1,0:T(8,128)S(1)} %get-tuple-element.81), channel_id=1, source_target_pairs={{0,2},{1,3},{2,0},{3,1},{4,6},{5,7},{6,4},{7,5},{8,10},{9,11},{10,... | collective-permute-start | bytes 221192 | tf_op jit(solution)/shard_map/ppermute | solution.py:476
  37.0 1.8 %shard_map.150 = (f32[4,64,128]{2,1,0:T(8,128)}, f32[4,64,128]{2,1,0:T(8,128)}, f32[144,128]{1,0:T(8,128)S(1)}, s32[8,128]{1,0:T(8,128)S(1)}) custom-call(f32[21,64,128]{2,1,0:T(8,128)S(1)} %get-tuple-element.46.fields.refs_0_, f32[21,72,256]{2,1,0:T(8,128)S(1)} %get-tuple-element.68.planes, f32[4,72,256]{2,1,0:T(8,128)S(1)} %get-tuple-element.69.mids, ...), custom_call_target="tpu_custom_call" | custom-call | flops 1073741824 | tf_op jit(solution)/shard_map/pallas_call | solution.py:613
  38.8 2.2 %collective-permute-done.5 = f32[144,128]{1,0:T(8,128)S(1)} collective-permute-done((f32[144,128]{1,0:T(8,128)S(1)}, f32[144,128]{1,0:T(8,128)S(1)}, u32[]{:S(2)}, u32[]{:S(2)}) %collective-permute-start.5) | collective-permute-done | bytes 73760 | tf_op jit(solution)/shard_map/ppermute | solution.py:476
  41.0 3.8 %collective-permute-start.8 = (f32[144,128]{1,0:T(8,128)S(1)}, f32[144,128]{1,0:T(8,128)S(1)}, u32[]{:S(2)}, u32[]{:S(2)}) collective-permute-start(f32[144,128]{1,0:T(8,128)S(1)} %add.12), channel_id=1, source_target_pairs={{0,12},{4,8},{8,4},{12,0},{1,13},{5,9},{9,5},{13,1},{2,14},{6,10},... | collective-permute-start | bytes 221192 | tf_op jit(solution)/shard_map/ppermute | solution.py:476
  44.7 0.0 collective-permute-start.7
  44.7 0.7 %collective-permute-start.6 = (f32[144,128]{1,0:T(8,128)S(1)}, f32[144,128]{1,0:T(8,128)S(1)}, u32[]{:S(2)}, u32[]{:S(2)}) collective-permute-start(f32[144,128]{1,0:T(8,128)S(1)} %add.12), channel_id=1, source_target_pairs={{0,4},{4,0},{8,12},{12,8},{1,5},{5,1},{9,13},{13,9},{2,6},{6,2},{1... | collective-permute-start | bytes 221192 | tf_op jit(solution)/shard_map/ppermute | solution.py:476
  45.4 2.3 %collective-permute-done.8 = f32[144,128]{1,0:T(8,128)S(1)} collective-permute-done((f32[144,128]{1,0:T(8,128)S(1)}, f32[144,128]{1,0:T(8,128)S(1)}, u32[]{:S(2)}, u32[]{:S(2)}) %collective-permute-start.8) | collective-permute-done | bytes 73760 | tf_op jit(solution)/shard_map/ppermute | solution.py:476
  47.8 2.9 %collective-permute-done.7 = f32[144,128]{1,0:T(8,128)S(1)} collective-permute-done((f32[144,128]{1,0:T(8,128)S(1)}, f32[144,128]{1,0:T(8,128)S(1)}, u32[]{:S(2)}, u32[]{:S(2)}) %collective-permute-start.7) | collective-permute-done | bytes 73760 | tf_op jit(solution)/shard_map/ppermute | solution.py:476
  50.7 0.0 collective-permute-done.6
  50.7 0.5 collective-permute-start.9
  51.2 4.0 %collective-permute-done.9 = f32[144,128]{1,0:T(8,128)S(1)} collective-permute-done((f32[144,128]{1,0:T(8,128)S(1)}, f32[144,128]{1,0:T(8,128)S(1)}, u32[]{:S(2)}, u32[]{:S(2)}) %collective-permute-start.9) | collective-permute-done | bytes 73760 | tf_op jit(solution)/shard_map/ppermute | solution.py:476
  55.2 0.1 collective-permute-start.10
  55.2 1.4 %collective-permute-done.10 = f32[288,128]{1,0:T(8,128)S(1)} collective-permute-done((f32[288,128]{1,0:T(8,128)S(1)}, f32[288,128]{1,0:T(8,128)S(1)}, u32[]{:S(2)}, u32[]{:S(2)}) %collective-permute-start.10) | collective-permute-done | bytes 147488 | tf_op jit(solution)/shard_map/ppermute | solution.py:476
  56.6 0.7 %shard_map.151 = (f32[12,256]{1,0:T(8,128)}, f32[256,256]{1,0:T(8,128)}, f32[4,256]{1,0:T(4,128)}) custom-call(f32[576,128]{1,0:T(8,128)S(1)} %pad_maximum_fusion.terms), custom_call_target="tpu_custom_call" | custom-call | tf_op jit(solution)/shard_map/pallas_call | solution.py:626
  (9 shorter events, 0.1 us)
Async XLA Ops:
  2.4 7.1 %collective-permute-start = (f32[64,128]{1,0:T(8,128)S(1)}, f32[64,128]{1,0:T(8,128)S(1)}, u32[]{:S(2)}, u32[]{:S(2)}) collective-permute-start(f32[64,128]{1,0:T(8,128)S(1)} %get-tuple-element.47), channel_id=1, source_target_pairs={{0,4},{4,8},{8,12},{12,0},{1,5},{5,9},{9,13},{13,1},{2,6},{6,10},{... | collective-permute-start | bytes 98312 | tf_op jit(solution)/shard_map/ppermute | solution.py:472
  5.5 4.3 %collective-permute-start.1 = (f32[64,128]{1,0:T(8,128)S(1)}, f32[64,128]{1,0:T(8,128)S(1)}, u32[]{:S(2)}, u32[]{:S(2)}) collective-permute-start(f32[64,128]{1,0:T(8,128)S(1)} %get-tuple-element.48), channel_id=1, source_target_pairs={{0,12},{4,0},{8,4},{12,8},{1,13},{5,1},{9,5},{13,9},{2,14},{6,2},{... | collective-permute-start | bytes 98312 | tf_op jit(solution)/shard_map/ppermute | solution.py:472
  9.7 3.5 %collective-permute-start.2 = (f32[23,4,128]{2,1,0:T(4,128)S(1)}, f32[23,4,128]{2,1,0:T(4,128)S(1)}, u32[]{:S(2)}, u32[]{:S(2)}) collective-permute-start(f32[23,4,128]{2,1,0:T(4,128)S(1)} %get-tuple-element.51), channel_id=1, source_target_pairs={{0,1},{1,2},{2,3},{3,0},{4,5},{5,6},{6,7},{7,4},{8,9},{9,10},{10,1... | collective-permute-start | bytes 141320 | tf_op jit(solution)/shard_map/ppermute | solution.py:472
  9.8 3.5 %collective-permute-start.3 = (f32[23,4,128]{2,1,0:T(4,128)S(1)}, f32[23,4,128]{2,1,0:T(4,128)S(1)}, u32[]{:S(2)}, u32[]{:S(2)}) collective-permute-start(f32[23,4,128]{2,1,0:T(4,128)S(1)} %get-tuple-element.52), channel_id=1, source_target_pairs={{0,3},{1,0},{2,1},{3,2},{4,7},{5,4},{6,5},{7,6},{8,11},{9,8},{10,9... | collective-permute-start | bytes 141320 | tf_op jit(solution)/shard_map/ppermute | solution.py:472
  33.7 2.7 %collective-permute-start.4 = (f32[288,128]{1,0:T(8,128)S(1)}, f32[288,128]{1,0:T(8,128)S(1)}, u32[]{:S(2)}, u32[]{:S(2)}) collective-permute-start(f32[288,128]{1,0:T(8,128)S(1)} %get-tuple-element.74), channel_id=1, source_target_pairs={{0,1},{1,0},{2,3},{3,2},{4,5},{5,4},{6,7},{7,6},{8,9},{9,8},{10,11... | collective-permute-start | bytes 442376 | tf_op jit(solution)/shard_map/ppermute | solution.py:476
  36.4 4.6 %collective-permute-start.5 = (f32[144,128]{1,0:T(8,128)S(1)}, f32[144,128]{1,0:T(8,128)S(1)}, u32[]{:S(2)}, u32[]{:S(2)}) collective-permute-start(f32[144,128]{1,0:T(8,128)S(1)} %get-tuple-element.81), channel_id=1, source_target_pairs={{0,2},{1,3},{2,0},{3,1},{4,6},{5,7},{6,4},{7,5},{8,10},{9,11},{10,... | collective-permute-start | bytes 221192 | tf_op jit(solution)/shard_map/ppermute | solution.py:476
  41.0 6.8 %collective-permute-start.8 = (f32[144,128]{1,0:T(8,128)S(1)}, f32[144,128]{1,0:T(8,128)S(1)}, u32[]{:S(2)}, u32[]{:S(2)}) collective-permute-start(f32[144,128]{1,0:T(8,128)S(1)} %add.12), channel_id=1, source_target_pairs={{0,12},{4,8},{8,4},{12,0},{1,13},{5,9},{9,5},{13,1},{2,14},{6,10},... | collective-permute-start | bytes 221192 | tf_op jit(solution)/shard_map/ppermute | solution.py:476
  44.7 5.9 %collective-permute-start.7 = (f32[144,128]{1,0:T(8,128)S(1)}, f32[144,128]{1,0:T(8,128)S(1)}, u32[]{:S(2)}, u32[]{:S(2)}) collective-permute-start(f32[144,128]{1,0:T(8,128)S(1)} %add.12), channel_id=1, source_target_pairs={{0,8},{4,12},{8,0},{12,4},{1,9},{5,13},{9,1},{13,5},{2,10},{6,14},... | collective-permute-start | bytes 221192 | tf_op jit(solution)/shard_map/ppermute | solution.py:476
  44.7 5.9 %collective-permute-start.6 = (f32[144,128]{1,0:T(8,128)S(1)}, f32[144,128]{1,0:T(8,128)S(1)}, u32[]{:S(2)}, u32[]{:S(2)}) collective-permute-start(f32[144,128]{1,0:T(8,128)S(1)} %add.12), channel_id=1, source_target_pairs={{0,4},{4,0},{8,12},{12,8},{1,5},{5,1},{9,13},{13,9},{2,6},{6,2},{1... | collective-permute-start | bytes 221192 | tf_op jit(solution)/shard_map/ppermute | solution.py:476
  50.7 4.4 %collective-permute-start.9 = (f32[144,128]{1,0:T(8,128)S(1)}, f32[144,128]{1,0:T(8,128)S(1)}, u32[]{:S(2)}, u32[]{:S(2)}) collective-permute-start(f32[144,128]{1,0:T(8,128)S(1)} %add_add_fusion), channel_id=1, source_target_pairs={{0,2},{1,3},{2,0},{3,1},{4,6},{5,7},{6,4},{7,5},{8,10},{9,11},{10,... | collective-permute-start | bytes 221192 | tf_op jit(solution)/shard_map/ppermute | solution.py:476
  55.2 1.4 %collective-permute-start.10 = (f32[288,128]{1,0:T(8,128)S(1)}, f32[288,128]{1,0:T(8,128)S(1)}, u32[]{:S(2)}, u32[]{:S(2)}) collective-permute-start(f32[288,128]{1,0:T(8,128)S(1)} %pad_maximum_fusion.1), channel_id=1, source_target_pairs={{0,1},{1,0},{2,3},{3,2},{4,5},{5,4},{6,7},{7,6},{8,9},{9,8},{10,11... | collective-permute-start | bytes 442376 | tf_op jit(solution)/shard_map/ppermute | solution.py:476

commit v11 on v10

--- a/solution.py
+++ b/solution.py
@@ -13,7 +13,7 @@
 
 WIDE = 4
 LANES = 128
-PART = 8
+PART = 4
 EARLY = 2
 DEEP = 16
 SHALLOW = 8

time: 57.5 us -> 57.6 us (level)
  Pallas kernels: 28 us -> 28.6 us
  transfers between devices with their start and end apart: 11 -> 11, of which waited for: 9 -> 7; matrix products, arithmetic and copies ran while one was open for 0% -> 0% of each run, Pallas kernels for 9% -> 10%
where the time goes in v11:
time: 57.6 us; the launch traced here: 57.4 us
  Pallas kernels  28.6 us (50%)
  starting transfers between devices  14 us (24%)
  waiting for transfers between devices  14 us (24%)
  between operations  0.73 us (1%)
    pallas_call x1, Pallas kernels, body(): pl.pallas_call(functools.partial(main_kernel, bands), out_shape=(field, f...  20.4 us
    ppermute x7, waiting for transfers between devices, swapped(): lax.ppermute(value, axis, [(i, i ^ bit) for i in range(lax.axis_size(axis...  13.7 us
    ppermute x7, starting transfers between devices, swapped(): lax.ppermute(value, axis, [(i, i ^ bit) for i in range(lax.axis_size(axis...  7.06 us
    ppermute x4, starting transfers between devices, along(): lax.ppermute(value, axis, [(i, (i + step) % count) for i in range(count)])  6.96 us
    pallas_call x2, Pallas kernels, early(): pl.pallas_call(functools.partial(early_kernel, k * tall), out_shape=(kept...  3.87 us
    pallas_call x1, Pallas kernels, body(): pl.pallas_call(late_kernel, out_shape=(field, field, half_terms(bands)[0]...  1.82 us
    pallas_call x1, Pallas kernels, body(): pl.pallas_call(pack_kernel, out_shape=(strip, strip, edge, edge, jax.Shap...  1.74 us
  transfers between devices with their start and end apart: 11, of which 7 were waited for; matrix products, arithmetic and copies ran while one was open for 0% of the time, Pallas kernels for 10%

profile of v11, /device:TPU:0, one launch (start us, length us, event | category | flops | bytes accessed | tf_op | source)
XLA Modules:
  0.0 57.4 jit_solution(6431037132194487415)
XLA Ops:
  0.6 1.7 %shard_map.144 = (f32[64,128]{1,0:T(8,128)S(1)}, f32[64,128]{1,0:T(8,128)S(1)}, f32[21,4,128]{2,1,0:T(4,128)S(1)}, f32[21,4,128]{2,1,0:T(4,128)S(1)}, f32[21,64,...) custom-call(f32[4,64,128]{2,1,0:T(8,128)} %now.1, ...), custom_call_target="tpu_custom_call" | custom-call | tf_op jit(solution)/shard_map/pallas_call | solution.py:516
  2.4 3.1 %collective-permute-start = (f32[64,128]{1,0:T(8,128)S(1)}, f32[64,128]{1,0:T(8,128)S(1)}, u32[]{:S(2)}, u32[]{:S(2)}) collective-permute-start(f32[64,128]{1,0:T(8,128)S(1)} %get-tuple-element.47), channel_id=1, source_target_pairs={{0,4},{4,8},{8,12},{12,0},{1,5},{5,9},{9,13},{13,1},{2,6},{6,10},{... | collective-permute-start | bytes 98312 | tf_op jit(solution)/shard_map/ppermute | solution.py:472
  5.5 2.1 %collective-permute-start.1 = (f32[64,128]{1,0:T(8,128)S(1)}, f32[64,128]{1,0:T(8,128)S(1)}, u32[]{:S(2)}, u32[]{:S(2)}) collective-permute-start(f32[64,128]{1,0:T(8,128)S(1)} %get-tuple-element.48), channel_id=1, source_target_pairs={{0,12},{4,0},{8,4},{12,8},{1,13},{5,1},{9,5},{13,9},{2,14},{6,2},{... | collective-permute-start | bytes 98312 | tf_op jit(solution)/shard_map/ppermute | solution.py:472
  7.6 2.0 %shard_map.146 = (f32[8,256,512]{2,1,0:T(8,128)S(1)}, f32[8,256,512]{2,1,0:T(8,128)S(1)}, f32[256,128]{1,0:T(8,128)S(1)}, bf16[16,256]{1,0:T(8,128)(2,1)S(1)}, b...) custom-call(f32[21,64,128]{2,1,0:T(8,128)S(1)} %get-tuple-element.46, ...), custom_call_target="tpu_custom_call" | custom-call | flops 1610612736 | tf_op jit(solution)/shard_map/pallas_call | solution.py:532
  9.5 0.0 collective-permute-done.left.refs_0_.refs_1_
  9.5 0.2 collective-permute-done.1.right.refs_2_
  9.7 0.1 collective-permute-start.2
  9.8 1.7 %collective-permute-start.3 = (f32[23,4,128]{2,1,0:T(4,128)S(1)}, f32[23,4,128]{2,1,0:T(4,128)S(1)}, u32[]{:S(2)}, u32[]{:S(2)}) collective-permute-start(f32[23,4,128]{2,1,0:T(4,128)S(1)} %get-tuple-element.52), channel_id=1, source_target_pairs={{0,3},{1,0},{2,1},{3,2},{4,7},{5,4},{6,5},{7,6},{8,11},{9,8},{10,9... | collective-permute-start | bytes 141320 | tf_op jit(solution)/shard_map/ppermute | solution.py:472
  11.5 1.9 %shard_map.147 = (f32[8,256,512]{2,1,0:T(8,128)S(1)}, f32[8,256,512]{2,1,0:T(8,128)S(1)}, f32[256,128]{1,0:T(8,128)S(1)}) custom-call(f32[21,64,128]{2,1,0:T(8,128)S(1)} %get-tuple-element.46.fields.refs_0_, f32[64,128]{1,0:T(8,128)S(1)} %collective-permute-done.left.refs_0_.refs_1_, bf16[256,16]{1,0:T(8,128)(2,1)S(1)} %get-tuple-element.57.refs_1_.refs_6_, ...), custom_call_target="tpu_custom_call" | custom-call | flops 1610612736 | tf_op jit(solution)/shard_map/pallas_call | solution.py:532
  13.5 0.0 collective-permute-done.2.refs_3_
  13.5 0.0 collective-permute-done.3.refs_4_
  13.5 20.4 %shard_map.148 = (f32[4,64,128]{2,1,0:T(8,128)}, f32[4,64,128]{2,1,0:T(8,128)}, f32[288,128]{1,0:T(8,128)S(1)}, f32[288,128]{1,0:T(8,128)S(1)}, f32[21,72,256]{2...) custom-call(f32[21,64,128]{2,1,0:T(8,128)S(1)} %get-tuple-element.46, ...), custom_call_target="tpu_custom_call" | custom-call | tf_op jit(solution)/shard_map/pallas_call | solution.py:575
  33.9 1.5 %collective-permute-start.4 = (f32[288,128]{1,0:T(8,128)S(1)}, f32[288,128]{1,0:T(8,128)S(1)}, u32[]{:S(2)}, u32[]{:S(2)}) collective-permute-start(f32[288,128]{1,0:T(8,128)S(1)} %get-tuple-element.74), channel_id=1, source_target_pairs={{0,1},{1,0},{2,3},{3,2},{4,5},{5,4},{6,7},{7,6},{8,9},{9,8},{10,11... | collective-permute-start | bytes 442376 | tf_op jit(solution)/shard_map/ppermute | solution.py:476
  35.4 1.0 %collective-permute-done.4.got = f32[288,128]{1,0:T(8,128)S(1)} collective-permute-done((f32[288,128]{1,0:T(8,128)S(1)}, f32[288,128]{1,0:T(8,128)S(1)}, u32[]{:S(2)}, u32[]{:S(2)}) %collective-permute-start.4) | collective-permute-done | bytes 147488 | tf_op jit(solution)/shard_map/ppermute | solution.py:476
  36.4 0.6 %collective-permute-start.5 = (f32[144,128]{1,0:T(8,128)S(1)}, f32[144,128]{1,0:T(8,128)S(1)}, u32[]{:S(2)}, u32[]{:S(2)}) collective-permute-start(f32[144,128]{1,0:T(8,128)S(1)} %get-tuple-element.81), channel_id=1, source_target_pairs={{0,2},{1,3},{2,0},{3,1},{4,6},{5,7},{6,4},{7,5},{8,10},{9,11},{10,... | collective-permute-start | bytes 221192 | tf_op jit(solution)/shard_map/ppermute | solution.py:476
  37.0 1.8 %shard_map.150 = (f32[4,64,128]{2,1,0:T(8,128)}, f32[4,64,128]{2,1,0:T(8,128)}, f32[144,128]{1,0:T(8,128)S(1)}, s32[8,128]{1,0:T(8,128)S(1)}) custom-call(f32[21,64,128]{2,1,0:T(8,128)S(1)} %get-tuple-element.46.fields.refs_0_, f32[21,72,256]{2,1,0:T(8,128)S(1)} %get-tuple-element.68.planes, f32[4,72,256]{2,1,0:T(8,128)S(1)} %get-tuple-element.69.mids, ...), custom_call_target="tpu_custom_call" | custom-call | flops 1073741824 | tf_op jit(solution)/shard_map/pallas_call | solution.py:613
  38.8 2.2 %collective-permute-done.5 = f32[144,128]{1,0:T(8,128)S(1)} collective-permute-done((f32[144,128]{1,0:T(8,128)S(1)}, f32[144,128]{1,0:T(8,128)S(1)}, u32[]{:S(2)}, u32[]{:S(2)}) %collective-permute-start.5) | collective-permute-done | bytes 73760 | tf_op jit(solution)/shard_map/ppermute | solution.py:476
  41.0 3.8 %collective-permute-start.8 = (f32[144,128]{1,0:T(8,128)S(1)}, f32[144,128]{1,0:T(8,128)S(1)}, u32[]{:S(2)}, u32[]{:S(2)}) collective-permute-start(f32[144,128]{1,0:T(8,128)S(1)} %add.12), channel_id=1, source_target_pairs={{0,12},{4,8},{8,4},{12,0},{1,13},{5,9},{9,5},{13,1},{2,14},{6,10},... | collective-permute-start | bytes 221192 | tf_op jit(solution)/shard_map/ppermute | solution.py:476
  44.8 0.0 collective-permute-start.7
  44.8 0.7 %collective-permute-start.6 = (f32[144,128]{1,0:T(8,128)S(1)}, f32[144,128]{1,0:T(8,128)S(1)}, u32[]{:S(2)}, u32[]{:S(2)}) collective-permute-start(f32[144,128]{1,0:T(8,128)S(1)} %add.12), channel_id=1, source_target_pairs={{0,4},{4,0},{8,12},{12,8},{1,5},{5,1},{9,13},{13,9},{2,6},{6,2},{1... | collective-permute-start | bytes 221192 | tf_op jit(solution)/shard_map/ppermute | solution.py:476
  45.5 2.4 %collective-permute-done.8 = f32[144,128]{1,0:T(8,128)S(1)} collective-permute-done((f32[144,128]{1,0:T(8,128)S(1)}, f32[144,128]{1,0:T(8,128)S(1)}, u32[]{:S(2)}, u32[]{:S(2)}) %collective-permute-start.8) | collective-permute-done | bytes 73760 | tf_op jit(solution)/shard_map/ppermute | solution.py:476
  47.8 2.9 %collective-permute-done.7 = f32[144,128]{1,0:T(8,128)S(1)} collective-permute-done((f32[144,128]{1,0:T(8,128)S(1)}, f32[144,128]{1,0:T(8,128)S(1)}, u32[]{:S(2)}, u32[]{:S(2)}) %collective-permute-start.7) | collective-permute-done | bytes 73760 | tf_op jit(solution)/shard_map/ppermute | solution.py:476
  50.7 0.0 collective-permute-done.6
  50.7 0.4 collective-permute-start.9
  51.2 4.0 %collective-permute-done.9 = f32[144,128]{1,0:T(8,128)S(1)} collective-permute-done((f32[144,128]{1,0:T(8,128)S(1)}, f32[144,128]{1,0:T(8,128)S(1)}, u32[]{:S(2)}, u32[]{:S(2)}) %collective-permute-start.9) | collective-permute-done | bytes 73760 | tf_op jit(solution)/shard_map/ppermute | solution.py:476
  55.2 0.1 collective-permute-start.10
  55.3 1.4 %collective-permute-done.10 = f32[288,128]{1,0:T(8,128)S(1)} collective-permute-done((f32[288,128]{1,0:T(8,128)S(1)}, f32[288,128]{1,0:T(8,128)S(1)}, u32[]{:S(2)}, u32[]{:S(2)}) %collective-permute-start.10) | collective-permute-done | bytes 147488 | tf_op jit(solution)/shard_map/ppermute | solution.py:476
  56.7 0.7 %shard_map.151 = (f32[12,256]{1,0:T(8,128)}, f32[256,256]{1,0:T(8,128)}, f32[4,256]{1,0:T(4,128)}) custom-call(f32[576,128]{1,0:T(8,128)S(1)} %pad_maximum_fusion.terms), custom_call_target="tpu_custom_call" | custom-call | tf_op jit(solution)/shard_map/pallas_call | solution.py:626
  (9 shorter events, 0.1 us)
Async XLA Ops:
  2.4 7.1 %collective-permute-start = (f32[64,128]{1,0:T(8,128)S(1)}, f32[64,128]{1,0:T(8,128)S(1)}, u32[]{:S(2)}, u32[]{:S(2)}) collective-permute-start(f32[64,128]{1,0:T(8,128)S(1)} %get-tuple-element.47), channel_id=1, source_target_pairs={{0,4},{4,8},{8,12},{12,0},{1,5},{5,9},{9,13},{13,1},{2,6},{6,10},{... | collective-permute-start | bytes 98312 | tf_op jit(solution)/shard_map/ppermute | solution.py:472
  5.5 4.3 %collective-permute-start.1 = (f32[64,128]{1,0:T(8,128)S(1)}, f32[64,128]{1,0:T(8,128)S(1)}, u32[]{:S(2)}, u32[]{:S(2)}) collective-permute-start(f32[64,128]{1,0:T(8,128)S(1)} %get-tuple-element.48), channel_id=1, source_target_pairs={{0,12},{4,0},{8,4},{12,8},{1,13},{5,1},{9,5},{13,9},{2,14},{6,2},{... | collective-permute-start | bytes 98312 | tf_op jit(solution)/shard_map/ppermute | solution.py:472
  9.7 3.7 %collective-permute-start.2 = (f32[23,4,128]{2,1,0:T(4,128)S(1)}, f32[23,4,128]{2,1,0:T(4,128)S(1)}, u32[]{:S(2)}, u32[]{:S(2)}) collective-permute-start(f32[23,4,128]{2,1,0:T(4,128)S(1)} %get-tuple-element.51), channel_id=1, source_target_pairs={{0,1},{1,2},{2,3},{3,0},{4,5},{5,6},{6,7},{7,4},{8,9},{9,10},{10,1... | collective-permute-start | bytes 141320 | tf_op jit(solution)/shard_map/ppermute | solution.py:472
  9.8 3.7 %collective-permute-start.3 = (f32[23,4,128]{2,1,0:T(4,128)S(1)}, f32[23,4,128]{2,1,0:T(4,128)S(1)}, u32[]{:S(2)}, u32[]{:S(2)}) collective-permute-start(f32[23,4,128]{2,1,0:T(4,128)S(1)} %get-tuple-element.52), channel_id=1, source_target_pairs={{0,3},{1,0},{2,1},{3,2},{4,7},{5,4},{6,5},{7,6},{8,11},{9,8},{10,9... | collective-permute-start | bytes 141320 | tf_op jit(solution)/shard_map/ppermute | solution.py:472
  33.9 2.5 %collective-permute-start.4 = (f32[288,128]{1,0:T(8,128)S(1)}, f32[288,128]{1,0:T(8,128)S(1)}, u32[]{:S(2)}, u32[]{:S(2)}) collective-permute-start(f32[288,128]{1,0:T(8,128)S(1)} %get-tuple-element.74), channel_id=1, source_target_pairs={{0,1},{1,0},{2,3},{3,2},{4,5},{5,4},{6,7},{7,6},{8,9},{9,8},{10,11... | collective-permute-start | bytes 442376 | tf_op jit(solution)/shard_map/ppermute | solution.py:476
  36.4 4.6 %collective-permute-start.5 = (f32[144,128]{1,0:T(8,128)S(1)}, f32[144,128]{1,0:T(8,128)S(1)}, u32[]{:S(2)}, u32[]{:S(2)}) collective-permute-start(f32[144,128]{1,0:T(8,128)S(1)} %get-tuple-element.81), channel_id=1, source_target_pairs={{0,2},{1,3},{2,0},{3,1},{4,6},{5,7},{6,4},{7,5},{8,10},{9,11},{10,... | collective-permute-start | bytes 221192 | tf_op jit(solution)/shard_map/ppermute | solution.py:476
  41.0 6.8 %collective-permute-start.8 = (f32[144,128]{1,0:T(8,128)S(1)}, f32[144,128]{1,0:T(8,128)S(1)}, u32[]{:S(2)}, u32[]{:S(2)}) collective-permute-start(f32[144,128]{1,0:T(8,128)S(1)} %add.12), channel_id=1, source_target_pairs={{0,12},{4,8},{8,4},{12,0},{1,13},{5,9},{9,5},{13,1},{2,14},{6,10},... | collective-permute-start | bytes 221192 | tf_op jit(solution)/shard_map/ppermute | solution.py:476
  44.8 5.9 %collective-permute-start.7 = (f32[144,128]{1,0:T(8,128)S(1)}, f32[144,128]{1,0:T(8,128)S(1)}, u32[]{:S(2)}, u32[]{:S(2)}) collective-permute-start(f32[144,128]{1,0:T(8,128)S(1)} %add.12), channel_id=1, source_target_pairs={{0,8},{4,12},{8,0},{12,4},{1,9},{5,13},{9,1},{13,5},{2,10},{6,14},... | collective-permute-start | bytes 221192 | tf_op jit(solution)/shard_map/ppermute | solution.py:476
  44.8 5.9 %collective-permute-start.6 = (f32[144,128]{1,0:T(8,128)S(1)}, f32[144,128]{1,0:T(8,128)S(1)}, u32[]{:S(2)}, u32[]{:S(2)}) collective-permute-start(f32[144,128]{1,0:T(8,128)S(1)} %add.12), channel_id=1, source_target_pairs={{0,4},{4,0},{8,12},{12,8},{1,5},{5,1},{9,13},{13,9},{2,6},{6,2},{1... | collective-permute-start | bytes 221192 | tf_op jit(solution)/shard_map/ppermute | solution.py:476
  50.7 4.4 %collective-permute-start.9 = (f32[144,128]{1,0:T(8,128)S(1)}, f32[144,128]{1,0:T(8,128)S(1)}, u32[]{:S(2)}, u32[]{:S(2)}) collective-permute-start(f32[144,128]{1,0:T(8,128)S(1)} %add_add_fusion), channel_id=1, source_target_pairs={{0,2},{1,3},{2,0},{3,1},{4,6},{5,7},{6,4},{7,5},{8,10},{9,11},{10,... | collective-permute-start | bytes 221192 | tf_op jit(solution)/shard_map/ppermute | solution.py:476
  55.2 1.4 %collective-permute-start.10 = (f32[288,128]{1,0:T(8,128)S(1)}, f32[288,128]{1,0:T(8,128)S(1)}, u32[]{:S(2)}, u32[]{:S(2)}) collective-permute-start(f32[288,128]{1,0:T(8,128)S(1)} %pad_maximum_fusion.1), channel_id=1, source_target_pairs={{0,1},{1,0},{2,3},{3,2},{4,5},{5,4},{6,7},{7,6},{8,9},{9,8},{10,11... | collective-permute-start | bytes 442376 | tf_op jit(solution)/shard_map/ppermute | solution.py:476

commit v12 on v10

--- a/solution.py
+++ b/solution.py
@@ -429,17 +429,34 @@
     kept[...] = jnp.where(upper, value[half:], value[:half])
 
 
-def halve_kernel(bit, held, got, sent, kept):
-    halve(held[...] + got[...], bit, sent, kept)
+def quarter_of(ref, place):
+    rows = ref.shape[0] // 4
+    return ref.at[pl.ds(pl.multiple_of(place * rows, 8), rows)]
+
+
+def deal_kernel(held, got, own, *refs):
+    sent, total = refs[:-1], refs[-1]
+    total[...] = held[...] + got[...]
+    place = lax.axis_index("lon") & 3
+    own[...] = quarter_of(total, place)[...]
+    for k, ref in enumerate(sent):
+        ref[...] = quarter_of(total, place ^ (k + 1))[...]
+
+
+def collect_kernel(own, *refs):
+    got, whole = refs[:-1], refs[-1]
+    place = lax.axis_index("lon") & 3
+    quarter_of(whole, place)[...] = own[...]
+    for k, ref in enumerate(got):
+        quarter_of(whole, place ^ (k + 1))[...] = ref[...]
 
 
 def late_kernel(
-    fields, planes, mids, olds, cl, gradients, held, h_new, h_now, o_held, o_place, o_new, o_now, sems, df, dfh, dfx
+    fields, planes, mids, olds, cl, gradients, held, h_new, h_now, o_held, o_new, o_now, sems, df, dfh, dfx
 ):
     levels, rows, cols = o_new.shape
     block = Block(levels, rows)
     o_held[...] = held[...]
-    o_place[...] = jnp.zeros_like(o_place) + lax.axis_index("lat")
     df[...] = gradients[...]
     beside = jnp.zeros((rows, LANES), F32)
     beyond = jnp.zeros((2 * WIDE, 2 * LANES), F32)
@@ -458,12 +475,16 @@
         copy.wait()
 
 
-def scale_kernel(factor, terms, g_in, g_mid, g_out):
+def scale_kernel(factor, mine, other, g_in, g_mid, g_out, terms):
+    half = mine.shape[0]
+    upper = (lax.axis_index("lat") & 1) != 0
+    terms[pl.ds(0, half), :] = jnp.where(upper, other[...], mine[...]) * factor
+    terms[pl.ds(half, half), :] = jnp.where(upper, mine[...], other[...]) * factor
     hidden = g_mid.shape[0]
     start = 0
     for ref, deep in ((g_mid, hidden), (g_in, DEEP), (g_out, DEEP)):
         for half in range(hidden // LANES):
-            ref[:, half * LANES : (half + 1) * LANES] = terms[pl.ds(start, ref.shape[0]), :] * factor
+            ref[:, half * LANES : (half + 1) * LANES] = terms[pl.ds(start, ref.shape[0]), :]
             start += deep
 
 
@@ -476,8 +497,7 @@
     return lax.ppermute(value, axis, [(i, i ^ bit) for i in range(lax.axis_size(axis))])
 
 
-def added_up(value, axis):
-    bit = 1
+def added_up(value, axis, bit):
     while bit < lax.axis_size(axis):
         near = swapped(value, axis, bit)
         if 2 * bit < lax.axis_size(axis):
@@ -486,16 +506,6 @@
         else:
             value = value + near
             bit *= 2
-    return value
-
-
-def put_together(value, place, axis):
-    bit = lax.axis_size(axis) // 2
-    while bit:
-        upper = (place & bit) != 0
-        other = swapped(value, axis, bit)
-        value = jnp.concatenate([jnp.where(upper, other, value), jnp.where(upper, value, other)], 0)
-        bit //= 2
     return value
 
 
@@ -560,7 +570,7 @@
 
     bands = lax.axis_size("lat")
     halves = hidden // LANES
-    terms_rows = -(-halves * (hidden + 2 * DEEP) // (8 * bands)) * 8 * bands
+    terms_rows = -(-halves * (hidden + 2 * DEEP) // 64) * 64
     field = jax.ShapeDtypeStruct((levels, rows, cols), F32)
     ext_planes = jax.ShapeDtypeStruct((levels, ext, 2 * LANES), F32)
     staged = pltpu.VMEM((levels, rows, cols), F32)
@@ -568,13 +578,13 @@
     def tiles(deep):
         return [pltpu.VMEM((n * deep, LANES), F32) for n in (slots, 16 * packs, 2 * WIDE)]
 
-    def half_terms(parts):
-        return (jax.ShapeDtypeStruct((terms_rows // parts, LANES), F32),) * 2
+    half = jax.ShapeDtypeStruct((terms_rows // 2, LANES), F32)
+    eighth = jax.ShapeDtypeStruct((terms_rows // 8, LANES), F32)
 
     kept_halo = pltpu.VMEM((hidden, (8 + packs) * LANES), F32)
     state_mid, grad_old, sent, held, planes, mids, olds, closures, gradients = pl.pallas_call(
         functools.partial(main_kernel, bands),
-        out_shape=(field, field, *half_terms(2))
+        out_shape=(field, field, half, half)
         + (jax.ShapeDtypeStruct((count, ext, 2 * LANES), F32), ext_planes, ext_planes)
         + tuple(jax.ShapeDtypeStruct((slots * deep, LANES), F32) for deep in (SHALLOW, DEEP)),
         in_specs=[vmem] * (11 + 3 * EARLY),
@@ -598,30 +608,37 @@
         compiler_params=pltpu.CompilerParams(vmem_limit_bytes=32 * 2**20),
     )(fields, left, right, low, high, wi, wi_t, wm_t, weights[1], wo, wo_t, *done)
 
-    bit = 1
-    while 2 * bit < bands:
-        got = swapped(sent, "lat", bit)
-        bit *= 2
-        sent, held = pl.pallas_call(
-            functools.partial(halve_kernel, bit),
-            out_shape=half_terms(2 * bit),
-            in_specs=[vmem] * 2,
-            out_specs=(vmem,) * 2,
-            compiler_params=pltpu.CompilerParams(vmem_limit_bytes=4 * 2**20),
-        )(held, got)
-    got = swapped(sent, "lat", bit)
-    state_new, grad_now, held, place = pl.pallas_call(
+    got = swapped(sent, "lat", 1)
+    own, *quarters = pl.pallas_call(
+        deal_kernel,
+        out_shape=(eighth,) * 4,
+        in_specs=[vmem] * 2,
+        out_specs=(vmem,) * 4,
+        scratch_shapes=[pltpu.VMEM(half.shape, F32)],
+        compiler_params=pltpu.CompilerParams(vmem_limit_bytes=4 * 2**20),
+    )(held, got)
+    got = [swapped(quarter, "lon", k + 1) for k, quarter in enumerate(quarters)]
+    state_new, grad_now, own = pl.pallas_call(
         late_kernel,
-        out_shape=(field, field, half_terms(bands)[0], jax.ShapeDtypeStruct((8, LANES), jnp.int32)),
+        out_shape=(field, field, eighth),
         in_specs=[vmem] * 7,
-        out_specs=(hbm,) * 2 + (vmem,) * 2,
+        out_specs=(hbm,) * 2 + (vmem,),
         scratch_shapes=[staged, staged, pltpu.SemaphoreType.DMA((2,)), *tiles(DEEP)],
         compiler_params=pltpu.CompilerParams(vmem_limit_bytes=16 * 2**20),
         cost_estimate=pl.CostEstimate(
             flops=2 * hidden * hidden * rows * cols, bytes_accessed=0, transcendentals=0
         ),
-    )(fields, planes, mids, olds, closures, gradients, held)
-    summed = put_together(added_up(held + got, "lon"), place[:1], "lat")
+    )(fields, planes, mids, olds, closures, gradients, own)
+    own = (own + got[0]) + (got[1] + got[2])
+    own = added_up(added_up(own, "lat", 2), "lon", 4)
+    mine = pl.pallas_call(
+        collect_kernel,
+        out_shape=half,
+        in_specs=[vmem] * 4,
+        out_specs=vmem,
+        compiler_params=pltpu.CompilerParams(vmem_limit_bytes=4 * 2**20),
+    )(own, *(swapped(own, "lon", k) for k in (1, 2, 3)))
+    other = swapped(mine, "lat", 1)
     cells_all = rows * lax.axis_size("lat") * cols * lax.axis_size("lon")
     grad_in, grad_mid, grad_out = pl.pallas_call(
         functools.partial(scale_kernel, GAIN_GRAD / cells_all**0.5),
@@ -630,10 +647,11 @@
             jax.ShapeDtypeStruct((hidden, hidden), F32),
             jax.ShapeDtypeStruct((levels, hidden), F32),
         ),
-        in_specs=[vmem],
+        in_specs=[vmem] * 2,
         out_specs=(vmem,) * 3,
+        scratch_shapes=[pltpu.VMEM((terms_rows, LANES), F32)],
         compiler_params=pltpu.CompilerParams(vmem_limit_bytes=8 * 2**20),
-    )(summed)
+    )(mine, other)
     return state_mid, state_new, grad_old, grad_now, grad_in, grad_mid, grad_out.T
 
 

time: 57.5 us -> 59.2 us (1.030)
  starting transfers between devices: 14.2 us -> 18 us
  waiting for transfers between devices: 14.3 us -> 12.3 us
    ppermute x7 -> x9, starting transfers between devices: 7.27 us -> 11 us  [swapped(): lax.ppermute(value, axis, [(i, i ^ bit) for i in range(lax.axis_size(axis...]
    ppermute x7 -> x9, waiting for transfers between devices: 13.7 us -> 11.7 us  [swapped(): lax.ppermute(value, axis, [(i, i ^ bit) for i in range(lax.axis_size(axis...]
    pallas_call x2 -> x3, Pallas kernels: 1.84 us -> 1.86 us  [the longest x1 1.82 us: body(): pl.pallas_call(late_kernel, out_shape=(field, field, eighth), in_specs=[v...]
  transfers between devices with their start and end apart: 11 -> 13, of which waited for: 9 -> 10; matrix products, arithmetic and copies ran while one was open for 0% -> 0% of each run, Pallas kernels for 9% -> 9%
where the time goes in v12:
time: 59.2 us; the launch traced here: 59 us
  Pallas kernels  28.1 us (47%)
  starting transfers between devices  18 us (30%)
  waiting for transfers between devices  12.3 us (21%)
  between operations  0.71 us (1%)
    pallas_call x1, Pallas kernels, body(): pl.pallas_call(functools.partial(main_kernel, bands), out_shape=(field, f...  20.4 us
    ppermute x9, waiting for transfers between devices, swapped(): lax.ppermute(value, axis, [(i, i ^ bit) for i in range(lax.axis_size(axis...  11.7 us
    ppermute x9, starting transfers between devices, swapped(): lax.ppermute(value, axis, [(i, i ^ bit) for i in range(lax.axis_size(axis...  11 us
    ppermute x4, starting transfers between devices, along(): lax.ppermute(value, axis, [(i, (i + step) % count) for i in range(count)])  6.96 us
    pallas_call x2, Pallas kernels, early(): pl.pallas_call(functools.partial(early_kernel, k * tall), out_shape=(kept...  3.36 us
    pallas_call x1, Pallas kernels, body(): pl.pallas_call(late_kernel, out_shape=(field, field, eighth), in_specs=[v...  1.82 us
    pallas_call x1, Pallas kernels, body(): pl.pallas_call(pack_kernel, out_shape=(strip, strip, edge, edge, jax.Shap...  1.74 us
  transfers between devices with their start and end apart: 13, of which 10 were waited for; matrix products, arithmetic and copies ran while one was open for 0% of the time, Pallas kernels for 9%

profile of v12, /device:TPU:0, one launch (start us, length us, event | category | flops | bytes accessed | tf_op | source)
XLA Modules:
  0.0 59.0 jit_solution(10297922083741715182)
XLA Ops:
  0.6 1.7 %shard_map.144 = (f32[64,128]{1,0:T(8,128)S(1)}, f32[64,128]{1,0:T(8,128)S(1)}, f32[21,4,128]{2,1,0:T(4,128)S(1)}, f32[21,4,128]{2,1,0:T(4,128)S(1)}, f32[21,64,...) custom-call(f32[4,64,128]{2,1,0:T(8,128)} %now.1, ...), custom_call_target="tpu_custom_call" | custom-call | tf_op jit(solution)/shard_map/pallas_call | solution.py:526
  2.4 3.1 %collective-permute-start = (f32[64,128]{1,0:T(8,128)S(1)}, f32[64,128]{1,0:T(8,128)S(1)}, u32[]{:S(2)}, u32[]{:S(2)}) collective-permute-start(f32[64,128]{1,0:T(8,128)S(1)} %get-tuple-element.48), channel_id=1, source_target_pairs={{0,4},{4,8},{8,12},{12,0},{1,5},{5,9},{9,13},{13,1},{2,6},{6,10},{... | collective-permute-start | bytes 98312 | tf_op jit(solution)/shard_map/ppermute | solution.py:493
  5.5 2.1 %collective-permute-start.1 = (f32[64,128]{1,0:T(8,128)S(1)}, f32[64,128]{1,0:T(8,128)S(1)}, u32[]{:S(2)}, u32[]{:S(2)}) collective-permute-start(f32[64,128]{1,0:T(8,128)S(1)} %get-tuple-element.49), channel_id=1, source_target_pairs={{0,12},{4,0},{8,4},{12,8},{1,13},{5,1},{9,5},{13,9},{2,14},{6,2},{... | collective-permute-start | bytes 98312 | tf_op jit(solution)/shard_map/ppermute | solution.py:493
  7.6 1.7 %shard_map.146 = (f32[4,256,1024]{2,1,0:T(8,128)S(1)}, f32[4,256,1024]{2,1,0:T(8,128)S(1)}, f32[256,128]{1,0:T(8,128)S(1)}, bf16[16,256]{1,0:T(8,128)(2,1)S(1)},...) custom-call(f32[21,64,128]{2,1,0:T(8,128)S(1)} %get-tuple-element.47, ...), custom_call_target="tpu_custom_call" | custom-call | flops 1610612736 | tf_op jit(solution)/shard_map/pallas_call | solution.py:542
  9.3 0.2 collective-permute-done.left.refs_0_.refs_1_
  9.5 0.2 collective-permute-done.1.right.refs_2_
  9.7 0.1 collective-permute-start.2
  9.8 1.7 %collective-permute-start.3 = (f32[23,4,128]{2,1,0:T(4,128)S(1)}, f32[23,4,128]{2,1,0:T(4,128)S(1)}, u32[]{:S(2)}, u32[]{:S(2)}) collective-permute-start(f32[23,4,128]{2,1,0:T(4,128)S(1)} %get-tuple-element.53), channel_id=1, source_target_pairs={{0,3},{1,0},{2,1},{3,2},{4,7},{5,4},{6,5},{7,6},{8,11},{9,8},{10,9... | collective-permute-start | bytes 141320 | tf_op jit(solution)/shard_map/ppermute | solution.py:493
  11.5 1.6 %shard_map.147 = (f32[4,256,1024]{2,1,0:T(8,128)S(1)}, f32[4,256,1024]{2,1,0:T(8,128)S(1)}, f32[256,128]{1,0:T(8,128)S(1)}) custom-call(f32[21,64,128]{2,1,0:T(8,128)S(1)} %get-tuple-element.47.fields.refs_0_, f32[64,128]{1,0:T(8,128)S(1)} %collective-permute-done.left.refs_0_.refs_1_, bf16[256,16]{1,0:T(8,128)(2,1)S(1)} %get-tuple-element.58.refs_1_.refs_6_, ...), custom_call_target="tpu_custom_call" | custom-call | flops 1610612736 | tf_op jit(solution)/shard_map/pallas_call | solution.py:542
  13.2 0.1 collective-permute-done.2.refs_3_
  13.3 0.0 collective-permute-done.3.refs_4_
  13.3 20.4 %shard_map.148 = (f32[4,64,128]{2,1,0:T(8,128)}, f32[4,64,128]{2,1,0:T(8,128)}, f32[288,128]{1,0:T(8,128)S(1)}, f32[288,128]{1,0:T(8,128)S(1)}, f32[21,72,256]{2...) custom-call(f32[21,64,128]{2,1,0:T(8,128)S(1)} %get-tuple-element.47, ...), custom_call_target="tpu_custom_call" | custom-call | tf_op jit(solution)/shard_map/pallas_call | solution.py:585
  33.7 1.7 %collective-permute-start.4 = (f32[288,128]{1,0:T(8,128)S(1)}, f32[288,128]{1,0:T(8,128)S(1)}, u32[]{:S(2)}, u32[]{:S(2)}) collective-permute-start(f32[288,128]{1,0:T(8,128)S(1)} %get-tuple-element.75), channel_id=1, source_target_pairs={{0,1},{1,0},{2,3},{3,2},{4,5},{5,4},{6,7},{7,6},{8,9},{9,8},{10,11... | collective-permute-start | bytes 442376 | tf_op jit(solution)/shard_map/ppermute | solution.py:497
  35.3 1.0 %collective-permute-done.4.got = f32[288,128]{1,0:T(8,128)S(1)} collective-permute-done((f32[288,128]{1,0:T(8,128)S(1)}, f32[288,128]{1,0:T(8,128)S(1)}, u32[]{:S(2)}, u32[]{:S(2)}) %collective-permute-start.4) | collective-permute-done | bytes 147488 | tf_op jit(solution)/shard_map/ppermute | solution.py:497
  36.4 1.3 %collective-permute-start.5 = (f32[72,128]{1,0:T(8,128)S(1)}, f32[72,128]{1,0:T(8,128)S(1)}, u32[]{:S(2)}, u32[]{:S(2)}) collective-permute-start(f32[72,128]{1,0:T(8,128)S(1)} %get-tuple-element.81), channel_id=1, source_target_pairs={{0,4},{4,0},{8,12},{12,8},{1,5},{5,1},{9,13},{13,9},{2,6},{6,2},{1... | collective-permute-start | bytes 110600 | tf_op jit(solution)/shard_map/ppermute | solution.py:497
  37.7 3.0 %collective-permute-start.6 = (f32[72,128]{1,0:T(8,128)S(1)}, f32[72,128]{1,0:T(8,128)S(1)}, u32[]{:S(2)}, u32[]{:S(2)}) collective-permute-start(f32[72,128]{1,0:T(8,128)S(1)} %get-tuple-element.82), channel_id=1, source_target_pairs={{0,8},{4,12},{8,0},{12,4},{1,9},{5,13},{9,1},{13,5},{2,10},{6,14},... | collective-permute-start | bytes 110600 | tf_op jit(solution)/shard_map/ppermute | solution.py:497
  40.7 0.1 collective-permute-start.7
  40.8 1.8 %shard_map.150 = (f32[4,64,128]{2,1,0:T(8,128)}, f32[4,64,128]{2,1,0:T(8,128)}, f32[72,128]{1,0:T(8,128)S(1)}) custom-call(f32[21,64,128]{2,1,0:T(8,128)S(1)} %get-tuple-element.47.fields.refs_0_, f32[21,72,256]{2,1,0:T(8,128)S(1)} %get-tuple-element.69.planes, f32[4,72,256]{2,1,0:T(8,128)S(1)} %get-tuple-element.70.mids, ...), custom_call_target="tpu_custom_call" | custom-call | flops 1073741824 | tf_op jit(solution)/shard_map/pallas_call | solution.py:621
  42.7 0.0 collective-permute-done.5
  42.7 0.7 %collective-permute-done.6 = f32[72,128]{1,0:T(8,128)S(1)} collective-permute-done((f32[72,128]{1,0:T(8,128)S(1)}, f32[72,128]{1,0:T(8,128)S(1)}, u32[]{:S(2)}, u32[]{:S(2)}) %collective-permute-start.6) | collective-permute-done | bytes 36896 | tf_op jit(solution)/shard_map/ppermute | solution.py:497
  43.4 3.1 %collective-permute-done.7 = f32[72,128]{1,0:T(8,128)S(1)} collective-permute-done((f32[72,128]{1,0:T(8,128)S(1)}, f32[72,128]{1,0:T(8,128)S(1)}, u32[]{:S(2)}, u32[]{:S(2)}) %collective-permute-start.7) | collective-permute-done | bytes 36896 | tf_op jit(solution)/shard_map/ppermute | solution.py:497
  46.5 0.4 collective-permute-start.8
  46.9 3.6 %collective-permute-done.8 = f32[72,128]{1,0:T(8,128)S(1)} collective-permute-done((f32[72,128]{1,0:T(8,128)S(1)}, f32[72,128]{1,0:T(8,128)S(1)}, u32[]{:S(2)}, u32[]{:S(2)}) %collective-permute-start.8) | collective-permute-done | bytes 36896 | tf_op jit(solution)/shard_map/ppermute | solution.py:497
  50.5 0.5 collective-permute-start.11
  51.0 0.0 collective-permute-start.10
  51.0 3.9 %collective-permute-start.9 = (f32[72,128]{1,0:T(8,128)S(1)}, f32[72,128]{1,0:T(8,128)S(1)}, u32[]{:S(2)}, u32[]{:S(2)}) collective-permute-start(f32[72,128]{1,0:T(8,128)S(1)} %add.15.own), channel_id=1, source_target_pairs={{0,4},{4,0},{8,12},{12,8},{1,5},{5,1},{9,13},{13,9},{2,6},{6,2},{1... | collective-permute-start | bytes 110600 | tf_op jit(solution)/shard_map/ppermute | solution.py:497
  54.9 1.4 %collective-permute-done.11.refs_2_ = f32[72,128]{1,0:T(8,128)S(1)} collective-permute-done((f32[72,128]{1,0:T(8,128)S(1)}, f32[72,128]{1,0:T(8,128)S(1)}, u32[]{:S(2)}, u32[]{:S(2)}) %collective-permute-start.11) | collective-permute-done | bytes 36896 | tf_op jit(solution)/shard_map/ppermute | solution.py:497
  56.3 0.0 collective-permute-done.10.refs_1_
  56.3 0.6 collective-permute-done.9.refs_0_
  56.9 0.1 collective-permute-start.12
  56.9 1.4 %collective-permute-done.12.other = f32[288,128]{1,0:T(8,128)S(1)} collective-permute-done((f32[288,128]{1,0:T(8,128)S(1)}, f32[288,128]{1,0:T(8,128)S(1)}, u32[]{:S(2)}, u32[]{:S(2)}) %collective-permute-start.12) | collective-permute-done | bytes 147488 | tf_op jit(solution)/shard_map/ppermute | solution.py:497
  58.3 0.7 %shard_map.152 = (f32[12,256]{1,0:T(8,128)}, f32[256,256]{1,0:T(8,128)}, f32[4,256]{1,0:T(4,128)}) custom-call(f32[288,128]{1,0:T(8,128)S(1)} %shard_map.151.mine, f32[288,128]{1,0:T(8,128)S(1)} %collective-permute-done.12.other), custom_call_target="tpu_custom_call" | custom-call | tf_op jit(solution)/shard_map/pallas_call | solution.py:643
  (5 shorter events, 0.1 us)
Async XLA Ops:
  2.4 7.1 %collective-permute-start = (f32[64,128]{1,0:T(8,128)S(1)}, f32[64,128]{1,0:T(8,128)S(1)}, u32[]{:S(2)}, u32[]{:S(2)}) collective-permute-start(f32[64,128]{1,0:T(8,128)S(1)} %get-tuple-element.48), channel_id=1, source_target_pairs={{0,4},{4,8},{8,12},{12,0},{1,5},{5,9},{9,13},{13,1},{2,6},{6,10},{... | collective-permute-start | bytes 98312 | tf_op jit(solution)/shard_map/ppermute | solution.py:493
  5.5 4.3 %collective-permute-start.1 = (f32[64,128]{1,0:T(8,128)S(1)}, f32[64,128]{1,0:T(8,128)S(1)}, u32[]{:S(2)}, u32[]{:S(2)}) collective-permute-start(f32[64,128]{1,0:T(8,128)S(1)} %get-tuple-element.49), channel_id=1, source_target_pairs={{0,12},{4,0},{8,4},{12,8},{1,13},{5,1},{9,5},{13,9},{2,14},{6,2},{... | collective-permute-start | bytes 98312 | tf_op jit(solution)/shard_map/ppermute | solution.py:493
  9.7 3.5 %collective-permute-start.2 = (f32[23,4,128]{2,1,0:T(4,128)S(1)}, f32[23,4,128]{2,1,0:T(4,128)S(1)}, u32[]{:S(2)}, u32[]{:S(2)}) collective-permute-start(f32[23,4,128]{2,1,0:T(4,128)S(1)} %get-tuple-element.52), channel_id=1, source_target_pairs={{0,1},{1,2},{2,3},{3,0},{4,5},{5,6},{6,7},{7,4},{8,9},{9,10},{10,1... | collective-permute-start | bytes 141320 | tf_op jit(solution)/shard_map/ppermute | solution.py:493
  9.8 3.5 %collective-permute-start.3 = (f32[23,4,128]{2,1,0:T(4,128)S(1)}, f32[23,4,128]{2,1,0:T(4,128)S(1)}, u32[]{:S(2)}, u32[]{:S(2)}) collective-permute-start(f32[23,4,128]{2,1,0:T(4,128)S(1)} %get-tuple-element.53), channel_id=1, source_target_pairs={{0,3},{1,0},{2,1},{3,2},{4,7},{5,4},{6,5},{7,6},{8,11},{9,8},{10,9... | collective-permute-start | bytes 141320 | tf_op jit(solution)/shard_map/ppermute | solution.py:493
  33.7 2.7 %collective-permute-start.4 = (f32[288,128]{1,0:T(8,128)S(1)}, f32[288,128]{1,0:T(8,128)S(1)}, u32[]{:S(2)}, u32[]{:S(2)}) collective-permute-start(f32[288,128]{1,0:T(8,128)S(1)} %get-tuple-element.75), channel_id=1, source_target_pairs={{0,1},{1,0},{2,3},{3,2},{4,5},{5,4},{6,7},{7,6},{8,9},{9,8},{10,11... | collective-permute-start | bytes 442376 | tf_op jit(solution)/shard_map/ppermute | solution.py:497
  36.4 6.3 %collective-permute-start.5 = (f32[72,128]{1,0:T(8,128)S(1)}, f32[72,128]{1,0:T(8,128)S(1)}, u32[]{:S(2)}, u32[]{:S(2)}) collective-permute-start(f32[72,128]{1,0:T(8,128)S(1)} %get-tuple-element.81), channel_id=1, source_target_pairs={{0,4},{4,0},{8,12},{12,8},{1,5},{5,1},{9,13},{13,9},{2,6},{6,2},{1... | collective-permute-start | bytes 110600 | tf_op jit(solution)/shard_map/ppermute | solution.py:497
  37.7 5.7 %collective-permute-start.6 = (f32[72,128]{1,0:T(8,128)S(1)}, f32[72,128]{1,0:T(8,128)S(1)}, u32[]{:S(2)}, u32[]{:S(2)}) collective-permute-start(f32[72,128]{1,0:T(8,128)S(1)} %get-tuple-element.82), channel_id=1, source_target_pairs={{0,8},{4,12},{8,0},{12,4},{1,9},{5,13},{9,1},{13,5},{2,10},{6,14},... | collective-permute-start | bytes 110600 | tf_op jit(solution)/shard_map/ppermute | solution.py:497
  40.7 5.8 %collective-permute-start.7 = (f32[72,128]{1,0:T(8,128)S(1)}, f32[72,128]{1,0:T(8,128)S(1)}, u32[]{:S(2)}, u32[]{:S(2)}) collective-permute-start(f32[72,128]{1,0:T(8,128)S(1)} %get-tuple-element.83), channel_id=1, source_target_pairs={{0,12},{4,8},{8,4},{12,0},{1,13},{5,9},{9,5},{13,1},{2,14},{6,10},... | collective-permute-start | bytes 110600 | tf_op jit(solution)/shard_map/ppermute | solution.py:497
  46.5 4.0 %collective-permute-start.8 = (f32[72,128]{1,0:T(8,128)S(1)}, f32[72,128]{1,0:T(8,128)S(1)}, u32[]{:S(2)}, u32[]{:S(2)}) collective-permute-start(f32[72,128]{1,0:T(8,128)S(1)} %add_add_fusion), channel_id=1, source_target_pairs={{0,2},{1,3},{2,0},{3,1},{4,6},{5,7},{6,4},{7,5},{8,10},{9,11},{10,... | collective-permute-start | bytes 110600 | tf_op jit(solution)/shard_map/ppermute | solution.py:497
  50.5 5.8 %collective-permute-start.11 = (f32[72,128]{1,0:T(8,128)S(1)}, f32[72,128]{1,0:T(8,128)S(1)}, u32[]{:S(2)}, u32[]{:S(2)}) collective-permute-start(f32[72,128]{1,0:T(8,128)S(1)} %add.15.own), channel_id=1, source_target_pairs={{0,12},{4,8},{8,4},{12,0},{1,13},{5,9},{9,5},{13,1},{2,14},{6,10},... | collective-permute-start | bytes 110600 | tf_op jit(solution)/shard_map/ppermute | solution.py:497
  51.0 5.3 %collective-permute-start.10 = (f32[72,128]{1,0:T(8,128)S(1)}, f32[72,128]{1,0:T(8,128)S(1)}, u32[]{:S(2)}, u32[]{:S(2)}) collective-permute-start(f32[72,128]{1,0:T(8,128)S(1)} %add.15.own), channel_id=1, source_target_pairs={{0,8},{4,12},{8,0},{12,4},{1,9},{5,13},{9,1},{13,5},{2,10},{6,14},... | collective-permute-start | bytes 110600 | tf_op jit(solution)/shard_map/ppermute | solution.py:497
  51.0 5.9 %collective-permute-start.9 = (f32[72,128]{1,0:T(8,128)S(1)}, f32[72,128]{1,0:T(8,128)S(1)}, u32[]{:S(2)}, u32[]{:S(2)}) collective-permute-start(f32[72,128]{1,0:T(8,128)S(1)} %add.15.own), channel_id=1, source_target_pairs={{0,4},{4,0},{8,12},{12,8},{1,5},{5,1},{9,13},{13,9},{2,6},{6,2},{1... | collective-permute-start | bytes 110600 | tf_op jit(solution)/shard_map/ppermute | solution.py:497
  56.9 1.4 %collective-permute-start.12 = (f32[288,128]{1,0:T(8,128)S(1)}, f32[288,128]{1,0:T(8,128)S(1)}, u32[]{:S(2)}, u32[]{:S(2)}) collective-permute-start(f32[288,128]{1,0:T(8,128)S(1)} %shard_map.151.mine), channel_id=1, source_target_pairs={{0,1},{1,0},{2,3},{3,2},{4,5},{5,4},{6,7},{7,6},{8,9},{9,8},{10,11... | collective-permute-start | bytes 442376 | tf_op jit(solution)/shard_map/ppermute | solution.py:497

commit v13 on v10

--- a/solution.py
+++ b/solution.py
@@ -14,6 +14,7 @@
 WIDE = 4
 LANES = 128
 PART = 8
+DEFERRED = 3
 EARLY = 2
 DEEP = 16
 SHALLOW = 8
@@ -307,7 +308,7 @@
         yield
         return dz_one, dz_two
 
-    def second_part(base, tiles, sums):
+    def second_part(base, tiles, sums, later):
         x = inputs_at(ft2, base, tiles)
         cot = cotangents_at(base, tiles)
         first, second, low_first, low_second = yield from forward_stages(x, wi_t, wm_t)
@@ -316,8 +317,11 @@
             put_lanes(cl, SHALLOW, base, tiles, closure(low_second, wo_t))
         dz_one, dz_two = yield from backward_stages(first, second, cot)
         dfeat = feature_gradients(dz_one, wi)
-        if sums is not None:
-            add_terms(sums, (low_first, dz_two), (x, dz_one), (low_second, cot))
+        pairs = (low_first, dz_two), (x, dz_one), (low_second, cot)
+        if later is not None:
+            later.append(pairs)
+        elif sums is not None:
+            add_terms(sums, *pairs)
         yield
         put_lanes(df, DEEP, base, tiles, dfeat)
 
@@ -356,7 +360,14 @@
         yield
         put_lanes(cl, SHALLOW, base, tiles, closure(low_second, wo_t))
 
-    staggered([first_part(rows, len(block.rim))])
+    def second_cotangents():
+        for level in range(levels):
+            masked = planes[block.wet] * (2.0 * DT * planes[3 * levels + level])
+            block.spread(masked, level, SHALLOW, dc, dcx, dch, False)
+            yield
+        block.pack_halo(block.outer, SHALLOW, dc, dcx, dch)
+
+    staggered([first_part(rows, len(block.rim)), second_cotangents()])
     block.unpack_halo(block.rim, SHALLOW, cl, clx, clh)
     for level in range(levels):
         closed = block.gathered(level, SHALLOW, cl, clx, clh, True)
@@ -366,37 +377,48 @@
     copies = copied_out([(o_mid, h_mid)], sems.at[pl.ds(0, 1)])
 
     features_of(mids, ft2, block.outer, False)
-    for level in range(levels):
-        masked = planes[block.wet] * (2.0 * DT * planes[3 * levels + level])
-        block.spread(masked, level, SHALLOW, dc, dcx, dch, False)
-    block.pack_halo(block.outer, SHALLOW, dc, dcx, dch)
-    sums = [None] * 3
+    sums, later = [None] * 3, []
+    last = rows // PART - DEFERRED
     staggered(
-        [second_part(rows, len(block.outer), None)]
-        + [second_part(k * PART, PART, sums) for k in range(rows // PART)]
+        [second_part(rows, len(block.outer), None, None)]
+        + [second_part(k * PART, PART, sums, None if k < last else later) for k in range(rows // PART)]
     )
-    for acc, total in zip((acc_mid, acc_in, acc_out), sums):
-        acc[...] = total
-    block.unpack_halo(block.outer, DEEP, df, dfx, dfh)
-    for level in range(levels):
-        weighted = 2.0 * DT * planes[3 * levels + level]
-        grad = planes[4 * levels + level] + block.adjoint(planes, weighted, level, (df, dfx, dfh), False)
-        o_old[level] = grad[:rows, :LANES]
-        olds[level] = grad
-    copies += copied_out([(o_old, h_old)], sems.at[pl.ds(1, 1)])
 
     near = block.rim_near
     row = lax.broadcasted_iota(jnp.int32, (ext, LANES), 0)
     inside = (lane > 0) & (lane < LANES - 1) & (row > 0) & (row < rows - 1)
-    for level in range(levels):
-        masked = planes[block.wet] * (2.0 * DT * olds[level])
-        body = masked[:, :LANES]
-        dc[pl.ds(level, rows, stride=SHALLOW), :] = jnp.where(inside, body, 0.0)[:rows]
-        dcx[pl.ds(level, 2 * WIDE, stride=SHALLOW), :] = body[rows:]
-        dch[pl.ds(level, ext, stride=SHALLOW), :] = block.with_rim(masked)
-        for k, r in enumerate(near[:2]):
-            dc[pl.ds((rows + k) * SHALLOW + level, 1), :] = body[r : r + 1]
-    block.pack_halo(near, SHALLOW, dc, dcx, dch, False)
+
+    def second_gradient():
+        block.unpack_halo(block.outer, DEEP, df, dfx, dfh)
+        for level in range(levels):
+            yield
+            weighted = 2.0 * DT * planes[3 * levels + level]
+            grad = planes[4 * levels + level] + block.adjoint(planes, weighted, level, (df, dfx, dfh), False)
+            o_old[level] = grad[:rows, :LANES]
+            olds[level] = grad
+            masked = planes[block.wet] * (2.0 * DT * grad)
+            body = masked[:, :LANES]
+            dc[pl.ds(level, rows, stride=SHALLOW), :] = jnp.where(inside, body, 0.0)[:rows]
+            dcx[pl.ds(level, 2 * WIDE, stride=SHALLOW), :] = body[rows:]
+            dch[pl.ds(level, ext, stride=SHALLOW), :] = block.with_rim(masked)
+            for k, r in enumerate(near[:2]):
+                dc[pl.ds((rows + k) * SHALLOW + level, 1), :] = body[r : r + 1]
+        yield
+        block.pack_halo(near, SHALLOW, dc, dcx, dch, False)
+
+    def deferred_terms():
+        for pairs in later:
+            for k, pair in enumerate(pairs):
+                sums[k] = sums[k] + dot_nt(*pair)
+                if k == 0:
+                    yield
+            yield
+
+    staggered([second_gradient(), deferred_terms()])
+    for acc, total in zip((acc_mid, acc_in, acc_out), sums):
+        acc[...] = total
+    copies += copied_out([(o_old, h_old)], sems.at[pl.ds(1, 1)])
+
     at = lax.broadcasted_iota(jnp.int32, (1, len(near) * LANES), 1)
     tile, place = at >> 7, at & (LANES - 1)
     side_row = (tile - 4) * 16 + (place >> 3)

time: 57.5 us -> 57.4 us (level)
  no operation moved by 1% of the time
where the time goes in v13:
time: 57.4 us; the launch traced here: 57.3 us
  Pallas kernels  27.9 us (49%)
  waiting for transfers between devices  14.3 us (25%)
  starting transfers between devices  14.2 us (25%)
  between operations  0.72 us (1%)
    pallas_call x1, Pallas kernels, body(): pl.pallas_call(functools.partial(main_kernel, bands), out_shape=(field, f...  20.3 us
    ppermute x7, waiting for transfers between devices, swapped(): lax.ppermute(value, axis, [(i, i ^ bit) for i in range(lax.axis_size(axis...  13.7 us
    ppermute x7, starting transfers between devices, swapped(): lax.ppermute(value, axis, [(i, i ^ bit) for i in range(lax.axis_size(axis...  7.25 us
    ppermute x4, starting transfers between devices, along(): lax.ppermute(value, axis, [(i, (i + step) % count) for i in range(count)])  6.96 us
    pallas_call x2, Pallas kernels, early(): pl.pallas_call(functools.partial(early_kernel, k * tall), out_shape=(kept...  3.36 us
    pallas_call x1, Pallas kernels, body(): pl.pallas_call(late_kernel, out_shape=(field, field, half_terms(bands)[0]...  1.82 us
    pallas_call x1, Pallas kernels, body(): pl.pallas_call(pack_kernel, out_shape=(strip, strip, edge, edge, jax.Shap...  1.74 us
  transfers between devices with their start and end apart: 11, of which 9 were waited for; matrix products, arithmetic and copies ran while one was open for 0% of the time, Pallas kernels for 9%

profile of v13, /device:TPU:0, one launch (start us, length us, event | category | flops | bytes accessed | tf_op | source)
XLA Modules:
  0.0 57.3 jit_solution(16526188824261276085)
XLA Ops:
  0.6 1.7 %shard_map.144 = (f32[64,128]{1,0:T(8,128)S(1)}, f32[64,128]{1,0:T(8,128)S(1)}, f32[21,4,128]{2,1,0:T(4,128)S(1)}, f32[21,4,128]{2,1,0:T(4,128)S(1)}, f32[21,64,...) custom-call(f32[4,64,128]{2,1,0:T(8,128)} %now.1, ...), custom_call_target="tpu_custom_call" | custom-call | tf_op jit(solution)/shard_map/pallas_call | solution.py:538
  2.4 3.1 %collective-permute-start = (f32[64,128]{1,0:T(8,128)S(1)}, f32[64,128]{1,0:T(8,128)S(1)}, u32[]{:S(2)}, u32[]{:S(2)}) collective-permute-start(f32[64,128]{1,0:T(8,128)S(1)} %get-tuple-element.47), channel_id=1, source_target_pairs={{0,4},{4,8},{8,12},{12,0},{1,5},{5,9},{9,13},{13,1},{2,6},{6,10},{... | collective-permute-start | bytes 98312 | tf_op jit(solution)/shard_map/ppermute | solution.py:494
  5.5 2.1 %collective-permute-start.1 = (f32[64,128]{1,0:T(8,128)S(1)}, f32[64,128]{1,0:T(8,128)S(1)}, u32[]{:S(2)}, u32[]{:S(2)}) collective-permute-start(f32[64,128]{1,0:T(8,128)S(1)} %get-tuple-element.48), channel_id=1, source_target_pairs={{0,12},{4,0},{8,4},{12,8},{1,13},{5,1},{9,5},{13,9},{2,14},{6,2},{... | collective-permute-start | bytes 98312 | tf_op jit(solution)/shard_map/ppermute | solution.py:494
  7.6 1.7 %shard_map.146 = (f32[4,256,1024]{2,1,0:T(8,128)S(1)}, f32[4,256,1024]{2,1,0:T(8,128)S(1)}, f32[256,128]{1,0:T(8,128)S(1)}, bf16[16,256]{1,0:T(8,128)(2,1)S(1)},...) custom-call(f32[21,64,128]{2,1,0:T(8,128)S(1)} %get-tuple-element.46, ...), custom_call_target="tpu_custom_call" | custom-call | flops 1610612736 | tf_op jit(solution)/shard_map/pallas_call | solution.py:554
  9.3 0.2 collective-permute-done.left.refs_0_.refs_1_
  9.5 0.2 collective-permute-done.1.right.refs_2_
  9.7 0.1 collective-permute-start.2
  9.8 1.7 %collective-permute-start.3 = (f32[23,4,128]{2,1,0:T(4,128)S(1)}, f32[23,4,128]{2,1,0:T(4,128)S(1)}, u32[]{:S(2)}, u32[]{:S(2)}) collective-permute-start(f32[23,4,128]{2,1,0:T(4,128)S(1)} %get-tuple-element.52), channel_id=1, source_target_pairs={{0,3},{1,0},{2,1},{3,2},{4,7},{5,4},{6,5},{7,6},{8,11},{9,8},{10,9... | collective-permute-start | bytes 141320 | tf_op jit(solution)/shard_map/ppermute | solution.py:494
  11.5 1.6 %shard_map.147 = (f32[4,256,1024]{2,1,0:T(8,128)S(1)}, f32[4,256,1024]{2,1,0:T(8,128)S(1)}, f32[256,128]{1,0:T(8,128)S(1)}) custom-call(f32[21,64,128]{2,1,0:T(8,128)S(1)} %get-tuple-element.46.fields.refs_0_, f32[64,128]{1,0:T(8,128)S(1)} %collective-permute-done.left.refs_0_.refs_1_, bf16[256,16]{1,0:T(8,128)(2,1)S(1)} %get-tuple-element.57.refs_1_.refs_6_, ...), custom_call_target="tpu_custom_call" | custom-call | flops 1610612736 | tf_op jit(solution)/shard_map/pallas_call | solution.py:554
  13.2 0.1 collective-permute-done.2.refs_3_
  13.3 0.0 collective-permute-done.3.refs_4_
  13.3 20.3 %shard_map.148 = (f32[4,64,128]{2,1,0:T(8,128)}, f32[4,64,128]{2,1,0:T(8,128)}, f32[288,128]{1,0:T(8,128)S(1)}, f32[288,128]{1,0:T(8,128)S(1)}, f32[21,72,256]{2...) custom-call(f32[21,64,128]{2,1,0:T(8,128)S(1)} %get-tuple-element.46, ...), custom_call_target="tpu_custom_call" | custom-call | tf_op jit(solution)/shard_map/pallas_call | solution.py:597
  33.5 1.7 %collective-permute-start.4 = (f32[288,128]{1,0:T(8,128)S(1)}, f32[288,128]{1,0:T(8,128)S(1)}, u32[]{:S(2)}, u32[]{:S(2)}) collective-permute-start(f32[288,128]{1,0:T(8,128)S(1)} %get-tuple-element.74), channel_id=1, source_target_pairs={{0,1},{1,0},{2,3},{3,2},{4,5},{5,4},{6,7},{7,6},{8,9},{9,8},{10,11... | collective-permute-start | bytes 442376 | tf_op jit(solution)/shard_map/ppermute | solution.py:498
  35.2 1.0 %collective-permute-done.4.got = f32[288,128]{1,0:T(8,128)S(1)} collective-permute-done((f32[288,128]{1,0:T(8,128)S(1)}, f32[288,128]{1,0:T(8,128)S(1)}, u32[]{:S(2)}, u32[]{:S(2)}) %collective-permute-start.4) | collective-permute-done | bytes 147488 | tf_op jit(solution)/shard_map/ppermute | solution.py:498
  36.3 0.6 %collective-permute-start.5 = (f32[144,128]{1,0:T(8,128)S(1)}, f32[144,128]{1,0:T(8,128)S(1)}, u32[]{:S(2)}, u32[]{:S(2)}) collective-permute-start(f32[144,128]{1,0:T(8,128)S(1)} %get-tuple-element.81), channel_id=1, source_target_pairs={{0,2},{1,3},{2,0},{3,1},{4,6},{5,7},{6,4},{7,5},{8,10},{9,11},{10,... | collective-permute-start | bytes 221192 | tf_op jit(solution)/shard_map/ppermute | solution.py:498
  36.9 1.8 %shard_map.150 = (f32[4,64,128]{2,1,0:T(8,128)}, f32[4,64,128]{2,1,0:T(8,128)}, f32[144,128]{1,0:T(8,128)S(1)}, s32[8,128]{1,0:T(8,128)S(1)}) custom-call(f32[21,64,128]{2,1,0:T(8,128)S(1)} %get-tuple-element.46.fields.refs_0_, f32[21,72,256]{2,1,0:T(8,128)S(1)} %get-tuple-element.68.planes, f32[4,72,256]{2,1,0:T(8,128)S(1)} %get-tuple-element.69.mids, ...), custom_call_target="tpu_custom_call" | custom-call | flops 1073741824 | tf_op jit(solution)/shard_map/pallas_call | solution.py:635
  38.7 2.2 %collective-permute-done.5 = f32[144,128]{1,0:T(8,128)S(1)} collective-permute-done((f32[144,128]{1,0:T(8,128)S(1)}, f32[144,128]{1,0:T(8,128)S(1)}, u32[]{:S(2)}, u32[]{:S(2)}) %collective-permute-start.5) | collective-permute-done | bytes 73760 | tf_op jit(solution)/shard_map/ppermute | solution.py:498
  40.9 3.8 %collective-permute-start.8 = (f32[144,128]{1,0:T(8,128)S(1)}, f32[144,128]{1,0:T(8,128)S(1)}, u32[]{:S(2)}, u32[]{:S(2)}) collective-permute-start(f32[144,128]{1,0:T(8,128)S(1)} %add.12), channel_id=1, source_target_pairs={{0,12},{4,8},{8,4},{12,0},{1,13},{5,9},{9,5},{13,1},{2,14},{6,10},... | collective-permute-start | bytes 221192 | tf_op jit(solution)/shard_map/ppermute | solution.py:498
  44.6 0.0 collective-permute-start.7
  44.6 0.7 %collective-permute-start.6 = (f32[144,128]{1,0:T(8,128)S(1)}, f32[144,128]{1,0:T(8,128)S(1)}, u32[]{:S(2)}, u32[]{:S(2)}) collective-permute-start(f32[144,128]{1,0:T(8,128)S(1)} %add.12), channel_id=1, source_target_pairs={{0,4},{4,0},{8,12},{12,8},{1,5},{5,1},{9,13},{13,9},{2,6},{6,2},{1... | collective-permute-start | bytes 221192 | tf_op jit(solution)/shard_map/ppermute | solution.py:498
  45.3 2.3 %collective-permute-done.8 = f32[144,128]{1,0:T(8,128)S(1)} collective-permute-done((f32[144,128]{1,0:T(8,128)S(1)}, f32[144,128]{1,0:T(8,128)S(1)}, u32[]{:S(2)}, u32[]{:S(2)}) %collective-permute-start.8) | collective-permute-done | bytes 73760 | tf_op jit(solution)/shard_map/ppermute | solution.py:498
  47.7 2.9 %collective-permute-done.7 = f32[144,128]{1,0:T(8,128)S(1)} collective-permute-done((f32[144,128]{1,0:T(8,128)S(1)}, f32[144,128]{1,0:T(8,128)S(1)}, u32[]{:S(2)}, u32[]{:S(2)}) %collective-permute-start.7) | collective-permute-done | bytes 73760 | tf_op jit(solution)/shard_map/ppermute | solution.py:498
  50.6 0.0 collective-permute-done.6
  50.6 0.4 collective-permute-start.9
  51.0 4.0 %collective-permute-done.9 = f32[144,128]{1,0:T(8,128)S(1)} collective-permute-done((f32[144,128]{1,0:T(8,128)S(1)}, f32[144,128]{1,0:T(8,128)S(1)}, u32[]{:S(2)}, u32[]{:S(2)}) %collective-permute-start.9) | collective-permute-done | bytes 73760 | tf_op jit(solution)/shard_map/ppermute | solution.py:498
  55.0 0.1 collective-permute-start.10
  55.1 1.4 %collective-permute-done.10 = f32[288,128]{1,0:T(8,128)S(1)} collective-permute-done((f32[288,128]{1,0:T(8,128)S(1)}, f32[288,128]{1,0:T(8,128)S(1)}, u32[]{:S(2)}, u32[]{:S(2)}) %collective-permute-start.10) | collective-permute-done | bytes 147488 | tf_op jit(solution)/shard_map/ppermute | solution.py:498
  56.5 0.7 %shard_map.151 = (f32[12,256]{1,0:T(8,128)}, f32[256,256]{1,0:T(8,128)}, f32[4,256]{1,0:T(4,128)}) custom-call(f32[576,128]{1,0:T(8,128)S(1)} %pad_maximum_fusion.terms), custom_call_target="tpu_custom_call" | custom-call | tf_op jit(solution)/shard_map/pallas_call | solution.py:648
  (9 shorter events, 0.1 us)
Async XLA Ops:
  2.4 7.1 %collective-permute-start = (f32[64,128]{1,0:T(8,128)S(1)}, f32[64,128]{1,0:T(8,128)S(1)}, u32[]{:S(2)}, u32[]{:S(2)}) collective-permute-start(f32[64,128]{1,0:T(8,128)S(1)} %get-tuple-element.47), channel_id=1, source_target_pairs={{0,4},{4,8},{8,12},{12,0},{1,5},{5,9},{9,13},{13,1},{2,6},{6,10},{... | collective-permute-start | bytes 98312 | tf_op jit(solution)/shard_map/ppermute | solution.py:494
  5.5 4.3 %collective-permute-start.1 = (f32[64,128]{1,0:T(8,128)S(1)}, f32[64,128]{1,0:T(8,128)S(1)}, u32[]{:S(2)}, u32[]{:S(2)}) collective-permute-start(f32[64,128]{1,0:T(8,128)S(1)} %get-tuple-element.48), channel_id=1, source_target_pairs={{0,12},{4,0},{8,4},{12,8},{1,13},{5,1},{9,5},{13,9},{2,14},{6,2},{... | collective-permute-start | bytes 98312 | tf_op jit(solution)/shard_map/ppermute | solution.py:494
  9.7 3.5 %collective-permute-start.2 = (f32[23,4,128]{2,1,0:T(4,128)S(1)}, f32[23,4,128]{2,1,0:T(4,128)S(1)}, u32[]{:S(2)}, u32[]{:S(2)}) collective-permute-start(f32[23,4,128]{2,1,0:T(4,128)S(1)} %get-tuple-element.51), channel_id=1, source_target_pairs={{0,1},{1,2},{2,3},{3,0},{4,5},{5,6},{6,7},{7,4},{8,9},{9,10},{10,1... | collective-permute-start | bytes 141320 | tf_op jit(solution)/shard_map/ppermute | solution.py:494
  9.8 3.5 %collective-permute-start.3 = (f32[23,4,128]{2,1,0:T(4,128)S(1)}, f32[23,4,128]{2,1,0:T(4,128)S(1)}, u32[]{:S(2)}, u32[]{:S(2)}) collective-permute-start(f32[23,4,128]{2,1,0:T(4,128)S(1)} %get-tuple-element.52), channel_id=1, source_target_pairs={{0,3},{1,0},{2,1},{3,2},{4,7},{5,4},{6,5},{7,6},{8,11},{9,8},{10,9... | collective-permute-start | bytes 141320 | tf_op jit(solution)/shard_map/ppermute | solution.py:494
  33.5 2.7 %collective-permute-start.4 = (f32[288,128]{1,0:T(8,128)S(1)}, f32[288,128]{1,0:T(8,128)S(1)}, u32[]{:S(2)}, u32[]{:S(2)}) collective-permute-start(f32[288,128]{1,0:T(8,128)S(1)} %get-tuple-element.74), channel_id=1, source_target_pairs={{0,1},{1,0},{2,3},{3,2},{4,5},{5,4},{6,7},{7,6},{8,9},{9,8},{10,11... | collective-permute-start | bytes 442376 | tf_op jit(solution)/shard_map/ppermute | solution.py:498
  36.3 4.6 %collective-permute-start.5 = (f32[144,128]{1,0:T(8,128)S(1)}, f32[144,128]{1,0:T(8,128)S(1)}, u32[]{:S(2)}, u32[]{:S(2)}) collective-permute-start(f32[144,128]{1,0:T(8,128)S(1)} %get-tuple-element.81), channel_id=1, source_target_pairs={{0,2},{1,3},{2,0},{3,1},{4,6},{5,7},{6,4},{7,5},{8,10},{9,11},{10,... | collective-permute-start | bytes 221192 | tf_op jit(solution)/shard_map/ppermute | solution.py:498
  40.9 6.8 %collective-permute-start.8 = (f32[144,128]{1,0:T(8,128)S(1)}, f32[144,128]{1,0:T(8,128)S(1)}, u32[]{:S(2)}, u32[]{:S(2)}) collective-permute-start(f32[144,128]{1,0:T(8,128)S(1)} %add.12), channel_id=1, source_target_pairs={{0,12},{4,8},{8,4},{12,0},{1,13},{5,9},{9,5},{13,1},{2,14},{6,10},... | collective-permute-start | bytes 221192 | tf_op jit(solution)/shard_map/ppermute | solution.py:498
  44.6 5.9 %collective-permute-start.7 = (f32[144,128]{1,0:T(8,128)S(1)}, f32[144,128]{1,0:T(8,128)S(1)}, u32[]{:S(2)}, u32[]{:S(2)}) collective-permute-start(f32[144,128]{1,0:T(8,128)S(1)} %add.12), channel_id=1, source_target_pairs={{0,8},{4,12},{8,0},{12,4},{1,9},{5,13},{9,1},{13,5},{2,10},{6,14},... | collective-permute-start | bytes 221192 | tf_op jit(solution)/shard_map/ppermute | solution.py:498
  44.6 5.9 %collective-permute-start.6 = (f32[144,128]{1,0:T(8,128)S(1)}, f32[144,128]{1,0:T(8,128)S(1)}, u32[]{:S(2)}, u32[]{:S(2)}) collective-permute-start(f32[144,128]{1,0:T(8,128)S(1)} %add.12), channel_id=1, source_target_pairs={{0,4},{4,0},{8,12},{12,8},{1,5},{5,1},{9,13},{13,9},{2,6},{6,2},{1... | collective-permute-start | bytes 221192 | tf_op jit(solution)/shard_map/ppermute | solution.py:498
  50.6 4.4 %collective-permute-start.9 = (f32[144,128]{1,0:T(8,128)S(1)}, f32[144,128]{1,0:T(8,128)S(1)}, u32[]{:S(2)}, u32[]{:S(2)}) collective-permute-start(f32[144,128]{1,0:T(8,128)S(1)} %add_add_fusion), channel_id=1, source_target_pairs={{0,2},{1,3},{2,0},{3,1},{4,6},{5,7},{6,4},{7,5},{8,10},{9,11},{10,... | collective-permute-start | bytes 221192 | tf_op jit(solution)/shard_map/ppermute | solution.py:498
  55.0 1.4 %collective-permute-start.10 = (f32[288,128]{1,0:T(8,128)S(1)}, f32[288,128]{1,0:T(8,128)S(1)}, u32[]{:S(2)}, u32[]{:S(2)}) collective-permute-start(f32[288,128]{1,0:T(8,128)S(1)} %pad_maximum_fusion.1), channel_id=1, source_target_pairs={{0,1},{1,0},{2,3},{3,2},{4,5},{5,4},{6,7},{7,6},{8,9},{9,8},{10,11... | collective-permute-start | bytes 442376 | tf_op jit(solution)/shard_map/ppermute | solution.py:498

commit v14 on v10

--- a/solution.py
+++ b/solution.py
@@ -14,6 +14,7 @@
 WIDE = 4
 LANES = 128
 PART = 8
+ROUNDS = 2
 EARLY = 2
 DEEP = 16
 SHALLOW = 8
@@ -267,8 +268,6 @@
     hidden = w_mid.shape[0]
     block = Block(levels, rows)
     count, ext, lane = block.wet + 1, block.ext, block.lane
-    kept1 = [ref.at[k] for ref in early[0::3] for k in range(ref.shape[0])]
-    kept2 = [ref.at[k] for ref in early[1::3] for k in range(ref.shape[0])]
 
     band = lax.axis_index("lat")
     has_low = jnp.where(band > 0, 1.0, 0.0)
@@ -356,7 +355,14 @@
         yield
         put_lanes(cl, SHALLOW, base, tiles, closure(low_second, wo_t))
 
-    staggered([first_part(rows, len(block.rim))])
+    def second_cotangents():
+        for level in range(levels):
+            masked = planes[block.wet] * (2.0 * DT * planes[3 * levels + level])
+            block.spread(masked, level, SHALLOW, dc, dcx, dch, False)
+            yield
+        block.pack_halo(block.outer, SHALLOW, dc, dcx, dch)
+
+    staggered([first_part(rows, len(block.rim)), second_cotangents()])
     block.unpack_halo(block.rim, SHALLOW, cl, clx, clh)
     for level in range(levels):
         closed = block.gathered(level, SHALLOW, cl, clx, clh, True)
@@ -366,30 +372,38 @@
     copies = copied_out([(o_mid, h_mid)], sems.at[pl.ds(0, 1)])
 
     features_of(mids, ft2, block.outer, False)
-    for level in range(levels):
-        masked = planes[block.wet] * (2.0 * DT * planes[3 * levels + level])
-        block.spread(masked, level, SHALLOW, dc, dcx, dch, False)
-    block.pack_halo(block.outer, SHALLOW, dc, dcx, dch)
-    sums = [None] * 3
-    staggered(
-        [second_part(rows, len(block.outer), None)]
-        + [second_part(k * PART, PART, sums) for k in range(rows // PART)]
-    )
-    for acc, total in zip((acc_mid, acc_in, acc_out), sums):
-        acc[...] = total
+    for acc in (acc_mid, acc_in, acc_out):
+        acc[...] = jnp.zeros_like(acc)
+
+    def keep_terms(sums):
+        for acc, total in zip((acc_mid, acc_in, acc_out), sums):
+            acc[...] += total
+
+    halo_tiles = -(-len(block.outer) // ROUNDS)
+
+    def second_round(c, carry):
+        sums = [None] * 3
+        parts = [c * (rows // PART // ROUNDS) + k for k in range(rows // PART // ROUNDS)]
+        staggered(
+            [second_part(rows + c * halo_tiles, halo_tiles, None)]
+            + [second_part(pl.multiple_of(k * PART, PART), PART, sums) for k in parts]
+        )
+        keep_terms(sums)
+        return carry
+
+    lax.fori_loop(0, ROUNDS, second_round, 0)
+
+    near = block.rim_near
+    row = lax.broadcasted_iota(jnp.int32, (ext, LANES), 0)
+    inside = (lane > 0) & (lane < LANES - 1) & (row > 0) & (row < rows - 1)
+
     block.unpack_halo(block.outer, DEEP, df, dfx, dfh)
     for level in range(levels):
         weighted = 2.0 * DT * planes[3 * levels + level]
         grad = planes[4 * levels + level] + block.adjoint(planes, weighted, level, (df, dfx, dfh), False)
         o_old[level] = grad[:rows, :LANES]
         olds[level] = grad
-    copies += copied_out([(o_old, h_old)], sems.at[pl.ds(1, 1)])
-
-    near = block.rim_near
-    row = lax.broadcasted_iota(jnp.int32, (ext, LANES), 0)
-    inside = (lane > 0) & (lane < LANES - 1) & (row > 0) & (row < rows - 1)
-    for level in range(levels):
-        masked = planes[block.wet] * (2.0 * DT * olds[level])
+        masked = planes[block.wet] * (2.0 * DT * grad)
         body = masked[:, :LANES]
         dc[pl.ds(level, rows, stride=SHALLOW), :] = jnp.where(inside, body, 0.0)[:rows]
         dcx[pl.ds(level, 2 * WIDE, stride=SHALLOW), :] = body[rows:]
@@ -397,20 +411,34 @@
         for k, r in enumerate(near[:2]):
             dc[pl.ds((rows + k) * SHALLOW + level, 1), :] = body[r : r + 1]
     block.pack_halo(near, SHALLOW, dc, dcx, dch, False)
-    at = lax.broadcasted_iota(jnp.int32, (1, len(near) * LANES), 1)
-    tile, place = at >> 7, at & (LANES - 1)
-    side_row = (tile - 4) * 16 + (place >> 3)
+    copies += copied_out([(o_old, h_old)], sems.at[pl.ds(1, 1)])
+
+    at = lax.broadcasted_iota(jnp.int32, (1, halo_tiles * LANES), 1)
+    place = at & (LANES - 1)
     edge = ((place & 7) == 0) | ((place & 7) == 7)
-    counted = (tile < 2) | ((tile >= 4) & edge & (side_row > 0) & (side_row < rows - 1))
-    wide = pl.ds(0, len(near) * LANES)
-    sums = [None] * 3
-    staggered(
-        [third_part(rows, len(near), halo1.at[:, wide], halo2.at[:, wide], counted, sums)]
-        + [third_part(k * PART, PART, kept1[k], kept2[k], None, sums) for k in range(rows // PART)]
-    )
+
+    def third_round(c, carry):
+        tile = (at >> 7) + c * halo_tiles
+        side_row = (tile - 4) * 16 + (place >> 3)
+        counted = (tile < 2) | ((tile >= 4) & edge & (side_row > 0) & (side_row < rows - 1))
+        wide = pl.ds(pl.multiple_of(c * halo_tiles * LANES, LANES), halo_tiles * LANES)
+        sums = [None] * 3
+        parts = [third_part(rows + c * halo_tiles, halo_tiles, halo1.at[:, wide], halo2.at[:, wide], counted, sums)]
+        for e in range(EARLY):
+            held1, held2 = early[3 * e], early[3 * e + 1]
+            share = held1.shape[0]
+            for k in range(share // ROUNDS):
+                own = c * (share // ROUNDS) + k
+                base = pl.multiple_of((e * share + own) * PART, PART)
+                parts.append(third_part(base, PART, held1.at[own], held2.at[own], None, sums))
+        staggered(parts)
+        keep_terms(sums)
+        return carry
+
+    lax.fori_loop(0, ROUNDS, third_round, 0)
 
     start = 0
-    for total in (acc_mid[...] + sums[0], acc_in[...] + sums[1], (acc_out[...] + sums[2]).T):
+    for total in (acc_mid[...], acc_in[...], acc_out[...].T):
         deep = total.shape[0]
         for half in range(hidden // LANES):
             o_grad[pl.ds(start, deep), :] = total[:, half * LANES : (half + 1) * LANES]

time: 57.5 us -> 59.3 us (1.031)
  Pallas kernels: 28 us -> 29.8 us
    pallas_call x1, Pallas kernels: 20.4 us -> 22.2 us  [body(): pl.pallas_call(functools.partial(main_kernel, bands), out_shape=(field, f...]
where the time goes in v14:
time: 59.3 us; the launch traced here: 59.2 us
  Pallas kernels  29.8 us (50%)
  waiting for transfers between devices  14.3 us (24%)
  starting transfers between devices  14.2 us (24%)
  between operations  0.72 us (1%)
    pallas_call x1, Pallas kernels, body(): pl.pallas_call(functools.partial(main_kernel, bands), out_shape=(field, f...  22.2 us
    ppermute x7, waiting for transfers between devices, swapped(): lax.ppermute(value, axis, [(i, i ^ bit) for i in range(lax.axis_size(axis...  13.7 us
    ppermute x7, starting transfers between devices, swapped(): lax.ppermute(value, axis, [(i, i ^ bit) for i in range(lax.axis_size(axis...  7.25 us
    ppermute x4, starting transfers between devices, along(): lax.ppermute(value, axis, [(i, (i + step) % count) for i in range(count)])  6.96 us
    pallas_call x2, Pallas kernels, early(): pl.pallas_call(functools.partial(early_kernel, k * tall), out_shape=(kept...  3.35 us
    pallas_call x1, Pallas kernels, body(): pl.pallas_call(late_kernel, out_shape=(field, field, half_terms(bands)[0]...  1.82 us
    pallas_call x1, Pallas kernels, body(): pl.pallas_call(pack_kernel, out_shape=(strip, strip, edge, edge, jax.Shap...  1.74 us
  transfers between devices with their start and end apart: 11, of which 9 were waited for; matrix products, arithmetic and copies ran while one was open for 0% of the time, Pallas kernels for 9%

profile of v14, /device:TPU:0, one launch (start us, length us, event | category | flops | bytes accessed | tf_op | source)
XLA Modules:
  0.0 59.2 jit_solution(4855015860914568542)
XLA Ops:
  0.6 1.7 %shard_map.144 = (f32[64,128]{1,0:T(8,128)S(1)}, f32[64,128]{1,0:T(8,128)S(1)}, f32[21,4,128]{2,1,0:T(4,128)S(1)}, f32[21,4,128]{2,1,0:T(4,128)S(1)}, f32[21,64,...) custom-call(f32[4,64,128]{2,1,0:T(8,128)} %now.1, ...), custom_call_target="tpu_custom_call" | custom-call | tf_op jit(solution)/shard_map/pallas_call | solution.py:544
  2.4 3.1 %collective-permute-start = (f32[64,128]{1,0:T(8,128)S(1)}, f32[64,128]{1,0:T(8,128)S(1)}, u32[]{:S(2)}, u32[]{:S(2)}) collective-permute-start(f32[64,128]{1,0:T(8,128)S(1)} %get-tuple-element.47), channel_id=1, source_target_pairs={{0,4},{4,8},{8,12},{12,0},{1,5},{5,9},{9,13},{13,1},{2,6},{6,10},{... | collective-permute-start | bytes 98312 | tf_op jit(solution)/shard_map/ppermute | solution.py:500
  5.5 2.1 %collective-permute-start.1 = (f32[64,128]{1,0:T(8,128)S(1)}, f32[64,128]{1,0:T(8,128)S(1)}, u32[]{:S(2)}, u32[]{:S(2)}) collective-permute-start(f32[64,128]{1,0:T(8,128)S(1)} %get-tuple-element.48), channel_id=1, source_target_pairs={{0,12},{4,0},{8,4},{12,8},{1,13},{5,1},{9,5},{13,9},{2,14},{6,2},{... | collective-permute-start | bytes 98312 | tf_op jit(solution)/shard_map/ppermute | solution.py:500
  7.6 1.7 %shard_map.146 = (f32[4,256,1024]{2,1,0:T(8,128)S(1)}, f32[4,256,1024]{2,1,0:T(8,128)S(1)}, f32[256,128]{1,0:T(8,128)S(1)}, bf16[16,256]{1,0:T(8,128)(2,1)S(1)},...) custom-call(f32[21,64,128]{2,1,0:T(8,128)S(1)} %get-tuple-element.46, ...), custom_call_target="tpu_custom_call" | custom-call | flops 1610612736 | tf_op jit(solution)/shard_map/pallas_call | solution.py:560
  9.3 0.2 collective-permute-done.left.refs_0_.refs_1_
  9.5 0.2 collective-permute-done.1.right.refs_2_
  9.7 0.1 collective-permute-start.2
  9.8 1.7 %collective-permute-start.3 = (f32[23,4,128]{2,1,0:T(4,128)S(1)}, f32[23,4,128]{2,1,0:T(4,128)S(1)}, u32[]{:S(2)}, u32[]{:S(2)}) collective-permute-start(f32[23,4,128]{2,1,0:T(4,128)S(1)} %get-tuple-element.52), channel_id=1, source_target_pairs={{0,3},{1,0},{2,1},{3,2},{4,7},{5,4},{6,5},{7,6},{8,11},{9,8},{10,9... | collective-permute-start | bytes 141320 | tf_op jit(solution)/shard_map/ppermute | solution.py:500
  11.5 1.6 %shard_map.147 = (f32[4,256,1024]{2,1,0:T(8,128)S(1)}, f32[4,256,1024]{2,1,0:T(8,128)S(1)}, f32[256,128]{1,0:T(8,128)S(1)}) custom-call(f32[21,64,128]{2,1,0:T(8,128)S(1)} %get-tuple-element.46.fields.refs_0_, f32[64,128]{1,0:T(8,128)S(1)} %collective-permute-done.left.refs_0_.refs_1_, bf16[256,16]{1,0:T(8,128)(2,1)S(1)} %get-tuple-element.57.refs_1_.refs_6_, ...), custom_call_target="tpu_custom_call" | custom-call | flops 1610612736 | tf_op jit(solution)/shard_map/pallas_call | solution.py:560
  13.2 0.1 collective-permute-done.2.refs_3_
  13.3 0.0 collective-permute-done.3.refs_4_
  13.3 22.2 %shard_map.148 = (f32[4,64,128]{2,1,0:T(8,128)}, f32[4,64,128]{2,1,0:T(8,128)}, f32[288,128]{1,0:T(8,128)S(1)}, f32[288,128]{1,0:T(8,128)S(1)}, f32[21,72,256]{2...) custom-call(f32[21,64,128]{2,1,0:T(8,128)S(1)} %get-tuple-element.46, ...), custom_call_target="tpu_custom_call" | custom-call | tf_op jit(solution)/shard_map/pallas_call | solution.py:603
  35.5 1.7 %collective-permute-start.4 = (f32[288,128]{1,0:T(8,128)S(1)}, f32[288,128]{1,0:T(8,128)S(1)}, u32[]{:S(2)}, u32[]{:S(2)}) collective-permute-start(f32[288,128]{1,0:T(8,128)S(1)} %get-tuple-element.74), channel_id=1, source_target_pairs={{0,1},{1,0},{2,3},{3,2},{4,5},{5,4},{6,7},{7,6},{8,9},{9,8},{10,11... | collective-permute-start | bytes 442376 | tf_op jit(solution)/shard_map/ppermute | solution.py:504
  37.1 1.0 %collective-permute-done.4.got = f32[288,128]{1,0:T(8,128)S(1)} collective-permute-done((f32[288,128]{1,0:T(8,128)S(1)}, f32[288,128]{1,0:T(8,128)S(1)}, u32[]{:S(2)}, u32[]{:S(2)}) %collective-permute-start.4) | collective-permute-done | bytes 147488 | tf_op jit(solution)/shard_map/ppermute | solution.py:504
  38.2 0.6 %collective-permute-start.5 = (f32[144,128]{1,0:T(8,128)S(1)}, f32[144,128]{1,0:T(8,128)S(1)}, u32[]{:S(2)}, u32[]{:S(2)}) collective-permute-start(f32[144,128]{1,0:T(8,128)S(1)} %get-tuple-element.81), channel_id=1, source_target_pairs={{0,2},{1,3},{2,0},{3,1},{4,6},{5,7},{6,4},{7,5},{8,10},{9,11},{10,... | collective-permute-start | bytes 221192 | tf_op jit(solution)/shard_map/ppermute | solution.py:504
  38.8 1.8 %shard_map.150 = (f32[4,64,128]{2,1,0:T(8,128)}, f32[4,64,128]{2,1,0:T(8,128)}, f32[144,128]{1,0:T(8,128)S(1)}, s32[8,128]{1,0:T(8,128)S(1)}) custom-call(f32[21,64,128]{2,1,0:T(8,128)S(1)} %get-tuple-element.46.fields.refs_0_, f32[21,72,256]{2,1,0:T(8,128)S(1)} %get-tuple-element.68.planes, f32[4,72,256]{2,1,0:T(8,128)S(1)} %get-tuple-element.69.mids, ...), custom_call_target="tpu_custom_call" | custom-call | flops 1073741824 | tf_op jit(solution)/shard_map/pallas_call | solution.py:641
  40.6 2.2 %collective-permute-done.5 = f32[144,128]{1,0:T(8,128)S(1)} collective-permute-done((f32[144,128]{1,0:T(8,128)S(1)}, f32[144,128]{1,0:T(8,128)S(1)}, u32[]{:S(2)}, u32[]{:S(2)}) %collective-permute-start.5) | collective-permute-done | bytes 73760 | tf_op jit(solution)/shard_map/ppermute | solution.py:504
  42.8 3.8 %collective-permute-start.8 = (f32[144,128]{1,0:T(8,128)S(1)}, f32[144,128]{1,0:T(8,128)S(1)}, u32[]{:S(2)}, u32[]{:S(2)}) collective-permute-start(f32[144,128]{1,0:T(8,128)S(1)} %add.12), channel_id=1, source_target_pairs={{0,12},{4,8},{8,4},{12,0},{1,13},{5,9},{9,5},{13,1},{2,14},{6,10},... | collective-permute-start | bytes 221192 | tf_op jit(solution)/shard_map/ppermute | solution.py:504
  46.6 0.0 collective-permute-start.7
  46.6 0.7 %collective-permute-start.6 = (f32[144,128]{1,0:T(8,128)S(1)}, f32[144,128]{1,0:T(8,128)S(1)}, u32[]{:S(2)}, u32[]{:S(2)}) collective-permute-start(f32[144,128]{1,0:T(8,128)S(1)} %add.12), channel_id=1, source_target_pairs={{0,4},{4,0},{8,12},{12,8},{1,5},{5,1},{9,13},{13,9},{2,6},{6,2},{1... | collective-permute-start | bytes 221192 | tf_op jit(solution)/shard_map/ppermute | solution.py:504
  47.2 2.3 %collective-permute-done.8 = f32[144,128]{1,0:T(8,128)S(1)} collective-permute-done((f32[144,128]{1,0:T(8,128)S(1)}, f32[144,128]{1,0:T(8,128)S(1)}, u32[]{:S(2)}, u32[]{:S(2)}) %collective-permute-start.8) | collective-permute-done | bytes 73760 | tf_op jit(solution)/shard_map/ppermute | solution.py:504
  49.6 2.9 %collective-permute-done.7 = f32[144,128]{1,0:T(8,128)S(1)} collective-permute-done((f32[144,128]{1,0:T(8,128)S(1)}, f32[144,128]{1,0:T(8,128)S(1)}, u32[]{:S(2)}, u32[]{:S(2)}) %collective-permute-start.7) | collective-permute-done | bytes 73760 | tf_op jit(solution)/shard_map/ppermute | solution.py:504
  52.5 0.0 collective-permute-done.6
  52.5 0.4 collective-permute-start.9
  53.0 4.0 %collective-permute-done.9 = f32[144,128]{1,0:T(8,128)S(1)} collective-permute-done((f32[144,128]{1,0:T(8,128)S(1)}, f32[144,128]{1,0:T(8,128)S(1)}, u32[]{:S(2)}, u32[]{:S(2)}) %collective-permute-start.9) | collective-permute-done | bytes 73760 | tf_op jit(solution)/shard_map/ppermute | solution.py:504
  57.0 0.1 collective-permute-start.10
  57.0 1.4 %collective-permute-done.10 = f32[288,128]{1,0:T(8,128)S(1)} collective-permute-done((f32[288,128]{1,0:T(8,128)S(1)}, f32[288,128]{1,0:T(8,128)S(1)}, u32[]{:S(2)}, u32[]{:S(2)}) %collective-permute-start.10) | collective-permute-done | bytes 147488 | tf_op jit(solution)/shard_map/ppermute | solution.py:504
  58.5 0.7 %shard_map.151 = (f32[12,256]{1,0:T(8,128)}, f32[256,256]{1,0:T(8,128)}, f32[4,256]{1,0:T(4,128)}) custom-call(f32[576,128]{1,0:T(8,128)S(1)} %pad_maximum_fusion.terms), custom_call_target="tpu_custom_call" | custom-call | tf_op jit(solution)/shard_map/pallas_call | solution.py:654
  (9 shorter events, 0.1 us)
Async XLA Ops:
  2.4 7.1 %collective-permute-start = (f32[64,128]{1,0:T(8,128)S(1)}, f32[64,128]{1,0:T(8,128)S(1)}, u32[]{:S(2)}, u32[]{:S(2)}) collective-permute-start(f32[64,128]{1,0:T(8,128)S(1)} %get-tuple-element.47), channel_id=1, source_target_pairs={{0,4},{4,8},{8,12},{12,0},{1,5},{5,9},{9,13},{13,1},{2,6},{6,10},{... | collective-permute-start | bytes 98312 | tf_op jit(solution)/shard_map/ppermute | solution.py:500
  5.5 4.3 %collective-permute-start.1 = (f32[64,128]{1,0:T(8,128)S(1)}, f32[64,128]{1,0:T(8,128)S(1)}, u32[]{:S(2)}, u32[]{:S(2)}) collective-permute-start(f32[64,128]{1,0:T(8,128)S(1)} %get-tuple-element.48), channel_id=1, source_target_pairs={{0,12},{4,0},{8,4},{12,8},{1,13},{5,1},{9,5},{13,9},{2,14},{6,2},{... | collective-permute-start | bytes 98312 | tf_op jit(solution)/shard_map/ppermute | solution.py:500
  9.7 3.5 %collective-permute-start.2 = (f32[23,4,128]{2,1,0:T(4,128)S(1)}, f32[23,4,128]{2,1,0:T(4,128)S(1)}, u32[]{:S(2)}, u32[]{:S(2)}) collective-permute-start(f32[23,4,128]{2,1,0:T(4,128)S(1)} %get-tuple-element.51), channel_id=1, source_target_pairs={{0,1},{1,2},{2,3},{3,0},{4,5},{5,6},{6,7},{7,4},{8,9},{9,10},{10,1... | collective-permute-start | bytes 141320 | tf_op jit(solution)/shard_map/ppermute | solution.py:500
  9.8 3.5 %collective-permute-start.3 = (f32[23,4,128]{2,1,0:T(4,128)S(1)}, f32[23,4,128]{2,1,0:T(4,128)S(1)}, u32[]{:S(2)}, u32[]{:S(2)}) collective-permute-start(f32[23,4,128]{2,1,0:T(4,128)S(1)} %get-tuple-element.52), channel_id=1, source_target_pairs={{0,3},{1,0},{2,1},{3,2},{4,7},{5,4},{6,5},{7,6},{8,11},{9,8},{10,9... | collective-permute-start | bytes 141320 | tf_op jit(solution)/shard_map/ppermute | solution.py:500
  35.5 2.7 %collective-permute-start.4 = (f32[288,128]{1,0:T(8,128)S(1)}, f32[288,128]{1,0:T(8,128)S(1)}, u32[]{:S(2)}, u32[]{:S(2)}) collective-permute-start(f32[288,128]{1,0:T(8,128)S(1)} %get-tuple-element.74), channel_id=1, source_target_pairs={{0,1},{1,0},{2,3},{3,2},{4,5},{5,4},{6,7},{7,6},{8,9},{9,8},{10,11... | collective-permute-start | bytes 442376 | tf_op jit(solution)/shard_map/ppermute | solution.py:504
  38.2 4.6 %collective-permute-start.5 = (f32[144,128]{1,0:T(8,128)S(1)}, f32[144,128]{1,0:T(8,128)S(1)}, u32[]{:S(2)}, u32[]{:S(2)}) collective-permute-start(f32[144,128]{1,0:T(8,128)S(1)} %get-tuple-element.81), channel_id=1, source_target_pairs={{0,2},{1,3},{2,0},{3,1},{4,6},{5,7},{6,4},{7,5},{8,10},{9,11},{10,... | collective-permute-start | bytes 221192 | tf_op jit(solution)/shard_map/ppermute | solution.py:504
  42.8 6.8 %collective-permute-start.8 = (f32[144,128]{1,0:T(8,128)S(1)}, f32[144,128]{1,0:T(8,128)S(1)}, u32[]{:S(2)}, u32[]{:S(2)}) collective-permute-start(f32[144,128]{1,0:T(8,128)S(1)} %add.12), channel_id=1, source_target_pairs={{0,12},{4,8},{8,4},{12,0},{1,13},{5,9},{9,5},{13,1},{2,14},{6,10},... | collective-permute-start | bytes 221192 | tf_op jit(solution)/shard_map/ppermute | solution.py:504
  46.6 5.9 %collective-permute-start.7 = (f32[144,128]{1,0:T(8,128)S(1)}, f32[144,128]{1,0:T(8,128)S(1)}, u32[]{:S(2)}, u32[]{:S(2)}) collective-permute-start(f32[144,128]{1,0:T(8,128)S(1)} %add.12), channel_id=1, source_target_pairs={{0,8},{4,12},{8,0},{12,4},{1,9},{5,13},{9,1},{13,5},{2,10},{6,14},... | collective-permute-start | bytes 221192 | tf_op jit(solution)/shard_map/ppermute | solution.py:504
  46.6 5.9 %collective-permute-start.6 = (f32[144,128]{1,0:T(8,128)S(1)}, f32[144,128]{1,0:T(8,128)S(1)}, u32[]{:S(2)}, u32[]{:S(2)}) collective-permute-start(f32[144,128]{1,0:T(8,128)S(1)} %add.12), channel_id=1, source_target_pairs={{0,4},{4,0},{8,12},{12,8},{1,5},{5,1},{9,13},{13,9},{2,6},{6,2},{1... | collective-permute-start | bytes 221192 | tf_op jit(solution)/shard_map/ppermute | solution.py:504
  52.5 4.4 %collective-permute-start.9 = (f32[144,128]{1,0:T(8,128)S(1)}, f32[144,128]{1,0:T(8,128)S(1)}, u32[]{:S(2)}, u32[]{:S(2)}) collective-permute-start(f32[144,128]{1,0:T(8,128)S(1)} %add_add_fusion), channel_id=1, source_target_pairs={{0,2},{1,3},{2,0},{3,1},{4,6},{5,7},{6,4},{7,5},{8,10},{9,11},{10,... | collective-permute-start | bytes 221192 | tf_op jit(solution)/shard_map/ppermute | solution.py:504
  57.0 1.4 %collective-permute-start.10 = (f32[288,128]{1,0:T(8,128)S(1)}, f32[288,128]{1,0:T(8,128)S(1)}, u32[]{:S(2)}, u32[]{:S(2)}) collective-permute-start(f32[288,128]{1,0:T(8,128)S(1)} %pad_maximum_fusion.1), channel_id=1, source_target_pairs={{0,1},{1,0},{2,3},{3,2},{4,5},{5,4},{6,7},{7,6},{8,9},{9,8},{10,11... | collective-permute-start | bytes 442376 | tf_op jit(solution)/shard_map/ppermute | solution.py:504

commit v15 on v13

--- a/solution.py
+++ b/solution.py
@@ -263,7 +263,7 @@
     early, refs = refs[: 3 * EARLY], refs[3 * EARLY :]
     h_mid, h_old, o_sent, o_kept, planes, mids, olds, cl, df, *refs = refs
     o_mid, o_old, sems, ft1, ft2, fth, ftx, clh, clx, dc, dch, dcx, dfh, dfx, halo1, halo2, *refs = refs
-    acc_mid, acc_in, acc_out, o_grad = refs
+    acc_mid, acc_in, acc_out, o_grad, columns = refs
     levels, rows, cols = o_mid.shape
     hidden = w_mid.shape[0]
     block = Block(levels, rows)
@@ -297,8 +297,19 @@
         part = lanes_of(dc, SHALLOW, base, tiles)
         return jnp.concatenate([part, jnp.zeros_like(part)], 0).astype(BF16)
 
+    for level in range(levels):
+        columns[level] = jnp.broadcast_to(wo[...].astype(F32)[:, level : level + 1], (hidden, LANES))
+
+    def spread_out(cot):
+        rows_of = cot.astype(F32)
+        pieces = []
+        for at in range(0, cot.shape[1], LANES):
+            terms = [columns[level] * rows_of[level : level + 1, at : at + LANES] for level in range(levels)]
+            pieces.append(functools.reduce(jnp.add, terms))
+        return jnp.concatenate(pieces, 1)
+
     def backward_stages(first, second, cot):
-        g_two = dot(wo[...], cot)
+        g_two = spread_out(cot)
         yield
         dz_two = (g_two * (1.0 - second * second)).astype(BF16)
         yield
@@ -616,6 +627,7 @@
             pltpu.VMEM((DEEP, hidden), F32),
             pltpu.VMEM((hidden, DEEP), F32),
             pltpu.VMEM((terms_rows, LANES), F32),
+            pltpu.VMEM((levels, hidden, LANES), F32),
         ],
         compiler_params=pltpu.CompilerParams(vmem_limit_bytes=32 * 2**20),
     )(fields, left, right, low, high, wi, wi_t, wm_t, weights[1], wo, wo_t, *done)

time: 57.4 us -> 58.1 us (1.012)
  Pallas kernels: 27.9 us -> 28.6 us
    pallas_call x1, Pallas kernels: 20.3 us -> 20.9 us  [body(): pl.pallas_call(functools.partial(main_kernel, bands), out_shape=(field, f...]
where the time goes in v15:
time: 58.1 us; the launch traced here: 57.9 us
  Pallas kernels  28.6 us (49%)
  waiting for transfers between devices  14.3 us (25%)
  starting transfers between devices  14.2 us (24%)
  between operations  0.72 us (1%)
    pallas_call x1, Pallas kernels, body(): pl.pallas_call(functools.partial(main_kernel, bands), out_shape=(field, f...  20.9 us
    ppermute x7, waiting for transfers between devices, swapped(): lax.ppermute(value, axis, [(i, i ^ bit) for i in range(lax.axis_size(axis...  13.7 us
    ppermute x7, starting transfers between devices, swapped(): lax.ppermute(value, axis, [(i, i ^ bit) for i in range(lax.axis_size(axis...  7.25 us
    ppermute x4, starting transfers between devices, along(): lax.ppermute(value, axis, [(i, (i + step) % count) for i in range(count)])  6.96 us
    pallas_call x2, Pallas kernels, early(): pl.pallas_call(functools.partial(early_kernel, k * tall), out_shape=(kept...  3.36 us
    pallas_call x1, Pallas kernels, body(): pl.pallas_call(late_kernel, out_shape=(field, field, half_terms(bands)[0]...  1.82 us
    pallas_call x1, Pallas kernels, body(): pl.pallas_call(pack_kernel, out_shape=(strip, strip, edge, edge, jax.Shap...  1.74 us
  transfers between devices with their start and end apart: 11, of which 9 were waited for; matrix products, arithmetic and copies ran while one was open for 0% of the time, Pallas kernels for 9%

profile of v15, /device:TPU:0, one launch (start us, length us, event | category | flops | bytes accessed | tf_op | source)
XLA Modules:
  0.0 57.9 jit_solution(7837461099355019114)
XLA Ops:
  0.6 1.7 %shard_map.144 = (f32[64,128]{1,0:T(8,128)S(1)}, f32[64,128]{1,0:T(8,128)S(1)}, f32[21,4,128]{2,1,0:T(4,128)S(1)}, f32[21,4,128]{2,1,0:T(4,128)S(1)}, f32[21,64,...) custom-call(f32[4,64,128]{2,1,0:T(8,128)} %now.1, ...), custom_call_target="tpu_custom_call" | custom-call | tf_op jit(solution)/shard_map/pallas_call | solution.py:549
  2.4 3.1 %collective-permute-start = (f32[64,128]{1,0:T(8,128)S(1)}, f32[64,128]{1,0:T(8,128)S(1)}, u32[]{:S(2)}, u32[]{:S(2)}) collective-permute-start(f32[64,128]{1,0:T(8,128)S(1)} %get-tuple-element.47), channel_id=1, source_target_pairs={{0,4},{4,8},{8,12},{12,0},{1,5},{5,9},{9,13},{13,1},{2,6},{6,10},{... | collective-permute-start | bytes 98312 | tf_op jit(solution)/shard_map/ppermute | solution.py:505
  5.5 2.1 %collective-permute-start.1 = (f32[64,128]{1,0:T(8,128)S(1)}, f32[64,128]{1,0:T(8,128)S(1)}, u32[]{:S(2)}, u32[]{:S(2)}) collective-permute-start(f32[64,128]{1,0:T(8,128)S(1)} %get-tuple-element.48), channel_id=1, source_target_pairs={{0,12},{4,0},{8,4},{12,8},{1,13},{5,1},{9,5},{13,9},{2,14},{6,2},{... | collective-permute-start | bytes 98312 | tf_op jit(solution)/shard_map/ppermute | solution.py:505
  7.6 1.7 %shard_map.146 = (f32[4,256,1024]{2,1,0:T(8,128)S(1)}, f32[4,256,1024]{2,1,0:T(8,128)S(1)}, f32[256,128]{1,0:T(8,128)S(1)}, bf16[16,256]{1,0:T(8,128)(2,1)S(1)},...) custom-call(f32[21,64,128]{2,1,0:T(8,128)S(1)} %get-tuple-element.46, ...), custom_call_target="tpu_custom_call" | custom-call | flops 1610612736 | tf_op jit(solution)/shard_map/pallas_call | solution.py:565
  9.3 0.2 collective-permute-done.left.refs_0_.refs_1_
  9.5 0.2 collective-permute-done.1.right.refs_2_
  9.7 0.1 collective-permute-start.2
  9.8 1.7 %collective-permute-start.3 = (f32[23,4,128]{2,1,0:T(4,128)S(1)}, f32[23,4,128]{2,1,0:T(4,128)S(1)}, u32[]{:S(2)}, u32[]{:S(2)}) collective-permute-start(f32[23,4,128]{2,1,0:T(4,128)S(1)} %get-tuple-element.52), channel_id=1, source_target_pairs={{0,3},{1,0},{2,1},{3,2},{4,7},{5,4},{6,5},{7,6},{8,11},{9,8},{10,9... | collective-permute-start | bytes 141320 | tf_op jit(solution)/shard_map/ppermute | solution.py:505
  11.5 1.6 %shard_map.147 = (f32[4,256,1024]{2,1,0:T(8,128)S(1)}, f32[4,256,1024]{2,1,0:T(8,128)S(1)}, f32[256,128]{1,0:T(8,128)S(1)}) custom-call(f32[21,64,128]{2,1,0:T(8,128)S(1)} %get-tuple-element.46.fields.refs_0_, f32[64,128]{1,0:T(8,128)S(1)} %collective-permute-done.left.refs_0_.refs_1_, bf16[256,16]{1,0:T(8,128)(2,1)S(1)} %get-tuple-element.57.refs_1_.refs_6_, ...), custom_call_target="tpu_custom_call" | custom-call | flops 1610612736 | tf_op jit(solution)/shard_map/pallas_call | solution.py:565
  13.2 0.1 collective-permute-done.2.refs_3_
  13.3 0.0 collective-permute-done.3.refs_4_
  13.3 20.9 %shard_map.148 = (f32[4,64,128]{2,1,0:T(8,128)}, f32[4,64,128]{2,1,0:T(8,128)}, f32[288,128]{1,0:T(8,128)S(1)}, f32[288,128]{1,0:T(8,128)S(1)}, f32[21,72,256]{2...) custom-call(f32[21,64,128]{2,1,0:T(8,128)S(1)} %get-tuple-element.46, ...), custom_call_target="tpu_custom_call" | custom-call | tf_op jit(solution)/shard_map/pallas_call | solution.py:608
  34.2 1.7 %collective-permute-start.4 = (f32[288,128]{1,0:T(8,128)S(1)}, f32[288,128]{1,0:T(8,128)S(1)}, u32[]{:S(2)}, u32[]{:S(2)}) collective-permute-start(f32[288,128]{1,0:T(8,128)S(1)} %get-tuple-element.74), channel_id=1, source_target_pairs={{0,1},{1,0},{2,3},{3,2},{4,5},{5,4},{6,7},{7,6},{8,9},{9,8},{10,11... | collective-permute-start | bytes 442376 | tf_op jit(solution)/shard_map/ppermute | solution.py:509
  35.9 1.0 %collective-permute-done.4.got = f32[288,128]{1,0:T(8,128)S(1)} collective-permute-done((f32[288,128]{1,0:T(8,128)S(1)}, f32[288,128]{1,0:T(8,128)S(1)}, u32[]{:S(2)}, u32[]{:S(2)}) %collective-permute-start.4) | collective-permute-done | bytes 147488 | tf_op jit(solution)/shard_map/ppermute | solution.py:509
  36.9 0.6 %collective-permute-start.5 = (f32[144,128]{1,0:T(8,128)S(1)}, f32[144,128]{1,0:T(8,128)S(1)}, u32[]{:S(2)}, u32[]{:S(2)}) collective-permute-start(f32[144,128]{1,0:T(8,128)S(1)} %get-tuple-element.81), channel_id=1, source_target_pairs={{0,2},{1,3},{2,0},{3,1},{4,6},{5,7},{6,4},{7,5},{8,10},{9,11},{10,... | collective-permute-start | bytes 221192 | tf_op jit(solution)/shard_map/ppermute | solution.py:509
  37.5 1.8 %shard_map.150 = (f32[4,64,128]{2,1,0:T(8,128)}, f32[4,64,128]{2,1,0:T(8,128)}, f32[144,128]{1,0:T(8,128)S(1)}, s32[8,128]{1,0:T(8,128)S(1)}) custom-call(f32[21,64,128]{2,1,0:T(8,128)S(1)} %get-tuple-element.46.fields.refs_0_, f32[21,72,256]{2,1,0:T(8,128)S(1)} %get-tuple-element.68.planes, f32[4,72,256]{2,1,0:T(8,128)S(1)} %get-tuple-element.69.mids, ...), custom_call_target="tpu_custom_call" | custom-call | flops 1073741824 | tf_op jit(solution)/shard_map/pallas_call | solution.py:647
  39.3 2.2 %collective-permute-done.5 = f32[144,128]{1,0:T(8,128)S(1)} collective-permute-done((f32[144,128]{1,0:T(8,128)S(1)}, f32[144,128]{1,0:T(8,128)S(1)}, u32[]{:S(2)}, u32[]{:S(2)}) %collective-permute-start.5) | collective-permute-done | bytes 73760 | tf_op jit(solution)/shard_map/ppermute | solution.py:509
  41.5 3.8 %collective-permute-start.8 = (f32[144,128]{1,0:T(8,128)S(1)}, f32[144,128]{1,0:T(8,128)S(1)}, u32[]{:S(2)}, u32[]{:S(2)}) collective-permute-start(f32[144,128]{1,0:T(8,128)S(1)} %add.12), channel_id=1, source_target_pairs={{0,12},{4,8},{8,4},{12,0},{1,13},{5,9},{9,5},{13,1},{2,14},{6,10},... | collective-permute-start | bytes 221192 | tf_op jit(solution)/shard_map/ppermute | solution.py:509
  45.3 0.0 collective-permute-start.7
  45.3 0.7 %collective-permute-start.6 = (f32[144,128]{1,0:T(8,128)S(1)}, f32[144,128]{1,0:T(8,128)S(1)}, u32[]{:S(2)}, u32[]{:S(2)}) collective-permute-start(f32[144,128]{1,0:T(8,128)S(1)} %add.12), channel_id=1, source_target_pairs={{0,4},{4,0},{8,12},{12,8},{1,5},{5,1},{9,13},{13,9},{2,6},{6,2},{1... | collective-permute-start | bytes 221192 | tf_op jit(solution)/shard_map/ppermute | solution.py:509
  46.0 2.3 %collective-permute-done.8 = f32[144,128]{1,0:T(8,128)S(1)} collective-permute-done((f32[144,128]{1,0:T(8,128)S(1)}, f32[144,128]{1,0:T(8,128)S(1)}, u32[]{:S(2)}, u32[]{:S(2)}) %collective-permute-start.8) | collective-permute-done | bytes 73760 | tf_op jit(solution)/shard_map/ppermute | solution.py:509
  48.3 2.9 %collective-permute-done.7 = f32[144,128]{1,0:T(8,128)S(1)} collective-permute-done((f32[144,128]{1,0:T(8,128)S(1)}, f32[144,128]{1,0:T(8,128)S(1)}, u32[]{:S(2)}, u32[]{:S(2)}) %collective-permute-start.7) | collective-permute-done | bytes 73760 | tf_op jit(solution)/shard_map/ppermute | solution.py:509
  51.2 0.0 collective-permute-done.6
  51.2 0.4 collective-permute-start.9
  51.7 4.0 %collective-permute-done.9 = f32[144,128]{1,0:T(8,128)S(1)} collective-permute-done((f32[144,128]{1,0:T(8,128)S(1)}, f32[144,128]{1,0:T(8,128)S(1)}, u32[]{:S(2)}, u32[]{:S(2)}) %collective-permute-start.9) | collective-permute-done | bytes 73760 | tf_op jit(solution)/shard_map/ppermute | solution.py:509
  55.7 0.1 collective-permute-start.10
  55.8 1.4 %collective-permute-done.10 = f32[288,128]{1,0:T(8,128)S(1)} collective-permute-done((f32[288,128]{1,0:T(8,128)S(1)}, f32[288,128]{1,0:T(8,128)S(1)}, u32[]{:S(2)}, u32[]{:S(2)}) %collective-permute-start.10) | collective-permute-done | bytes 147488 | tf_op jit(solution)/shard_map/ppermute | solution.py:509
  57.2 0.7 %shard_map.151 = (f32[12,256]{1,0:T(8,128)}, f32[256,256]{1,0:T(8,128)}, f32[4,256]{1,0:T(4,128)}) custom-call(f32[576,128]{1,0:T(8,128)S(1)} %pad_maximum_fusion.terms), custom_call_target="tpu_custom_call" | custom-call | tf_op jit(solution)/shard_map/pallas_call | solution.py:660
  (9 shorter events, 0.1 us)
Async XLA Ops:
  2.4 7.1 %collective-permute-start = (f32[64,128]{1,0:T(8,128)S(1)}, f32[64,128]{1,0:T(8,128)S(1)}, u32[]{:S(2)}, u32[]{:S(2)}) collective-permute-start(f32[64,128]{1,0:T(8,128)S(1)} %get-tuple-element.47), channel_id=1, source_target_pairs={{0,4},{4,8},{8,12},{12,0},{1,5},{5,9},{9,13},{13,1},{2,6},{6,10},{... | collective-permute-start | bytes 98312 | tf_op jit(solution)/shard_map/ppermute | solution.py:505
  5.5 4.3 %collective-permute-start.1 = (f32[64,128]{1,0:T(8,128)S(1)}, f32[64,128]{1,0:T(8,128)S(1)}, u32[]{:S(2)}, u32[]{:S(2)}) collective-permute-start(f32[64,128]{1,0:T(8,128)S(1)} %get-tuple-element.48), channel_id=1, source_target_pairs={{0,12},{4,0},{8,4},{12,8},{1,13},{5,1},{9,5},{13,9},{2,14},{6,2},{... | collective-permute-start | bytes 98312 | tf_op jit(solution)/shard_map/ppermute | solution.py:505
  9.7 3.5 %collective-permute-start.2 = (f32[23,4,128]{2,1,0:T(4,128)S(1)}, f32[23,4,128]{2,1,0:T(4,128)S(1)}, u32[]{:S(2)}, u32[]{:S(2)}) collective-permute-start(f32[23,4,128]{2,1,0:T(4,128)S(1)} %get-tuple-element.51), channel_id=1, source_target_pairs={{0,1},{1,2},{2,3},{3,0},{4,5},{5,6},{6,7},{7,4},{8,9},{9,10},{10,1... | collective-permute-start | bytes 141320 | tf_op jit(solution)/shard_map/ppermute | solution.py:505
  9.8 3.5 %collective-permute-start.3 = (f32[23,4,128]{2,1,0:T(4,128)S(1)}, f32[23,4,128]{2,1,0:T(4,128)S(1)}, u32[]{:S(2)}, u32[]{:S(2)}) collective-permute-start(f32[23,4,128]{2,1,0:T(4,128)S(1)} %get-tuple-element.52), channel_id=1, source_target_pairs={{0,3},{1,0},{2,1},{3,2},{4,7},{5,4},{6,5},{7,6},{8,11},{9,8},{10,9... | collective-permute-start | bytes 141320 | tf_op jit(solution)/shard_map/ppermute | solution.py:505
  34.2 2.7 %collective-permute-start.4 = (f32[288,128]{1,0:T(8,128)S(1)}, f32[288,128]{1,0:T(8,128)S(1)}, u32[]{:S(2)}, u32[]{:S(2)}) collective-permute-start(f32[288,128]{1,0:T(8,128)S(1)} %get-tuple-element.74), channel_id=1, source_target_pairs={{0,1},{1,0},{2,3},{3,2},{4,5},{5,4},{6,7},{7,6},{8,9},{9,8},{10,11... | collective-permute-start | bytes 442376 | tf_op jit(solution)/shard_map/ppermute | solution.py:509
  36.9 4.6 %collective-permute-start.5 = (f32[144,128]{1,0:T(8,128)S(1)}, f32[144,128]{1,0:T(8,128)S(1)}, u32[]{:S(2)}, u32[]{:S(2)}) collective-permute-start(f32[144,128]{1,0:T(8,128)S(1)} %get-tuple-element.81), channel_id=1, source_target_pairs={{0,2},{1,3},{2,0},{3,1},{4,6},{5,7},{6,4},{7,5},{8,10},{9,11},{10,... | collective-permute-start | bytes 221192 | tf_op jit(solution)/shard_map/ppermute | solution.py:509
  41.5 6.8 %collective-permute-start.8 = (f32[144,128]{1,0:T(8,128)S(1)}, f32[144,128]{1,0:T(8,128)S(1)}, u32[]{:S(2)}, u32[]{:S(2)}) collective-permute-start(f32[144,128]{1,0:T(8,128)S(1)} %add.12), channel_id=1, source_target_pairs={{0,12},{4,8},{8,4},{12,0},{1,13},{5,9},{9,5},{13,1},{2,14},{6,10},... | collective-permute-start | bytes 221192 | tf_op jit(solution)/shard_map/ppermute | solution.py:509
  45.3 5.9 %collective-permute-start.7 = (f32[144,128]{1,0:T(8,128)S(1)}, f32[144,128]{1,0:T(8,128)S(1)}, u32[]{:S(2)}, u32[]{:S(2)}) collective-permute-start(f32[144,128]{1,0:T(8,128)S(1)} %add.12), channel_id=1, source_target_pairs={{0,8},{4,12},{8,0},{12,4},{1,9},{5,13},{9,1},{13,5},{2,10},{6,14},... | collective-permute-start | bytes 221192 | tf_op jit(solution)/shard_map/ppermute | solution.py:509
  45.3 5.9 %collective-permute-start.6 = (f32[144,128]{1,0:T(8,128)S(1)}, f32[144,128]{1,0:T(8,128)S(1)}, u32[]{:S(2)}, u32[]{:S(2)}) collective-permute-start(f32[144,128]{1,0:T(8,128)S(1)} %add.12), channel_id=1, source_target_pairs={{0,4},{4,0},{8,12},{12,8},{1,5},{5,1},{9,13},{13,9},{2,6},{6,2},{1... | collective-permute-start | bytes 221192 | tf_op jit(solution)/shard_map/ppermute | solution.py:509
  51.2 4.4 %collective-permute-start.9 = (f32[144,128]{1,0:T(8,128)S(1)}, f32[144,128]{1,0:T(8,128)S(1)}, u32[]{:S(2)}, u32[]{:S(2)}) collective-permute-start(f32[144,128]{1,0:T(8,128)S(1)} %add_add_fusion), channel_id=1, source_target_pairs={{0,2},{1,3},{2,0},{3,1},{4,6},{5,7},{6,4},{7,5},{8,10},{9,11},{10,... | collective-permute-start | bytes 221192 | tf_op jit(solution)/shard_map/ppermute | solution.py:509
  55.7 1.4 %collective-permute-start.10 = (f32[288,128]{1,0:T(8,128)S(1)}, f32[288,128]{1,0:T(8,128)S(1)}, u32[]{:S(2)}, u32[]{:S(2)}) collective-permute-start(f32[288,128]{1,0:T(8,128)S(1)} %pad_maximum_fusion.1), channel_id=1, source_target_pairs={{0,1},{1,0},{2,3},{3,2},{4,5},{5,4},{6,7},{7,6},{8,9},{9,8},{10,11... | collective-permute-start | bytes 442376 | tf_op jit(solution)/shard_map/ppermute | solution.py:509

commit v16 on v10

--- a/solution.py
+++ b/solution.py
@@ -14,6 +14,7 @@
 WIDE = 4
 LANES = 128
 PART = 8
+FINE = 4
 EARLY = 2
 DEEP = 16
 SHALLOW = 8
@@ -260,15 +261,17 @@
 def main_kernel(bands, *refs):
     fields, left, right, low, high, wi, wi_t, wm_t, w_mid, wo, wo_t, *refs = refs
     early, refs = refs[: 3 * EARLY], refs[3 * EARLY :]
-    h_mid, h_old, o_sent, o_kept, planes, mids, olds, cl, df, *refs = refs
-    o_mid, o_old, sems, ft1, ft2, fth, ftx, clh, clx, dc, dch, dcx, dfh, dfx, halo1, halo2, *refs = refs
+    h_mid, h_old, o_sent, o_kept, planes, mids, olds, seconds, dz_ones, dz_halo, *refs = refs
+    o_mid, o_old, sems, ft1, ft2, fth, ftx, cl, clh, clx, dc, dch, dcx, df, dfh, dfx, halo1, halo2, *refs = refs
     acc_mid, acc_in, acc_out, o_grad = refs
     levels, rows, cols = o_mid.shape
     hidden = w_mid.shape[0]
     block = Block(levels, rows)
     count, ext, lane = block.wet + 1, block.ext, block.lane
-    kept1 = [ref.at[k] for ref in early[0::3] for k in range(ref.shape[0])]
-    kept2 = [ref.at[k] for ref in early[1::3] for k in range(ref.shape[0])]
+    span = FINE * LANES
+    cuts = [pl.ds(at, span) for at in range(0, PART * LANES, span)]
+    kept1 = [ref.at[k, :, cut] for ref in early[0::3] for k in range(ref.shape[0]) for cut in cuts]
+    kept2 = [ref.at[k, :, cut] for ref in early[1::3] for k in range(ref.shape[0]) for cut in cuts]
 
     band = lax.axis_index("lat")
     has_low = jnp.where(band > 0, 1.0, 0.0)
@@ -307,13 +310,13 @@
         yield
         return dz_one, dz_two
 
-    def second_part(base, tiles, sums):
+    def second_part(base, tiles, held, sums):
         x = inputs_at(ft2, base, tiles)
         cot = cotangents_at(base, tiles)
         first, second, low_first, low_second = yield from forward_stages(x, wi_t, wm_t)
-        yield
-        if sums is not None:
-            put_lanes(cl, SHALLOW, base, tiles, closure(low_second, wo_t))
+        if held is not None:
+            held[...] = low_second
+        yield
         dz_one, dz_two = yield from backward_stages(first, second, cot)
         dfeat = feature_gradients(dz_one, wi)
         if sums is not None:
@@ -321,18 +324,17 @@
         yield
         put_lanes(df, DEEP, base, tiles, dfeat)
 
-    def third_part(base, tiles, held1, held2, counted, sums):
+    def third_part(base, tiles, held1, held2, held, counted, sums):
         cot = cotangents_at(base, tiles)
         first = held1[...]
         second = held2[...]
         dz_one, dz_two = yield from backward_stages(first, second, cot)
-        dfeat = feature_gradients(dz_one, wi)
+        held[...] = dz_one
+        yield
         x = inputs_at(ft1, base, tiles)
         if counted is not None:
             dz_one, dz_two, cot = (jnp.where(counted, v.astype(F32), 0.0).astype(BF16) for v in (dz_one, dz_two, cot))
         add_terms(sums, (first.astype(BF16), dz_two), (x, dz_one), (second.astype(BF16), cot))
-        yield
-        put_lanes(df, DEEP, base, tiles, dfeat)
 
     def add_terms(sums, *pairs):
         for k, pair in enumerate(pairs):
@@ -372,8 +374,8 @@
     block.pack_halo(block.outer, SHALLOW, dc, dcx, dch)
     sums = [None] * 3
     staggered(
-        [second_part(rows, len(block.outer), None)]
-        + [second_part(k * PART, PART, sums) for k in range(rows // PART)]
+        [second_part(rows, len(block.outer), None, None)]
+        + [second_part(k * FINE, FINE, seconds.at[k], sums) for k in range(rows // FINE)]
     )
     for acc, total in zip((acc_mid, acc_in, acc_out), sums):
         acc[...] = total
@@ -405,8 +407,8 @@
     wide = pl.ds(0, len(near) * LANES)
     sums = [None] * 3
     staggered(
-        [third_part(rows, len(near), halo1.at[:, wide], halo2.at[:, wide], counted, sums)]
-        + [third_part(k * PART, PART, kept1[k], kept2[k], None, sums) for k in range(rows // PART)]
+        [third_part(rows, len(near), halo1.at[:, wide], halo2.at[:, wide], dz_halo, counted, sums)]
+        + [third_part(k * FINE, FINE, kept1[k], kept2[k], dz_ones.at[k], None, sums) for k in range(rows // FINE)]
     )
 
     start = 0
@@ -433,14 +435,18 @@
     halve(held[...] + got[...], bit, sent, kept)
 
 
-def late_kernel(
-    fields, planes, mids, olds, cl, gradients, held, h_new, h_now, o_held, o_place, o_new, o_now, sems, df, dfh, dfx
-):
+def late_kernel(fields, planes, mids, olds, seconds, dz_ones, dz_halo, wi, wo_t, held, *refs):
+    h_new, h_now, o_held, o_place, o_new, o_now, sems, cl, df, dfh, dfx = refs
     levels, rows, cols = o_new.shape
     block = Block(levels, rows)
     o_held[...] = held[...]
     o_place[...] = jnp.zeros_like(o_place) + lax.axis_index("lat")
-    df[...] = gradients[...]
+    put_lanes(df, DEEP, rows, len(block.rim_near), feature_gradients(dz_halo[...], wi))
+    for k in range(0, rows // FINE, 2):
+        for ref, put, deep, kind in ((dz_ones, df, DEEP, 0), (seconds, cl, SHALLOW, 1)):
+            both = jnp.concatenate([ref[k], ref[k + 1]], 1)
+            value = closure(both, wo_t) if kind else feature_gradients(both, wi)
+            put_lanes(put, deep, k * FINE, 2 * FINE, value)
     beside = jnp.zeros((rows, LANES), F32)
     beyond = jnp.zeros((2 * WIDE, 2 * LANES), F32)
     for level in range(levels):
@@ -563,6 +569,8 @@
     terms_rows = -(-halves * (hidden + 2 * DEEP) // (8 * bands)) * 8 * bands
     field = jax.ShapeDtypeStruct((levels, rows, cols), F32)
     ext_planes = jax.ShapeDtypeStruct((levels, ext, 2 * LANES), F32)
+    low_kept = jax.ShapeDtypeStruct((rows // FINE, hidden, FINE * LANES), BF16)
+    near = (4 + packs) * LANES
     staged = pltpu.VMEM((levels, rows, cols), F32)
 
     def tiles(deep):
@@ -572,22 +580,22 @@
         return (jax.ShapeDtypeStruct((terms_rows // parts, LANES), F32),) * 2
 
     kept_halo = pltpu.VMEM((hidden, (8 + packs) * LANES), F32)
-    state_mid, grad_old, sent, held, planes, mids, olds, closures, gradients = pl.pallas_call(
+    state_mid, grad_old, sent, held, planes, mids, olds, seconds, dz_ones, dz_halo = pl.pallas_call(
         functools.partial(main_kernel, bands),
         out_shape=(field, field, *half_terms(2))
         + (jax.ShapeDtypeStruct((count, ext, 2 * LANES), F32), ext_planes, ext_planes)
-        + tuple(jax.ShapeDtypeStruct((slots * deep, LANES), F32) for deep in (SHALLOW, DEEP)),
+        + (low_kept, low_kept, jax.ShapeDtypeStruct((hidden, near), BF16)),
         in_specs=[vmem] * (11 + 3 * EARLY),
-        out_specs=(hbm,) * 2 + (vmem,) * 7,
+        out_specs=(hbm,) * 2 + (vmem,) * 8,
         scratch_shapes=[
             staged,
             staged,
             pltpu.SemaphoreType.DMA((2,)),
             tiles(DEEP)[0],
             *tiles(DEEP),
-            *tiles(SHALLOW)[1:],
             *tiles(SHALLOW),
-            *tiles(DEEP)[1:],
+            *tiles(SHALLOW),
+            *tiles(DEEP),
             kept_halo,
             kept_halo,
             pltpu.VMEM((hidden, hidden), F32),
@@ -595,7 +603,7 @@
             pltpu.VMEM((hidden, DEEP), F32),
             pltpu.VMEM((terms_rows, LANES), F32),
         ],
-        compiler_params=pltpu.CompilerParams(vmem_limit_bytes=32 * 2**20),
+        compiler_params=pltpu.CompilerParams(vmem_limit_bytes=24 * 2**20),
     )(fields, left, right, low, high, wi, wi_t, wm_t, weights[1], wo, wo_t, *done)
 
     bit = 1
@@ -613,14 +621,20 @@
     state_new, grad_now, held, place = pl.pallas_call(
         late_kernel,
         out_shape=(field, field, half_terms(bands)[0], jax.ShapeDtypeStruct((8, LANES), jnp.int32)),
-        in_specs=[vmem] * 7,
+        in_specs=[vmem] * 10,
         out_specs=(hbm,) * 2 + (vmem,) * 2,
-        scratch_shapes=[staged, staged, pltpu.SemaphoreType.DMA((2,)), *tiles(DEEP)],
+        scratch_shapes=[
+            staged,
+            staged,
+            pltpu.SemaphoreType.DMA((2,)),
+            tiles(SHALLOW)[0],
+            *tiles(DEEP),
+        ],
         compiler_params=pltpu.CompilerParams(vmem_limit_bytes=16 * 2**20),
         cost_estimate=pl.CostEstimate(
-            flops=2 * hidden * hidden * rows * cols, bytes_accessed=0, transcendentals=0
+            flops=4 * DEEP * hidden * rows * cols, bytes_accessed=0, transcendentals=0
         ),
-    )(fields, planes, mids, olds, closures, gradients, held)
+    )(fields, planes, mids, olds, seconds, dz_ones, dz_halo, wi, wo_t, held)
     summed = put_together(added_up(held + got, "lon"), place[:1], "lat")
     cells_all = rows * lax.axis_size("lat") * cols * lax.axis_size("lon")
     grad_in, grad_mid, grad_out = pl.pallas_call(

time: 57.5 us -> 56.1 us (0.976)
  Pallas kernels: 28 us -> 26.9 us
    pallas_call x1, Pallas kernels: 20.4 us -> 18.9 us  [body(): pl.pallas_call(functools.partial(main_kernel, bands), out_shape=(field, f...]
  transfers between devices with their start and end apart: 11 -> 11, of which waited for: 9 -> 9; matrix products, arithmetic and copies ran while one was open for 0% -> 0% of each run, Pallas kernels for 9% -> 10%
where the time goes in v16:
time: 56.1 us; the launch traced here: 56 us
  Pallas kernels  26.9 us (48%)
  starting transfers between devices  14.2 us (25%)
  waiting for transfers between devices  14 us (25%)
  between operations  0.72 us (1%)
    pallas_call x1, Pallas kernels, body(): pl.pallas_call(functools.partial(main_kernel, bands), out_shape=(field, f...  18.9 us
    ppermute x7, waiting for transfers between devices, swapped(): lax.ppermute(value, axis, [(i, i ^ bit) for i in range(lax.axis_size(axis...  13.4 us
    ppermute x7, starting transfers between devices, swapped(): lax.ppermute(value, axis, [(i, i ^ bit) for i in range(lax.axis_size(axis...  7.25 us
    ppermute x4, starting transfers between devices, along(): lax.ppermute(value, axis, [(i, (i + step) % count) for i in range(count)])  6.96 us
    pallas_call x2, Pallas kernels, early(): pl.pallas_call(functools.partial(early_kernel, k * tall), out_shape=(kept...  3.36 us
    pallas_call x1, Pallas kernels, body(): pl.pallas_call(late_kernel, out_shape=(field, field, half_terms(bands)[0]...  2.13 us
    pallas_call x1, Pallas kernels, body(): pl.pallas_call(pack_kernel, out_shape=(strip, strip, edge, edge, jax.Shap...  1.74 us
  transfers between devices with their start and end apart: 11, of which 9 were waited for; matrix products, arithmetic and copies ran while one was open for 0% of the time, Pallas kernels for 10%

profile of v16, /device:TPU:0, one launch (start us, length us, event | category | flops | bytes accessed | tf_op | source)
XLA Modules:
  0.0 56.0 jit_solution(1475345761833269606)
XLA Ops:
  0.6 1.7 %shard_map.144 = (f32[64,128]{1,0:T(8,128)S(1)}, f32[64,128]{1,0:T(8,128)S(1)}, f32[21,4,128]{2,1,0:T(4,128)S(1)}, f32[21,4,128]{2,1,0:T(4,128)S(1)}, f32[21,64,...) custom-call(f32[4,64,128]{2,1,0:T(8,128)} %now.1, ...), custom_call_target="tpu_custom_call" | custom-call | tf_op jit(solution)/shard_map/pallas_call | solution.py:522
  2.4 3.1 %collective-permute-start = (f32[64,128]{1,0:T(8,128)S(1)}, f32[64,128]{1,0:T(8,128)S(1)}, u32[]{:S(2)}, u32[]{:S(2)}) collective-permute-start(f32[64,128]{1,0:T(8,128)S(1)} %get-tuple-element.48), channel_id=1, source_target_pairs={{0,4},{4,8},{8,12},{12,0},{1,5},{5,9},{9,13},{13,1},{2,6},{6,10},{... | collective-permute-start | bytes 98312 | tf_op jit(solution)/shard_map/ppermute | solution.py:478
  5.5 2.1 %collective-permute-start.1 = (f32[64,128]{1,0:T(8,128)S(1)}, f32[64,128]{1,0:T(8,128)S(1)}, u32[]{:S(2)}, u32[]{:S(2)}) collective-permute-start(f32[64,128]{1,0:T(8,128)S(1)} %get-tuple-element.49), channel_id=1, source_target_pairs={{0,12},{4,0},{8,4},{12,8},{1,13},{5,1},{9,5},{13,9},{2,14},{6,2},{... | collective-permute-start | bytes 98312 | tf_op jit(solution)/shard_map/ppermute | solution.py:478
  7.6 1.7 %shard_map.146 = (f32[4,256,1024]{2,1,0:T(8,128)S(1)}, f32[4,256,1024]{2,1,0:T(8,128)S(1)}, f32[256,128]{1,0:T(8,128)S(1)}, bf16[16,256]{1,0:T(8,128)(2,1)S(1)},...) custom-call(f32[21,64,128]{2,1,0:T(8,128)S(1)} %get-tuple-element.47, ...), custom_call_target="tpu_custom_call" | custom-call | flops 1610612736 | tf_op jit(solution)/shard_map/pallas_call | solution.py:538
  9.3 0.2 collective-permute-done.left.refs_0_.refs_1_
  9.5 0.2 collective-permute-done.1.right.refs_2_
  9.7 0.1 collective-permute-start.2
  9.8 1.7 %collective-permute-start.3 = (f32[23,4,128]{2,1,0:T(4,128)S(1)}, f32[23,4,128]{2,1,0:T(4,128)S(1)}, u32[]{:S(2)}, u32[]{:S(2)}) collective-permute-start(f32[23,4,128]{2,1,0:T(4,128)S(1)} %get-tuple-element.53), channel_id=1, source_target_pairs={{0,3},{1,0},{2,1},{3,2},{4,7},{5,4},{6,5},{7,6},{8,11},{9,8},{10,9... | collective-permute-start | bytes 141320 | tf_op jit(solution)/shard_map/ppermute | solution.py:478
  11.5 1.6 %shard_map.147 = (f32[4,256,1024]{2,1,0:T(8,128)S(1)}, f32[4,256,1024]{2,1,0:T(8,128)S(1)}, f32[256,128]{1,0:T(8,128)S(1)}) custom-call(f32[21,64,128]{2,1,0:T(8,128)S(1)} %get-tuple-element.47.fields.refs_0_, f32[64,128]{1,0:T(8,128)S(1)} %collective-permute-done.left.refs_0_.refs_1_, bf16[256,16]{1,0:T(8,128)(2,1)S(1)} %get-tuple-element.58.refs_1_.refs_6_, ...), custom_call_target="tpu_custom_call" | custom-call | flops 1610612736 | tf_op jit(solution)/shard_map/pallas_call | solution.py:538
  13.2 0.1 collective-permute-done.2.refs_3_
  13.3 0.0 collective-permute-done.3.refs_4_
  13.3 18.9 %shard_map.148 = (f32[4,64,128]{2,1,0:T(8,128)}, f32[4,64,128]{2,1,0:T(8,128)}, f32[288,128]{1,0:T(8,128)S(1)}, f32[288,128]{1,0:T(8,128)S(1)}, f32[21,72,256]{2...) custom-call(f32[21,64,128]{2,1,0:T(8,128)S(1)} %get-tuple-element.47, ...), custom_call_target="tpu_custom_call" | custom-call | tf_op jit(solution)/shard_map/pallas_call | solution.py:583
  32.2 1.7 %collective-permute-start.4 = (f32[288,128]{1,0:T(8,128)S(1)}, f32[288,128]{1,0:T(8,128)S(1)}, u32[]{:S(2)}, u32[]{:S(2)}) collective-permute-start(f32[288,128]{1,0:T(8,128)S(1)} %get-tuple-element.76), channel_id=1, source_target_pairs={{0,1},{1,0},{2,3},{3,2},{4,5},{5,4},{6,7},{7,6},{8,9},{9,8},{10,11... | collective-permute-start | bytes 442376 | tf_op jit(solution)/shard_map/ppermute | solution.py:482
  33.9 1.0 %collective-permute-done.4.got = f32[288,128]{1,0:T(8,128)S(1)} collective-permute-done((f32[288,128]{1,0:T(8,128)S(1)}, f32[288,128]{1,0:T(8,128)S(1)}, u32[]{:S(2)}, u32[]{:S(2)}) %collective-permute-start.4) | collective-permute-done | bytes 147488 | tf_op jit(solution)/shard_map/ppermute | solution.py:482
  34.9 0.6 %collective-permute-start.5 = (f32[144,128]{1,0:T(8,128)S(1)}, f32[144,128]{1,0:T(8,128)S(1)}, u32[]{:S(2)}, u32[]{:S(2)}) collective-permute-start(f32[144,128]{1,0:T(8,128)S(1)} %get-tuple-element.83), channel_id=1, source_target_pairs={{0,2},{1,3},{2,0},{3,1},{4,6},{5,7},{6,4},{7,5},{8,10},{9,11},{10,... | collective-permute-start | bytes 221192 | tf_op jit(solution)/shard_map/ppermute | solution.py:482
  35.6 2.1 %shard_map.150 = (f32[4,64,128]{2,1,0:T(8,128)}, f32[4,64,128]{2,1,0:T(8,128)}, f32[144,128]{1,0:T(8,128)S(1)}, s32[8,128]{1,0:T(8,128)S(1)}) custom-call(f32[21,64,128]{2,1,0:T(8,128)S(1)} %get-tuple-element.47.fields.refs_0_, f32[21,72,256]{2,1,0:T(8,128)S(1)} %get-tuple-element.69.planes, f32[4,72,256]{2,1,0:T(8,128)S(1)} %get-tuple-element.70.mids, ...), custom_call_target="tpu_custom_call" | custom-call | flops 134217728 | tf_op jit(solution)/shard_map/pallas_call | solution.py:621
  37.7 1.8 %collective-permute-done.5 = f32[144,128]{1,0:T(8,128)S(1)} collective-permute-done((f32[144,128]{1,0:T(8,128)S(1)}, f32[144,128]{1,0:T(8,128)S(1)}, u32[]{:S(2)}, u32[]{:S(2)}) %collective-permute-start.5) | collective-permute-done | bytes 73760 | tf_op jit(solution)/shard_map/ppermute | solution.py:482
  39.6 3.8 %collective-permute-start.8 = (f32[144,128]{1,0:T(8,128)S(1)}, f32[144,128]{1,0:T(8,128)S(1)}, u32[]{:S(2)}, u32[]{:S(2)}) collective-permute-start(f32[144,128]{1,0:T(8,128)S(1)} %add.12), channel_id=1, source_target_pairs={{0,12},{4,8},{8,4},{12,0},{1,13},{5,9},{9,5},{13,1},{2,14},{6,10},... | collective-permute-start | bytes 221192 | tf_op jit(solution)/shard_map/ppermute | solution.py:482
  43.3 0.0 collective-permute-start.7
  43.3 0.7 %collective-permute-start.6 = (f32[144,128]{1,0:T(8,128)S(1)}, f32[144,128]{1,0:T(8,128)S(1)}, u32[]{:S(2)}, u32[]{:S(2)}) collective-permute-start(f32[144,128]{1,0:T(8,128)S(1)} %add.12), channel_id=1, source_target_pairs={{0,4},{4,0},{8,12},{12,8},{1,5},{5,1},{9,13},{13,9},{2,6},{6,2},{1... | collective-permute-start | bytes 221192 | tf_op jit(solution)/shard_map/ppermute | solution.py:482
  44.0 2.3 %collective-permute-done.8 = f32[144,128]{1,0:T(8,128)S(1)} collective-permute-done((f32[144,128]{1,0:T(8,128)S(1)}, f32[144,128]{1,0:T(8,128)S(1)}, u32[]{:S(2)}, u32[]{:S(2)}) %collective-permute-start.8) | collective-permute-done | bytes 73760 | tf_op jit(solution)/shard_map/ppermute | solution.py:482
  46.3 2.9 %collective-permute-done.7 = f32[144,128]{1,0:T(8,128)S(1)} collective-permute-done((f32[144,128]{1,0:T(8,128)S(1)}, f32[144,128]{1,0:T(8,128)S(1)}, u32[]{:S(2)}, u32[]{:S(2)}) %collective-permute-start.7) | collective-permute-done | bytes 73760 | tf_op jit(solution)/shard_map/ppermute | solution.py:482
  49.2 0.0 collective-permute-done.6
  49.3 0.4 collective-permute-start.9
  49.7 4.0 %collective-permute-done.9 = f32[144,128]{1,0:T(8,128)S(1)} collective-permute-done((f32[144,128]{1,0:T(8,128)S(1)}, f32[144,128]{1,0:T(8,128)S(1)}, u32[]{:S(2)}, u32[]{:S(2)}) %collective-permute-start.9) | collective-permute-done | bytes 73760 | tf_op jit(solution)/shard_map/ppermute | solution.py:482
  53.7 0.1 collective-permute-start.10
  53.8 1.4 %collective-permute-done.10 = f32[288,128]{1,0:T(8,128)S(1)} collective-permute-done((f32[288,128]{1,0:T(8,128)S(1)}, f32[288,128]{1,0:T(8,128)S(1)}, u32[]{:S(2)}, u32[]{:S(2)}) %collective-permute-start.10) | collective-permute-done | bytes 147488 | tf_op jit(solution)/shard_map/ppermute | solution.py:482
  55.2 0.7 %shard_map.151 = (f32[12,256]{1,0:T(8,128)}, f32[256,256]{1,0:T(8,128)}, f32[4,256]{1,0:T(4,128)}) custom-call(f32[576,128]{1,0:T(8,128)S(1)} %pad_maximum_fusion.terms), custom_call_target="tpu_custom_call" | custom-call | tf_op jit(solution)/shard_map/pallas_call | solution.py:640
  (9 shorter events, 0.1 us)
Async XLA Ops:
  2.4 7.1 %collective-permute-start = (f32[64,128]{1,0:T(8,128)S(1)}, f32[64,128]{1,0:T(8,128)S(1)}, u32[]{:S(2)}, u32[]{:S(2)}) collective-permute-start(f32[64,128]{1,0:T(8,128)S(1)} %get-tuple-element.48), channel_id=1, source_target_pairs={{0,4},{4,8},{8,12},{12,0},{1,5},{5,9},{9,13},{13,1},{2,6},{6,10},{... | collective-permute-start | bytes 98312 | tf_op jit(solution)/shard_map/ppermute | solution.py:478
  5.5 4.3 %collective-permute-start.1 = (f32[64,128]{1,0:T(8,128)S(1)}, f32[64,128]{1,0:T(8,128)S(1)}, u32[]{:S(2)}, u32[]{:S(2)}) collective-permute-start(f32[64,128]{1,0:T(8,128)S(1)} %get-tuple-element.49), channel_id=1, source_target_pairs={{0,12},{4,0},{8,4},{12,8},{1,13},{5,1},{9,5},{13,9},{2,14},{6,2},{... | collective-permute-start | bytes 98312 | tf_op jit(solution)/shard_map/ppermute | solution.py:478
  9.7 3.5 %collective-permute-start.2 = (f32[23,4,128]{2,1,0:T(4,128)S(1)}, f32[23,4,128]{2,1,0:T(4,128)S(1)}, u32[]{:S(2)}, u32[]{:S(2)}) collective-permute-start(f32[23,4,128]{2,1,0:T(4,128)S(1)} %get-tuple-element.52), channel_id=1, source_target_pairs={{0,1},{1,2},{2,3},{3,0},{4,5},{5,6},{6,7},{7,4},{8,9},{9,10},{10,1... | collective-permute-start | bytes 141320 | tf_op jit(solution)/shard_map/ppermute | solution.py:478
  9.8 3.5 %collective-permute-start.3 = (f32[23,4,128]{2,1,0:T(4,128)S(1)}, f32[23,4,128]{2,1,0:T(4,128)S(1)}, u32[]{:S(2)}, u32[]{:S(2)}) collective-permute-start(f32[23,4,128]{2,1,0:T(4,128)S(1)} %get-tuple-element.53), channel_id=1, source_target_pairs={{0,3},{1,0},{2,1},{3,2},{4,7},{5,4},{6,5},{7,6},{8,11},{9,8},{10,9... | collective-permute-start | bytes 141320 | tf_op jit(solution)/shard_map/ppermute | solution.py:478
  32.2 2.7 %collective-permute-start.4 = (f32[288,128]{1,0:T(8,128)S(1)}, f32[288,128]{1,0:T(8,128)S(1)}, u32[]{:S(2)}, u32[]{:S(2)}) collective-permute-start(f32[288,128]{1,0:T(8,128)S(1)} %get-tuple-element.76), channel_id=1, source_target_pairs={{0,1},{1,0},{2,3},{3,2},{4,5},{5,4},{6,7},{7,6},{8,9},{9,8},{10,11... | collective-permute-start | bytes 442376 | tf_op jit(solution)/shard_map/ppermute | solution.py:482
  34.9 4.6 %collective-permute-start.5 = (f32[144,128]{1,0:T(8,128)S(1)}, f32[144,128]{1,0:T(8,128)S(1)}, u32[]{:S(2)}, u32[]{:S(2)}) collective-permute-start(f32[144,128]{1,0:T(8,128)S(1)} %get-tuple-element.83), channel_id=1, source_target_pairs={{0,2},{1,3},{2,0},{3,1},{4,6},{5,7},{6,4},{7,5},{8,10},{9,11},{10,... | collective-permute-start | bytes 221192 | tf_op jit(solution)/shard_map/ppermute | solution.py:482
  39.6 6.8 %collective-permute-start.8 = (f32[144,128]{1,0:T(8,128)S(1)}, f32[144,128]{1,0:T(8,128)S(1)}, u32[]{:S(2)}, u32[]{:S(2)}) collective-permute-start(f32[144,128]{1,0:T(8,128)S(1)} %add.12), channel_id=1, source_target_pairs={{0,12},{4,8},{8,4},{12,0},{1,13},{5,9},{9,5},{13,1},{2,14},{6,10},... | collective-permute-start | bytes 221192 | tf_op jit(solution)/shard_map/ppermute | solution.py:482
  43.3 5.9 %collective-permute-start.7 = (f32[144,128]{1,0:T(8,128)S(1)}, f32[144,128]{1,0:T(8,128)S(1)}, u32[]{:S(2)}, u32[]{:S(2)}) collective-permute-start(f32[144,128]{1,0:T(8,128)S(1)} %add.12), channel_id=1, source_target_pairs={{0,8},{4,12},{8,0},{12,4},{1,9},{5,13},{9,1},{13,5},{2,10},{6,14},... | collective-permute-start | bytes 221192 | tf_op jit(solution)/shard_map/ppermute | solution.py:482
  43.3 5.9 %collective-permute-start.6 = (f32[144,128]{1,0:T(8,128)S(1)}, f32[144,128]{1,0:T(8,128)S(1)}, u32[]{:S(2)}, u32[]{:S(2)}) collective-permute-start(f32[144,128]{1,0:T(8,128)S(1)} %add.12), channel_id=1, source_target_pairs={{0,4},{4,0},{8,12},{12,8},{1,5},{5,1},{9,13},{13,9},{2,6},{6,2},{1... | collective-permute-start | bytes 221192 | tf_op jit(solution)/shard_map/ppermute | solution.py:482
  49.3 4.4 %collective-permute-start.9 = (f32[144,128]{1,0:T(8,128)S(1)}, f32[144,128]{1,0:T(8,128)S(1)}, u32[]{:S(2)}, u32[]{:S(2)}) collective-permute-start(f32[144,128]{1,0:T(8,128)S(1)} %add_add_fusion), channel_id=1, source_target_pairs={{0,2},{1,3},{2,0},{3,1},{4,6},{5,7},{6,4},{7,5},{8,10},{9,11},{10,... | collective-permute-start | bytes 221192 | tf_op jit(solution)/shard_map/ppermute | solution.py:482
  53.7 1.4 %collective-permute-start.10 = (f32[288,128]{1,0:T(8,128)S(1)}, f32[288,128]{1,0:T(8,128)S(1)}, u32[]{:S(2)}, u32[]{:S(2)}) collective-permute-start(f32[288,128]{1,0:T(8,128)S(1)} %pad_maximum_fusion.1), channel_id=1, source_target_pairs={{0,1},{1,0},{2,3},{3,2},{4,5},{5,4},{6,7},{7,6},{8,9},{9,8},{10,11... | collective-permute-start | bytes 442376 | tf_op jit(solution)/shard_map/ppermute | solution.py:482

commit v17 on v16

--- a/solution.py
+++ b/solution.py
@@ -351,14 +351,23 @@
     for k, ref in enumerate(early[2::3]):
         cl[pl.ds(k * ref.shape[0], ref.shape[0]), :] = ref[...]
 
-    def first_part(base, tiles):
+    def first_part(at, tiles):
+        base = rows + at
         first, second, unused, low_second = yield from forward_stages(inputs_at(ft1, base, tiles), wi_t, wm_t)
-        halo1[...] = first
-        halo2[...] = second
+        halo1[:, pl.ds(at * LANES, tiles * LANES)] = first
+        halo2[:, pl.ds(at * LANES, tiles * LANES)] = second
         yield
         put_lanes(cl, SHALLOW, base, tiles, closure(low_second, wo_t))
 
-    staggered([first_part(rows, len(block.rim))])
+    def second_cotangents():
+        for level in range(levels):
+            masked = planes[block.wet] * (2.0 * DT * planes[3 * levels + level])
+            block.spread(masked, level, SHALLOW, dc, dcx, dch, False)
+            yield
+        block.pack_halo(block.outer, SHALLOW, dc, dcx, dch)
+
+    half = len(block.rim) // 2
+    staggered([first_part(0, half), first_part(half, len(block.rim) - half), second_cotangents()])
     block.unpack_halo(block.rim, SHALLOW, cl, clx, clh)
     for level in range(levels):
         closed = block.gathered(level, SHALLOW, cl, clx, clh, True)
@@ -368,10 +377,6 @@
     copies = copied_out([(o_mid, h_mid)], sems.at[pl.ds(0, 1)])
 
     features_of(mids, ft2, block.outer, False)
-    for level in range(levels):
-        masked = planes[block.wet] * (2.0 * DT * planes[3 * levels + level])
-        block.spread(masked, level, SHALLOW, dc, dcx, dch, False)
-    block.pack_halo(block.outer, SHALLOW, dc, dcx, dch)
     sums = [None] * 3
     staggered(
         [second_part(rows, len(block.outer), None, None)]

time: 56.1 us -> 56.1 us (level)
  no operation moved by 1% of the time
where the time goes in v17:
time: 56.1 us; the launch traced here: 56 us
  Pallas kernels  26.9 us (48%)
  starting transfers between devices  14.2 us (25%)
  waiting for transfers between devices  14 us (25%)
  between operations  0.72 us (1%)
    pallas_call x1, Pallas kernels, body(): pl.pallas_call(functools.partial(main_kernel, bands), out_shape=(field, f...  18.9 us
    ppermute x7, waiting for transfers between devices, swapped(): lax.ppermute(value, axis, [(i, i ^ bit) for i in range(lax.axis_size(axis...  13.4 us
    ppermute x7, starting transfers between devices, swapped(): lax.ppermute(value, axis, [(i, i ^ bit) for i in range(lax.axis_size(axis...  7.25 us
    ppermute x4, starting transfers between devices, along(): lax.ppermute(value, axis, [(i, (i + step) % count) for i in range(count)])  6.96 us
    pallas_call x2, Pallas kernels, early(): pl.pallas_call(functools.partial(early_kernel, k * tall), out_shape=(kept...  3.36 us
    pallas_call x1, Pallas kernels, body(): pl.pallas_call(late_kernel, out_shape=(field, field, half_terms(bands)[0]...  2.13 us
    pallas_call x1, Pallas kernels, body(): pl.pallas_call(pack_kernel, out_shape=(strip, strip, edge, edge, jax.Shap...  1.74 us
  transfers between devices with their start and end apart: 11, of which 9 were waited for; matrix products, arithmetic and copies ran while one was open for 0% of the time, Pallas kernels for 10%

profile of v17, /device:TPU:0, one launch (start us, length us, event | category | flops | bytes accessed | tf_op | source)
XLA Modules:
  0.0 56.0 jit_solution(2723897535024223260)
XLA Ops:
  0.6 1.7 %shard_map.144 = (f32[64,128]{1,0:T(8,128)S(1)}, f32[64,128]{1,0:T(8,128)S(1)}, f32[21,4,128]{2,1,0:T(4,128)S(1)}, f32[21,4,128]{2,1,0:T(4,128)S(1)}, f32[21,64,...) custom-call(f32[4,64,128]{2,1,0:T(8,128)} %now.1, ...), custom_call_target="tpu_custom_call" | custom-call | tf_op jit(solution)/shard_map/pallas_call | solution.py:527
  2.4 3.1 %collective-permute-start = (f32[64,128]{1,0:T(8,128)S(1)}, f32[64,128]{1,0:T(8,128)S(1)}, u32[]{:S(2)}, u32[]{:S(2)}) collective-permute-start(f32[64,128]{1,0:T(8,128)S(1)} %get-tuple-element.48), channel_id=1, source_target_pairs={{0,4},{4,8},{8,12},{12,0},{1,5},{5,9},{9,13},{13,1},{2,6},{6,10},{... | collective-permute-start | bytes 98312 | tf_op jit(solution)/shard_map/ppermute | solution.py:483
  5.5 2.1 %collective-permute-start.1 = (f32[64,128]{1,0:T(8,128)S(1)}, f32[64,128]{1,0:T(8,128)S(1)}, u32[]{:S(2)}, u32[]{:S(2)}) collective-permute-start(f32[64,128]{1,0:T(8,128)S(1)} %get-tuple-element.49), channel_id=1, source_target_pairs={{0,12},{4,0},{8,4},{12,8},{1,13},{5,1},{9,5},{13,9},{2,14},{6,2},{... | collective-permute-start | bytes 98312 | tf_op jit(solution)/shard_map/ppermute | solution.py:483
  7.6 1.7 %shard_map.146 = (f32[4,256,1024]{2,1,0:T(8,128)S(1)}, f32[4,256,1024]{2,1,0:T(8,128)S(1)}, f32[256,128]{1,0:T(8,128)S(1)}, bf16[16,256]{1,0:T(8,128)(2,1)S(1)},...) custom-call(f32[21,64,128]{2,1,0:T(8,128)S(1)} %get-tuple-element.47, ...), custom_call_target="tpu_custom_call" | custom-call | flops 1610612736 | tf_op jit(solution)/shard_map/pallas_call | solution.py:543
  9.3 0.2 collective-permute-done.left.refs_0_.refs_1_
  9.5 0.2 collective-permute-done.1.right.refs_2_
  9.7 0.1 collective-permute-start.2
  9.8 1.7 %collective-permute-start.3 = (f32[23,4,128]{2,1,0:T(4,128)S(1)}, f32[23,4,128]{2,1,0:T(4,128)S(1)}, u32[]{:S(2)}, u32[]{:S(2)}) collective-permute-start(f32[23,4,128]{2,1,0:T(4,128)S(1)} %get-tuple-element.53), channel_id=1, source_target_pairs={{0,3},{1,0},{2,1},{3,2},{4,7},{5,4},{6,5},{7,6},{8,11},{9,8},{10,9... | collective-permute-start | bytes 141320 | tf_op jit(solution)/shard_map/ppermute | solution.py:483
  11.5 1.6 %shard_map.147 = (f32[4,256,1024]{2,1,0:T(8,128)S(1)}, f32[4,256,1024]{2,1,0:T(8,128)S(1)}, f32[256,128]{1,0:T(8,128)S(1)}) custom-call(f32[21,64,128]{2,1,0:T(8,128)S(1)} %get-tuple-element.47.fields.refs_0_, f32[64,128]{1,0:T(8,128)S(1)} %collective-permute-done.left.refs_0_.refs_1_, bf16[256,16]{1,0:T(8,128)(2,1)S(1)} %get-tuple-element.58.refs_1_.refs_6_, ...), custom_call_target="tpu_custom_call" | custom-call | flops 1610612736 | tf_op jit(solution)/shard_map/pallas_call | solution.py:543
  13.2 0.1 collective-permute-done.2.refs_3_
  13.3 0.0 collective-permute-done.3.refs_4_
  13.3 18.9 %shard_map.148 = (f32[4,64,128]{2,1,0:T(8,128)}, f32[4,64,128]{2,1,0:T(8,128)}, f32[288,128]{1,0:T(8,128)S(1)}, f32[288,128]{1,0:T(8,128)S(1)}, f32[21,72,256]{2...) custom-call(f32[21,64,128]{2,1,0:T(8,128)S(1)} %get-tuple-element.47, ...), custom_call_target="tpu_custom_call" | custom-call | tf_op jit(solution)/shard_map/pallas_call | solution.py:588
  32.2 1.7 %collective-permute-start.4 = (f32[288,128]{1,0:T(8,128)S(1)}, f32[288,128]{1,0:T(8,128)S(1)}, u32[]{:S(2)}, u32[]{:S(2)}) collective-permute-start(f32[288,128]{1,0:T(8,128)S(1)} %get-tuple-element.76), channel_id=1, source_target_pairs={{0,1},{1,0},{2,3},{3,2},{4,5},{5,4},{6,7},{7,6},{8,9},{9,8},{10,11... | collective-permute-start | bytes 442376 | tf_op jit(solution)/shard_map/ppermute | solution.py:487
  33.9 1.0 %collective-permute-done.4.got = f32[288,128]{1,0:T(8,128)S(1)} collective-permute-done((f32[288,128]{1,0:T(8,128)S(1)}, f32[288,128]{1,0:T(8,128)S(1)}, u32[]{:S(2)}, u32[]{:S(2)}) %collective-permute-start.4) | collective-permute-done | bytes 147488 | tf_op jit(solution)/shard_map/ppermute | solution.py:487
  35.0 0.6 %collective-permute-start.5 = (f32[144,128]{1,0:T(8,128)S(1)}, f32[144,128]{1,0:T(8,128)S(1)}, u32[]{:S(2)}, u32[]{:S(2)}) collective-permute-start(f32[144,128]{1,0:T(8,128)S(1)} %get-tuple-element.83), channel_id=1, source_target_pairs={{0,2},{1,3},{2,0},{3,1},{4,6},{5,7},{6,4},{7,5},{8,10},{9,11},{10,... | collective-permute-start | bytes 221192 | tf_op jit(solution)/shard_map/ppermute | solution.py:487
  35.6 2.1 %shard_map.150 = (f32[4,64,128]{2,1,0:T(8,128)}, f32[4,64,128]{2,1,0:T(8,128)}, f32[144,128]{1,0:T(8,128)S(1)}, s32[8,128]{1,0:T(8,128)S(1)}) custom-call(f32[21,64,128]{2,1,0:T(8,128)S(1)} %get-tuple-element.47.fields.refs_0_, f32[21,72,256]{2,1,0:T(8,128)S(1)} %get-tuple-element.69.planes, f32[4,72,256]{2,1,0:T(8,128)S(1)} %get-tuple-element.70.mids, ...), custom_call_target="tpu_custom_call" | custom-call | flops 134217728 | tf_op jit(solution)/shard_map/pallas_call | solution.py:626
  37.7 1.8 %collective-permute-done.5 = f32[144,128]{1,0:T(8,128)S(1)} collective-permute-done((f32[144,128]{1,0:T(8,128)S(1)}, f32[144,128]{1,0:T(8,128)S(1)}, u32[]{:S(2)}, u32[]{:S(2)}) %collective-permute-start.5) | collective-permute-done | bytes 73760 | tf_op jit(solution)/shard_map/ppermute | solution.py:487
  39.6 3.8 %collective-permute-start.8 = (f32[144,128]{1,0:T(8,128)S(1)}, f32[144,128]{1,0:T(8,128)S(1)}, u32[]{:S(2)}, u32[]{:S(2)}) collective-permute-start(f32[144,128]{1,0:T(8,128)S(1)} %add.12), channel_id=1, source_target_pairs={{0,12},{4,8},{8,4},{12,0},{1,13},{5,9},{9,5},{13,1},{2,14},{6,10},... | collective-permute-start | bytes 221192 | tf_op jit(solution)/shard_map/ppermute | solution.py:487
  43.3 0.0 collective-permute-start.7
  43.3 0.7 %collective-permute-start.6 = (f32[144,128]{1,0:T(8,128)S(1)}, f32[144,128]{1,0:T(8,128)S(1)}, u32[]{:S(2)}, u32[]{:S(2)}) collective-permute-start(f32[144,128]{1,0:T(8,128)S(1)} %add.12), channel_id=1, source_target_pairs={{0,4},{4,0},{8,12},{12,8},{1,5},{5,1},{9,13},{13,9},{2,6},{6,2},{1... | collective-permute-start | bytes 221192 | tf_op jit(solution)/shard_map/ppermute | solution.py:487
  44.0 2.3 %collective-permute-done.8 = f32[144,128]{1,0:T(8,128)S(1)} collective-permute-done((f32[144,128]{1,0:T(8,128)S(1)}, f32[144,128]{1,0:T(8,128)S(1)}, u32[]{:S(2)}, u32[]{:S(2)}) %collective-permute-start.8) | collective-permute-done | bytes 73760 | tf_op jit(solution)/shard_map/ppermute | solution.py:487
  46.4 2.9 %collective-permute-done.7 = f32[144,128]{1,0:T(8,128)S(1)} collective-permute-done((f32[144,128]{1,0:T(8,128)S(1)}, f32[144,128]{1,0:T(8,128)S(1)}, u32[]{:S(2)}, u32[]{:S(2)}) %collective-permute-start.7) | collective-permute-done | bytes 73760 | tf_op jit(solution)/shard_map/ppermute | solution.py:487
  49.3 0.0 collective-permute-done.6
  49.3 0.4 collective-permute-start.9
  49.7 4.0 %collective-permute-done.9 = f32[144,128]{1,0:T(8,128)S(1)} collective-permute-done((f32[144,128]{1,0:T(8,128)S(1)}, f32[144,128]{1,0:T(8,128)S(1)}, u32[]{:S(2)}, u32[]{:S(2)}) %collective-permute-start.9) | collective-permute-done | bytes 73760 | tf_op jit(solution)/shard_map/ppermute | solution.py:487
  53.7 0.1 collective-permute-start.10
  53.8 1.4 %collective-permute-done.10 = f32[288,128]{1,0:T(8,128)S(1)} collective-permute-done((f32[288,128]{1,0:T(8,128)S(1)}, f32[288,128]{1,0:T(8,128)S(1)}, u32[]{:S(2)}, u32[]{:S(2)}) %collective-permute-start.10) | collective-permute-done | bytes 147488 | tf_op jit(solution)/shard_map/ppermute | solution.py:487
  55.2 0.7 %shard_map.151 = (f32[12,256]{1,0:T(8,128)}, f32[256,256]{1,0:T(8,128)}, f32[4,256]{1,0:T(4,128)}) custom-call(f32[576,128]{1,0:T(8,128)S(1)} %pad_maximum_fusion.terms), custom_call_target="tpu_custom_call" | custom-call | tf_op jit(solution)/shard_map/pallas_call | solution.py:645
  (9 shorter events, 0.1 us)
Async XLA Ops:
  2.4 7.1 %collective-permute-start = (f32[64,128]{1,0:T(8,128)S(1)}, f32[64,128]{1,0:T(8,128)S(1)}, u32[]{:S(2)}, u32[]{:S(2)}) collective-permute-start(f32[64,128]{1,0:T(8,128)S(1)} %get-tuple-element.48), channel_id=1, source_target_pairs={{0,4},{4,8},{8,12},{12,0},{1,5},{5,9},{9,13},{13,1},{2,6},{6,10},{... | collective-permute-start | bytes 98312 | tf_op jit(solution)/shard_map/ppermute | solution.py:483
  5.5 4.3 %collective-permute-start.1 = (f32[64,128]{1,0:T(8,128)S(1)}, f32[64,128]{1,0:T(8,128)S(1)}, u32[]{:S(2)}, u32[]{:S(2)}) collective-permute-start(f32[64,128]{1,0:T(8,128)S(1)} %get-tuple-element.49), channel_id=1, source_target_pairs={{0,12},{4,0},{8,4},{12,8},{1,13},{5,1},{9,5},{13,9},{2,14},{6,2},{... | collective-permute-start | bytes 98312 | tf_op jit(solution)/shard_map/ppermute | solution.py:483
  9.7 3.5 %collective-permute-start.2 = (f32[23,4,128]{2,1,0:T(4,128)S(1)}, f32[23,4,128]{2,1,0:T(4,128)S(1)}, u32[]{:S(2)}, u32[]{:S(2)}) collective-permute-start(f32[23,4,128]{2,1,0:T(4,128)S(1)} %get-tuple-element.52), channel_id=1, source_target_pairs={{0,1},{1,2},{2,3},{3,0},{4,5},{5,6},{6,7},{7,4},{8,9},{9,10},{10,1... | collective-permute-start | bytes 141320 | tf_op jit(solution)/shard_map/ppermute | solution.py:483
  9.8 3.5 %collective-permute-start.3 = (f32[23,4,128]{2,1,0:T(4,128)S(1)}, f32[23,4,128]{2,1,0:T(4,128)S(1)}, u32[]{:S(2)}, u32[]{:S(2)}) collective-permute-start(f32[23,4,128]{2,1,0:T(4,128)S(1)} %get-tuple-element.53), channel_id=1, source_target_pairs={{0,3},{1,0},{2,1},{3,2},{4,7},{5,4},{6,5},{7,6},{8,11},{9,8},{10,9... | collective-permute-start | bytes 141320 | tf_op jit(solution)/shard_map/ppermute | solution.py:483
  32.2 2.7 %collective-permute-start.4 = (f32[288,128]{1,0:T(8,128)S(1)}, f32[288,128]{1,0:T(8,128)S(1)}, u32[]{:S(2)}, u32[]{:S(2)}) collective-permute-start(f32[288,128]{1,0:T(8,128)S(1)} %get-tuple-element.76), channel_id=1, source_target_pairs={{0,1},{1,0},{2,3},{3,2},{4,5},{5,4},{6,7},{7,6},{8,9},{9,8},{10,11... | collective-permute-start | bytes 442376 | tf_op jit(solution)/shard_map/ppermute | solution.py:487
  35.0 4.6 %collective-permute-start.5 = (f32[144,128]{1,0:T(8,128)S(1)}, f32[144,128]{1,0:T(8,128)S(1)}, u32[]{:S(2)}, u32[]{:S(2)}) collective-permute-start(f32[144,128]{1,0:T(8,128)S(1)} %get-tuple-element.83), channel_id=1, source_target_pairs={{0,2},{1,3},{2,0},{3,1},{4,6},{5,7},{6,4},{7,5},{8,10},{9,11},{10,... | collective-permute-start | bytes 221192 | tf_op jit(solution)/shard_map/ppermute | solution.py:487
  39.6 6.8 %collective-permute-start.8 = (f32[144,128]{1,0:T(8,128)S(1)}, f32[144,128]{1,0:T(8,128)S(1)}, u32[]{:S(2)}, u32[]{:S(2)}) collective-permute-start(f32[144,128]{1,0:T(8,128)S(1)} %add.12), channel_id=1, source_target_pairs={{0,12},{4,8},{8,4},{12,0},{1,13},{5,9},{9,5},{13,1},{2,14},{6,10},... | collective-permute-start | bytes 221192 | tf_op jit(solution)/shard_map/ppermute | solution.py:487
  43.3 5.9 %collective-permute-start.7 = (f32[144,128]{1,0:T(8,128)S(1)}, f32[144,128]{1,0:T(8,128)S(1)}, u32[]{:S(2)}, u32[]{:S(2)}) collective-permute-start(f32[144,128]{1,0:T(8,128)S(1)} %add.12), channel_id=1, source_target_pairs={{0,8},{4,12},{8,0},{12,4},{1,9},{5,13},{9,1},{13,5},{2,10},{6,14},... | collective-permute-start | bytes 221192 | tf_op jit(solution)/shard_map/ppermute | solution.py:487
  43.3 5.9 %collective-permute-start.6 = (f32[144,128]{1,0:T(8,128)S(1)}, f32[144,128]{1,0:T(8,128)S(1)}, u32[]{:S(2)}, u32[]{:S(2)}) collective-permute-start(f32[144,128]{1,0:T(8,128)S(1)} %add.12), channel_id=1, source_target_pairs={{0,4},{4,0},{8,12},{12,8},{1,5},{5,1},{9,13},{13,9},{2,6},{6,2},{1... | collective-permute-start | bytes 221192 | tf_op jit(solution)/shard_map/ppermute | solution.py:487
  49.3 4.4 %collective-permute-start.9 = (f32[144,128]{1,0:T(8,128)S(1)}, f32[144,128]{1,0:T(8,128)S(1)}, u32[]{:S(2)}, u32[]{:S(2)}) collective-permute-start(f32[144,128]{1,0:T(8,128)S(1)} %add_add_fusion), channel_id=1, source_target_pairs={{0,2},{1,3},{2,0},{3,1},{4,6},{5,7},{6,4},{7,5},{8,10},{9,11},{10,... | collective-permute-start | bytes 221192 | tf_op jit(solution)/shard_map/ppermute | solution.py:487
  53.7 1.4 %collective-permute-start.10 = (f32[288,128]{1,0:T(8,128)S(1)}, f32[288,128]{1,0:T(8,128)S(1)}, u32[]{:S(2)}, u32[]{:S(2)}) collective-permute-start(f32[288,128]{1,0:T(8,128)S(1)} %pad_maximum_fusion.1), channel_id=1, source_target_pairs={{0,1},{1,0},{2,3},{3,2},{4,5},{5,4},{6,7},{7,6},{8,9},{9,8},{10,11... | collective-permute-start | bytes 442376 | tf_op jit(solution)/shard_map/ppermute | solution.py:487
